TPU v7x, 32 devices: a whole 2x2x4 slice. The times are simulated.
32 devices in a mesh: seq: 4 (over y, x), exp: 8 (over z, core).
Axes of the slice: x: 2, y: 2, z: 4, core: 2. Of those that a mesh axis runs over, the one named last changes fastest.
Arguments:
- hidden_in: bfloat16 [2048, 2048], P(('seq', 'exp')), may hold values from -6 to 6
- query_proj: bfloat16 [2048, 2048], P('seq', 'exp'), may hold values from -40 to 40
- key_proj: bfloat16 [2048, 2048], P('seq', 'exp'), may hold values from -40 to 40
- value_proj: bfloat16 [2048, 4096], P('seq', 'exp'), may hold values from -6 to 6
- gate_proj: bfloat16 [2048, 4096], P('seq', 'exp'), may hold values from -6 to 6
- log_decay: float32 [32, 2048], P('exp', 'seq'), may hold values from -0.6 to 0
- write_rate: float32 [32, 2048], P('exp', 'seq'), may hold values from 0 to 1
- head_gain: float32 [128], replicated, may hold values from 0.1 to 1.9
- out_weight: bfloat16 [4096, 2048], P('exp'), may hold values from -0.09375 to 0.09375
- post_gain: float32 [2048], replicated, may hold values from 0.1 to 1.9
- expert_ids: int32 [2048, 4], P(('seq', 'exp')), may hold values from 0 to 7, all different within a row; in each aligned block of 64 rows (0 to 63, 64 to 127, ...) at most 64 rows name the same one
- route_weight: bfloat16 [2048, 4], P(('seq', 'exp')), may hold values from 0.19921875 to 1
- gate_weight: bfloat16 [8, 2048, 512], P('exp'), may hold values from -0.125 to 0.125
- up_weight: bfloat16 [8, 2048, 512], P('exp'), may hold values from -0.125 to 0.125
- down_weight: bfloat16 [8, 512, 2048], P('exp'), may hold values from -0.25 to 0.25
Outputs:
- layer_out: bfloat16 [2048, 2048], P(('seq', 'exp'))
Inputs may be any that keep to these rules, and one draw needn't show every extreme that they name: `expert_ids`: each token names 4 different experts. Within the tokens of one device (aligned blocks of 64 tokens in sequence order) no expert is named by more than 64 tokens, and in every draw some block names some expert exactly 64 times.
All inputs are finite; a program needn't handle non-finite values.
Results may differ from a plain program's by a relative error of at most 0.02.
Values may be sent and summed in bfloat16 or wider, within the bound.
No kernel may reach another device: no remote copies, remote signals or barrier semaphores. Data moves between devices by JAX's collectives and lax.ppermute only.
A program may use at most 128 MiB of HBM per device.

v0:
```python
import functools

import jax
import jax.numpy as jnp
from jax import lax
from jax.experimental import pallas as pl
from jax.experimental.pallas import tpu as pltpu
from jax.sharding import PartitionSpec as P

DK = 128
DV = 128
EPS = 1e-06
BLOCK = 128
LANES = 128
F32 = jnp.float32
BF16 = jnp.bfloat16
EXACT = lax.Precision.HIGHEST
VMEM_BYTES = 48 * 1024 * 1024


def whole(memory_space=pltpu.VMEM):
    return pl.BlockSpec(memory_space=memory_space)


def mm(a, b):
    return jnp.dot(a.astype(BF16), b.astype(BF16), preferred_element_type=F32)


def mm_nt(a, b, precision=None):
    return lax.dot_general(
        a, b, (((1,), (1,)), ((), ())), preferred_element_type=F32, precision=precision
    )


def split(a):
    high = a.astype(BF16)
    return high, (a - high.astype(F32)).astype(BF16)


def mm_left2(a, b):
    high, low = split(a)
    return jnp.dot(
        jnp.concatenate([high, low], axis=1),
        jnp.concatenate([b, b], axis=0),
        preferred_element_type=F32,
    )


def mm_right2(a, b):
    high, low = split(b)
    return jnp.dot(
        jnp.concatenate([a, a], axis=1),
        jnp.concatenate([high, low], axis=0),
        preferred_element_type=F32,
    )


def mm_both2(a, b):
    a_high, a_low = split(a)
    b_high, b_low = split(b)
    return jnp.dot(
        jnp.concatenate([a_high, a_low, a_high], axis=1),
        jnp.concatenate([b_high, b_high, b_low], axis=0),
        preferred_element_type=F32,
    )


def grids():
    row = lax.broadcasted_iota(jnp.int32, (BLOCK, BLOCK), 0)
    col = lax.broadcasted_iota(jnp.int32, (BLOCK, BLOCK), 1)
    return row, col


def stacked(ref, blocks):
    return jnp.concatenate([ref[:, c * BLOCK : (c + 1) * BLOCK] for c in range(blocks)], axis=0)


def decays(decay_ref, blocks, row, col):
    by_row = stacked(decay_ref, blocks)
    upto = jnp.where(row >= col, 1.0, 0.0).astype(F32)
    cum_rows = mm_nt(by_row, upto, EXACT)
    cum_cols = mm_nt(upto, by_row, EXACT)
    return cum_rows, cum_cols


def state_kernel(key_ref, value_ref, decay_ref, rate_ref, wu_ref, prefix_ref, total_ref):
    heads = decay_ref.shape[0]
    key_heads = key_ref.shape[1] // DK
    group = heads // key_heads
    blocks = key_ref.shape[0] // BLOCK
    row, col = grids()
    gap_bits = jnp.bitwise_xor(row, col)
    strict = row > col
    diagonal = row == col
    eye = jnp.where(diagonal, 1.0, 0.0).astype(F32)
    cum_rows, cum_cols = decays(decay_ref, blocks, row, col)
    rate_rows = stacked(rate_ref, blocks)
    rate_cols = mm_nt(eye, rate_rows, EXACT)
    carried = [None] * heads
    for c in range(blocks):
        tokens = slice(c * BLOCK, (c + 1) * BLOCK)
        keys, keys_t, grams, unit_rows, unit_cols = [], [], [], [], []
        for g in range(key_heads):
            key = key_ref[tokens, g * DK : (g + 1) * DK]
            gram = mm_nt(key, key)
            on_diagonal = jnp.where(diagonal, gram, 0.0)
            unit_rows.append(lax.rsqrt(jnp.sum(on_diagonal, axis=0, keepdims=True) + EPS))
            unit_cols.append(lax.rsqrt(jnp.sum(on_diagonal, axis=1, keepdims=True) + EPS))
            keys.append(key)
            keys_t.append(key.astype(F32).T.astype(BF16))
            grams.append(gram * unit_rows[g] * unit_cols[g])
        lower, solve = [], []
        for h in range(heads):
            at = c * heads + h
            cum_row, cum_col = cum_rows[at : at + 1, :], cum_cols[:, at : at + 1]
            fade = jnp.exp(jnp.where(strict, cum_col - cum_row, 0.0))
            part = jnp.where(strict, grams[h // group] * fade * rate_cols[:, at : at + 1], 0.0)
            lower.append(part)
            solve.append(eye - jnp.where(gap_bits == 1, part, 0.0))
        size = 2
        while size < BLOCK:
            shift = size.bit_length() - 1
            inside = lax.shift_right_logical(gap_bits, shift) == 1
            right = [
                mm(jnp.where(inside, lower[h], 0.0), solve[h]) for h in range(heads)
            ]
            solve = [solve[h] - mm(solve[h], right[h]) for h in range(heads)]
            size *= 2
        first = [s.astype(BF16) for s in solve]
        rest = [eye - first[h].astype(F32) - mm_left2(lower[h], first[h]) for h in range(heads)]
        solve = [first[h].astype(F32) + mm(first[h], rest[h]) for h in range(heads)]
        for h in range(heads):
            at = c * heads + h
            g = h // group
            cum_row, cum_col = cum_rows[at : at + 1, :], cum_cols[:, at : at + 1]
            rate_row = rate_rows[at : at + 1, :]
            end = cum_row[:, BLOCK - 1 :]
            w = mm_left2(solve[h] * (rate_row * jnp.exp(cum_row) * unit_rows[g]), keys[g])
            u = mm_left2(solve[h] * rate_row, value_ref[tokens, h * DV : (h + 1) * DV])
            wu = jnp.concatenate([w, u], axis=1)
            wu_ref[h, c] = wu.astype(BF16)
            tail = mm_right2(keys_t[g], wu * (jnp.exp(end - cum_col) * unit_cols[g]))
            kept = jnp.exp(end)
            bias = jnp.concatenate([jnp.zeros((DK, DK), F32), tail[:, DK:]], axis=1)
            if c == 0:
                start = jnp.concatenate([eye, jnp.zeros((DK, DV), F32)], axis=1)
                prefix_ref[h, c] = start.astype(BF16)
                carried[h] = jnp.concatenate([kept * eye - tail[:, :DK], tail[:, DK:]], axis=1)
            else:
                prefix_ref[h, c] = carried[h].astype(BF16)
                carried[h] = kept * carried[h] + bias - mm_both2(tail[:, :DK], carried[h])
    for h in range(heads):
        total_ref[h] = carried[h].astype(BF16)


def readout_kernel(query_ref, key_ref, gate_ref, gain_ref, decay_ref, wu_ref, prefix_ref,
                   lin_ref, own_ref, gated_ref):
    heads = decay_ref.shape[0]
    key_heads = key_ref.shape[1] // DK
    group = heads // key_heads
    blocks = key_ref.shape[0] // BLOCK
    row, col = grids()
    causal = row >= col
    diagonal = row == col
    cum_rows, cum_cols = decays(decay_ref, blocks, row, col)
    for c in range(blocks):
        tokens = slice(c * BLOCK, (c + 1) * BLOCK)
        for g in range(key_heads):
            key = key_ref[tokens, g * DK : (g + 1) * DK]
            query = query_ref[tokens, g * DK : (g + 1) * DK]
            key_f, query_f = key.astype(F32), query.astype(F32)
            gram = jnp.where(diagonal, mm_nt(key, key), 0.0)
            unit_row = lax.rsqrt(jnp.sum(gram, axis=0, keepdims=True) + EPS)
            query_unit = query_f * (
                lax.rsqrt(jnp.sum(query_f * query_f, axis=1, keepdims=True) + EPS) * DK ** (-0.5)
            )
            query_scale = lax.rsqrt(
                jnp.sum(query_f * query_f, axis=1, keepdims=True) + EPS
            ) * DK ** (-0.5)
            plain = mm_nt(query, key) * unit_row * query_scale
            for h in range(g * group, (g + 1) * group):
                at = c * heads + h
                cum_row, cum_col = cum_rows[at : at + 1, :], cum_cols[:, at : at + 1]
                fade = jnp.exp(jnp.where(causal, cum_col - cum_row, 0.0))
                scores = jnp.where(causal, plain * fade, 0.0)
                mixed_wu = mm(scores, wu_ref[h, c])
                reach = query_unit * jnp.exp(cum_col) - mixed_wu[:, :DK]
                lanes = slice(h * DV, (h + 1) * DV)
                if c == 0:
                    lin_ref[tokens, lanes] = reach.astype(BF16)
                    own_ref[tokens, lanes] = mixed_wu[:, DK:]
                else:
                    spread = mm(reach, prefix_ref[h, c])
                    lin_ref[tokens, lanes] = spread[:, :DK].astype(BF16)
                    own_ref[tokens, lanes] = mixed_wu[:, DK:] + spread[:, DK:]
        for h in range(heads):
            lanes = slice(h * DV, (h + 1) * DV)
            gate = gate_ref[tokens, lanes].astype(F32)
            gated_ref[tokens, lanes] = gain_ref[...] * gate / (1.0 + jnp.exp(-gate))


def compose_kernel(own_ref, got_ref, out_ref):
    for h in range(own_ref.shape[0]):
        out = mm(own_ref[h, :, :DK], got_ref[h])
        bias = own_ref[h, :, DK:].astype(F32)
        out_ref[h] = (
            out + jnp.concatenate([jnp.zeros((DK, DK), F32), bias], axis=1)
        ).astype(BF16)


def compose(own, got):
    return pl.pallas_call(
        compose_kernel,
        out_shape=jax.ShapeDtypeStruct(own.shape, BF16),
        in_specs=[whole(), whole()],
        out_specs=whole(),
    )(own, got)


def bias_kernel(own_ref, got_ref, out_ref):
    for h in range(own_ref.shape[0]):
        out = mm(own_ref[h, :, :DK], got_ref[h])
        out_ref[h] = (out + own_ref[h, :, DK:].astype(F32)).astype(BF16)


def compose_bias(own, got):
    return pl.pallas_call(
        bias_kernel,
        out_shape=jax.ShapeDtypeStruct(got.shape, BF16),
        in_specs=[whole(), whole()],
        out_specs=whole(),
    )(own, got)


def mix_kernel(core_ref, state_ref, lin_ref, own_ref, gated_ref, keep_ref, send_ref):
    core = core_ref[0]
    heads = state_ref.shape[0]
    rows = keep_ref.shape[1]
    for z in range(keep_ref.shape[0]):
        for out_ref, side in ((send_ref, 1 - core), (keep_ref, core)):
            tokens = pl.ds(pl.multiple_of((2 * z + side) * rows, rows), rows)
            for h in range(heads):
                lanes = slice(h * DV, (h + 1) * DV)
                readout = own_ref[tokens, lanes] + mm(lin_ref[tokens, lanes], state_ref[h])
                scale = lax.rsqrt(jnp.mean(readout * readout, axis=1, keepdims=True) + EPS)
                out_ref[z, :, lanes] = (readout * scale * gated_ref[tokens, lanes]).astype(BF16)


def norm_kernel(hidden_ref, mine_ref, right_ref, left_ref, gain_ref, ids_ref, weight_ref,
                residual_ref, out_ref):
    residual = (
        hidden_ref[...].astype(F32)
        + mine_ref[...].astype(F32)
        + right_ref[...].astype(F32)
        + left_ref[...].astype(F32)
    )
    residual_ref[...] = residual
    scale = lax.rsqrt(jnp.mean(residual * residual, axis=1, keepdims=True) + EPS)
    width = residual.shape[1]
    out_ref[:, :width] = (residual * scale * gain_ref[...]).astype(BF16)
    lane = lax.broadcasted_iota(jnp.int32, (residual.shape[0], LANES), 1)
    routes = jnp.zeros((residual.shape[0], LANES), F32)
    for k in range(ids_ref.shape[1]):
        routes += jnp.where(
            ids_ref[:, k : k + 1] == lane, weight_ref[:, k : k + 1].astype(F32), 0.0
        )
    out_ref[:, width:] = routes.astype(BF16)


def expert_kernel(places, halves, place_ref, *refs):
    slots = refs[: 2 * places - 1]
    gate_own, up_own, down_own, gate_sib, up_sib, down_sib, out_ref, x_ref, sum_ref = refs[
        2 * places - 1 :
    ]
    step = pl.program_id(0)
    place, core = place_ref[0], place_ref[1]
    rows = slots[0].shape[0]
    width = out_ref.shape[-1]

    @pl.when(step == 0)
    def _():
        for number, slot in enumerate(slots):
            spot = place + number - (places - 1)

            @pl.when(jnp.logical_and(spot >= 0, spot < places))
            def _(slot=slot, spot=spot):
                x_ref[pl.ds(pl.multiple_of(spot * rows, rows), rows), :] = slot[...]

    def add(gate, up, down, expert, fresh):
        x = x_ref[:, :width]
        gate_act = jnp.dot(x, gate[0], preferred_element_type=F32)
        up_act = jnp.dot(x, up[0], preferred_element_type=F32)
        inner = (gate_act / (1.0 + jnp.exp(-gate_act)) * up_act).astype(BF16)
        routes = x_ref[:, width:].astype(F32)
        lane = lax.broadcasted_iota(jnp.int32, routes.shape, 1)
        weight = jnp.sum(jnp.where(lane == expert, routes, 0.0), axis=1, keepdims=True)
        more = jnp.dot(inner, down[0], preferred_element_type=F32) * weight

        @pl.when(fresh)
        def _():
            sum_ref[...] = more

        @pl.when(jnp.logical_not(fresh))
        def _():
            sum_ref[...] += more

    @pl.when(step < halves)
    def _():
        add(gate_own, up_own, down_own, 2 * place + core, step == 0)

    @pl.when(step >= halves)
    def _():
        add(gate_sib, up_sib, down_sib, 2 * place + 1 - core, step < 0)

    @pl.when(step == 2 * halves - 1)
    def _():
        out_ref[...] = sum_ref[...].astype(BF16).reshape(out_ref.shape)


def experts(place, core, slots, own, sib, places):
    rows = slots[0].shape[0]
    width = own[0].shape[1]
    inner = own[0].shape[2]
    tile = 256
    halves = inner // tile

    def specs(at):
        return [
            pl.BlockSpec((1, width, tile), lambda i: (0, 0, at(i))),
            pl.BlockSpec((1, width, tile), lambda i: (0, 0, at(i))),
            pl.BlockSpec((1, tile, width), lambda i: (0, at(i), 0)),
        ]

    return pl.pallas_call(
        functools.partial(expert_kernel, places, halves),
        grid=(2 * halves,),
        out_shape=jax.ShapeDtypeStruct((places, rows, width), BF16),
        in_specs=[whole(pltpu.SMEM)]
        + [whole()] * len(slots)
        + specs(lambda i: jnp.minimum(i, halves - 1))
        + specs(lambda i: jnp.maximum(i - halves, 0)),
        out_specs=whole(),
        scratch_shapes=[
            pltpu.VMEM((places * rows, slots[0].shape[1]), BF16),
            pltpu.VMEM((places * rows, width), F32),
        ],
        compiler_params=pltpu.CompilerParams(vmem_limit_bytes=VMEM_BYTES),
    )(jnp.stack([place, core]).astype(jnp.int32), *slots, *own, *sib)


def rightward(places, count):
    return [(2 * i + c, 2 * i + 2 + c) for i in range(min(count, places - 1)) for c in range(2)]


def leftward(places, count):
    return [
        (2 * i + c, 2 * i - 2 + c)
        for i in range(places - 1, max(places - 1 - count, 0), -1)
        for c in range(2)
    ]


def line_scatter(parts, place, places):
    def part(at):
        return lax.dynamic_index_in_dim(parts, jnp.clip(at, 0, places - 1), 0, False)

    right = left = None
    for t in range(1, places):
        to_right, to_left = part(places - t + place), part(t + place - places)
        if t > 1:
            to_right = (to_right.astype(F32) + right.astype(F32)).astype(BF16)
            to_left = (to_left.astype(F32) + left.astype(F32)).astype(BF16)
        right = lax.ppermute(to_right, "exp", rightward(places, t))
        left = lax.ppermute(to_left, "exp", leftward(places, t))
    return part(place), right, left


def line_gather(own, places):
    slots = {0: own}
    right = left = own
    for t in range(1, places):
        right = lax.ppermute(
            right, "exp", [(a, b) for a, b in rightward(places, places) if a // 2 >= t - 1]
        )
        left = lax.ppermute(
            left, "exp", [(a, b) for a, b in leftward(places, places) if a // 2 <= places - t]
        )
        slots[-t], slots[t] = right, left
    return [slots[t] for t in range(1 - places, places)]


def per_device(
    hidden_in,
    query_proj,
    key_proj,
    value_proj,
    gate_proj,
    log_decay,
    write_rate,
    head_gain,
    out_weight,
    post_gain,
    expert_ids,
    route_weight,
    gate_weight,
    up_weight,
    down_weight,
):
    length = value_proj.shape[0]
    heads = value_proj.shape[1] // DV
    blocks = length // BLOCK
    tok, width = hidden_in.shape
    seqs, exps = lax.axis_size("seq"), lax.axis_size("exp")
    places = exps // 2
    me = lax.axis_index("exp")
    place, core = me // 2, me % 2
    swap = [(i, i ^ 1) for i in range(exps)]

    out_sib = lax.ppermute(out_weight, "exp", swap)
    own = (gate_weight, up_weight, down_weight)
    sib = tuple(lax.ppermute(w, "exp", swap) for w in own)

    wide = jax.ShapeDtypeStruct((heads, blocks, DK, DK + DV), BF16)
    wu, prefixes, total = pl.pallas_call(
        state_kernel,
        out_shape=(wide, wide, jax.ShapeDtypeStruct((heads, DK, DK + DV), BF16)),
        in_specs=[whole()] * 4,
        out_specs=(whole(),) * 3,
        compiler_params=pltpu.CompilerParams(vmem_limit_bytes=VMEM_BYTES),
        cost_estimate=pl.CostEstimate(flops=10**10, bytes_accessed=4 * 10**6, transcendentals=0),
    )(key_proj, value_proj, log_decay, write_rate)

    lin, own_read, gated = pl.pallas_call(
        readout_kernel,
        out_shape=(
            jax.ShapeDtypeStruct((length, heads * DV), BF16),
            jax.ShapeDtypeStruct((length, heads * DV), F32),
            jax.ShapeDtypeStruct((length, heads * DV), F32),
        ),
        in_specs=[whole()] * 7,
        out_specs=(whole(),) * 3,
        compiler_params=pltpu.CompilerParams(vmem_limit_bytes=VMEM_BYTES),
        cost_estimate=pl.CostEstimate(flops=6 * 10**9, bytes_accessed=4 * 10**6, transcendentals=0),
    )(query_proj, key_proj, gate_proj, head_gain.reshape(1, DV), log_decay, wu, prefixes)

    upto, before, step = total, None, 1
    while step < seqs:
        pairs = [(i, i + step) for i in range(seqs - step)]
        last = 2 * step >= seqs
        sent = upto[:, :, DK:] if last and before is not None else upto
        got = lax.ppermute(sent, "seq", pairs)
        if last:
            state = got[:, :, DK:] if before is None else compose_bias(before, got)
        else:
            upto = compose(upto, got)
            before = got if before is None else compose(before, got)
        step *= 2

    half = jax.ShapeDtypeStruct((places, tok, heads * DV), BF16)
    keep, send = pl.pallas_call(
        mix_kernel,
        out_shape=(half, half),
        in_specs=[whole(pltpu.SMEM)] + [whole()] * 4,
        out_specs=(whole(),) * 2,
        compiler_params=pltpu.CompilerParams(vmem_limit_bytes=VMEM_BYTES),
    )(core.reshape(1).astype(jnp.int32), state, lin, own_read, gated)
    got = lax.ppermute(send, "exp", swap)
    parts = (
        jnp.dot(keep.reshape(-1, heads * DV), out_weight, preferred_element_type=F32)
        + jnp.dot(got.reshape(-1, heads * DV), out_sib, preferred_element_type=F32)
    ).astype(BF16).reshape(places, tok, width)

    mine, right, left = line_scatter(parts, place, places)
    residual, normed = pl.pallas_call(
        norm_kernel,
        out_shape=(
            jax.ShapeDtypeStruct((tok, width), F32),
            jax.ShapeDtypeStruct((tok, width + LANES), BF16),
        ),
        in_specs=[whole()] * 7,
        out_specs=(whole(),) * 2,
    )(hidden_in, mine, right, left, post_gain.reshape(1, width), expert_ids, route_weight)
    slots = line_gather(normed, places)
    sums = experts(place, core, slots, own, sib, places)
    mine, right, left = line_scatter(sums, place, places)
    return (
        residual + mine.astype(F32) + right.astype(F32) + left.astype(F32)
    ).astype(BF16)


def solution(mesh):
    in_specs = (
        P(("seq", "exp"), None),
        P("seq", "exp"),
        P("seq", "exp"),
        P("seq", "exp"),
        P("seq", "exp"),
        P("exp", "seq"),
        P("exp", "seq"),
        P(),
        P("exp", None),
        P(),
        P(("seq", "exp"), None),
        P(("seq", "exp"), None),
        P("exp", None, None),
        P("exp", None, None),
        P("exp", None, None),
    )
    out_specs = P(("seq", "exp"), None)
    return jax.shard_map(
        per_device, mesh=mesh, in_specs=in_specs, out_specs=out_specs, check_vma=False
    )
```

profile of v0, /device:TPU:0, one launch (start us, length us, event | category | flops | bytes accessed | tf_op | source)
XLA Modules:
  0.0 176.9 jit_solution(7571543969536616317)
XLA Ops:
  0.5 1.0 copy-done.4
  1.5 0.9 copy-done.6
  3.9 13.8 %shard_map.145 = (bf16[4,4,128,256]{3,2,1,0:T(8,128)(2,1)S(1)}, bf16[4,4,128,256]{3,2,1,0:T(8,128)(2,1)S(1)}, bf16[4,128,256]{2,1,0:T(8,128)(2,1)S(1)}) custom-call(bf16[512,256]{1,0:T(8,128)(2,1)S(1)} %copy-done.6, bf16[512,512]{1,0:T(8,128)(2,1)S(1)} %copy-done.4, f32[4,512]{1,0:T(4,128)S(1)} %copy-done.10, f32[4,512]{1,0:T(4,128)S(1)} %copy-done.9), custom_call_target="tpu_custom_call" | custom-call | flops 10000000000 | bytes 4000000 | tf_op jit(solution)/shard_map/pallas_call | solution.py:424
  17.6 1.0 copy-done.13
  18.6 4.4 %collective-permute-start = (bf16[4,128,256]{2,1,0:T(8,128)(2,1)S(1)}, bf16[4,128,256]{2,1,0:T(8,128)(2,1)S(1)}, u32[]{:S(2)}, u32[]{:S(2)}) collective-permute-start(bf16[4,128,256]{2,1,0:T(8,128)(2,1)S(1)} %get-tuple-element.15.own_ref), channel_id=1, source_target_pairs={{0,8},{8,16},{16,24},{1,9},{9,17},{17,25},{2,10},{10,18},{18,26},{... | collective-permute-start | bytes 786440 | tf_op jit(solution)/shard_map/ppermute | solution.py:451
  23.0 6.2 %collective-permute-done.got_ref.own_ref = bf16[4,128,256]{2,1,0:T(8,128)(2,1)S(1)} collective-permute-done((bf16[4,128,256]{2,1,0:T(8,128)(2,1)S(1)}, bf16[4,128,256]{2,1,0:T(8,128)(2,1)S(1)}, u32[]{:S(2)}, u32[]{:S(2)}) %collective-permute-start) | collective-permute-done | bytes 262176 | tf_op jit(solution)/shard_map/ppermute | solution.py:451
  29.9 1.9 %shard_map.146 = bf16[4,128,256]{2,1,0:T(8,128)(2,1)} custom-call(bf16[4,128,256]{2,1,0:T(8,128)(2,1)} %copy-done.3, bf16[4,128,256]{2,1,0:T(8,128)(2,1)} %copy-done.18), custom_call_target="tpu_custom_call" | custom-call | tf_op jit(solution)/shard_map/pallas_call | solution.py:212
  31.9 0.9 slice.4
  32.8 6.0 %collective-permute-start.1 = (bf16[4,128,128]{2,1,0:T(8,128)(2,1)S(1)}, bf16[4,128,128]{2,1,0:T(8,128)(2,1)}, u32[]{:S(2)}, u32[]{:S(2)}) collective-permute-start(bf16[4,128,128]{2,1,0:T(8,128)(2,1)S(1)} %slice.4), channel_id=1, source_target_pairs={{0,16},{8,24},{1,17},{9,25},{2,18},{10,26},{3,19},{11,27},{4,20},{... | collective-permute-start | bytes 393224 | tf_op jit(solution)/shard_map/ppermute | solution.py:451
  38.8 0.9 copy-done.8
  39.7 1.2 copy-done.14
  41.0 1.2 copy-done.16
  42.2 2.7 %shard_map.148 = (bf16[512,512]{1,0:T(8,128)(2,1)S(1)}, f32[512,512]{1,0:T(8,128)S(1)}, f32[512,512]{1,0:T(8,128)S(1)}) custom-call(bf16[512,256]{1,0:T(8,128)(2,1)S(1)} %copy-done.8, bf16[512,256]{1,0:T(8,128)(2,1)S(1)} %copy-done.7, bf16[512,512]{1,0:T(8,128)(2,1)S(1)} %copy-done.5, f32[1,128]{1,0:T(1,128)S(1)} %bitcast.49, f32[4,512]{1,0:T(4,128)S(1)} %copy-done.11, ...), custom_call_target="tpu_custom_call" | custom-call | flops 6000000000 | bytes 4000000 | tf_op jit(solution)/shard_map/pallas_call | solution.py:433
  44.9 1.8 %shard_map.147.state_ref = bf16[4,128,128]{2,1,0:T(8,128)(2,1)} custom-call(bf16[4,128,256]{2,1,0:T(8,128)(2,1)} %copy-done.18, bf16[4,128,128]{2,1,0:T(8,128)(2,1)} %collective-permute-done.1.got_ref), custom_call_target="tpu_custom_call" | custom-call | tf_op jit(solution)/shard_map/pallas_call | solution.py:227
  46.7 0.9 copy-done.1
  48.3 1.5 collective-permute-done.2
  49.8 2.4 %fusion.12 = f32[256,2048]{1,0:T(8,128)S(1)} fusion(bf16[256,512]{1,0:T(8,128)(2,1)S(1)} %bitcast.54, bf16[512,2048]{1,0:T(8,128)(2,1)} %collective-permute-done.3), kind=kOutput, calls=%fused_computation.28 | convolution fusion | flops 536870912 | bytes 4456448 | tf_op jit(solution)/shard_map/dot_general | solution.py:470
  53.9 1.3 collective-permute-start.7
  55.2 4.2 %collective-permute-start.4 = (bf16[64,2048]{1,0:T(8,128)(2,1)S(1)}, bf16[64,2048]{1,0:T(8,128)(2,1)}, u32[]{:S(2)}, u32[]{:S(2)}) collective-permute-start(bf16[64,2048]{1,0:T(8,128)(2,1)S(1)} %get-tuple-element.32), channel_id=1, source_target_pairs={{0,2},{1,3},{8,10},{9,11},{16,18},{17,19},{24,26},{25,27}} | collective-permute-start | bytes 786440 | tf_op jit(solution)/shard_map/ppermute | solution.py:373
  59.4 1.7 fusion.8
  61.1 1.3 collective-permute-start.8
  63.0 1.6 collective-permute-done.4
  64.6 1.9 %fusion.9 = (bf16[64,2048]{1,0:T(8,128)(2,1)S(1)}, bf16[64,2048]{1,0:T(8,128)(2,1)}) fusion(bf16[64,2048]{1,0:T(8,128)(2,1)} %collective-permute-done.8, bf16[4,64,2048]{2,1,0:T(8,128)(2,1)S(1)} %bitcast.52, s32[]{:T(128)S(6)} %min.33, bf16[64,2048]{1,0:T(8,128)(2,1)} %collective-permute-done.4, s32[]{:T(128)S(6)} %min.31), kind=kLoop, calls=%fused_computation.17 | loop fusion | flops 1048576 | bytes 1572872 | tf_op jit(solution)/shard_map/convert_element_type | solution.py:372
  66.4 15.3 %collective-permute-start.5 = (bf16[64,2048]{1,0:T(8,128)(2,1)}, bf16[64,2048]{1,0:T(8,128)(2,1)}, u32[]{:S(2)}, u32[]{:S(2)}) collective-permute-start(bf16[64,2048]{1,0:T(8,128)(2,1)} %get-tuple-element.30), channel_id=1, source_target_pairs={{0,2},{1,3},{2,4},{3,5},{8,10},{9,11},{10,12},{11,13},{16,18},{17,... | collective-permute-start | bytes 786440 | tf_op jit(solution)/shard_map/ppermute | solution.py:373
  81.8 1.3 collective-permute-start.9
  83.0 2.7 %collective-permute-done.5 = bf16[64,2048]{1,0:T(8,128)(2,1)} collective-permute-done((bf16[64,2048]{1,0:T(8,128)(2,1)}, bf16[64,2048]{1,0:T(8,128)(2,1)}, u32[]{:S(2)}, u32[]{:S(2)}) %collective-permute-start.5) | collective-permute-done | bytes 262176 | tf_op jit(solution)/shard_map/ppermute | solution.py:373
  85.8 1.7 fusion.11
  87.5 4.4 %collective-permute-start.6 = (bf16[64,2048]{1,0:T(8,128)(2,1)}, bf16[64,2048]{1,0:T(8,128)(2,1)S(1)}, u32[]{:S(2)}, u32[]{:S(2)}) collective-permute-start(bf16[64,2048]{1,0:T(8,128)(2,1)} %fusion.11), channel_id=1, source_target_pairs={{0,2},{1,3},{2,4},{3,5},{4,6},{5,7},{8,10},{9,11},{10,12},{11,13},... | collective-permute-start | bytes 786440 | tf_op jit(solution)/shard_map/ppermute | solution.py:373
  93.3 2.8 %collective-permute-done.6.right_ref = bf16[64,2048]{1,0:T(8,128)(2,1)S(1)} collective-permute-done((bf16[64,2048]{1,0:T(8,128)(2,1)}, bf16[64,2048]{1,0:T(8,128)(2,1)S(1)}, u32[]{:S(2)}, u32[]{:S(2)}) %collective-permute-start.6) | collective-permute-done | bytes 262176 | tf_op jit(solution)/shard_map/ppermute | solution.py:373
  96.7 2.3 %shard_map.150 = (f32[64,2048]{1,0:T(8,128)}, bf16[64,2176]{1,0:T(8,128)(2,1)}) custom-call(bf16[64,2048]{1,0:T(8,128)(2,1)} %hidden_ref.1, bf16[64,2048]{1,0:T(8,128)(2,1)} %get-tuple-element.33.mine_ref, bf16[64,2048]{1,0:T(8,128)(2,1)} %copy-done.20, bf16[64,2048]{1,0:T(8,128)(2,1)} %collective-permute-done.9.left_ref, f32[1,2048]{1,0:T(1,128)} %bitcast.55, ...), custom_call_target="tpu_custom_call" | custom-call | tf_op jit(solution)/shard_map/pallas_call | solution.py:474
  99.0 4.3 %collective-permute-start.10 = (bf16[64,2176]{1,0:T(8,128)(2,1)}, bf16[64,2176]{1,0:T(8,128)(2,1)S(1)}, u32[]{:S(2)}, u32[]{:S(2)}) collective-permute-start(bf16[64,2176]{1,0:T(8,128)(2,1)} %get-tuple-element.24.refs_3_), channel_id=1, source_target_pairs={{0,2},{1,3},{2,4},{3,5},{4,6},{5,7},{8,10},{9,11},{10,12},{11,13},... | collective-permute-start | bytes 835592 | tf_op jit(solution)/shard_map/ppermute | solution.py:382
  103.3 1.3 collective-permute-start.13
  104.6 3.0 %collective-permute-done.10.refs_2_ = bf16[64,2176]{1,0:T(8,128)(2,1)S(1)} collective-permute-done((bf16[64,2176]{1,0:T(8,128)(2,1)}, bf16[64,2176]{1,0:T(8,128)(2,1)S(1)}, u32[]{:S(2)}, u32[]{:S(2)}) %collective-permute-start.10) | collective-permute-done | bytes 278560 | tf_op jit(solution)/shard_map/ppermute | solution.py:382
  108.3 3.9 %collective-permute-done.13.refs_4_ = bf16[64,2176]{1,0:T(8,128)(2,1)S(1)} collective-permute-done((bf16[64,2176]{1,0:T(8,128)(2,1)}, bf16[64,2176]{1,0:T(8,128)(2,1)S(1)}, u32[]{:S(2)}, u32[]{:S(2)}) %collective-permute-start.13) | collective-permute-done | bytes 278560 | tf_op jit(solution)/shard_map/ppermute | solution.py:385
  112.2 1.3 collective-permute-start.14
  114.2 7.8 %collective-permute-done.14.refs_5_ = bf16[64,2176]{1,0:T(8,128)(2,1)S(1)} collective-permute-done((bf16[64,2176]{1,0:T(8,128)(2,1)S(1)}, bf16[64,2176]{1,0:T(8,128)(2,1)S(1)}, u32[]{:S(2)}, u32[]{:S(2)}) %collective-permute-start.14) | collective-permute-done | bytes 278560 | tf_op jit(solution)/shard_map/ppermute | solution.py:385
  122.0 1.3 collective-permute-start.15
  123.4 7.0 %collective-permute-done.15.refs_6_ = bf16[64,2176]{1,0:T(8,128)(2,1)S(1)} collective-permute-done((bf16[64,2176]{1,0:T(8,128)(2,1)S(1)}, bf16[64,2176]{1,0:T(8,128)(2,1)S(1)}, u32[]{:S(2)}, u32[]{:S(2)}) %collective-permute-start.15) | collective-permute-done | bytes 278560 | tf_op jit(solution)/shard_map/ppermute | solution.py:385
  130.4 1.0 copy-done.2
  131.4 8.6 %shard_map.151 = bf16[4,64,2048]{2,1,0:T(8,128)(2,1)S(1)} custom-call(s32[2]{0:T(128)S(1)} %pad_add_fusion.place_ref, bf16[64,2176]{1,0:T(8,128)(2,1)S(1)} %collective-permute-done.12.refs_0_, bf16[64,2176]{1,0:T(8,128)(2,1)S(1)} %collective-permute-done.11.refs_1_, bf16[64,2176]{1,0:T(8,128)(2,1)S(1)} %collective-permute-done.10.refs_2_, ...), custom_call_target="tpu_custom_call" | custom-call | tf_op jit(solution)/shard_map/pallas_call | solution.py:334
  140.0 1.6 collective-permute-start.19
  142.3 5.5 %collective-permute-done.19 = bf16[64,2048]{1,0:T(8,128)(2,1)S(1)} collective-permute-done((bf16[64,2048]{1,0:T(8,128)(2,1)S(1)}, bf16[64,2048]{1,0:T(8,128)(2,1)S(1)}, u32[]{:S(2)}, u32[]{:S(2)}) %collective-permute-start.19) | collective-permute-done | bytes 262176 | tf_op jit(solution)/shard_map/ppermute | solution.py:373
  147.9 4.4 %collective-permute-start.20 = (bf16[64,2048]{1,0:T(8,128)(2,1)S(1)}, bf16[64,2048]{1,0:T(8,128)(2,1)S(1)}, u32[]{:S(2)}, u32[]{:S(2)}) collective-permute-start(bf16[64,2048]{1,0:T(8,128)(2,1)S(1)} %fusion.3), channel_id=1, source_target_pairs={{0,2},{1,3},{2,4},{3,5},{8,10},{9,11},{10,12},{11,13},{16,18},{17,... | collective-permute-start | bytes 786440 | tf_op jit(solution)/shard_map/ppermute | solution.py:373
  152.3 6.5 %collective-permute-done.20 = bf16[64,2048]{1,0:T(8,128)(2,1)S(1)} collective-permute-done((bf16[64,2048]{1,0:T(8,128)(2,1)S(1)}, bf16[64,2048]{1,0:T(8,128)(2,1)S(1)}, u32[]{:S(2)}, u32[]{:S(2)}) %collective-permute-start.20) | collective-permute-done | bytes 262176 | tf_op jit(solution)/shard_map/ppermute | solution.py:373
  159.7 5.0 %collective-permute-start.21 = (bf16[64,2048]{1,0:T(8,128)(2,1)S(1)}, bf16[64,2048]{1,0:T(8,128)(2,1)S(1)}, u32[]{:S(2)}, u32[]{:S(2)}) collective-permute-start(bf16[64,2048]{1,0:T(8,128)(2,1)S(1)} %get-tuple-element.25), channel_id=1, source_target_pairs={{0,2},{1,3},{2,4},{3,5},{4,6},{5,7},{8,10},{9,11},{10,12},{11,13},... | collective-permute-start | bytes 786440 | tf_op jit(solution)/shard_map/ppermute | solution.py:373
  164.8 1.3 collective-permute-start.24
  166.1 2.5 %collective-permute-done.21 = bf16[64,2048]{1,0:T(8,128)(2,1)S(1)} collective-permute-done((bf16[64,2048]{1,0:T(8,128)(2,1)S(1)}, bf16[64,2048]{1,0:T(8,128)(2,1)S(1)}, u32[]{:S(2)}, u32[]{:S(2)}) %collective-permute-start.21) | collective-permute-done | bytes 262176 | tf_op jit(solution)/shard_map/ppermute | solution.py:373
  168.6 7.5 %collective-permute-done.24 = bf16[64,2048]{1,0:T(8,128)(2,1)S(1)} collective-permute-done((bf16[64,2048]{1,0:T(8,128)(2,1)S(1)}, bf16[64,2048]{1,0:T(8,128)(2,1)S(1)}, u32[]{:S(2)}, u32[]{:S(2)}) %collective-permute-start.24) | collective-permute-done | bytes 262176 | tf_op jit(solution)/shard_map/ppermute | solution.py:374
  (70 shorter events, 11.4 us)
Async XLA Ops:
  0.0 49.7 %collective-permute-start.3 = (bf16[512,2048]{1,0:T(8,128)(2,1)}, bf16[512,2048]{1,0:T(8,128)(2,1)}, u32[]{:S(2)}, u32[]{:S(2)}) collective-permute-start(bf16[512,2048]{1,0:T(8,128)(2,1)} %param.23), channel_id=1, source_target_pairs={{0,1},{1,0},{2,3},{3,2},{4,5},{5,4},{6,7},{7,6},{8,9},{9,8},{10,11... | collective-permute-start | bytes 6291464 | tf_op jit(solution)/shard_map/ppermute | solution.py:419
  0.5 1.0 copy-start.4
  1.5 0.9 copy-start.6
  2.4 0.7 copy-start.9
  3.1 0.7 copy-start.10
  3.8 34.9 %copy-start.5 = (bf16[512,512]{1,0:T(8,128)(2,1)S(1)}, bf16[512,512]{1,0:T(8,128)(2,1)}, u32[]{:S(2)}) copy-start(bf16[512,512]{1,0:T(8,128)(2,1)} %gate_ref.1) | copy-start | bytes 1572868
  3.8 34.9 %copy-start.7 = (bf16[512,256]{1,0:T(8,128)(2,1)S(1)}, bf16[512,256]{1,0:T(8,128)(2,1)}, u32[]{:S(2)}) copy-start(bf16[512,256]{1,0:T(8,128)(2,1)} %key_ref.3) | copy-start | bytes 786436
  3.8 34.9 %copy-start.11 = (f32[4,512]{1,0:T(4,128)S(1)}, f32[4,512]{1,0:T(4,128)}, u32[]{:S(2)}) copy-start(f32[4,512]{1,0:T(4,128)} %decay_ref.3) | copy-start | bytes 24580
  3.8 34.9 %copy-start.12 = (f32[128]{0:T(128)S(1)}, f32[128]{0:T(128)}, u32[]{:S(2)}) copy-start(f32[128]{0:T(128)} %param.22) | copy-start | bytes 1540
  17.6 1.0 copy-start.13
  18.6 10.6 %copy-start.3 = (bf16[4,128,256]{2,1,0:T(8,128)(2,1)}, bf16[4,128,256]{2,1,0:T(8,128)(2,1)S(1)}, u32[]{:S(2)}) copy-start(bf16[4,128,256]{2,1,0:T(8,128)(2,1)S(1)} %get-tuple-element.15.own_ref) | copy-start | bytes 786436
  18.6 20.2 %copy-start.15 = (bf16[4,4,128,256]{3,2,1,0:T(8,128)(2,1)}, bf16[4,4,128,256]{3,2,1,0:T(8,128)(2,1)S(1)}, u32[]{:S(2)}) copy-start(bf16[4,4,128,256]{3,2,1,0:T(8,128)(2,1)S(1)} %get-tuple-element.17.prefix_ref) | copy-start | bytes 3145732
  18.6 10.6 %collective-permute-start = (bf16[4,128,256]{2,1,0:T(8,128)(2,1)S(1)}, bf16[4,128,256]{2,1,0:T(8,128)(2,1)S(1)}, u32[]{:S(2)}, u32[]{:S(2)}) collective-permute-start(bf16[4,128,256]{2,1,0:T(8,128)(2,1)S(1)} %get-tuple-element.15.own_ref), channel_id=1, source_target_pairs={{0,8},{8,16},{16,24},{1,9},{9,17},{17,25},{2,10},{10,18},{18,26},{... | collective-permute-start | bytes 786440 | tf_op jit(solution)/shard_map/ppermute | solution.py:451
  29.2 0.7 copy-start.18
  32.8 12.1 %collective-permute-start.1 = (bf16[4,128,128]{2,1,0:T(8,128)(2,1)S(1)}, bf16[4,128,128]{2,1,0:T(8,128)(2,1)}, u32[]{:S(2)}, u32[]{:S(2)}) collective-permute-start(bf16[4,128,128]{2,1,0:T(8,128)(2,1)S(1)} %slice.4), channel_id=1, source_target_pairs={{0,16},{8,24},{1,17},{9,25},{2,18},{10,26},{3,19},{11,27},{4,20},{... | collective-permute-start | bytes 393224 | tf_op jit(solution)/shard_map/ppermute | solution.py:451
  38.8 1.0 copy-start.8
  39.7 1.2 copy-start.14
  41.0 1.2 copy-start.16
  46.7 0.9 copy-start.1
  48.1 1.6 collective-permute-start.2
  49.7 2.5 %copy-start.17 = (bf16[512,2048]{1,0:T(8,128)(2,1)S(1)}, bf16[512,2048]{1,0:T(8,128)(2,1)}, u32[]{:S(2)}) copy-start(bf16[512,2048]{1,0:T(8,128)(2,1)} %param.23) | copy-start | bytes 6291460
  53.0 9.5 %copy-start = (bf16[1,2048,512]{2,1,0:T(8,128)(2,1)S(1)}, bf16[1,2048,512]{2,1,0:T(8,128)(2,1)}, u32[]{:S(2)}) copy-start(bf16[1,2048,512]{2,1,0:T(8,128)(2,1)} %refs_7_.1) | copy-start | bytes 6291460
  53.0 38.9 %copy-start.21 = (s32[64,4]{0,1:T(4,128)S(1)}, s32[64,4]{0,1:T(4,128)}, u32[]{:S(2)}) copy-start(s32[64,4]{0,1:T(4,128)} %param.25) | copy-start | bytes 3076
  53.0 39.6 %copy-start.22 = (bf16[64,4]{0,1:T(4,128)(2,1)S(1)}, bf16[64,4]{0,1:T(4,128)(2,1)}, u32[]{:S(2)}) copy-start(bf16[64,4]{0,1:T(4,128)(2,1)} %param.26) | copy-start | bytes 1540
  53.9 5.5 %collective-permute-start.7 = (bf16[64,2048]{1,0:T(8,128)(2,1)}, bf16[64,2048]{1,0:T(8,128)(2,1)}, u32[]{:S(2)}, u32[]{:S(2)}) collective-permute-start(bf16[64,2048]{1,0:T(8,128)(2,1)} %get-tuple-element.31), channel_id=1, source_target_pairs={{6,4},{7,5},{14,12},{15,13},{22,20},{23,21},{30,28},{31,29}} | collective-permute-start | bytes 786440 | tf_op jit(solution)/shard_map/ppermute | solution.py:374
  55.2 9.3 %collective-permute-start.4 = (bf16[64,2048]{1,0:T(8,128)(2,1)S(1)}, bf16[64,2048]{1,0:T(8,128)(2,1)}, u32[]{:S(2)}, u32[]{:S(2)}) collective-permute-start(bf16[64,2048]{1,0:T(8,128)(2,1)S(1)} %get-tuple-element.32), channel_id=1, source_target_pairs={{0,2},{1,3},{8,10},{9,11},{16,18},{17,19},{24,26},{25,27}} | collective-permute-start | bytes 786440 | tf_op jit(solution)/shard_map/ppermute | solution.py:373
  61.1 3.4 %collective-permute-start.8 = (bf16[64,2048]{1,0:T(8,128)(2,1)}, bf16[64,2048]{1,0:T(8,128)(2,1)}, u32[]{:S(2)}, u32[]{:S(2)}) collective-permute-start(bf16[64,2048]{1,0:T(8,128)(2,1)} %fusion.8), channel_id=1, source_target_pairs={{6,4},{7,5},{4,2},{5,3},{14,12},{15,13},{12,10},{13,11},{22,20},{2... | collective-permute-start | bytes 786440 | tf_op jit(solution)/shard_map/ppermute | solution.py:374
  62.5 60.9 %collective-permute-start.16 = (bf16[1,2048,512]{2,1,0:T(8,128)(2,1)S(1)}, bf16[1,2048,512]{2,1,0:T(8,128)(2,1)}, u32[]{:S(2)}, u32[]{:S(2)}) collective-permute-start(bf16[1,2048,512]{2,1,0:T(8,128)(2,1)S(1)} %copy-done), channel_id=1, source_target_pairs={{0,1},{1,0},{2,3},{3,2},{4,5},{5,4},{6,7},{7,6},{8,9},{9,8},{10,11... | collective-permute-start | bytes 6291464 | tf_op jit(solution)/shard_map/ppermute | solution.py:421
  62.5 60.9 %collective-permute-start.17 = (bf16[1,2048,512]{2,1,0:T(8,128)(2,1)}, bf16[1,2048,512]{2,1,0:T(8,128)(2,1)}, u32[]{:S(2)}, u32[]{:S(2)}) collective-permute-start(bf16[1,2048,512]{2,1,0:T(8,128)(2,1)} %refs_8_.1), channel_id=1, source_target_pairs={{0,1},{1,0},{2,3},{3,2},{4,5},{5,4},{6,7},{7,6},{8,9},{9,8},{10,11... | collective-permute-start | bytes 6291464 | tf_op jit(solution)/shard_map/ppermute | solution.py:421
  63.0 60.4 %collective-permute-start.18 = (bf16[1,512,2048]{2,1,0:T(8,128)(2,1)}, bf16[1,512,2048]{2,1,0:T(8,128)(2,1)}, u32[]{:S(2)}, u32[]{:S(2)}) collective-permute-start(bf16[1,512,2048]{2,1,0:T(8,128)(2,1)} %refs_9_.1), channel_id=1, source_target_pairs={{0,1},{1,0},{2,3},{3,2},{4,5},{5,4},{6,7},{7,6},{8,9},{9,8},{10,11... | collective-permute-start | bytes 6291464 | tf_op jit(solution)/shard_map/ppermute | solution.py:421
  66.4 19.3 %collective-permute-start.5 = (bf16[64,2048]{1,0:T(8,128)(2,1)}, bf16[64,2048]{1,0:T(8,128)(2,1)}, u32[]{:S(2)}, u32[]{:S(2)}) collective-permute-start(bf16[64,2048]{1,0:T(8,128)(2,1)} %get-tuple-element.30), channel_id=1, source_target_pairs={{0,2},{1,3},{2,4},{3,5},{8,10},{9,11},{10,12},{11,13},{16,18},{17,... | collective-permute-start | bytes 786440 | tf_op jit(solution)/shard_map/ppermute | solution.py:373
  81.8 11.5 %collective-permute-start.9 = (bf16[64,2048]{1,0:T(8,128)(2,1)S(1)}, bf16[64,2048]{1,0:T(8,128)(2,1)}, u32[]{:S(2)}, u32[]{:S(2)}) collective-permute-start(bf16[64,2048]{1,0:T(8,128)(2,1)S(1)} %get-tuple-element.29), channel_id=1, source_target_pairs={{6,4},{7,5},{4,2},{5,3},{2,0},{3,1},{14,12},{15,13},{12,10},{13,11... | collective-permute-start | bytes 786440 | tf_op jit(solution)/shard_map/ppermute | solution.py:374
  87.5 8.6 %collective-permute-start.6 = (bf16[64,2048]{1,0:T(8,128)(2,1)}, bf16[64,2048]{1,0:T(8,128)(2,1)S(1)}, u32[]{:S(2)}, u32[]{:S(2)}) collective-permute-start(bf16[64,2048]{1,0:T(8,128)(2,1)} %fusion.11), channel_id=1, source_target_pairs={{0,2},{1,3},{2,4},{3,5},{4,6},{5,7},{8,10},{9,11},{10,12},{11,13},... | collective-permute-start | bytes 786440 | tf_op jit(solution)/shard_map/ppermute | solution.py:373
  96.0 0.7 copy-start.20
  99.0 8.6 %collective-permute-start.10 = (bf16[64,2176]{1,0:T(8,128)(2,1)}, bf16[64,2176]{1,0:T(8,128)(2,1)S(1)}, u32[]{:S(2)}, u32[]{:S(2)}) collective-permute-start(bf16[64,2176]{1,0:T(8,128)(2,1)} %get-tuple-element.24.refs_3_), channel_id=1, source_target_pairs={{0,2},{1,3},{2,4},{3,5},{4,6},{5,7},{8,10},{9,11},{10,12},{11,13},... | collective-permute-start | bytes 835592 | tf_op jit(solution)/shard_map/ppermute | solution.py:382
  103.3 8.9 %collective-permute-start.13 = (bf16[64,2176]{1,0:T(8,128)(2,1)}, bf16[64,2176]{1,0:T(8,128)(2,1)S(1)}, u32[]{:S(2)}, u32[]{:S(2)}) collective-permute-start(bf16[64,2176]{1,0:T(8,128)(2,1)} %get-tuple-element.24.refs_3_), channel_id=1, source_target_pairs={{6,4},{7,5},{4,2},{5,3},{2,0},{3,1},{14,12},{15,13},{12,10},{13,11... | collective-permute-start | bytes 835592 | tf_op jit(solution)/shard_map/ppermute | solution.py:385
  107.6 5.9 %collective-permute-start.11 = (bf16[64,2176]{1,0:T(8,128)(2,1)S(1)}, bf16[64,2176]{1,0:T(8,128)(2,1)S(1)}, u32[]{:S(2)}, u32[]{:S(2)}) collective-permute-start(bf16[64,2176]{1,0:T(8,128)(2,1)S(1)} %collective-permute-done.10.refs_2_), channel_id=1, source_target_pairs={{2,4},{3,5},{4,6},{5,7},{10,12},{11,13},{12,14},{13,15},{18,20},{1... | collective-permute-start | bytes 835592 | tf_op jit(solution)/shard_map/ppermute | solution.py:382
  112.2 9.8 %collective-permute-start.14 = (bf16[64,2176]{1,0:T(8,128)(2,1)S(1)}, bf16[64,2176]{1,0:T(8,128)(2,1)S(1)}, u32[]{:S(2)}, u32[]{:S(2)}) collective-permute-start(bf16[64,2176]{1,0:T(8,128)(2,1)S(1)} %collective-permute-done.13.refs_4_), channel_id=1, source_target_pairs={{4,2},{5,3},{2,0},{3,1},{12,10},{13,11},{10,8},{11,9},{20,18},{21,... | collective-permute-start | bytes 835592 | tf_op jit(solution)/shard_map/ppermute | solution.py:385
  113.5 9.9 %collective-permute-start.12 = (bf16[64,2176]{1,0:T(8,128)(2,1)S(1)}, bf16[64,2176]{1,0:T(8,128)(2,1)S(1)}, u32[]{:S(2)}, u32[]{:S(2)}) collective-permute-start(bf16[64,2176]{1,0:T(8,128)(2,1)S(1)} %collective-permute-done.11.refs_1_), channel_id=1, source_target_pairs={{4,6},{5,7},{12,14},{13,15},{20,22},{21,23},{28,30},{29,31}} | collective-permute-start | bytes 835592 | tf_op jit(solution)/shard_map/ppermute | solution.py:382
  122.0 8.4 %collective-permute-start.15 = (bf16[64,2176]{1,0:T(8,128)(2,1)S(1)}, bf16[64,2176]{1,0:T(8,128)(2,1)S(1)}, u32[]{:S(2)}, u32[]{:S(2)}) collective-permute-start(bf16[64,2176]{1,0:T(8,128)(2,1)S(1)} %collective-permute-done.14.refs_5_), channel_id=1, source_target_pairs={{2,0},{3,1},{10,8},{11,9},{18,16},{19,17},{26,24},{27,25}} | collective-permute-start | bytes 835592 | tf_op jit(solution)/shard_map/ppermute | solution.py:385
  130.4 1.0 copy-start.2
  140.0 36.1 %copy-start.19 = (f32[64,2048]{1,0:T(8,128)S(1)}, f32[64,2048]{1,0:T(8,128)}, u32[]{:S(2)}) copy-start(f32[64,2048]{1,0:T(8,128)} %get-tuple-element.23) | copy-start | bytes 1572868
  140.0 7.8 %collective-permute-start.19 = (bf16[64,2048]{1,0:T(8,128)(2,1)S(1)}, bf16[64,2048]{1,0:T(8,128)(2,1)S(1)}, u32[]{:S(2)}, u32[]{:S(2)}) collective-permute-start(bf16[64,2048]{1,0:T(8,128)(2,1)S(1)} %get-tuple-element.27), channel_id=1, source_target_pairs={{0,2},{1,3},{8,10},{9,11},{16,18},{17,19},{24,26},{25,27}} | collective-permute-start | bytes 786440 | tf_op jit(solution)/shard_map/ppermute | solution.py:373
  141.6 10.7 %collective-permute-start.22 = (bf16[64,2048]{1,0:T(8,128)(2,1)S(1)}, bf16[64,2048]{1,0:T(8,128)(2,1)S(1)}, u32[]{:S(2)}, u32[]{:S(2)}) collective-permute-start(bf16[64,2048]{1,0:T(8,128)(2,1)S(1)} %get-tuple-element.28), channel_id=1, source_target_pairs={{6,4},{7,5},{14,12},{15,13},{22,20},{23,21},{30,28},{31,29}} | collective-permute-start | bytes 786440 | tf_op jit(solution)/shard_map/ppermute | solution.py:374
  147.9 10.9 %collective-permute-start.20 = (bf16[64,2048]{1,0:T(8,128)(2,1)S(1)}, bf16[64,2048]{1,0:T(8,128)(2,1)S(1)}, u32[]{:S(2)}, u32[]{:S(2)}) collective-permute-start(bf16[64,2048]{1,0:T(8,128)(2,1)S(1)} %fusion.3), channel_id=1, source_target_pairs={{0,2},{1,3},{2,4},{3,5},{8,10},{9,11},{10,12},{11,13},{16,18},{17,... | collective-permute-start | bytes 786440 | tf_op jit(solution)/shard_map/ppermute | solution.py:373
  159.0 5.7 %collective-permute-start.23 = (bf16[64,2048]{1,0:T(8,128)(2,1)S(1)}, bf16[64,2048]{1,0:T(8,128)(2,1)S(1)}, u32[]{:S(2)}, u32[]{:S(2)}) collective-permute-start(bf16[64,2048]{1,0:T(8,128)(2,1)S(1)} %get-tuple-element.26), channel_id=1, source_target_pairs={{6,4},{7,5},{4,2},{5,3},{14,12},{15,13},{12,10},{13,11},{22,20},{2... | collective-permute-start | bytes 786440 | tf_op jit(solution)/shard_map/ppermute | solution.py:374
  159.7 8.9 %collective-permute-start.21 = (bf16[64,2048]{1,0:T(8,128)(2,1)S(1)}, bf16[64,2048]{1,0:T(8,128)(2,1)S(1)}, u32[]{:S(2)}, u32[]{:S(2)}) collective-permute-start(bf16[64,2048]{1,0:T(8,128)(2,1)S(1)} %get-tuple-element.25), channel_id=1, source_target_pairs={{0,2},{1,3},{2,4},{3,5},{4,6},{5,7},{8,10},{9,11},{10,12},{11,13},... | collective-permute-start | bytes 786440 | tf_op jit(solution)/shard_map/ppermute | solution.py:373
  164.8 11.3 %collective-permute-start.24 = (bf16[64,2048]{1,0:T(8,128)(2,1)S(1)}, bf16[64,2048]{1,0:T(8,128)(2,1)S(1)}, u32[]{:S(2)}, u32[]{:S(2)}) collective-permute-start(bf16[64,2048]{1,0:T(8,128)(2,1)S(1)} %fusion.2), channel_id=1, source_target_pairs={{6,4},{7,5},{4,2},{5,3},{2,0},{3,1},{14,12},{15,13},{12,10},{13,11... | collective-permute-start | bytes 786440 | tf_op jit(solution)/shard_map/ppermute | solution.py:374
where the time goes:
time: 178 us; the launch traced here: 177 us
  starting transfers between devices  62.4 us (35%)
  waiting for transfers between devices  58.6 us (33%)
  Pallas kernels  31.6 us (18%)
  local copies, waits for them, and re-layouts  14.3 us (8%)
  other arithmetic  6.45 us (4%)
  matrix products  3.21 us (2%)
    ppermute x6, starting transfers between devices, line_scatter(): right = lax.ppermute(to_right, 'exp', rightward(places, t))  34.9 us
    ppermute x6, waiting for transfers between devices, line_scatter(): right = lax.ppermute(to_right, 'exp', rightward(places, t))  21.6 us
    ppermute x3, waiting for transfers between devices, line_gather(): lax.ppermute(left, 'exp', [(a, b) for a, b in leftward(places, places) if...  18.7 us
    pallas_call x1, Pallas kernels, per_device(): pl.pallas_call(state_kernel, out_shape=(wide, wide, jax.ShapeDtypeStruct(...  13.8 us
    unnamed x48, local copies, waits for them, and re-layouts  12.5 us
    ppermute x2, starting transfers between devices, per_device(): got = lax.ppermute(sent, 'seq', pairs)  10.4 us
    pallas_call x1, Pallas kernels, experts(): pl.pallas_call(functools.partial(expert_kernel, places, halves), grid=(2...  8.58 us
    ppermute x6, waiting for transfers between devices, line_scatter(): left = lax.ppermute(to_left, 'exp', leftward(places, t))  7.51 us
  transfers between devices with their start and end apart: 25, of which 13 were waited for; matrix products, arithmetic and copies ran while one was open for 4% of the time, Pallas kernels for 13%

commit v1 on v0

--- a/solution.py
+++ b/solution.py
@@ -15,11 +15,16 @@
 F32 = jnp.float32
 BF16 = jnp.bfloat16
 EXACT = lax.Precision.HIGHEST
-VMEM_BYTES = 48 * 1024 * 1024
+SMALL_VMEM = 20 * 1024 * 1024
+EXPERT_VMEM = 32 * 1024 * 1024
 
 
 def whole(memory_space=pltpu.VMEM):
     return pl.BlockSpec(memory_space=memory_space)
+
+
+def blocks_of(*arrays):
+    return [pl.BlockSpec(a.shape, lambda i, n=a.ndim: (0,) * n) for a in arrays]
 
 
 def mm(a, b):
@@ -153,8 +158,15 @@
         total_ref[h] = carried[h].astype(BF16)
 
 
-def readout_kernel(query_ref, key_ref, gate_ref, gain_ref, decay_ref, wu_ref, prefix_ref,
-                   lin_ref, own_ref, gated_ref):
+def readout_kernel(query_ref, key_ref, gate_ref, gain_ref, decay_ref, ids_ref, weight_ref, wu_ref, prefix_ref,
+                   lin_ref, own_ref, gated_ref, routes_ref):
+    expert = lax.broadcasted_iota(jnp.int32, (LANES, ids_ref.shape[1]), 0)
+    routes = jnp.zeros(expert.shape, F32)
+    for k in range(ids_ref.shape[0]):
+        routes += jnp.where(
+            ids_ref[k : k + 1, :] == expert, weight_ref[k : k + 1, :].astype(F32), 0.0
+        )
+    routes_ref[...] = routes.T.astype(BF16)
     heads = decay_ref.shape[0]
     key_heads = key_ref.shape[1] // DK
     group = heads // key_heads
@@ -199,92 +211,111 @@
             gated_ref[tokens, lanes] = gain_ref[...] * gate / (1.0 + jnp.exp(-gate))
 
 
-def compose_kernel(own_ref, got_ref, out_ref):
+def scan_kernel(last, later_ref, own_ref, got_ref, before_ref, total_ref, prefix_ref):
+    later = later_ref[0] == 1
     for h in range(own_ref.shape[0]):
-        out = mm(own_ref[h, :, :DK], got_ref[h])
-        bias = own_ref[h, :, DK:].astype(F32)
-        out_ref[h] = (
-            out + jnp.concatenate([jnp.zeros((DK, DK), F32), bias], axis=1)
-        ).astype(BF16)
-
-
-def compose(own, got):
+        own, got = own_ref[h], got_ref[h]
+        first = jnp.where(later, got, own)
+        second = jnp.where(later, own, got)
+        bias = second[:, DK:].astype(F32)
+        if last:
+            total_ref[h] = (mm(second[:, :DK], first[:, DK:]) + bias).astype(BF16)
+        else:
+            total_ref[h] = (
+                mm(second[:, :DK], first)
+                + jnp.concatenate([jnp.zeros((DK, DK), F32), bias], axis=1)
+            ).astype(BF16)
+        before = before_ref[h]
+        joined = mm(before[:, :DK], got) + jnp.concatenate(
+            [jnp.zeros((DK, DK), F32), before[:, DK:].astype(F32)], axis=1
+        )
+        prefix_ref[h] = jnp.where(later, joined.astype(BF16), before)
+
+
+def scan_step(later, own, got, before, last):
+    heads = own.shape[0]
+    total = jax.ShapeDtypeStruct((heads, DK, DV if last else DK + DV), BF16)
     return pl.pallas_call(
-        compose_kernel,
-        out_shape=jax.ShapeDtypeStruct(own.shape, BF16),
-        in_specs=[whole(), whole()],
-        out_specs=whole(),
-    )(own, got)
-
-
-def bias_kernel(own_ref, got_ref, out_ref):
-    for h in range(own_ref.shape[0]):
-        out = mm(own_ref[h, :, :DK], got_ref[h])
-        out_ref[h] = (out + own_ref[h, :, DK:].astype(F32)).astype(BF16)
-
-
-def compose_bias(own, got):
-    return pl.pallas_call(
-        bias_kernel,
-        out_shape=jax.ShapeDtypeStruct(got.shape, BF16),
-        in_specs=[whole(), whole()],
-        out_specs=whole(),
-    )(own, got)
-
-
-def mix_kernel(core_ref, state_ref, lin_ref, own_ref, gated_ref, keep_ref, send_ref):
-    core = core_ref[0]
-    heads = state_ref.shape[0]
+        functools.partial(scan_kernel, last),
+        out_shape=(total, jax.ShapeDtypeStruct(own.shape, BF16)),
+        in_specs=[whole(pltpu.SMEM)] + [whole()] * 3,
+        out_specs=(whole(),) * 2,
+        compiler_params=pltpu.CompilerParams(vmem_limit_bytes=SMALL_VMEM),
+    )(later, own, got, before)
+
+
+def mix_kernel(core_ref, prefix_ref, got_ref, lin_ref, own_ref, gated_ref, keep_ref, send_ref):
+    core, place, later = core_ref[0], core_ref[1], core_ref[2] == 1
+    heads = prefix_ref.shape[0]
+    places = keep_ref.shape[0]
     rows = keep_ref.shape[1]
-    for z in range(keep_ref.shape[0]):
+    states = []
+    for h in range(heads):
+        prefix = prefix_ref[h]
+        bias = prefix[:, DK:].astype(F32)
+        joined = mm(prefix[:, :DK], got_ref[h]) + bias
+        states.append(jnp.where(later, joined, bias).astype(BF16))
+    for d in range(places):
+        at = jnp.bitwise_xor(place, d)
         for out_ref, side in ((send_ref, 1 - core), (keep_ref, core)):
-            tokens = pl.ds(pl.multiple_of((2 * z + side) * rows, rows), rows)
+            tokens = pl.ds(pl.multiple_of((2 * at + side) * rows, rows), rows)
             for h in range(heads):
                 lanes = slice(h * DV, (h + 1) * DV)
-                readout = own_ref[tokens, lanes] + mm(lin_ref[tokens, lanes], state_ref[h])
+                readout = own_ref[tokens, lanes] + mm(lin_ref[tokens, lanes], states[h])
                 scale = lax.rsqrt(jnp.mean(readout * readout, axis=1, keepdims=True) + EPS)
-                out_ref[z, :, lanes] = (readout * scale * gated_ref[tokens, lanes]).astype(BF16)
-
-
-def norm_kernel(hidden_ref, mine_ref, right_ref, left_ref, gain_ref, ids_ref, weight_ref,
-                residual_ref, out_ref):
-    residual = (
-        hidden_ref[...].astype(F32)
-        + mine_ref[...].astype(F32)
-        + right_ref[...].astype(F32)
-        + left_ref[...].astype(F32)
-    )
+                out_ref[d, :, lanes] = (readout * scale * gated_ref[tokens, lanes]).astype(BF16)
+
+
+def project_kernel(keep_ref, got_ref, own_ref, sib_ref, *out_refs):
+    rows = keep_ref.shape[1]
+    depth = keep_ref.shape[2]
+    product = jnp.dot(
+        keep_ref[...].reshape(-1, depth), own_ref[...], preferred_element_type=F32
+    ) + jnp.dot(got_ref[...].reshape(-1, depth), sib_ref[...], preferred_element_type=F32)
+    for d, out_ref in enumerate(out_refs):
+        out_ref[...] = product[d * rows : (d + 1) * rows].astype(BF16)
+
+
+def project(keep, got, own, sib):
+    places, rows, depth = keep.shape
+    width = own.shape[1]
+    tile = 512
+    return pl.pallas_call(
+        project_kernel,
+        grid=(width // tile,),
+        out_shape=(jax.ShapeDtypeStruct((rows, width), BF16),) * places,
+        in_specs=[pl.BlockSpec((places, rows, depth), lambda i: (0, 0, 0))] * 2
+        + [pl.BlockSpec((depth, tile), lambda i: (0, i))] * 2,
+        out_specs=(pl.BlockSpec((rows, tile), lambda i: (0, i)),) * places,
+        compiler_params=pltpu.CompilerParams(vmem_limit_bytes=SMALL_VMEM),
+    )(keep, got, own, sib)
+
+
+def norm_kernel(hidden_ref, gain_ref, routes_ref, *refs):
+    *part_refs, residual_ref, out_ref = refs
+    residual = hidden_ref[...].astype(F32)
+    for part_ref in part_refs:
+        residual += part_ref[...].astype(F32)
     residual_ref[...] = residual
     scale = lax.rsqrt(jnp.mean(residual * residual, axis=1, keepdims=True) + EPS)
     width = residual.shape[1]
     out_ref[:, :width] = (residual * scale * gain_ref[...]).astype(BF16)
-    lane = lax.broadcasted_iota(jnp.int32, (residual.shape[0], LANES), 1)
-    routes = jnp.zeros((residual.shape[0], LANES), F32)
-    for k in range(ids_ref.shape[1]):
-        routes += jnp.where(
-            ids_ref[:, k : k + 1] == lane, weight_ref[:, k : k + 1].astype(F32), 0.0
-        )
-    out_ref[:, width:] = routes.astype(BF16)
+    out_ref[:, width:] = routes_ref[...]
 
 
 def expert_kernel(places, halves, place_ref, *refs):
-    slots = refs[: 2 * places - 1]
-    gate_own, up_own, down_own, gate_sib, up_sib, down_sib, out_ref, x_ref, sum_ref = refs[
-        2 * places - 1 :
-    ]
+    slots = refs[:places]
+    gate_own, up_own, down_own, gate_sib, up_sib, down_sib = refs[places : places + 6]
+    out_refs = refs[places + 6 : -2]
+    x_ref, sum_ref = refs[-2:]
     step = pl.program_id(0)
     place, core = place_ref[0], place_ref[1]
-    rows = slots[0].shape[0]
-    width = out_ref.shape[-1]
+    rows, width = out_refs[0].shape
 
     @pl.when(step == 0)
     def _():
-        for number, slot in enumerate(slots):
-            spot = place + number - (places - 1)
-
-            @pl.when(jnp.logical_and(spot >= 0, spot < places))
-            def _(slot=slot, spot=spot):
-                x_ref[pl.ds(pl.multiple_of(spot * rows, rows), rows), :] = slot[...]
+        for d, slot in enumerate(slots):
+            x_ref[d * rows : (d + 1) * rows, :] = slot[...]
 
     def add(gate, up, down, expert, fresh):
         x = x_ref[:, :width]
@@ -314,10 +345,12 @@
 
     @pl.when(step == 2 * halves - 1)
     def _():
-        out_ref[...] = sum_ref[...].astype(BF16).reshape(out_ref.shape)
-
-
-def experts(place, core, slots, own, sib, places):
+        for d, out_ref in enumerate(out_refs):
+            out_ref[...] = sum_ref[d * rows : (d + 1) * rows].astype(BF16)
+
+
+def experts(place_core, slots, own, sib):
+    places = len(slots)
     rows = slots[0].shape[0]
     width = own[0].shape[1]
     inner = own[0].shape[2]
@@ -334,59 +367,29 @@
     return pl.pallas_call(
         functools.partial(expert_kernel, places, halves),
         grid=(2 * halves,),
-        out_shape=jax.ShapeDtypeStruct((places, rows, width), BF16),
+        out_shape=(jax.ShapeDtypeStruct((rows, width), BF16),) * places,
         in_specs=[whole(pltpu.SMEM)]
-        + [whole()] * len(slots)
+        + [whole()] * places
         + specs(lambda i: jnp.minimum(i, halves - 1))
         + specs(lambda i: jnp.maximum(i - halves, 0)),
-        out_specs=whole(),
+        out_specs=(whole(),) * places,
         scratch_shapes=[
             pltpu.VMEM((places * rows, slots[0].shape[1]), BF16),
             pltpu.VMEM((places * rows, width), F32),
         ],
-        compiler_params=pltpu.CompilerParams(vmem_limit_bytes=VMEM_BYTES),
-    )(jnp.stack([place, core]).astype(jnp.int32), *slots, *own, *sib)
-
-
-def rightward(places, count):
-    return [(2 * i + c, 2 * i + 2 + c) for i in range(min(count, places - 1)) for c in range(2)]
-
-
-def leftward(places, count):
-    return [
-        (2 * i + c, 2 * i - 2 + c)
-        for i in range(places - 1, max(places - 1 - count, 0), -1)
-        for c in range(2)
+        compiler_params=pltpu.CompilerParams(vmem_limit_bytes=EXPERT_VMEM),
+    )(place_core, *slots, *own, *sib)
+
+
+def between_places(places, d):
+    return [(2 * i + c, 2 * (i ^ d) + c) for i in range(places) for c in range(2)]
+
+
+def exchange(pieces):
+    places = len(pieces)
+    return [pieces[0]] + [
+        lax.ppermute(pieces[d], "exp", between_places(places, d)) for d in range(1, places)
     ]
-
-
-def line_scatter(parts, place, places):
-    def part(at):
-        return lax.dynamic_index_in_dim(parts, jnp.clip(at, 0, places - 1), 0, False)
-
-    right = left = None
-    for t in range(1, places):
-        to_right, to_left = part(places - t + place), part(t + place - places)
-        if t > 1:
-            to_right = (to_right.astype(F32) + right.astype(F32)).astype(BF16)
-            to_left = (to_left.astype(F32) + left.astype(F32)).astype(BF16)
-        right = lax.ppermute(to_right, "exp", rightward(places, t))
-        left = lax.ppermute(to_left, "exp", leftward(places, t))
-    return part(place), right, left
-
-
-def line_gather(own, places):
-    slots = {0: own}
-    right = left = own
-    for t in range(1, places):
-        right = lax.ppermute(
-            right, "exp", [(a, b) for a, b in rightward(places, places) if a // 2 >= t - 1]
-        )
-        left = lax.ppermute(
-            left, "exp", [(a, b) for a, b in leftward(places, places) if a // 2 <= places - t]
-        )
-        slots[-t], slots[t] = right, left
-    return [slots[t] for t in range(1 - places, places)]
 
 
 def per_device(
@@ -413,7 +416,8 @@
     seqs, exps = lax.axis_size("seq"), lax.axis_size("exp")
     places = exps // 2
     me = lax.axis_index("exp")
-    place, core = me // 2, me % 2
+    place, core = lax.div(me, 2), lax.rem(me, 2)
+    here = lax.axis_index("seq")
     swap = [(i, i ^ 1) for i in range(exps)]
 
     out_sib = lax.ppermute(out_weight, "exp", swap)
@@ -424,68 +428,66 @@
     wu, prefixes, total = pl.pallas_call(
         state_kernel,
         out_shape=(wide, wide, jax.ShapeDtypeStruct((heads, DK, DK + DV), BF16)),
-        in_specs=[whole()] * 4,
+        grid=(1,),
+        in_specs=blocks_of(key_proj, value_proj, log_decay, write_rate),
         out_specs=(whole(),) * 3,
-        compiler_params=pltpu.CompilerParams(vmem_limit_bytes=VMEM_BYTES),
+        compiler_params=pltpu.CompilerParams(vmem_limit_bytes=SMALL_VMEM),
         cost_estimate=pl.CostEstimate(flops=10**10, bytes_accessed=4 * 10**6, transcendentals=0),
     )(key_proj, value_proj, log_decay, write_rate)
 
-    lin, own_read, gated = pl.pallas_call(
+    lin, own_read, gated, routes = pl.pallas_call(
         readout_kernel,
         out_shape=(
             jax.ShapeDtypeStruct((length, heads * DV), BF16),
             jax.ShapeDtypeStruct((length, heads * DV), F32),
             jax.ShapeDtypeStruct((length, heads * DV), F32),
+            jax.ShapeDtypeStruct((tok, LANES), BF16),
         ),
-        in_specs=[whole()] * 7,
-        out_specs=(whole(),) * 3,
-        compiler_params=pltpu.CompilerParams(vmem_limit_bytes=VMEM_BYTES),
+        grid=(1,),
+        in_specs=blocks_of(query_proj, key_proj, gate_proj, head_gain.reshape(1, DV), log_decay, expert_ids.T,
+                           route_weight.T) + [whole()] * 2,
+        out_specs=(whole(),) * 4,
+        compiler_params=pltpu.CompilerParams(vmem_limit_bytes=SMALL_VMEM),
         cost_estimate=pl.CostEstimate(flops=6 * 10**9, bytes_accessed=4 * 10**6, transcendentals=0),
-    )(query_proj, key_proj, gate_proj, head_gain.reshape(1, DV), log_decay, wu, prefixes)
-
-    upto, before, step = total, None, 1
+    )(query_proj, key_proj, gate_proj, head_gain.reshape(1, DV), log_decay, expert_ids.T, route_weight.T, wu, prefixes)
+
+    eye = jnp.concatenate([jnp.eye(DK, dtype=BF16), jnp.zeros((DK, DV), BF16)], axis=1)
+    before = jnp.broadcast_to(eye, total.shape)
+    summed, step = total, 1
+    got = jnp.zeros((heads, DK, DV), BF16)
+    later = jnp.zeros((), jnp.int32)
     while step < seqs:
-        pairs = [(i, i + step) for i in range(seqs - step)]
-        last = 2 * step >= seqs
-        sent = upto[:, :, DK:] if last and before is not None else upto
-        got = lax.ppermute(sent, "seq", pairs)
-        if last:
-            state = got[:, :, DK:] if before is None else compose_bias(before, got)
-        else:
-            upto = compose(upto, got)
-            before = got if before is None else compose(before, got)
+        later = lax.rem(lax.div(here, step), 2)
+        got = lax.ppermute(summed, "seq", [(i, i ^ step) for i in range(seqs)])
+        if step == 1:
+            got, out_sib, *sib = lax.optimization_barrier((got, out_sib, *sib))
+        if 2 * step < seqs:
+            summed, before = scan_step(later.reshape(1), summed, got, before, 4 * step >= seqs)
         step *= 2
 
     half = jax.ShapeDtypeStruct((places, tok, heads * DV), BF16)
     keep, send = pl.pallas_call(
         mix_kernel,
         out_shape=(half, half),
-        in_specs=[whole(pltpu.SMEM)] + [whole()] * 4,
+        in_specs=[whole(pltpu.SMEM)] + [whole()] * 5,
         out_specs=(whole(),) * 2,
-        compiler_params=pltpu.CompilerParams(vmem_limit_bytes=VMEM_BYTES),
-    )(core.reshape(1).astype(jnp.int32), state, lin, own_read, gated)
+        compiler_params=pltpu.CompilerParams(vmem_limit_bytes=SMALL_VMEM),
+    )(jnp.stack([core, place, later]), before, got, lin, own_read, gated)
     got = lax.ppermute(send, "exp", swap)
-    parts = (
-        jnp.dot(keep.reshape(-1, heads * DV), out_weight, preferred_element_type=F32)
-        + jnp.dot(got.reshape(-1, heads * DV), out_sib, preferred_element_type=F32)
-    ).astype(BF16).reshape(places, tok, width)
-
-    mine, right, left = line_scatter(parts, place, places)
+    summands = exchange(project(keep, got, out_weight, out_sib))
     residual, normed = pl.pallas_call(
         norm_kernel,
         out_shape=(
             jax.ShapeDtypeStruct((tok, width), F32),
             jax.ShapeDtypeStruct((tok, width + LANES), BF16),
         ),
-        in_specs=[whole()] * 7,
+        in_specs=[whole()] * (3 + places),
         out_specs=(whole(),) * 2,
-    )(hidden_in, mine, right, left, post_gain.reshape(1, width), expert_ids, route_weight)
-    slots = line_gather(normed, places)
-    sums = experts(place, core, slots, own, sib, places)
-    mine, right, left = line_scatter(sums, place, places)
-    return (
-        residual + mine.astype(F32) + right.astype(F32) + left.astype(F32)
-    ).astype(BF16)
+        compiler_params=pltpu.CompilerParams(vmem_limit_bytes=SMALL_VMEM),
+    )(hidden_in, post_gain.reshape(1, width), routes, *summands)
+    slots = exchange([normed] * places)
+    summands = exchange(experts(jnp.stack([place, core]), slots, own, sib))
+    return sum((s.astype(F32) for s in summands), residual).astype(BF16)
 
 
 def solution(mesh):

time: 178 us -> 141 us (0.79)
  starting transfers between devices: 62.4 us -> 23.8 us
  local copies, waits for them, and re-layouts: 14.3 us -> 22.2 us
  waiting for transfers between devices: 58.6 us -> 64.4 us
  other arithmetic: 6.45 us -> 1.05 us
  matrix products: 3.21 us -> 0 us
  Pallas kernels: 31.6 us -> 29.2 us
    ppermute x20 -> x11, starting transfers between devices: 61.4 us -> 22.7 us  [the longest x9 18 us: exchange(): lax.ppermute(pieces[d], 'exp', between_places(places, d))]
    unnamed x48 -> x54, local copies, waits for them, and re-layouts: 12.5 us -> 22.2 us
    ppermute x20 -> x11, waiting for transfers between devices: 57.1 us -> 62.9 us  [the longest x9 56.4 us: exchange(): lax.ppermute(pieces[d], 'exp', between_places(places, d))]
    convert_element_type x7 -> x1, other arithmetic: 6.37 us -> 0.87 us  [per_device(): return sum((s.astype(F32) for s in summands), residual).astype(BF16)]
    dot_general x2 -> x0, matrix products: 3.21 us -> none  [the longest x1 2.45 us: per_device(): jnp.dot(got.reshape(-1, heads * DV), out_sib, preferred_element_type=F32)]
    pallas_call x1, Pallas kernels: 2.27 us -> 0.28 us  [per_device(): pl.pallas_call(norm_kernel, out_shape=(jax.ShapeDtypeStruct((tok, width),...]
  transfers between devices with their start and end apart: 25 -> 16, of which waited for: 13 -> 8; matrix products, arithmetic and copies ran while one was open for 4% -> 0% of each run, Pallas kernels for 13% -> 12%
where the time goes in v1:
time: 141 us
  waiting for transfers between devices  64.4 us (46%)
  Pallas kernels  29.2 us (21%)
  starting transfers between devices  23.8 us (17%)
  local copies, waits for them, and re-layouts  22.2 us (16%)
    ppermute x9, waiting for transfers between devices, exchange(): lax.ppermute(pieces[d], 'exp', between_places(places, d))  56.4 us
    unnamed x54, local copies, waits for them, and re-layouts  22.2 us
    ppermute x9, starting transfers between devices, exchange(): lax.ppermute(pieces[d], 'exp', between_places(places, d))  18 us
    pallas_call x1, Pallas kernels, per_device(): pl.pallas_call(state_kernel, out_shape=(wide, wide, jax.ShapeDtypeStruct(...  13.8 us
    pallas_call x1, Pallas kernels, experts(): pl.pallas_call(functools.partial(expert_kernel, places, halves), grid=(2...  7.98 us
    ppermute x2, waiting for transfers between devices, per_device(): got = lax.ppermute(summed, 'seq', [(i, i ^ step) for i in range(seqs)])  6.44 us
    ppermute x2, starting transfers between devices, per_device(): got = lax.ppermute(summed, 'seq', [(i, i ^ step) for i in range(seqs)])  4.7 us
  transfers between devices with their start and end apart: 16, of which 8 were waited for; matrix products, arithmetic and copies ran while one was open for 0% of the time, Pallas kernels for 12%

profile of v1, /device:TPU:0, one launch (start us, length us, event | category | flops | bytes accessed | tf_op | source)
XLA Modules:
  0.0 140.8 jit_solution(6474057007008615085)
XLA Ops:
  0.0 0.5 collective-permute-start.1
  0.5 0.5 collective-permute-start.3
  1.0 1.0 copy-done.12
  2.1 0.9 copy-done.15
  3.0 0.7 copy-done.17
  3.7 0.7 copy-done.18
  4.4 13.8 %shard_map.145 = (bf16[4,4,128,256]{3,2,1,0:T(8,128)(2,1)S(1)}, bf16[4,4,128,256]{3,2,1,0:T(8,128)(2,1)S(1)}, bf16[4,128,256]{2,1,0:T(8,128)(2,1)S(1)}) custom-call(bf16[512,256]{1,0:T(8,128)(2,1)S(1)} %copy-done.15, bf16[512,512]{1,0:T(8,128)(2,1)S(1)} %copy-done.12, f32[4,512]{1,0:T(4,128)S(1)} %copy-done.18, f32[4,512]{1,0:T(4,128)S(1)} %copy-done.17), custom_call_target="tpu_custom_call" | custom-call | flops 10000000000 | bytes 4000000 | tf_op jit(solution)/shard_map/pallas_call | solution.py:428
  18.2 1.0 copy-done.23
  19.2 1.0 copy-done.25
  20.1 2.9 %collective-permute-start = (bf16[4,128,256]{2,1,0:T(8,128)(2,1)S(1)}, bf16[4,128,256]{2,1,0:T(8,128)(2,1)S(1)}, u32[]{:S(2)}, u32[]{:S(2)}) collective-permute-start(bf16[4,128,256]{2,1,0:T(8,128)(2,1)S(1)} %get-tuple-element.34.own_ref), channel_id=1, source_target_pairs={{0,8},{8,0},{16,24},{24,16},{1,9},{9,1},{17,25},{25,17},{2,10},{10... | collective-permute-start | bytes 786440 | tf_op jit(solution)/shard_map/ppermute | solution.py:461
  23.1 6.4 %collective-permute-done.got_ref = bf16[4,128,256]{2,1,0:T(8,128)(2,1)S(1)} collective-permute-done((bf16[4,128,256]{2,1,0:T(8,128)(2,1)S(1)}, bf16[4,128,256]{2,1,0:T(8,128)(2,1)S(1)}, u32[]{:S(2)}, u32[]{:S(2)}) %collective-permute-start) | collective-permute-done | bytes 262176 | tf_op jit(solution)/shard_map/ppermute | solution.py:461
  29.5 1.4 copy-done.1
  31.0 0.9 shard_map.147
  31.9 1.8 %collective-permute-start.5 = (bf16[4,128,128]{2,1,0:T(8,128)(2,1)}, bf16[4,128,128]{2,1,0:T(8,128)(2,1)S(1)}, u32[]{:S(2)}, u32[]{:S(2)}) collective-permute-start(bf16[4,128,128]{2,1,0:T(8,128)(2,1)} %get-tuple-element.37), channel_id=1, source_target_pairs={{0,16},{8,24},{16,0},{24,8},{1,17},{9,25},{17,1},{25,9},{2,18},{10... | collective-permute-start | bytes 393224 | tf_op jit(solution)/shard_map/ppermute | solution.py:461
  33.6 1.0 copy-done.13
  34.7 0.9 copy-done.14
  35.6 0.9 copy-done.16
  36.6 0.7 copy-done.19
  37.3 0.7 copy-done.20
  38.0 0.7 copy-done.21
  38.6 0.7 copy-done.22
  39.3 1.2 copy-done.24
  40.5 1.2 copy-done.26
  41.8 2.7 %shard_map.146 = (bf16[512,512]{1,0:T(8,128)(2,1)S(1)}, f32[512,512]{1,0:T(8,128)S(1)}, f32[512,512]{1,0:T(8,128)S(1)}, bf16[64,128]{1,0:T(8,128)(2,1)S(1)}) custom-call(bf16[512,256]{1,0:T(8,128)(2,1)S(1)} %copy-done.14, bf16[512,256]{1,0:T(8,128)(2,1)S(1)} %copy-done.16, bf16[512,512]{1,0:T(8,128)(2,1)S(1)} %copy-done.13, f32[1,128]{1,0:T(1,128)S(1)} %bitcast.11, ...), custom_call_target="tpu_custom_call" | custom-call | flops 6000000000 | bytes 4000000 | tf_op jit(solution)/shard_map/pallas_call | solution.py:438
  44.5 1.0 copy-done.6
  45.4 0.8 copy-done.8
  46.3 1.4 copy-done.7
  47.7 1.0 copy-done.9
  48.7 1.2 shard_map.148
  50.0 1.5 %collective-permute-done.6.got_ref = bf16[4,64,512]{2,1,0:T(8,128)(2,1)S(1)} collective-permute-done((bf16[4,64,512]{2,1,0:T(8,128)(2,1)S(1)}, bf16[4,64,512]{2,1,0:T(8,128)(2,1)S(1)}, u32[]{:S(2)}, u32[]{:S(2)}) %collective-permute-start.6) | collective-permute-done | bytes 262176 | tf_op jit(solution)/shard_map/ppermute | solution.py:476
  51.5 1.6 %copy-done.2 = bf16[512,2048]{1,0:T(8,128)(2,1)S(1)} copy-done((bf16[512,2048]{1,0:T(8,128)(2,1)S(1)}, bf16[512,2048]{1,0:T(8,128)(2,1)}, u32[]{:S(2)}) %copy-start.2) | copy-done | bytes 2097176
  53.1 2.4 %shard_map.149 = (bf16[64,2048]{1,0:T(8,128)(2,1)S(1)}, bf16[64,2048]{1,0:T(8,128)(2,1)S(1)}, bf16[64,2048]{1,0:T(8,128)(2,1)S(1)}, bf16[64,2048]{1,0:T(8,128)(2,1)S(1)}) custom-call(bf16[4,64,512]{2,1,0:T(8,128)(2,1)S(1)} %get-tuple-element.41.keep_ref, bf16[4,64,512]{2,1,0:T(8,128)(2,1)S(1)} %collective-permute-done.6.got_ref, ...), custom_call_target="tpu_custom_call" | custom-call | tf_op jit(solution)/shard_map/pallas_call | solution.py:283
  55.5 1.6 %collective-permute-start.7 = (bf16[64,2048]{1,0:T(8,128)(2,1)S(1)}, bf16[64,2048]{1,0:T(8,128)(2,1)S(1)}, u32[]{:S(2)}, u32[]{:S(2)}) collective-permute-start(bf16[64,2048]{1,0:T(8,128)(2,1)S(1)} %get-tuple-element.45), channel_id=1, source_target_pairs={{0,2},{1,3},{2,0},{3,1},{4,6},{5,7},{6,4},{7,5},{8,10},{9,11},{10,... | collective-permute-start | bytes 786440 | tf_op jit(solution)/shard_map/ppermute | solution.py:391
  57.2 2.6 %collective-permute-start.8 = (bf16[64,2048]{1,0:T(8,128)(2,1)S(1)}, bf16[64,2048]{1,0:T(8,128)(2,1)S(1)}, u32[]{:S(2)}, u32[]{:S(2)}) collective-permute-start(bf16[64,2048]{1,0:T(8,128)(2,1)S(1)} %get-tuple-element.46), channel_id=1, source_target_pairs={{0,4},{1,5},{2,6},{3,7},{4,0},{5,1},{6,2},{7,3},{8,12},{9,13},{10,... | collective-permute-start | bytes 786440 | tf_op jit(solution)/shard_map/ppermute | solution.py:391
  60.0 9.0 %collective-permute-done.7.refs_1_ = bf16[64,2048]{1,0:T(8,128)(2,1)S(1)} collective-permute-done((bf16[64,2048]{1,0:T(8,128)(2,1)S(1)}, bf16[64,2048]{1,0:T(8,128)(2,1)S(1)}, u32[]{:S(2)}, u32[]{:S(2)}) %collective-permute-start.7) | collective-permute-done | bytes 262176 | tf_op jit(solution)/shard_map/ppermute | solution.py:391
  69.0 9.5 %collective-permute-done.8.refs_2_ = bf16[64,2048]{1,0:T(8,128)(2,1)S(1)} collective-permute-done((bf16[64,2048]{1,0:T(8,128)(2,1)S(1)}, bf16[64,2048]{1,0:T(8,128)(2,1)S(1)}, u32[]{:S(2)}, u32[]{:S(2)}) %collective-permute-start.8) | collective-permute-done | bytes 262176 | tf_op jit(solution)/shard_map/ppermute | solution.py:391
  78.8 5.2 %collective-permute-start.10 = (bf16[64,2176]{1,0:T(8,128)(2,1)S(1)}, bf16[64,2176]{1,0:T(8,128)(2,1)S(1)}, u32[]{:S(2)}, u32[]{:S(2)}) collective-permute-start(bf16[64,2176]{1,0:T(8,128)(2,1)S(1)} %get-tuple-element.49.refs_0_), channel_id=1, source_target_pairs={{0,2},{1,3},{2,0},{3,1},{4,6},{5,7},{6,4},{7,5},{8,10},{9,11},{10,... | collective-permute-start | bytes 835592 | tf_op jit(solution)/shard_map/ppermute | solution.py:391
  84.0 1.1 collective-permute-start.11
  85.1 1.4 collective-permute-start.12
  86.5 8.1 %collective-permute-done.10.refs_1_ = bf16[64,2176]{1,0:T(8,128)(2,1)S(1)} collective-permute-done((bf16[64,2176]{1,0:T(8,128)(2,1)S(1)}, bf16[64,2176]{1,0:T(8,128)(2,1)S(1)}, u32[]{:S(2)}, u32[]{:S(2)}) %collective-permute-start.10) | collective-permute-done | bytes 278560 | tf_op jit(solution)/shard_map/ppermute | solution.py:391
  94.6 11.8 %collective-permute-done.11.refs_2_ = bf16[64,2176]{1,0:T(8,128)(2,1)S(1)} collective-permute-done((bf16[64,2176]{1,0:T(8,128)(2,1)S(1)}, bf16[64,2176]{1,0:T(8,128)(2,1)S(1)}, u32[]{:S(2)}, u32[]{:S(2)}) %collective-permute-start.11) | collective-permute-done | bytes 278560 | tf_op jit(solution)/shard_map/ppermute | solution.py:391
  106.4 1.6 %copy-done.5 = bf16[1,512,2048]{2,1,0:T(8,128)(2,1)S(1)} copy-done((bf16[1,512,2048]{2,1,0:T(8,128)(2,1)S(1)}, bf16[1,512,2048]{2,1,0:T(8,128)(2,1)}, u32[]{:S(2)}) %copy-start.5) | copy-done | bytes 2097176
  108.0 8.0 %shard_map.151 = (bf16[64,2048]{1,0:T(8,128)(2,1)S(1)}, bf16[64,2048]{1,0:T(8,128)(2,1)S(1)}, bf16[64,2048]{1,0:T(8,128)(2,1)S(1)}, bf16[64,2048]{1,0:T(8,128)(2,1)S(1)}) custom-call(s32[2]{0:T(128)S(1)} %pad_add_fusion.1.place_ref, bf16[64,2176]{1,0:T(8,128)(2,1)S(1)} %get-tuple-element.49.refs_0_, bf16[64,2176]{1,0:T(8,128)(2,1)S(1)} %collective-permute-done.10.refs_1_, ...), custom_call_target="tpu_custom_call" | custom-call | tf_op jit(solution)/shard_map/pallas_call | solution.py:367
  116.0 2.6 %collective-permute-start.15 = (bf16[64,2048]{1,0:T(8,128)(2,1)S(1)}, bf16[64,2048]{1,0:T(8,128)(2,1)S(1)}, u32[]{:S(2)}, u32[]{:S(2)}) collective-permute-start(bf16[64,2048]{1,0:T(8,128)(2,1)S(1)} %get-tuple-element.56), channel_id=1, source_target_pairs={{0,6},{1,7},{2,4},{3,5},{4,2},{5,3},{6,0},{7,1},{8,14},{9,15},{10,... | collective-permute-start | bytes 786440 | tf_op jit(solution)/shard_map/ppermute | solution.py:391
  118.6 3.3 %collective-permute-start.14 = (bf16[64,2048]{1,0:T(8,128)(2,1)S(1)}, bf16[64,2048]{1,0:T(8,128)(2,1)S(1)}, u32[]{:S(2)}, u32[]{:S(2)}) collective-permute-start(bf16[64,2048]{1,0:T(8,128)(2,1)S(1)} %get-tuple-element.55), channel_id=1, source_target_pairs={{0,4},{1,5},{2,6},{3,7},{4,0},{5,1},{6,2},{7,3},{8,12},{9,13},{10,... | collective-permute-start | bytes 786440 | tf_op jit(solution)/shard_map/ppermute | solution.py:391
  121.9 4.2 %collective-permute-done.15 = bf16[64,2048]{1,0:T(8,128)(2,1)S(1)} collective-permute-done((bf16[64,2048]{1,0:T(8,128)(2,1)S(1)}, bf16[64,2048]{1,0:T(8,128)(2,1)S(1)}, u32[]{:S(2)}, u32[]{:S(2)}) %collective-permute-start.15) | collective-permute-done | bytes 262176 | tf_op jit(solution)/shard_map/ppermute | solution.py:391
  126.2 13.8 %collective-permute-done.14 = bf16[64,2048]{1,0:T(8,128)(2,1)S(1)} collective-permute-done((bf16[64,2048]{1,0:T(8,128)(2,1)S(1)}, bf16[64,2048]{1,0:T(8,128)(2,1)S(1)}, u32[]{:S(2)}, u32[]{:S(2)}) %collective-permute-start.14) | collective-permute-done | bytes 262176 | tf_op jit(solution)/shard_map/ppermute | solution.py:391
  140.0 0.9 add_convert_fusion
  (51 shorter events, 1.1 us)
Async XLA Ops:
  0.0 29.5 %collective-permute-start.1 = (bf16[512,2048]{1,0:T(8,128)(2,1)}, bf16[512,2048]{1,0:T(8,128)(2,1)S(1)}, u32[]{:S(2)}, u32[]{:S(2)}) collective-permute-start(bf16[512,2048]{1,0:T(8,128)(2,1)} %own_ref.1), channel_id=1, source_target_pairs={{0,1},{1,0},{2,3},{3,2},{4,5},{5,4},{6,7},{7,6},{8,9},{9,8},{10,11... | collective-permute-start | bytes 6291464 | tf_op jit(solution)/shard_map/ppermute | solution.py:423
  0.5 30.5 %collective-permute-start.2 = (bf16[1,2048,512]{2,1,0:T(8,128)(2,1)}, bf16[1,2048,512]{2,1,0:T(8,128)(2,1)}, u32[]{:S(2)}, u32[]{:S(2)}) collective-permute-start(bf16[1,2048,512]{2,1,0:T(8,128)(2,1)} %refs_4_.1), channel_id=1, source_target_pairs={{0,1},{1,0},{2,3},{3,2},{4,5},{5,4},{6,7},{7,6},{8,9},{9,8},{10,11... | collective-permute-start | bytes 6291464 | tf_op jit(solution)/shard_map/ppermute | solution.py:425
  0.5 30.4 %collective-permute-start.3 = (bf16[1,2048,512]{2,1,0:T(8,128)(2,1)}, bf16[1,2048,512]{2,1,0:T(8,128)(2,1)}, u32[]{:S(2)}, u32[]{:S(2)}) collective-permute-start(bf16[1,2048,512]{2,1,0:T(8,128)(2,1)} %refs_5_.1), channel_id=1, source_target_pairs={{0,1},{1,0},{2,3},{3,2},{4,5},{5,4},{6,7},{7,6},{8,9},{9,8},{10,11... | collective-permute-start | bytes 6291464 | tf_op jit(solution)/shard_map/ppermute | solution.py:425
  1.0 30.0 %collective-permute-start.4 = (bf16[1,512,2048]{2,1,0:T(8,128)(2,1)}, bf16[1,512,2048]{2,1,0:T(8,128)(2,1)}, u32[]{:S(2)}, u32[]{:S(2)}) collective-permute-start(bf16[1,512,2048]{2,1,0:T(8,128)(2,1)} %refs_6_.1), channel_id=1, source_target_pairs={{0,1},{1,0},{2,3},{3,2},{4,5},{5,4},{6,7},{7,6},{8,9},{9,8},{10,11... | collective-permute-start | bytes 6291464 | tf_op jit(solution)/shard_map/ppermute | solution.py:425
  1.0 1.0 copy-start.12
  2.1 0.9 copy-start.15
  3.0 0.7 copy-start.17
  3.7 0.7 copy-start.18
  18.2 1.0 copy-start.23
  19.2 1.0 copy-start.25
  20.1 9.4 %collective-permute-start = (bf16[4,128,256]{2,1,0:T(8,128)(2,1)S(1)}, bf16[4,128,256]{2,1,0:T(8,128)(2,1)S(1)}, u32[]{:S(2)}, u32[]{:S(2)}) collective-permute-start(bf16[4,128,256]{2,1,0:T(8,128)(2,1)S(1)} %get-tuple-element.34.own_ref), channel_id=1, source_target_pairs={{0,8},{8,0},{16,24},{24,16},{1,9},{9,1},{17,25},{25,17},{2,10},{10... | collective-permute-start | bytes 786440 | tf_op jit(solution)/shard_map/ppermute | solution.py:461
  29.5 1.4 copy-start.1
  31.9 14.5 %collective-permute-start.5 = (bf16[4,128,128]{2,1,0:T(8,128)(2,1)}, bf16[4,128,128]{2,1,0:T(8,128)(2,1)S(1)}, u32[]{:S(2)}, u32[]{:S(2)}) collective-permute-start(bf16[4,128,128]{2,1,0:T(8,128)(2,1)} %get-tuple-element.37), channel_id=1, source_target_pairs={{0,16},{8,24},{16,0},{24,8},{1,17},{9,25},{17,1},{25,9},{2,18},{10... | collective-permute-start | bytes 393224 | tf_op jit(solution)/shard_map/ppermute | solution.py:461
  33.6 1.0 copy-start.13
  34.7 0.9 copy-start.14
  35.6 0.9 copy-start.16
  36.6 0.7 copy-start.19
  37.3 0.7 copy-start.20
  38.0 0.7 copy-start.21
  38.6 0.7 copy-start.22
  39.3 1.2 copy-start.24
  40.5 1.2 copy-start.26
  44.5 1.0 copy-start.6
  45.4 0.8 copy-start.8
  46.2 5.3 %copy-start = (bf16[512,2048]{1,0:T(8,128)(2,1)S(1)}, bf16[512,2048]{1,0:T(8,128)(2,1)}, u32[]{:S(2)}) copy-start(bf16[512,2048]{1,0:T(8,128)(2,1)} %own_ref.1) | copy-start | bytes 6291460
  46.3 1.4 copy-start.7
  47.7 1.0 copy-start.9
  49.9 1.6 %collective-permute-start.6 = (bf16[4,64,512]{2,1,0:T(8,128)(2,1)S(1)}, bf16[4,64,512]{2,1,0:T(8,128)(2,1)S(1)}, u32[]{:S(2)}, u32[]{:S(2)}) collective-permute-start(bf16[4,64,512]{2,1,0:T(8,128)(2,1)S(1)} %get-tuple-element.42), channel_id=1, source_target_pairs={{0,1},{1,0},{2,3},{3,2},{4,5},{5,4},{6,7},{7,6},{8,9},{9,8},{10,11... | collective-permute-start | bytes 786440 | tf_op jit(solution)/shard_map/ppermute | solution.py:476
  51.5 1.6 %copy-start.2 = (bf16[512,2048]{1,0:T(8,128)(2,1)S(1)}, bf16[512,2048]{1,0:T(8,128)(2,1)}, u32[]{:S(2)}) copy-start(bf16[512,2048]{1,0:T(8,128)(2,1)} %copy-done.1) | copy-start | bytes 6291460
  53.1 25.4 %copy-start.10 = (bf16[64,2048]{1,0:T(8,128)(2,1)S(1)}, bf16[64,2048]{1,0:T(8,128)(2,1)}, u32[]{:S(2)}) copy-start(bf16[64,2048]{1,0:T(8,128)(2,1)} %hidden_ref.1) | copy-start | bytes 786436
  53.1 25.4 %copy-start.11 = (f32[2048]{0:T(1024)S(1)}, f32[2048]{0:T(1024)}, u32[]{:S(2)}) copy-start(f32[2048]{0:T(1024)} %param.24) | copy-start | bytes 24580
  53.1 53.3 %copy-start.3 = (bf16[1,2048,512]{2,1,0:T(8,128)(2,1)S(1)}, bf16[1,2048,512]{2,1,0:T(8,128)(2,1)}, u32[]{:S(2)}) copy-start(bf16[1,2048,512]{2,1,0:T(8,128)(2,1)} %refs_4_.1) | copy-start | bytes 6291460
  53.1 53.3 %copy-start.4 = (bf16[1,2048,512]{2,1,0:T(8,128)(2,1)S(1)}, bf16[1,2048,512]{2,1,0:T(8,128)(2,1)}, u32[]{:S(2)}) copy-start(bf16[1,2048,512]{2,1,0:T(8,128)(2,1)} %refs_5_.1) | copy-start | bytes 6291460
  55.5 13.4 %collective-permute-start.7 = (bf16[64,2048]{1,0:T(8,128)(2,1)S(1)}, bf16[64,2048]{1,0:T(8,128)(2,1)S(1)}, u32[]{:S(2)}, u32[]{:S(2)}) collective-permute-start(bf16[64,2048]{1,0:T(8,128)(2,1)S(1)} %get-tuple-element.45), channel_id=1, source_target_pairs={{0,2},{1,3},{2,0},{3,1},{4,6},{5,7},{6,4},{7,5},{8,10},{9,11},{10,... | collective-permute-start | bytes 786440 | tf_op jit(solution)/shard_map/ppermute | solution.py:391
  57.2 21.3 %collective-permute-start.8 = (bf16[64,2048]{1,0:T(8,128)(2,1)S(1)}, bf16[64,2048]{1,0:T(8,128)(2,1)S(1)}, u32[]{:S(2)}, u32[]{:S(2)}) collective-permute-start(bf16[64,2048]{1,0:T(8,128)(2,1)S(1)} %get-tuple-element.46), channel_id=1, source_target_pairs={{0,4},{1,5},{2,6},{3,7},{4,0},{5,1},{6,2},{7,3},{8,12},{9,13},{10,... | collective-permute-start | bytes 786440 | tf_op jit(solution)/shard_map/ppermute | solution.py:391
  59.8 18.7 %collective-permute-start.9 = (bf16[64,2048]{1,0:T(8,128)(2,1)S(1)}, bf16[64,2048]{1,0:T(8,128)(2,1)S(1)}, u32[]{:S(2)}, u32[]{:S(2)}) collective-permute-start(bf16[64,2048]{1,0:T(8,128)(2,1)S(1)} %get-tuple-element.47), channel_id=1, source_target_pairs={{0,6},{1,7},{2,4},{3,5},{4,2},{5,3},{6,0},{7,1},{8,14},{9,15},{10,... | collective-permute-start | bytes 786440 | tf_op jit(solution)/shard_map/ppermute | solution.py:391
  78.8 15.8 %collective-permute-start.10 = (bf16[64,2176]{1,0:T(8,128)(2,1)S(1)}, bf16[64,2176]{1,0:T(8,128)(2,1)S(1)}, u32[]{:S(2)}, u32[]{:S(2)}) collective-permute-start(bf16[64,2176]{1,0:T(8,128)(2,1)S(1)} %get-tuple-element.49.refs_0_), channel_id=1, source_target_pairs={{0,2},{1,3},{2,0},{3,1},{4,6},{5,7},{6,4},{7,5},{8,10},{9,11},{10,... | collective-permute-start | bytes 835592 | tf_op jit(solution)/shard_map/ppermute | solution.py:391
  84.0 22.4 %collective-permute-start.11 = (bf16[64,2176]{1,0:T(8,128)(2,1)S(1)}, bf16[64,2176]{1,0:T(8,128)(2,1)S(1)}, u32[]{:S(2)}, u32[]{:S(2)}) collective-permute-start(bf16[64,2176]{1,0:T(8,128)(2,1)S(1)} %get-tuple-element.49.refs_0_), channel_id=1, source_target_pairs={{0,4},{1,5},{2,6},{3,7},{4,0},{5,1},{6,2},{7,3},{8,12},{9,13},{10,... | collective-permute-start | bytes 835592 | tf_op jit(solution)/shard_map/ppermute | solution.py:391
  85.1 21.3 %collective-permute-start.12 = (bf16[64,2176]{1,0:T(8,128)(2,1)S(1)}, bf16[64,2176]{1,0:T(8,128)(2,1)S(1)}, u32[]{:S(2)}, u32[]{:S(2)}) collective-permute-start(bf16[64,2176]{1,0:T(8,128)(2,1)S(1)} %get-tuple-element.49.refs_0_), channel_id=1, source_target_pairs={{0,6},{1,7},{2,4},{3,5},{4,2},{5,3},{6,0},{7,1},{8,14},{9,15},{10,... | collective-permute-start | bytes 835592 | tf_op jit(solution)/shard_map/ppermute | solution.py:391
  106.4 1.6 %copy-start.5 = (bf16[1,512,2048]{2,1,0:T(8,128)(2,1)S(1)}, bf16[1,512,2048]{2,1,0:T(8,128)(2,1)}, u32[]{:S(2)}) copy-start(bf16[1,512,2048]{2,1,0:T(8,128)(2,1)} %refs_6_.1) | copy-start | bytes 6291460
  116.0 10.1 %collective-permute-start.15 = (bf16[64,2048]{1,0:T(8,128)(2,1)S(1)}, bf16[64,2048]{1,0:T(8,128)(2,1)S(1)}, u32[]{:S(2)}, u32[]{:S(2)}) collective-permute-start(bf16[64,2048]{1,0:T(8,128)(2,1)S(1)} %get-tuple-element.56), channel_id=1, source_target_pairs={{0,6},{1,7},{2,4},{3,5},{4,2},{5,3},{6,0},{7,1},{8,14},{9,15},{10,... | collective-permute-start | bytes 786440 | tf_op jit(solution)/shard_map/ppermute | solution.py:391
  118.6 21.4 %collective-permute-start.14 = (bf16[64,2048]{1,0:T(8,128)(2,1)S(1)}, bf16[64,2048]{1,0:T(8,128)(2,1)S(1)}, u32[]{:S(2)}, u32[]{:S(2)}) collective-permute-start(bf16[64,2048]{1,0:T(8,128)(2,1)S(1)} %get-tuple-element.55), channel_id=1, source_target_pairs={{0,4},{1,5},{2,6},{3,7},{4,0},{5,1},{6,2},{7,3},{8,12},{9,13},{10,... | collective-permute-start | bytes 786440 | tf_op jit(solution)/shard_map/ppermute | solution.py:391
  121.8 18.1 %collective-permute-start.13 = (bf16[64,2048]{1,0:T(8,128)(2,1)S(1)}, bf16[64,2048]{1,0:T(8,128)(2,1)S(1)}, u32[]{:S(2)}, u32[]{:S(2)}) collective-permute-start(bf16[64,2048]{1,0:T(8,128)(2,1)S(1)} %get-tuple-element.54), channel_id=1, source_target_pairs={{0,2},{1,3},{2,0},{3,1},{4,6},{5,7},{6,4},{7,5},{8,10},{9,11},{10,... | collective-permute-start | bytes 786440 | tf_op jit(solution)/shard_map/ppermute | solution.py:391

commit v2 on v1

v2 whole, which is shorter than its diff:
```python
import functools

import jax
import jax.numpy as jnp
from jax import lax
from jax.experimental import pallas as pl
from jax.experimental.pallas import tpu as pltpu
from jax.sharding import PartitionSpec as P

DK = 128
DV = 128
EPS = 1e-06
BLOCK = 128
LANES = 128
F32 = jnp.float32
BF16 = jnp.bfloat16
EXACT = lax.Precision.HIGHEST
LARGE_VMEM = 60 * 1024 * 1024
SMALL_VMEM = 20 * 1024 * 1024
EXPERT_VMEM = 32 * 1024 * 1024
CHUNKS = 2
PAIRS_AT_ONCE = 16


def whole(memory_space=pltpu.VMEM):
    return pl.BlockSpec(memory_space=memory_space)


def blocks_of(*arrays):
    return [pl.BlockSpec(a.shape, lambda i, n=a.ndim: (0,) * n) for a in arrays]


def call(kernel, outs, *arrays, scalars=None, flops=0, vmem=LARGE_VMEM, scratch=()):
    params = pltpu.CompilerParams(vmem_limit_bytes=vmem)
    moved = sum(a.size * a.dtype.itemsize for a in (*arrays, *outs))
    return pl.pallas_call(
        kernel,
        grid=(1,),
        out_shape=tuple(outs),
        in_specs=([] if scalars is None else [whole(pltpu.SMEM)]) + blocks_of(*arrays),
        out_specs=tuple(blocks_of(*outs)),
        scratch_shapes=list(scratch),
        compiler_params=params,
        cost_estimate=pl.CostEstimate(flops=flops, bytes_accessed=moved, transcendentals=0),
    )(*(() if scalars is None else (scalars,)), *arrays)


def shape(dims, dtype):
    return jax.ShapeDtypeStruct(dims, dtype)


def mm(a, b):
    return jnp.dot(a.astype(BF16), b.astype(BF16), preferred_element_type=F32)


def mm_nt(a, b, precision=None):
    return lax.dot_general(
        a, b, (((1,), (1,)), ((), ())), preferred_element_type=F32, precision=precision
    )


def split(a):
    high = a.astype(BF16)
    return high, (a - high.astype(F32)).astype(BF16)


def mm_left2(a, b):
    high, low = split(a)
    return jnp.dot(
        jnp.concatenate([high, low], axis=1),
        jnp.concatenate([b, b], axis=0),
        preferred_element_type=F32,
    )


def mm_right2(a, b):
    high, low = split(b)
    return jnp.dot(
        jnp.concatenate([a, a], axis=1),
        jnp.concatenate([high, low], axis=0),
        preferred_element_type=F32,
    )


def mm_both2(a, b):
    a_high, a_low = split(a)
    b_high, b_low = split(b)
    return jnp.dot(
        jnp.concatenate([a_high, a_low, a_high], axis=1),
        jnp.concatenate([b_high, b_high, b_low], axis=0),
        preferred_element_type=F32,
    )


def grids():
    row = lax.broadcasted_iota(jnp.int32, (BLOCK, BLOCK), 0)
    col = lax.broadcasted_iota(jnp.int32, (BLOCK, BLOCK), 1)
    return row, col


def stacked(ref, blocks):
    return jnp.concatenate([ref[:, c * BLOCK : (c + 1) * BLOCK] for c in range(blocks)], axis=0)


def decays(decay_ref, blocks, row, col):
    by_row = stacked(decay_ref, blocks)
    upto = jnp.where(row >= col, 1.0, 0.0).astype(F32)
    cum_rows = mm_nt(by_row, upto, EXACT)
    cum_cols = mm_nt(upto, by_row, EXACT)
    return cum_rows, cum_cols


def state_kernel(key_ref, value_ref, decay_ref, rate_ref, wu_ref, prefix_ref, total_ref):
    heads = decay_ref.shape[0]
    key_heads = key_ref.shape[1] // DK
    group = heads // key_heads
    blocks = key_ref.shape[0] // BLOCK
    row, col = grids()
    gap_bits = jnp.bitwise_xor(row, col)
    strict = row > col
    diagonal = row == col
    eye = jnp.where(diagonal, 1.0, 0.0).astype(F32)
    cum_rows, cum_cols = decays(decay_ref, blocks, row, col)
    rate_rows = stacked(rate_ref, blocks)
    rate_cols = mm_nt(eye, rate_rows, EXACT)
    carried = [None] * heads
    pairs = [(c, h) for c in range(blocks) for h in range(heads)]
    unit_rows, unit_cols, keys, keys_t, grams = {}, {}, {}, {}, {}
    for c in range(blocks):
        tokens = slice(c * BLOCK, (c + 1) * BLOCK)
        for g in range(key_heads):
            key = key_ref[tokens, g * DK : (g + 1) * DK]
            gram = mm_nt(key, key)
            on_diagonal = jnp.where(diagonal, gram, 0.0)
            unit_rows[c, g] = lax.rsqrt(jnp.sum(on_diagonal, axis=0, keepdims=True) + EPS)
            unit_cols[c, g] = lax.rsqrt(jnp.sum(on_diagonal, axis=1, keepdims=True) + EPS)
            keys[c, g] = key
            keys_t[c, g] = key.astype(F32).T.astype(BF16)
            grams[c, g] = gram * unit_rows[c, g] * unit_cols[c, g]
    for lead in range(0, len(pairs), PAIRS_AT_ONCE):
        some = pairs[lead : lead + PAIRS_AT_ONCE]
        lower, solve = {}, {}
        for c, h in some:
            at = c * heads + h
            cum_row, cum_col = cum_rows[at : at + 1, :], cum_cols[:, at : at + 1]
            fade = jnp.exp(jnp.where(strict, cum_col - cum_row, 0.0))
            part = jnp.where(strict, grams[c, h // group] * fade * rate_cols[:, at : at + 1], 0.0)
            lower[c, h] = part
            solve[c, h] = eye - jnp.where(gap_bits == 1, part, 0.0)
        size = 2
        while size < BLOCK:
            shift = size.bit_length() - 1
            inside = lax.shift_right_logical(gap_bits, shift) == 1
            right = {p: mm(jnp.where(inside, lower[p], 0.0), solve[p]) for p in some}
            solve = {p: solve[p] - mm(solve[p], right[p]) for p in some}
            size *= 2
        first = {p: solve[p].astype(BF16) for p in some}
        rest = {p: eye - first[p].astype(F32) - mm_left2(lower[p], first[p]) for p in some}
        solve = {p: first[p].astype(F32) + mm(first[p], rest[p]) for p in some}
        tails = {}
        for c, h in some:
            tokens = slice(c * BLOCK, (c + 1) * BLOCK)
            at = c * heads + h
            g = h // group
            cum_row, cum_col = cum_rows[at : at + 1, :], cum_cols[:, at : at + 1]
            rate_row = rate_rows[at : at + 1, :]
            end = cum_row[:, BLOCK - 1 :]
            w = mm_left2(solve[c, h] * (rate_row * jnp.exp(cum_row) * unit_rows[c, g]), keys[c, g])
            u = mm_left2(solve[c, h] * rate_row, value_ref[tokens, h * DV : (h + 1) * DV])
            wu = jnp.concatenate([w, u], axis=1)
            wu_ref[h, c] = wu.astype(BF16)
            tails[c, h] = mm_right2(keys_t[c, g], wu * (jnp.exp(end - cum_col) * unit_cols[c, g]))
        for c, h in some:
            at = c * heads + h
            kept = jnp.exp(cum_rows[at : at + 1, BLOCK - 1 :])
            tail = tails[c, h]
            if c == 0:
                start = jnp.concatenate([eye, jnp.zeros((DK, DV), F32)], axis=1)
                prefix_ref[h, c] = start.astype(BF16)
                carried[h] = jnp.concatenate([kept * eye - tail[:, :DK], tail[:, DK:]], axis=1)
            else:
                bias = jnp.concatenate([jnp.zeros((DK, DK), F32), tail[:, DK:]], axis=1)
                prefix_ref[h, c] = carried[h].astype(BF16)
                carried[h] = kept * carried[h] + bias - mm_both2(tail[:, :DK], carried[h])
    for h in range(heads):
        total_ref[h] = carried[h].astype(BF16)


def readout_kernel(query_ref, key_ref, decay_ref, ids_ref, weight_ref, wu_ref, prefix_ref,
                   lin_ref, own_ref, routes_ref):
    expert = lax.broadcasted_iota(jnp.int32, (LANES, ids_ref.shape[1]), 0)
    routes = jnp.zeros(expert.shape, F32)
    for k in range(ids_ref.shape[0]):
        routes += jnp.where(
            ids_ref[k : k + 1, :] == expert, weight_ref[k : k + 1, :].astype(F32), 0.0
        )
    routes_ref[...] = routes.T.astype(BF16)
    heads = decay_ref.shape[0]
    key_heads = key_ref.shape[1] // DK
    group = heads // key_heads
    blocks = key_ref.shape[0] // BLOCK
    row, col = grids()
    causal = row >= col
    diagonal = row == col
    cum_rows, cum_cols = decays(decay_ref, blocks, row, col)
    for c in range(blocks):
        tokens = slice(c * BLOCK, (c + 1) * BLOCK)
        for g in range(key_heads):
            key = key_ref[tokens, g * DK : (g + 1) * DK]
            query = query_ref[tokens, g * DK : (g + 1) * DK]
            key_f, query_f = key.astype(F32), query.astype(F32)
            gram = jnp.where(diagonal, mm_nt(key, key), 0.0)
            unit_row = lax.rsqrt(jnp.sum(gram, axis=0, keepdims=True) + EPS)
            query_unit = query_f * (
                lax.rsqrt(jnp.sum(query_f * query_f, axis=1, keepdims=True) + EPS) * DK ** (-0.5)
            )
            query_scale = lax.rsqrt(
                jnp.sum(query_f * query_f, axis=1, keepdims=True) + EPS
            ) * DK ** (-0.5)
            plain = mm_nt(query, key) * unit_row * query_scale
            for h in range(g * group, (g + 1) * group):
                at = c * heads + h
                cum_row, cum_col = cum_rows[at : at + 1, :], cum_cols[:, at : at + 1]
                fade = jnp.exp(jnp.where(causal, cum_col - cum_row, 0.0))
                scores = jnp.where(causal, plain * fade, 0.0)
                mixed_wu = mm(scores, wu_ref[h, c])
                reach = query_unit * jnp.exp(cum_col) - mixed_wu[:, :DK]
                lanes = slice(h * DV, (h + 1) * DV)
                if c == 0:
                    lin_ref[tokens, lanes] = reach.astype(BF16)
                    own_ref[tokens, lanes] = mixed_wu[:, DK:]
                else:
                    spread = mm(reach, prefix_ref[h, c])
                    lin_ref[tokens, lanes] = spread[:, :DK].astype(BF16)
                    own_ref[tokens, lanes] = mixed_wu[:, DK:] + spread[:, DK:]


def mix_kernel(spot_ref, gain_ref, gate_ref, lin_ref, own_ref, *refs):
    *total_refs, keep_ref, send_ref, totals_ref = refs
    core, place, here = spot_ref[0], spot_ref[1], spot_ref[2]
    heads = total_refs[0].shape[0]
    places = keep_ref.shape[0]
    rows = keep_ref.shape[1]
    for d, total_ref in enumerate(total_refs):
        totals_ref[d] = total_ref[...]
    states = [jnp.zeros((DK, DV), F32) for _ in range(heads)]
    for source in range(len(total_refs)):
        at = jnp.maximum(jnp.bitwise_xor(here, source) - 1, 0)
        for h in range(heads):
            step = totals_ref[at, h]
            moved = mm(step[:, :DK], states[h]) + step[:, DK:].astype(F32)
            states[h] = jnp.where(source < here, moved, states[h])
    states = [state.astype(BF16) for state in states]
    for d in range(places):
        at = jnp.bitwise_xor(place, d)
        for out_ref, side in ((send_ref, 1 - core), (keep_ref, core)):
            tokens = pl.ds(pl.multiple_of((2 * at + side) * rows, rows), rows)
            for h in range(heads):
                lanes = slice(h * DV, (h + 1) * DV)
                readout = own_ref[tokens, lanes] + mm(lin_ref[tokens, lanes], states[h])
                scale = lax.rsqrt(jnp.mean(readout * readout, axis=1, keepdims=True) + EPS)
                gate = gate_ref[tokens, lanes].astype(F32)
                gated = gain_ref[...] * gate / (1.0 + jnp.exp(-gate))
                out_ref[d, :, lanes] = (readout * scale * gated).astype(BF16)


def project_kernel(tile, keep_ref, got_ref, own_ref, sib_ref, *out_refs):
    places, rows, depth = keep_ref.shape
    product = jnp.dot(
        keep_ref[...].reshape(-1, depth), own_ref[...], preferred_element_type=F32
    ) + jnp.dot(got_ref[...].reshape(-1, depth), sib_ref[...], preferred_element_type=F32)
    part = out_refs[0].shape[0]
    lanes = pl.ds(pl.multiple_of(pl.program_id(0) * tile, tile), tile)
    for number, out_ref in enumerate(out_refs):
        start = number % places * rows + number // places * part
        out_ref[:, lanes] = product[start : start + part].astype(BF16)


def project(keep, got, own, sib):
    places, rows, depth = keep.shape
    width = own.shape[1]
    tile = 512
    part = rows // CHUNKS
    outs = pl.pallas_call(
        functools.partial(project_kernel, tile),
        grid=(width // tile,),
        out_shape=(shape((part, width), BF16),) * (places * CHUNKS),
        in_specs=blocks_of(keep, got) + [pl.BlockSpec((depth, tile), lambda i: (0, i))] * 2,
        out_specs=(pl.BlockSpec((part, width), lambda i: (0, 0)),) * (places * CHUNKS),
        compiler_params=pltpu.CompilerParams(vmem_limit_bytes=LARGE_VMEM),
    )(keep, got, own, sib)
    return [outs[c * places : (c + 1) * places] for c in range(CHUNKS)]


def norm_kernel(chunk, hidden_ref, gain_ref, routes_ref, *refs):
    *part_refs, residual_ref, out_ref = refs
    rows = residual_ref.shape[0]
    tokens = slice(chunk * rows, (chunk + 1) * rows)
    residual = hidden_ref[tokens, :].astype(F32)
    for part_ref in part_refs:
        residual += part_ref[...].astype(F32)
    residual_ref[...] = residual
    scale = lax.rsqrt(jnp.mean(residual * residual, axis=1, keepdims=True) + EPS)
    width = residual.shape[1]
    out_ref[:, :width] = (residual * scale * gain_ref[...]).astype(BF16)
    out_ref[:, width:] = routes_ref[tokens, :]


def expert_kernel(places, halves, place_ref, *refs):
    slots = refs[:places]
    gate_own, up_own, down_own, gate_sib, up_sib, down_sib = refs[places : places + 6]
    out_refs = refs[places + 6 : -2]
    x_ref, sum_ref = refs[-2:]
    step = pl.program_id(0)
    place, core = place_ref[0], place_ref[1]
    rows, width = out_refs[0].shape

    @pl.when(step == 0)
    def _():
        for d, slot in enumerate(slots):
            x_ref[d * rows : (d + 1) * rows, :] = slot[...]

    def add(gate, up, down, expert, fresh):
        x = x_ref[:, :width]
        gate_act = jnp.dot(x, gate[0], preferred_element_type=F32)
        up_act = jnp.dot(x, up[0], preferred_element_type=F32)
        inner = (gate_act / (1.0 + jnp.exp(-gate_act)) * up_act).astype(BF16)
        routes = x_ref[:, width:].astype(F32)
        lane = lax.broadcasted_iota(jnp.int32, routes.shape, 1)
        weight = jnp.sum(jnp.where(lane == expert, routes, 0.0), axis=1, keepdims=True)
        more = jnp.dot(inner, down[0], preferred_element_type=F32) * weight

        @pl.when(fresh)
        def _():
            sum_ref[...] = more

        @pl.when(jnp.logical_not(fresh))
        def _():
            sum_ref[...] += more

    @pl.when(step < halves)
    def _():
        add(gate_own, up_own, down_own, 2 * place + core, step == 0)

    @pl.when(step >= halves)
    def _():
        add(gate_sib, up_sib, down_sib, 2 * place + 1 - core, step < 0)

    @pl.when(step == 2 * halves - 1)
    def _():
        for d, out_ref in enumerate(out_refs):
            out_ref[...] = sum_ref[d * rows : (d + 1) * rows].astype(BF16)


def experts(place_core, slots, own, sib):
    places = len(slots)
    rows = slots[0].shape[0]
    width = own[0].shape[1]
    inner = own[0].shape[2]
    tile = 256
    halves = inner // tile

    def specs(at):
        return [
            pl.BlockSpec((1, width, tile), lambda i: (0, 0, at(i))),
            pl.BlockSpec((1, width, tile), lambda i: (0, 0, at(i))),
            pl.BlockSpec((1, tile, width), lambda i: (0, at(i), 0)),
        ]

    return pl.pallas_call(
        functools.partial(expert_kernel, places, halves),
        grid=(2 * halves,),
        out_shape=(jax.ShapeDtypeStruct((rows, width), BF16),) * places,
        in_specs=[whole(pltpu.SMEM)]
        + blocks_of(*slots)
        + specs(lambda i: jnp.minimum(i, halves - 1))
        + specs(lambda i: jnp.maximum(i - halves, 0)),
        out_specs=(pl.BlockSpec((rows, width), lambda i: (0, 0)),) * places,
        scratch_shapes=[
            pltpu.VMEM((places * rows, slots[0].shape[1]), BF16),
            pltpu.VMEM((places * rows, width), F32),
        ],
        compiler_params=pltpu.CompilerParams(vmem_limit_bytes=EXPERT_VMEM),
    )(place_core, *slots, *own, *sib)


def between_places(places, d):
    return [(2 * i + c, 2 * (i ^ d) + c) for i in range(places) for c in range(2)]


def exchange(pieces):
    places = len(pieces)
    return [pieces[0]] + [
        lax.ppermute(pieces[d], "exp", between_places(places, d)) for d in range(1, places)
    ]


def per_device(
    hidden_in,
    query_proj,
    key_proj,
    value_proj,
    gate_proj,
    log_decay,
    write_rate,
    head_gain,
    out_weight,
    post_gain,
    expert_ids,
    route_weight,
    gate_weight,
    up_weight,
    down_weight,
):
    length = value_proj.shape[0]
    heads = value_proj.shape[1] // DV
    blocks = length // BLOCK
    tok, width = hidden_in.shape
    seqs, exps = lax.axis_size("seq"), lax.axis_size("exp")
    places = exps // 2
    me = lax.axis_index("exp")
    place, core = lax.div(me, 2), lax.rem(me, 2)
    here = lax.axis_index("seq")
    swap = [(i, i ^ 1) for i in range(exps)]

    out_sib = lax.ppermute(out_weight, "exp", swap)
    own = (gate_weight, up_weight, down_weight)
    sib = tuple(lax.ppermute(w, "exp", swap) for w in own)

    wide = shape((heads, blocks, DK, DK + DV), BF16)
    wu, prefixes, total = call(
        state_kernel,
        (wide, wide, shape((heads, DK, DK + DV), BF16)),
        key_proj,
        value_proj,
        log_decay,
        write_rate,
        flops=10**10,
    )
    total, out_sib, sib = lax.optimization_barrier((total, out_sib, sib))
    lin, own_read, routes = call(
        readout_kernel,
        (
            shape((length, heads * DV), BF16),
            shape((length, heads * DV), F32),
            shape((tok, LANES), BF16),
        ),
        query_proj,
        key_proj,
        log_decay,
        expert_ids.T,
        route_weight.T,
        wu,
        prefixes,
        flops=4 * 10**9,
    )

    totals = [
        lax.ppermute(total, "seq", [(i, i ^ d) for i in range(seqs)]) for d in range(1, seqs)
    ]

    half = shape((places, tok, heads * DV), BF16)
    keep, send = call(
        mix_kernel,
        (half, half),
        head_gain.reshape(1, DV),
        gate_proj,
        lin,
        own_read,
        *totals,
        scalars=jnp.stack([core, place, here]),
        flops=10**9,
        scratch=[pltpu.VMEM((seqs - 1, *total.shape), BF16)],
    )
    got = lax.ppermute(send, "exp", swap)
    parts = [exchange(pieces) for pieces in project(keep, got, out_weight, out_sib)]
    spot = jnp.stack([place, core])
    outs = []
    for chunk, summands in enumerate(parts):
        rows = tok // CHUNKS
        residual, normed = call(
            functools.partial(norm_kernel, chunk),
            (shape((rows, width), F32), shape((rows, width + LANES), BF16)),
            hidden_in,
            post_gain.reshape(1, width),
            routes,
            *summands,
            vmem=SMALL_VMEM,
        )
        slots = exchange([normed] * places)
        summands = exchange(experts(spot, slots, own, sib))
        outs.append(sum((s.astype(F32) for s in summands), residual).astype(BF16))
    return jnp.concatenate(outs, axis=0)


def solution(mesh):
    in_specs = (
        P(("seq", "exp"), None),
        P("seq", "exp"),
        P("seq", "exp"),
        P("seq", "exp"),
        P("seq", "exp"),
        P("exp", "seq"),
        P("exp", "seq"),
        P(),
        P("exp", None),
        P(),
        P(("seq", "exp"), None),
        P(("seq", "exp"), None),
        P("exp", None, None),
        P("exp", None, None),
        P("exp", None, None),
    )
    out_specs = P(("seq", "exp"), None)
    return jax.shard_map(
        per_device, mesh=mesh, in_specs=in_specs, out_specs=out_specs, check_vma=False
    )
```

time: 141 us -> 120 us (0.85)
  waiting for transfers between devices: 64.4 us -> 19.2 us
  starting transfers between devices: 23.8 us -> 53.8 us
  local copies, waits for them, and re-layouts: 22.2 us -> 8.07 us
  Pallas kernels: 29.2 us -> 36.9 us
    ppermute x9 -> x18, waiting for transfers between devices: 56.4 us -> 8.73 us  [exchange(): lax.ppermute(pieces[d], 'exp', between_places(places, d))]
    ppermute x9 -> x18, starting transfers between devices: 18 us -> 48.4 us  [exchange(): lax.ppermute(pieces[d], 'exp', between_places(places, d))]
    unnamed x54 -> x28, local copies, waits for them, and re-layouts: 22.2 us -> 8.07 us
    pallas_call x1 -> x2, Pallas kernels: 7.98 us -> 12.1 us  [experts(): pl.pallas_call(functools.partial(expert_kernel, places, halves), grid=(2...]
    pallas_call x6, Pallas kernels: 21.2 us -> 24.8 us  [the longest x5 19.6 us: call(): pl.pallas_call(kernel, grid=(1,), out_shape=tuple(outs), in_specs=([] if...]
    ppermute x3, waiting for transfers between devices: 0.01 us -> 1.92 us  [per_device(): sib = tuple((lax.ppermute(w, 'exp', swap) for w in own))]
    ppermute x2 -> x3, waiting for transfers between devices: 6.44 us -> 6.82 us  [per_device(): lax.ppermute(total, 'seq', [(i, i ^ d) for i in range(seqs)])]
    ppermute x2 -> x3, starting transfers between devices: 4.7 us -> 4.38 us  [per_device(): lax.ppermute(total, 'seq', [(i, i ^ d) for i in range(seqs)])]
  transfers between devices with their start and end apart: 16 -> 26, of which waited for: 8 -> 7; matrix products, arithmetic and copies ran while one was open for 0% -> 1% of each run, Pallas kernels for 12% -> 23%
where the time goes in v2:
time: 120 us
  starting transfers between devices  53.8 us (45%)
  Pallas kernels  36.9 us (31%)
  waiting for transfers between devices  19.2 us (16%)
  local copies, waits for them, and re-layouts  8.07 us (7%)
  other arithmetic  1.61 us (1%)
    ppermute x18, starting transfers between devices, exchange(): lax.ppermute(pieces[d], 'exp', between_places(places, d))  48.4 us
    pallas_call x5, Pallas kernels, call(): pl.pallas_call(kernel, grid=(1,), out_shape=tuple(outs), in_specs=([] if...  19.6 us
    pallas_call x2, Pallas kernels, experts(): pl.pallas_call(functools.partial(expert_kernel, places, halves), grid=(2...  12.1 us
    ppermute x18, waiting for transfers between devices, exchange(): lax.ppermute(pieces[d], 'exp', between_places(places, d))  8.73 us
    unnamed x28, local copies, waits for them, and re-layouts  8.07 us
    ppermute x3, waiting for transfers between devices, per_device(): lax.ppermute(total, 'seq', [(i, i ^ d) for i in range(seqs)])  6.82 us
    pallas_call x1, Pallas kernels, project(): pl.pallas_call(functools.partial(project_kernel, tile), grid=(width // ti...  5.25 us
    ppermute x3, starting transfers between devices, per_device(): lax.ppermute(total, 'seq', [(i, i ^ d) for i in range(seqs)])  4.38 us
  transfers between devices with their start and end apart: 26, of which 7 were waited for; matrix products, arithmetic and copies ran while one was open for 1% of the time, Pallas kernels for 23%

profile of v2, /device:TPU:0, one launch (start us, length us, event | category | flops | bytes accessed | tf_op | source)
XLA Modules:
  0.0 119.7 jit_solution(4147871933367766123)
XLA Ops:
  0.0 0.5 collective-permute-start
  0.5 0.5 collective-permute-start.2
  1.0 0.6 pad_add_fusion.spot_ref
  1.7 10.0 %shard_map.145 = (bf16[4,4,128,256]{3,2,1,0:T(8,128)(2,1)}, bf16[4,4,128,256]{3,2,1,0:T(8,128)(2,1)}, bf16[4,128,256]{2,1,0:T(8,128)(2,1)}) custom-call(bf16[512,256]{1,0:T(8,128)(2,1)} %key_ref.3, bf16[512,512]{1,0:T(8,128)(2,1)} %value_ref.1, f32[4,512]{1,0:T(4,128)} %decay_ref.3, f32[4,512]{1,0:T(4,128)} %rate_ref.1), custom_call_target="tpu_custom_call" | custom-call | flops 10000000000 | bytes 3162112 | tf_op jit(solution)/shard_map/pallas_call | solution.py:36
  11.7 1.9 %collective-permute-done.3.refs_9_ = bf16[1,512,2048]{2,1,0:T(8,128)(2,1)} collective-permute-done((bf16[1,512,2048]{2,1,0:T(8,128)(2,1)}, bf16[1,512,2048]{2,1,0:T(8,128)(2,1)}, u32[]{:S(2)}, u32[]{:S(2)}) %collective-permute-start.3) | collective-permute-done | bytes 2097184 | tf_op jit(solution)/shard_map/ppermute | solution.py:428
  13.6 2.9 %collective-permute-start.4 = (bf16[4,128,256]{2,1,0:T(8,128)(2,1)}, bf16[4,128,256]{2,1,0:T(8,128)(2,1)S(1)}, u32[]{:S(2)}, u32[]{:S(2)}) collective-permute-start(bf16[4,128,256]{2,1,0:T(8,128)(2,1)} %get-tuple-element.44), channel_id=1, source_target_pairs={{0,8},{8,0},{16,24},{24,16},{1,9},{9,1},{17,25},{25,17},{2,10},{10... | collective-permute-start | bytes 786440 | tf_op jit(solution)/shard_map/ppermute | solution.py:459
  16.4 1.5 %collective-permute-start.5 = (bf16[4,128,256]{2,1,0:T(8,128)(2,1)}, bf16[4,128,256]{2,1,0:T(8,128)(2,1)S(1)}, u32[]{:S(2)}, u32[]{:S(2)}) collective-permute-start(bf16[4,128,256]{2,1,0:T(8,128)(2,1)} %get-tuple-element.44), channel_id=1, source_target_pairs={{0,16},{8,24},{16,0},{24,8},{1,17},{9,25},{17,1},{25,9},{2,18},{10... | collective-permute-start | bytes 786440 | tf_op jit(solution)/shard_map/ppermute | solution.py:459
  18.0 5.5 %shard_map.146 = (bf16[512,512]{1,0:T(8,128)(2,1)}, f32[512,512]{1,0:T(8,128)}, bf16[64,128]{1,0:T(8,128)(2,1)}) custom-call(bf16[512,256]{1,0:T(8,128)(2,1)} %query_ref.1, bf16[512,256]{1,0:T(8,128)(2,1)} %key_ref.3, f32[4,512]{1,0:T(4,128)} %decay_ref.3, s32[4,64]{1,0:T(4,128)} %bitcast.9, bf16[4,64]{1,0:T(4,128)(2,1)} %bitcast.10, ...), custom_call_target="tpu_custom_call" | custom-call | flops 4000000000 | bytes 4220416 | tf_op jit(solution)/shard_map/pallas_call | solution.py:36
  23.5 0.2 collective-permute-done.4.refs_0_
  23.7 6.6 %collective-permute-done.5.refs_1_ = bf16[4,128,256]{2,1,0:T(8,128)(2,1)S(1)} collective-permute-done((bf16[4,128,256]{2,1,0:T(8,128)(2,1)}, bf16[4,128,256]{2,1,0:T(8,128)(2,1)S(1)}, u32[]{:S(2)}, u32[]{:S(2)}) %collective-permute-start.5) | collective-permute-done | bytes 262176 | tf_op jit(solution)/shard_map/ppermute | solution.py:459
  30.4 0.7 copy-done.12
  31.1 3.7 %shard_map.147 = (bf16[4,64,512]{2,1,0:T(8,128)(2,1)}, bf16[4,64,512]{2,1,0:T(8,128)(2,1)}) custom-call(s32[3]{0:T(128)} %pad_add_fusion.spot_ref, f32[1,128]{1,0:T(1,128)} %bitcast.11, bf16[512,512]{1,0:T(8,128)(2,1)} %gate_ref.1, bf16[512,512]{1,0:T(8,128)(2,1)} %get-tuple-element.41.lin_ref, f32[512,512]{1,0:T(8,128)} %get-tuple-element.42.own_ref, ...), custom_call_target="tpu_custom_call" | custom-call | flops 1000000000 | bytes 3408384 | tf_op jit(solution)/shard_map/pallas_call | solution.py:36
  34.8 1.7 %collective-permute-done.7.got_ref = bf16[4,64,512]{2,1,0:T(8,128)(2,1)S(1)} collective-permute-done((bf16[4,64,512]{2,1,0:T(8,128)(2,1)}, bf16[4,64,512]{2,1,0:T(8,128)(2,1)S(1)}, u32[]{:S(2)}, u32[]{:S(2)}) %collective-permute-start.7) | collective-permute-done | bytes 262176 | tf_op jit(solution)/shard_map/ppermute | solution.py:475
  36.6 0.7 copy-done.10
  37.3 5.2 %shard_map.148 = (bf16[32,2048]{1,0:T(8,128)(2,1)}, bf16[32,2048]{1,0:T(8,128)(2,1)}, bf16[32,2048]{1,0:T(8,128)(2,1)}, bf16[32,2048]{1,0:T(8,128)(2,1)}, bf16[3...) custom-call(bf16[4,64,512]{2,1,0:T(8,128)(2,1)} %get-tuple-element.45.keep_r, ...), custom_call_target="tpu_custom_call" | custom-call | tf_op jit(solution)/shard_map/pallas_call | solution.py:284
  42.5 1.6 %collective-permute-start.17 = (bf16[32,2048]{1,0:T(8,128)(2,1)}, bf16[32,2048]{1,0:T(8,128)(2,1)S(1)}, u32[]{:S(2)}, u32[]{:S(2)}) collective-permute-start(bf16[32,2048]{1,0:T(8,128)(2,1)} %get-tuple-element.62), channel_id=1, source_target_pairs={{0,2},{1,3},{2,0},{3,1},{4,6},{5,7},{6,4},{7,5},{8,10},{9,11},{10,... | collective-permute-start | bytes 393224 | tf_op jit(solution)/shard_map/ppermute | solution.py:394
  44.1 2.6 %collective-permute-start.18 = (bf16[32,2048]{1,0:T(8,128)(2,1)}, bf16[32,2048]{1,0:T(8,128)(2,1)S(1)}, u32[]{:S(2)}, u32[]{:S(2)}) collective-permute-start(bf16[32,2048]{1,0:T(8,128)(2,1)} %get-tuple-element.63), channel_id=1, source_target_pairs={{0,4},{1,5},{2,6},{3,7},{4,0},{5,1},{6,2},{7,3},{8,12},{9,13},{10,... | collective-permute-start | bytes 393224 | tf_op jit(solution)/shard_map/ppermute | solution.py:394
  46.7 0.2 collective-permute-start.19
  47.0 0.7 collective-permute-start.8
  47.6 3.5 %collective-permute-start.9 = (bf16[32,2048]{1,0:T(8,128)(2,1)}, bf16[32,2048]{1,0:T(8,128)(2,1)S(1)}, u32[]{:S(2)}, u32[]{:S(2)}) collective-permute-start(bf16[32,2048]{1,0:T(8,128)(2,1)} %get-tuple-element.50), channel_id=1, source_target_pairs={{0,4},{1,5},{2,6},{3,7},{4,0},{5,1},{6,2},{7,3},{8,12},{9,13},{10,... | collective-permute-start | bytes 393224 | tf_op jit(solution)/shard_map/ppermute | solution.py:394
  51.1 3.5 %collective-permute-start.10 = (bf16[32,2048]{1,0:T(8,128)(2,1)}, bf16[32,2048]{1,0:T(8,128)(2,1)S(1)}, u32[]{:S(2)}, u32[]{:S(2)}) collective-permute-start(bf16[32,2048]{1,0:T(8,128)(2,1)} %get-tuple-element.51), channel_id=1, source_target_pairs={{0,6},{1,7},{2,4},{3,5},{4,2},{5,3},{6,0},{7,1},{8,14},{9,15},{10,... | collective-permute-start | bytes 393224 | tf_op jit(solution)/shard_map/ppermute | solution.py:394
  54.6 2.7 %collective-permute-done.18.refs_2_ = bf16[32,2048]{1,0:T(8,128)(2,1)S(1)} collective-permute-done((bf16[32,2048]{1,0:T(8,128)(2,1)}, bf16[32,2048]{1,0:T(8,128)(2,1)S(1)}, u32[]{:S(2)}, u32[]{:S(2)}) %collective-permute-start.18) | collective-permute-done | bytes 131104 | tf_op jit(solution)/shard_map/ppermute | solution.py:394
  57.3 0.9 copy-done.7
  58.2 0.2 shard_map.151
  58.4 9.1 %collective-permute-start.20 = (bf16[32,2176]{1,0:T(8,128)(2,1)S(1)}, bf16[32,2176]{1,0:T(8,128)(2,1)S(1)}, u32[]{:S(2)}, u32[]{:S(2)}) collective-permute-start(bf16[32,2176]{1,0:T(8,128)(2,1)S(1)} %get-tuple-element.66.refs_0_), channel_id=1, source_target_pairs={{0,2},{1,3},{2,0},{3,1},{4,6},{5,7},{6,4},{7,5},{8,10},{9,11},{10,... | collective-permute-start | bytes 417800 | tf_op jit(solution)/shard_map/ppermute | solution.py:394
  67.5 1.0 collective-permute-start.21
  68.5 1.4 %collective-permute-start.22 = (bf16[32,2176]{1,0:T(8,128)(2,1)S(1)}, bf16[32,2176]{1,0:T(8,128)(2,1)S(1)}, u32[]{:S(2)}, u32[]{:S(2)}) collective-permute-start(bf16[32,2176]{1,0:T(8,128)(2,1)S(1)} %get-tuple-element.66.refs_0_), channel_id=1, source_target_pairs={{0,6},{1,7},{2,4},{3,5},{4,2},{5,3},{6,0},{7,1},{8,14},{9,15},{10,... | collective-permute-start | bytes 417800 | tf_op jit(solution)/shard_map/ppermute | solution.py:394
  69.9 0.9 copy-done.6
  70.8 0.2 shard_map.149
  71.0 8.0 %collective-permute-start.11 = (bf16[32,2176]{1,0:T(8,128)(2,1)S(1)}, bf16[32,2176]{1,0:T(8,128)(2,1)S(1)}, u32[]{:S(2)}, u32[]{:S(2)}) collective-permute-start(bf16[32,2176]{1,0:T(8,128)(2,1)S(1)} %get-tuple-element.53.refs_0_), channel_id=1, source_target_pairs={{0,2},{1,3},{2,0},{3,1},{4,6},{5,7},{6,4},{7,5},{8,10},{9,11},{10,... | collective-permute-start | bytes 417800 | tf_op jit(solution)/shard_map/ppermute | solution.py:394
  79.1 4.1 %collective-permute-start.12 = (bf16[32,2176]{1,0:T(8,128)(2,1)S(1)}, bf16[32,2176]{1,0:T(8,128)(2,1)S(1)}, u32[]{:S(2)}, u32[]{:S(2)}) collective-permute-start(bf16[32,2176]{1,0:T(8,128)(2,1)S(1)} %get-tuple-element.53.refs_0_), channel_id=1, source_target_pairs={{0,4},{1,5},{2,6},{3,7},{4,0},{5,1},{6,2},{7,3},{8,12},{9,13},{10,... | collective-permute-start | bytes 417800 | tf_op jit(solution)/shard_map/ppermute | solution.py:394
  83.1 1.4 %collective-permute-start.13 = (bf16[32,2176]{1,0:T(8,128)(2,1)S(1)}, bf16[32,2176]{1,0:T(8,128)(2,1)S(1)}, u32[]{:S(2)}, u32[]{:S(2)}) collective-permute-start(bf16[32,2176]{1,0:T(8,128)(2,1)S(1)} %get-tuple-element.53.refs_0_), channel_id=1, source_target_pairs={{0,6},{1,7},{2,4},{3,5},{4,2},{5,3},{6,0},{7,1},{8,14},{9,15},{10,... | collective-permute-start | bytes 417800 | tf_op jit(solution)/shard_map/ppermute | solution.py:394
  84.6 1.6 %copy-done.1 = bf16[1,2048,512]{2,1,0:T(8,128)(2,1)S(1)} copy-done((bf16[1,2048,512]{2,1,0:T(8,128)(2,1)S(1)}, bf16[1,2048,512]{2,1,0:T(8,128)(2,1)}, u32[]{:S(2)}) %copy-start.1) | copy-done | bytes 2097176
  86.2 1.6 %copy-done.2 = bf16[1,512,2048]{2,1,0:T(8,128)(2,1)S(1)} copy-done((bf16[1,512,2048]{2,1,0:T(8,128)(2,1)S(1)}, bf16[1,512,2048]{2,1,0:T(8,128)(2,1)}, u32[]{:S(2)}) %copy-start.2) | copy-done | bytes 2097176
  87.8 1.6 %copy-done.4 = bf16[1,2048,512]{2,1,0:T(8,128)(2,1)S(1)} copy-done((bf16[1,2048,512]{2,1,0:T(8,128)(2,1)S(1)}, bf16[1,2048,512]{2,1,0:T(8,128)(2,1)}, u32[]{:S(2)}) %copy-start.4) | copy-done | bytes 2097176
  89.4 6.0 %shard_map.152 = (bf16[32,2048]{1,0:T(8,128)(2,1)S(1)}, bf16[32,2048]{1,0:T(8,128)(2,1)S(1)}, bf16[32,2048]{1,0:T(8,128)(2,1)S(1)}, bf16[32,2048]{1,0:T(8,128)(2,1)S(1)}) custom-call(s32[2]{0:T(128)S(1)} %pad_add_fusion.1.place_ref, bf16[32,2176]{1,0:T(8,128)(2,1)S(1)} %get-tuple-element.66.refs_0_, bf16[32,2176]{1,0:T(8,128)(2,1)S(1)} %collective-permute-done.20.refs_1_, ...), custom_call_target="tpu_custom_call" | custom-call | tf_op jit(solution)/shard_map/pallas_call | solution.py:370
  95.4 2.5 %collective-permute-start.25 = (bf16[32,2048]{1,0:T(8,128)(2,1)S(1)}, bf16[32,2048]{1,0:T(8,128)(2,1)S(1)}, u32[]{:S(2)}, u32[]{:S(2)}) collective-permute-start(bf16[32,2048]{1,0:T(8,128)(2,1)S(1)} %get-tuple-element.70), channel_id=1, source_target_pairs={{0,6},{1,7},{2,4},{3,5},{4,2},{5,3},{6,0},{7,1},{8,14},{9,15},{10,... | collective-permute-start | bytes 393224 | tf_op jit(solution)/shard_map/ppermute | solution.py:394
  97.9 3.9 %collective-permute-start.24 = (bf16[32,2048]{1,0:T(8,128)(2,1)S(1)}, bf16[32,2048]{1,0:T(8,128)(2,1)S(1)}, u32[]{:S(2)}, u32[]{:S(2)}) collective-permute-start(bf16[32,2048]{1,0:T(8,128)(2,1)S(1)} %get-tuple-element.69), channel_id=1, source_target_pairs={{0,4},{1,5},{2,6},{3,7},{4,0},{5,1},{6,2},{7,3},{8,12},{9,13},{10,... | collective-permute-start | bytes 393224 | tf_op jit(solution)/shard_map/ppermute | solution.py:394
  101.8 0.5 collective-permute-start.23
  102.3 6.0 %shard_map.150 = (bf16[32,2048]{1,0:T(8,128)(2,1)S(1)}, bf16[32,2048]{1,0:T(8,128)(2,1)S(1)}, bf16[32,2048]{1,0:T(8,128)(2,1)S(1)}, bf16[32,2048]{1,0:T(8,128)(2,1)S(1)}) custom-call(s32[2]{0:T(128)S(1)} %pad_add_fusion.1.place_ref, bf16[32,2176]{1,0:T(8,128)(2,1)S(1)} %get-tuple-element.53.refs_0_, bf16[32,2176]{1,0:T(8,128)(2,1)S(1)} %collective-permute-done.11.refs_1_, ...), custom_call_target="tpu_custom_call" | custom-call | tf_op jit(solution)/shard_map/pallas_call | solution.py:370
  108.4 2.4 %collective-permute-start.16 = (bf16[32,2048]{1,0:T(8,128)(2,1)S(1)}, bf16[32,2048]{1,0:T(8,128)(2,1)S(1)}, u32[]{:S(2)}, u32[]{:S(2)}) collective-permute-start(bf16[32,2048]{1,0:T(8,128)(2,1)S(1)} %get-tuple-element.60), channel_id=1, source_target_pairs={{0,6},{1,7},{2,4},{3,5},{4,2},{5,3},{6,0},{7,1},{8,14},{9,15},{10,... | collective-permute-start | bytes 393224 | tf_op jit(solution)/shard_map/ppermute | solution.py:394
  110.8 0.6 collective-permute-start.15
  111.4 1.4 %collective-permute-start.14 = (bf16[32,2048]{1,0:T(8,128)(2,1)S(1)}, bf16[32,2048]{1,0:T(8,128)(2,1)S(1)}, u32[]{:S(2)}, u32[]{:S(2)}) collective-permute-start(bf16[32,2048]{1,0:T(8,128)(2,1)S(1)} %get-tuple-element.58), channel_id=1, source_target_pairs={{0,2},{1,3},{2,0},{3,1},{4,6},{5,7},{6,4},{7,5},{8,10},{9,11},{10,... | collective-permute-start | bytes 393224 | tf_op jit(solution)/shard_map/ppermute | solution.py:394
  112.8 0.1 add_convert_fusion
  112.9 2.4 %collective-permute-done.16 = bf16[32,2048]{1,0:T(8,128)(2,1)S(1)} collective-permute-done((bf16[32,2048]{1,0:T(8,128)(2,1)S(1)}, bf16[32,2048]{1,0:T(8,128)(2,1)S(1)}, u32[]{:S(2)}, u32[]{:S(2)}) %collective-permute-start.16) | collective-permute-done | bytes 131104 | tf_op jit(solution)/shard_map/ppermute | solution.py:394
  115.3 3.6 %collective-permute-done.15 = bf16[32,2048]{1,0:T(8,128)(2,1)S(1)} collective-permute-done((bf16[32,2048]{1,0:T(8,128)(2,1)S(1)}, bf16[32,2048]{1,0:T(8,128)(2,1)S(1)}, u32[]{:S(2)}, u32[]{:S(2)}) %collective-permute-start.15) | collective-permute-done | bytes 131104 | tf_op jit(solution)/shard_map/ppermute | solution.py:394
  118.9 0.1 add_convert_fusion.1
  119.0 0.7 pad_maximum_fusion
  (45 shorter events, 0.4 us)
Async XLA Ops:
  0.0 11.6 %collective-permute-start = (bf16[512,2048]{1,0:T(8,128)(2,1)}, bf16[512,2048]{1,0:T(8,128)(2,1)}, u32[]{:S(2)}, u32[]{:S(2)}) collective-permute-start(bf16[512,2048]{1,0:T(8,128)(2,1)} %own_ref.1), channel_id=1, source_target_pairs={{0,1},{1,0},{2,3},{3,2},{4,5},{5,4},{6,7},{7,6},{8,9},{9,8},{10,11... | collective-permute-start | bytes 6291464 | tf_op jit(solution)/shard_map/ppermute | solution.py:426
  0.5 11.2 %collective-permute-start.1 = (bf16[1,2048,512]{2,1,0:T(8,128)(2,1)}, bf16[1,2048,512]{2,1,0:T(8,128)(2,1)S(1)}, u32[]{:S(2)}, u32[]{:S(2)}) collective-permute-start(bf16[1,2048,512]{2,1,0:T(8,128)(2,1)} %refs_4_.3), channel_id=1, source_target_pairs={{0,1},{1,0},{2,3},{3,2},{4,5},{5,4},{6,7},{7,6},{8,9},{9,8},{10,11... | collective-permute-start | bytes 6291464 | tf_op jit(solution)/shard_map/ppermute | solution.py:428
  0.5 11.1 %collective-permute-start.2 = (bf16[1,2048,512]{2,1,0:T(8,128)(2,1)}, bf16[1,2048,512]{2,1,0:T(8,128)(2,1)}, u32[]{:S(2)}, u32[]{:S(2)}) collective-permute-start(bf16[1,2048,512]{2,1,0:T(8,128)(2,1)} %refs_5_.3), channel_id=1, source_target_pairs={{0,1},{1,0},{2,3},{3,2},{4,5},{5,4},{6,7},{7,6},{8,9},{9,8},{10,11... | collective-permute-start | bytes 6291464 | tf_op jit(solution)/shard_map/ppermute | solution.py:428
  1.0 12.6 %collective-permute-start.3 = (bf16[1,512,2048]{2,1,0:T(8,128)(2,1)}, bf16[1,512,2048]{2,1,0:T(8,128)(2,1)}, u32[]{:S(2)}, u32[]{:S(2)}) collective-permute-start(bf16[1,512,2048]{2,1,0:T(8,128)(2,1)} %refs_6_.3), channel_id=1, source_target_pairs={{0,1},{1,0},{2,3},{3,2},{4,5},{5,4},{6,7},{7,6},{8,9},{9,8},{10,11... | collective-permute-start | bytes 6291464 | tf_op jit(solution)/shard_map/ppermute | solution.py:428
  11.6 11.9 %copy-start.3 = (bf16[1,2048,512]{2,1,0:T(8,128)(2,1)}, bf16[1,2048,512]{2,1,0:T(8,128)(2,1)S(1)}, u32[]{:S(2)}) copy-start(bf16[1,2048,512]{2,1,0:T(8,128)(2,1)S(1)} %collective-permute-done.1.refs_7_) | copy-start | bytes 6291460
  13.6 10.2 %collective-permute-start.4 = (bf16[4,128,256]{2,1,0:T(8,128)(2,1)}, bf16[4,128,256]{2,1,0:T(8,128)(2,1)S(1)}, u32[]{:S(2)}, u32[]{:S(2)}) collective-permute-start(bf16[4,128,256]{2,1,0:T(8,128)(2,1)} %get-tuple-element.44), channel_id=1, source_target_pairs={{0,8},{8,0},{16,24},{24,16},{1,9},{9,1},{17,25},{25,17},{2,10},{10... | collective-permute-start | bytes 786440 | tf_op jit(solution)/shard_map/ppermute | solution.py:459
  16.4 13.9 %collective-permute-start.5 = (bf16[4,128,256]{2,1,0:T(8,128)(2,1)}, bf16[4,128,256]{2,1,0:T(8,128)(2,1)S(1)}, u32[]{:S(2)}, u32[]{:S(2)}) collective-permute-start(bf16[4,128,256]{2,1,0:T(8,128)(2,1)} %get-tuple-element.44), channel_id=1, source_target_pairs={{0,16},{8,24},{16,0},{24,8},{1,17},{9,25},{17,1},{25,9},{2,18},{10... | collective-permute-start | bytes 786440 | tf_op jit(solution)/shard_map/ppermute | solution.py:459
  18.0 12.4 %collective-permute-start.6 = (bf16[4,128,256]{2,1,0:T(8,128)(2,1)}, bf16[4,128,256]{2,1,0:T(8,128)(2,1)S(1)}, u32[]{:S(2)}, u32[]{:S(2)}) collective-permute-start(bf16[4,128,256]{2,1,0:T(8,128)(2,1)} %get-tuple-element.44), channel_id=1, source_target_pairs={{0,24},{8,16},{16,8},{24,0},{1,25},{9,17},{17,9},{25,1},{2,26},{10... | collective-permute-start | bytes 786440 | tf_op jit(solution)/shard_map/ppermute | solution.py:459
  23.7 6.6 %copy-start.11 = (bf16[4,128,256]{2,1,0:T(8,128)(2,1)}, bf16[4,128,256]{2,1,0:T(8,128)(2,1)S(1)}, u32[]{:S(2)}) copy-start(bf16[4,128,256]{2,1,0:T(8,128)(2,1)S(1)} %collective-permute-done.4.refs_0_) | copy-start | bytes 786436
  30.3 0.7 copy-start.12
  30.3 0.8 copy-start.13
  34.8 1.7 %collective-permute-start.7 = (bf16[4,64,512]{2,1,0:T(8,128)(2,1)}, bf16[4,64,512]{2,1,0:T(8,128)(2,1)S(1)}, u32[]{:S(2)}, u32[]{:S(2)}) collective-permute-start(bf16[4,64,512]{2,1,0:T(8,128)(2,1)} %get-tuple-element.46), channel_id=1, source_target_pairs={{0,1},{1,0},{2,3},{3,2},{4,5},{5,4},{6,7},{7,6},{8,9},{9,8},{10,11... | collective-permute-start | bytes 786440 | tf_op jit(solution)/shard_map/ppermute | solution.py:475
  36.6 0.7 copy-start.10
  37.3 20.0 %copy-start.5 = (bf16[64,2048]{1,0:T(8,128)(2,1)S(1)}, bf16[64,2048]{1,0:T(8,128)(2,1)}, u32[]{:S(2)}) copy-start(bf16[64,2048]{1,0:T(8,128)(2,1)} %hidden_ref.3) | copy-start | bytes 786436
  37.3 20.0 %copy-start.8 = (bf16[64,128]{1,0:T(8,128)(2,1)S(1)}, bf16[64,128]{1,0:T(8,128)(2,1)}, u32[]{:S(2)}) copy-start(bf16[64,128]{1,0:T(8,128)(2,1)} %get-tuple-element.40.routes_ref) | copy-start | bytes 49156
  37.3 20.0 %copy-start.9 = (f32[2048]{0:T(1024)S(1)}, f32[2048]{0:T(1024)}, u32[]{:S(2)}) copy-start(f32[2048]{0:T(1024)} %param.24) | copy-start | bytes 24580
  37.3 47.3 %copy-start = (bf16[1,2048,512]{2,1,0:T(8,128)(2,1)S(1)}, bf16[1,2048,512]{2,1,0:T(8,128)(2,1)}, u32[]{:S(2)}) copy-start(bf16[1,2048,512]{2,1,0:T(8,128)(2,1)} %refs_4_.3) | copy-start | bytes 6291460
  42.5 8.6 %collective-permute-start.17 = (bf16[32,2048]{1,0:T(8,128)(2,1)}, bf16[32,2048]{1,0:T(8,128)(2,1)S(1)}, u32[]{:S(2)}, u32[]{:S(2)}) collective-permute-start(bf16[32,2048]{1,0:T(8,128)(2,1)} %get-tuple-element.62), channel_id=1, source_target_pairs={{0,2},{1,3},{2,0},{3,1},{4,6},{5,7},{6,4},{7,5},{8,10},{9,11},{10,... | collective-permute-start | bytes 393224 | tf_op jit(solution)/shard_map/ppermute | solution.py:394
  44.1 13.1 %collective-permute-start.18 = (bf16[32,2048]{1,0:T(8,128)(2,1)}, bf16[32,2048]{1,0:T(8,128)(2,1)S(1)}, u32[]{:S(2)}, u32[]{:S(2)}) collective-permute-start(bf16[32,2048]{1,0:T(8,128)(2,1)} %get-tuple-element.63), channel_id=1, source_target_pairs={{0,4},{1,5},{2,6},{3,7},{4,0},{5,1},{6,2},{7,3},{8,12},{9,13},{10,... | collective-permute-start | bytes 393224 | tf_op jit(solution)/shard_map/ppermute | solution.py:394
  46.7 10.6 %collective-permute-start.19 = (bf16[32,2048]{1,0:T(8,128)(2,1)}, bf16[32,2048]{1,0:T(8,128)(2,1)S(1)}, u32[]{:S(2)}, u32[]{:S(2)}) collective-permute-start(bf16[32,2048]{1,0:T(8,128)(2,1)} %get-tuple-element.64), channel_id=1, source_target_pairs={{0,6},{1,7},{2,4},{3,5},{4,2},{5,3},{6,0},{7,1},{8,14},{9,15},{10,... | collective-permute-start | bytes 393224 | tf_op jit(solution)/shard_map/ppermute | solution.py:394
  47.0 21.6 %collective-permute-start.8 = (bf16[32,2048]{1,0:T(8,128)(2,1)}, bf16[32,2048]{1,0:T(8,128)(2,1)S(1)}, u32[]{:S(2)}, u32[]{:S(2)}) collective-permute-start(bf16[32,2048]{1,0:T(8,128)(2,1)} %get-tuple-element.49), channel_id=1, source_target_pairs={{0,2},{1,3},{2,0},{3,1},{4,6},{5,7},{6,4},{7,5},{8,10},{9,11},{10,... | collective-permute-start | bytes 393224 | tf_op jit(solution)/shard_map/ppermute | solution.py:394
  47.6 22.3 %collective-permute-start.9 = (bf16[32,2048]{1,0:T(8,128)(2,1)}, bf16[32,2048]{1,0:T(8,128)(2,1)S(1)}, u32[]{:S(2)}, u32[]{:S(2)}) collective-permute-start(bf16[32,2048]{1,0:T(8,128)(2,1)} %get-tuple-element.50), channel_id=1, source_target_pairs={{0,4},{1,5},{2,6},{3,7},{4,0},{5,1},{6,2},{7,3},{8,12},{9,13},{10,... | collective-permute-start | bytes 393224 | tf_op jit(solution)/shard_map/ppermute | solution.py:394
  51.1 18.8 %collective-permute-start.10 = (bf16[32,2048]{1,0:T(8,128)(2,1)}, bf16[32,2048]{1,0:T(8,128)(2,1)S(1)}, u32[]{:S(2)}, u32[]{:S(2)}) collective-permute-start(bf16[32,2048]{1,0:T(8,128)(2,1)} %get-tuple-element.51), channel_id=1, source_target_pairs={{0,6},{1,7},{2,4},{3,5},{4,2},{5,3},{6,0},{7,1},{8,14},{9,15},{10,... | collective-permute-start | bytes 393224 | tf_op jit(solution)/shard_map/ppermute | solution.py:394
  57.3 0.9 copy-start.7
  58.4 24.7 %collective-permute-start.20 = (bf16[32,2176]{1,0:T(8,128)(2,1)S(1)}, bf16[32,2176]{1,0:T(8,128)(2,1)S(1)}, u32[]{:S(2)}, u32[]{:S(2)}) collective-permute-start(bf16[32,2176]{1,0:T(8,128)(2,1)S(1)} %get-tuple-element.66.refs_0_), channel_id=1, source_target_pairs={{0,2},{1,3},{2,0},{3,1},{4,6},{5,7},{6,4},{7,5},{8,10},{9,11},{10,... | collective-permute-start | bytes 417800 | tf_op jit(solution)/shard_map/ppermute | solution.py:394
  67.5 17.1 %collective-permute-start.21 = (bf16[32,2176]{1,0:T(8,128)(2,1)S(1)}, bf16[32,2176]{1,0:T(8,128)(2,1)S(1)}, u32[]{:S(2)}, u32[]{:S(2)}) collective-permute-start(bf16[32,2176]{1,0:T(8,128)(2,1)S(1)} %get-tuple-element.66.refs_0_), channel_id=1, source_target_pairs={{0,4},{1,5},{2,6},{3,7},{4,0},{5,1},{6,2},{7,3},{8,12},{9,13},{10,... | collective-permute-start | bytes 417800 | tf_op jit(solution)/shard_map/ppermute | solution.py:394
  68.5 16.1 %collective-permute-start.22 = (bf16[32,2176]{1,0:T(8,128)(2,1)S(1)}, bf16[32,2176]{1,0:T(8,128)(2,1)S(1)}, u32[]{:S(2)}, u32[]{:S(2)}) collective-permute-start(bf16[32,2176]{1,0:T(8,128)(2,1)S(1)} %get-tuple-element.66.refs_0_), channel_id=1, source_target_pairs={{0,6},{1,7},{2,4},{3,5},{4,2},{5,3},{6,0},{7,1},{8,14},{9,15},{10,... | collective-permute-start | bytes 417800 | tf_op jit(solution)/shard_map/ppermute | solution.py:394
  69.9 0.9 copy-start.6
  71.0 30.8 %collective-permute-start.11 = (bf16[32,2176]{1,0:T(8,128)(2,1)S(1)}, bf16[32,2176]{1,0:T(8,128)(2,1)S(1)}, u32[]{:S(2)}, u32[]{:S(2)}) collective-permute-start(bf16[32,2176]{1,0:T(8,128)(2,1)S(1)} %get-tuple-element.53.refs_0_), channel_id=1, source_target_pairs={{0,2},{1,3},{2,0},{3,1},{4,6},{5,7},{6,4},{7,5},{8,10},{9,11},{10,... | collective-permute-start | bytes 417800 | tf_op jit(solution)/shard_map/ppermute | solution.py:394
  79.1 23.2 %collective-permute-start.12 = (bf16[32,2176]{1,0:T(8,128)(2,1)S(1)}, bf16[32,2176]{1,0:T(8,128)(2,1)S(1)}, u32[]{:S(2)}, u32[]{:S(2)}) collective-permute-start(bf16[32,2176]{1,0:T(8,128)(2,1)S(1)} %get-tuple-element.53.refs_0_), channel_id=1, source_target_pairs={{0,4},{1,5},{2,6},{3,7},{4,0},{5,1},{6,2},{7,3},{8,12},{9,13},{10,... | collective-permute-start | bytes 417800 | tf_op jit(solution)/shard_map/ppermute | solution.py:394
  83.1 19.2 %collective-permute-start.13 = (bf16[32,2176]{1,0:T(8,128)(2,1)S(1)}, bf16[32,2176]{1,0:T(8,128)(2,1)S(1)}, u32[]{:S(2)}, u32[]{:S(2)}) collective-permute-start(bf16[32,2176]{1,0:T(8,128)(2,1)S(1)} %get-tuple-element.53.refs_0_), channel_id=1, source_target_pairs={{0,6},{1,7},{2,4},{3,5},{4,2},{5,3},{6,0},{7,1},{8,14},{9,15},{10,... | collective-permute-start | bytes 417800 | tf_op jit(solution)/shard_map/ppermute | solution.py:394
  84.6 1.6 %copy-start.1 = (bf16[1,2048,512]{2,1,0:T(8,128)(2,1)S(1)}, bf16[1,2048,512]{2,1,0:T(8,128)(2,1)}, u32[]{:S(2)}) copy-start(bf16[1,2048,512]{2,1,0:T(8,128)(2,1)} %refs_5_.3) | copy-start | bytes 6291460
  86.2 1.6 %copy-start.2 = (bf16[1,512,2048]{2,1,0:T(8,128)(2,1)S(1)}, bf16[1,512,2048]{2,1,0:T(8,128)(2,1)}, u32[]{:S(2)}) copy-start(bf16[1,512,2048]{2,1,0:T(8,128)(2,1)} %refs_6_.3) | copy-start | bytes 6291460
  87.8 1.6 %copy-start.4 = (bf16[1,2048,512]{2,1,0:T(8,128)(2,1)S(1)}, bf16[1,2048,512]{2,1,0:T(8,128)(2,1)}, u32[]{:S(2)}) copy-start(bf16[1,2048,512]{2,1,0:T(8,128)(2,1)} %copy-done.3) | copy-start | bytes 6291460
  95.4 16.0 %collective-permute-start.25 = (bf16[32,2048]{1,0:T(8,128)(2,1)S(1)}, bf16[32,2048]{1,0:T(8,128)(2,1)S(1)}, u32[]{:S(2)}, u32[]{:S(2)}) collective-permute-start(bf16[32,2048]{1,0:T(8,128)(2,1)S(1)} %get-tuple-element.70), channel_id=1, source_target_pairs={{0,6},{1,7},{2,4},{3,5},{4,2},{5,3},{6,0},{7,1},{8,14},{9,15},{10,... | collective-permute-start | bytes 393224 | tf_op jit(solution)/shard_map/ppermute | solution.py:394
  97.9 14.9 %collective-permute-start.24 = (bf16[32,2048]{1,0:T(8,128)(2,1)S(1)}, bf16[32,2048]{1,0:T(8,128)(2,1)S(1)}, u32[]{:S(2)}, u32[]{:S(2)}) collective-permute-start(bf16[32,2048]{1,0:T(8,128)(2,1)S(1)} %get-tuple-element.69), channel_id=1, source_target_pairs={{0,4},{1,5},{2,6},{3,7},{4,0},{5,1},{6,2},{7,3},{8,12},{9,13},{10,... | collective-permute-start | bytes 393224 | tf_op jit(solution)/shard_map/ppermute | solution.py:394
  101.8 11.0 %collective-permute-start.23 = (bf16[32,2048]{1,0:T(8,128)(2,1)S(1)}, bf16[32,2048]{1,0:T(8,128)(2,1)S(1)}, u32[]{:S(2)}, u32[]{:S(2)}) collective-permute-start(bf16[32,2048]{1,0:T(8,128)(2,1)S(1)} %get-tuple-element.68), channel_id=1, source_target_pairs={{0,2},{1,3},{2,0},{3,1},{4,6},{5,7},{6,4},{7,5},{8,10},{9,11},{10,... | collective-permute-start | bytes 393224 | tf_op jit(solution)/shard_map/ppermute | solution.py:394
  108.4 7.0 %collective-permute-start.16 = (bf16[32,2048]{1,0:T(8,128)(2,1)S(1)}, bf16[32,2048]{1,0:T(8,128)(2,1)S(1)}, u32[]{:S(2)}, u32[]{:S(2)}) collective-permute-start(bf16[32,2048]{1,0:T(8,128)(2,1)S(1)} %get-tuple-element.60), channel_id=1, source_target_pairs={{0,6},{1,7},{2,4},{3,5},{4,2},{5,3},{6,0},{7,1},{8,14},{9,15},{10,... | collective-permute-start | bytes 393224 | tf_op jit(solution)/shard_map/ppermute | solution.py:394
  110.8 8.1 %collective-permute-start.15 = (bf16[32,2048]{1,0:T(8,128)(2,1)S(1)}, bf16[32,2048]{1,0:T(8,128)(2,1)S(1)}, u32[]{:S(2)}, u32[]{:S(2)}) collective-permute-start(bf16[32,2048]{1,0:T(8,128)(2,1)S(1)} %get-tuple-element.59), channel_id=1, source_target_pairs={{0,4},{1,5},{2,6},{3,7},{4,0},{5,1},{6,2},{7,3},{8,12},{9,13},{10,... | collective-permute-start | bytes 393224 | tf_op jit(solution)/shard_map/ppermute | solution.py:394
  111.4 7.5 %collective-permute-start.14 = (bf16[32,2048]{1,0:T(8,128)(2,1)S(1)}, bf16[32,2048]{1,0:T(8,128)(2,1)S(1)}, u32[]{:S(2)}, u32[]{:S(2)}) collective-permute-start(bf16[32,2048]{1,0:T(8,128)(2,1)S(1)} %get-tuple-element.58), channel_id=1, source_target_pairs={{0,2},{1,3},{2,0},{3,1},{4,6},{5,7},{6,4},{7,5},{8,10},{9,11},{10,... | collective-permute-start | bytes 393224 | tf_op jit(solution)/shard_map/ppermute | solution.py:394

commit v3 on v2

--- a/solution.py
+++ b/solution.py
@@ -16,9 +16,10 @@
 BF16 = jnp.bfloat16
 EXACT = lax.Precision.HIGHEST
 LARGE_VMEM = 60 * 1024 * 1024
-SMALL_VMEM = 20 * 1024 * 1024
-EXPERT_VMEM = 32 * 1024 * 1024
+SMALL_VMEM = 24 * 1024 * 1024
+FETCH_VMEM = 24 * 1024 * 1024
 CHUNKS = 2
+SPARE = 256
 PAIRS_AT_ONCE = 16
 
 
@@ -30,7 +31,49 @@
     return [pl.BlockSpec(a.shape, lambda i, n=a.ndim: (0,) * n) for a in arrays]
 
 
-def call(kernel, outs, *arrays, scalars=None, flops=0, vmem=LARGE_VMEM, scratch=()):
+def fetch_kernel(*refs):
+    count = len(refs) // 2
+    copies = [
+        pltpu.make_async_copy(refs[i], refs[count + i], refs[-1].at[i]) for i in range(count)
+    ]
+    for copy in copies:
+        copy.start()
+    for copy in copies:
+        copy.wait()
+
+
+def fetch(*arrays):
+    return pl.pallas_call(
+        fetch_kernel,
+        out_shape=tuple(shape(a.shape, a.dtype) for a in arrays),
+        in_specs=[whole(pl.ANY)] * len(arrays),
+        out_specs=(whole(),) * len(arrays),
+        scratch_shapes=[pltpu.SemaphoreType.DMA((len(arrays),))],
+        compiler_params=pltpu.CompilerParams(vmem_limit_bytes=FETCH_VMEM),
+        cost_estimate=pl.CostEstimate(
+            flops=0, bytes_accessed=2 * sum(a.size * a.dtype.itemsize for a in arrays), transcendentals=0
+        ),
+    )(*arrays)
+
+
+def resident(kernel, outs, *arrays, scalars=None, flops=0, scratch=()):
+    moved = sum(a.size * a.dtype.itemsize for a in (*arrays, *outs))
+    return pl.pallas_call(
+        kernel,
+        out_shape=tuple(outs),
+        in_specs=([] if scalars is None else [whole(pltpu.SMEM)]) + [whole()] * len(arrays),
+        out_specs=(whole(),) * len(outs),
+        scratch_shapes=list(scratch),
+        compiler_params=pltpu.CompilerParams(vmem_limit_bytes=SMALL_VMEM),
+        cost_estimate=pl.CostEstimate(flops=flops, bytes_accessed=moved, transcendentals=0),
+    )(*(() if scalars is None else (scalars,)), *arrays)
+
+
+def after(value, *others):
+    return lax.optimization_barrier((value, *others))[0]
+
+
+def call(kernel, outs, *arrays, scalars=None, flops=0, vmem=LARGE_VMEM, scratch=(), stay=False):
     params = pltpu.CompilerParams(vmem_limit_bytes=vmem)
     moved = sum(a.size * a.dtype.itemsize for a in (*arrays, *outs))
     return pl.pallas_call(
@@ -38,7 +81,7 @@
         grid=(1,),
         out_shape=tuple(outs),
         in_specs=([] if scalars is None else [whole(pltpu.SMEM)]) + blocks_of(*arrays),
-        out_specs=tuple(blocks_of(*outs)),
+        out_specs=(whole(),) * len(outs) if stay else tuple(blocks_of(*outs)),
         scratch_shapes=list(scratch),
         compiler_params=params,
         cost_estimate=pl.CostEstimate(flops=flops, bytes_accessed=moved, transcendentals=0),
@@ -264,31 +307,30 @@
                 out_ref[d, :, lanes] = (readout * scale * gated).astype(BF16)
 
 
-def project_kernel(tile, keep_ref, got_ref, own_ref, sib_ref, *out_refs):
+def project_kernel(keep_ref, got_ref, own_ref, sib_ref, *out_refs):
     places, rows, depth = keep_ref.shape
-    product = jnp.dot(
-        keep_ref[...].reshape(-1, depth), own_ref[...], preferred_element_type=F32
-    ) + jnp.dot(got_ref[...].reshape(-1, depth), sib_ref[...], preferred_element_type=F32)
-    part = out_refs[0].shape[0]
-    lanes = pl.ds(pl.multiple_of(pl.program_id(0) * tile, tile), tile)
-    for number, out_ref in enumerate(out_refs):
-        start = number % places * rows + number // places * part
-        out_ref[:, lanes] = product[start : start + part].astype(BF16)
+    part, width = out_refs[0].shape
+    tile = 512
+    for lead in range(0, width, tile):
+        lanes = slice(lead, lead + tile)
+        product = jnp.dot(
+            keep_ref[...].reshape(-1, depth), own_ref[:, lanes], preferred_element_type=F32
+        ) + jnp.dot(got_ref[...].reshape(-1, depth), sib_ref[:, lanes], preferred_element_type=F32)
+        for number, out_ref in enumerate(out_refs):
+            start = number % places * rows + number // places * part
+            out_ref[:, lanes] = product[start : start + part].astype(BF16)
 
 
 def project(keep, got, own, sib):
-    places, rows, depth = keep.shape
-    width = own.shape[1]
-    tile = 512
-    part = rows // CHUNKS
-    outs = pl.pallas_call(
-        functools.partial(project_kernel, tile),
-        grid=(width // tile,),
-        out_shape=(shape((part, width), BF16),) * (places * CHUNKS),
-        in_specs=blocks_of(keep, got) + [pl.BlockSpec((depth, tile), lambda i: (0, i))] * 2,
-        out_specs=(pl.BlockSpec((part, width), lambda i: (0, 0)),) * (places * CHUNKS),
-        compiler_params=pltpu.CompilerParams(vmem_limit_bytes=LARGE_VMEM),
-    )(keep, got, own, sib)
+    places, rows, _ = keep.shape
+    outs = resident(
+        project_kernel,
+        (shape((rows // CHUNKS, own.shape[1]), BF16),) * (places * CHUNKS),
+        keep,
+        got,
+        own,
+        sib,
+    )
     return [outs[c * places : (c + 1) * places] for c in range(CHUNKS)]
 
 
@@ -298,7 +340,7 @@
     tokens = slice(chunk * rows, (chunk + 1) * rows)
     residual = hidden_ref[tokens, :].astype(F32)
     for part_ref in part_refs:
-        residual += part_ref[...].astype(F32)
+        residual += part_ref[:, : residual.shape[1]].astype(F32)
     residual_ref[...] = residual
     scale = lax.rsqrt(jnp.mean(residual * residual, axis=1, keepdims=True) + EPS)
     width = residual.shape[1]
@@ -306,93 +348,73 @@
     out_ref[:, width:] = routes_ref[tokens, :]
 
 
-def expert_kernel(places, halves, place_ref, *refs):
+def expert_kernel(places, spot_ref, *refs):
     slots = refs[:places]
-    gate_own, up_own, down_own, gate_sib, up_sib, down_sib = refs[places : places + 6]
-    out_refs = refs[places + 6 : -2]
-    x_ref, sum_ref = refs[-2:]
-    step = pl.program_id(0)
-    place, core = place_ref[0], place_ref[1]
+    weights = refs[places : places + 6]
+    out_refs = refs[places + 6 :]
+    place, core = spot_ref[0], spot_ref[1]
     rows, width = out_refs[0].shape
-
-    @pl.when(step == 0)
-    def _():
-        for d, slot in enumerate(slots):
-            x_ref[d * rows : (d + 1) * rows, :] = slot[...]
-
-    def add(gate, up, down, expert, fresh):
-        x = x_ref[:, :width]
-        gate_act = jnp.dot(x, gate[0], preferred_element_type=F32)
-        up_act = jnp.dot(x, up[0], preferred_element_type=F32)
-        inner = (gate_act / (1.0 + jnp.exp(-gate_act)) * up_act).astype(BF16)
-        routes = x_ref[:, width:].astype(F32)
-        lane = lax.broadcasted_iota(jnp.int32, routes.shape, 1)
-        weight = jnp.sum(jnp.where(lane == expert, routes, 0.0), axis=1, keepdims=True)
-        more = jnp.dot(inner, down[0], preferred_element_type=F32) * weight
-
-        @pl.when(fresh)
-        def _():
-            sum_ref[...] = more
-
-        @pl.when(jnp.logical_not(fresh))
-        def _():
-            sum_ref[...] += more
-
-    @pl.when(step < halves)
-    def _():
-        add(gate_own, up_own, down_own, 2 * place + core, step == 0)
-
-    @pl.when(step >= halves)
-    def _():
-        add(gate_sib, up_sib, down_sib, 2 * place + 1 - core, step < 0)
-
-    @pl.when(step == 2 * halves - 1)
-    def _():
+    x = jnp.concatenate([slot[:, :width] for slot in slots], axis=0)
+    routes = jnp.concatenate([slot[:, width:] for slot in slots], axis=0).astype(F32)
+    lane = lax.broadcasted_iota(jnp.int32, routes.shape, 1)
+    inners, shares = [], []
+    for number in range(2):
+        gate_ref, up_ref = weights[3 * number : 3 * number + 2]
+        expert = 2 * place + (core if number == 0 else 1 - core)
+        gate_act = jnp.dot(x, gate_ref[0], preferred_element_type=F32)
+        up_act = jnp.dot(x, up_ref[0], preferred_element_type=F32)
+        inners.append((gate_act / (1.0 + jnp.exp(-gate_act)) * up_act).astype(BF16))
+        shares.append(jnp.sum(jnp.where(lane == expert, routes, 0.0), axis=1, keepdims=True))
+    tile = 512
+    for lead in range(0, width, tile):
+        lanes = slice(lead, lead + tile)
+        total = jnp.dot(inners[0], weights[2][0, :, lanes], preferred_element_type=F32) * shares[0]
+        total += jnp.dot(inners[1], weights[5][0, :, lanes], preferred_element_type=F32) * shares[1]
         for d, out_ref in enumerate(out_refs):
-            out_ref[...] = sum_ref[d * rows : (d + 1) * rows].astype(BF16)
-
-
-def experts(place_core, slots, own, sib):
-    places = len(slots)
+            out_ref[:, lanes] = total[d * rows : (d + 1) * rows].astype(BF16)
+
+
+def experts(spot, slots, weights):
     rows = slots[0].shape[0]
-    width = own[0].shape[1]
-    inner = own[0].shape[2]
-    tile = 256
-    halves = inner // tile
-
-    def specs(at):
-        return [
-            pl.BlockSpec((1, width, tile), lambda i: (0, 0, at(i))),
-            pl.BlockSpec((1, width, tile), lambda i: (0, 0, at(i))),
-            pl.BlockSpec((1, tile, width), lambda i: (0, at(i), 0)),
-        ]
-
-    return pl.pallas_call(
-        functools.partial(expert_kernel, places, halves),
-        grid=(2 * halves,),
-        out_shape=(jax.ShapeDtypeStruct((rows, width), BF16),) * places,
-        in_specs=[whole(pltpu.SMEM)]
-        + blocks_of(*slots)
-        + specs(lambda i: jnp.minimum(i, halves - 1))
-        + specs(lambda i: jnp.maximum(i - halves, 0)),
-        out_specs=(pl.BlockSpec((rows, width), lambda i: (0, 0)),) * places,
-        scratch_shapes=[
-            pltpu.VMEM((places * rows, slots[0].shape[1]), BF16),
-            pltpu.VMEM((places * rows, width), F32),
-        ],
-        compiler_params=pltpu.CompilerParams(vmem_limit_bytes=EXPERT_VMEM),
-    )(place_core, *slots, *own, *sib)
+    width = weights[0].shape[1]
+    return resident(
+        functools.partial(expert_kernel, len(slots)),
+        (shape((rows, width), BF16),) * len(slots),
+        *slots,
+        *weights,
+        scalars=spot,
+        flops=3 * 10**9,
+    )
 
 
 def between_places(places, d):
     return [(2 * i + c, 2 * (i ^ d) + c) for i in range(places) for c in range(2)]
 
 
-def exchange(pieces):
-    places = len(pieces)
-    return [pieces[0]] + [
-        lax.ppermute(pieces[d], "exp", between_places(places, d)) for d in range(1, places)
-    ]
+def exchange(piece, d):
+    return lax.ppermute(piece, "exp", between_places(lax.axis_size("exp") // 2, d))
+
+
+def reduce_places(chunks, spare=0):
+    places = len(chunks[0])
+    crossed = [[exchange(pieces[e ^ 1], 1) for e in range(2, places, 2)] for pieces in chunks]
+    joined = []
+    done = None
+    for pieces, cross in zip(chunks, crossed):
+        joined.append([])
+        for e, got in zip(range(2, places, 2), cross):
+            if done is not None:
+                got = after(got, done)
+            done = (pieces[e].astype(F32) + got.astype(F32)).astype(BF16)
+            if len(joined) > 1:
+                done = jnp.pad(done, ((0, 0), (0, spare)))
+            joined[-1].append(done)
+    return [
+        [after(pieces[0], done)]
+        + [exchange(sent, 2 * i + 2) for i, sent in enumerate(mine)]
+        + [exchange(after(pieces[1], mine[-1]), 1)]
+        for pieces, mine in zip(chunks, joined)
+    ], done
 
 
 def per_device(
@@ -437,7 +459,7 @@
         write_rate,
         flops=10**10,
     )
-    total, out_sib, sib = lax.optimization_barrier((total, out_sib, sib))
+    total, out_sib = lax.optimization_barrier((total, out_sib))
     lin, own_read, routes = call(
         readout_kernel,
         (
@@ -453,18 +475,23 @@
         wu,
         prefixes,
         flops=4 * 10**9,
+        vmem=SMALL_VMEM,
+        stay=True,
     )
 
     totals = [
         lax.ppermute(total, "seq", [(i, i ^ d) for i in range(seqs)]) for d in range(1, seqs)
     ]
+    fetched = fetch(gate_proj, out_weight, out_sib)
+    totals, fetched, sib = lax.optimization_barrier((totals, fetched, sib))
+    gate_here, out_own, out_sib = fetched
 
     half = shape((places, tok, heads * DV), BF16)
-    keep, send = call(
+    keep, send = resident(
         mix_kernel,
         (half, half),
         head_gain.reshape(1, DV),
-        gate_proj,
+        gate_here,
         lin,
         own_read,
         *totals,
@@ -473,24 +500,45 @@
         scratch=[pltpu.VMEM((seqs - 1, *total.shape), BF16)],
     )
     got = lax.ppermute(send, "exp", swap)
-    parts = [exchange(pieces) for pieces in project(keep, got, out_weight, out_sib)]
     spot = jnp.stack([place, core])
-    outs = []
-    for chunk, summands in enumerate(parts):
-        rows = tok // CHUNKS
-        residual, normed = call(
+    rows = tok // CHUNKS
+    chunks, joined = reduce_places(project(keep, got, out_own, out_sib), SPARE)
+    sib = fetch(*(after(w, joined) for w in sib))
+    chunks[0][0] = after(chunks[0][0], *sib)
+    residuals, slots = [], []
+    for chunk, summands in enumerate(chunks):
+        if slots:
+            summands[0] = after(summands[0], slots[-1][1])
+        kept, sent = resident(
             functools.partial(norm_kernel, chunk),
             (shape((rows, width), F32), shape((rows, width + LANES), BF16)),
             hidden_in,
             post_gain.reshape(1, width),
             routes,
             *summands,
-            vmem=SMALL_VMEM,
         )
-        slots = exchange([normed] * places)
-        summands = exchange(experts(spot, slots, own, sib))
-        outs.append(sum((s.astype(F32) for s in summands), residual).astype(BF16))
-    return jnp.concatenate(outs, axis=0)
+        residuals.append(kept)
+        slot = [sent] + [None] * (places - 1)
+        for e in range(2, places, 2):
+            slot[e] = exchange(sent, e)
+        slot[1] = exchange(sent, 1)
+        slots.append(slot)
+    for slot in slots:
+        for e in range(2, places, 2):
+            slot[e + 1] = exchange(after(slot[e], slots[-1][0]), 1)
+    made = []
+    for slot in slots:
+        if made:
+            slot[0] = after(slot[0], made[-1][0])
+        made.append(experts(spot, slot, (*own, *sib)))
+    chunks, _ = reduce_places(made)
+    return jnp.concatenate(
+        [
+            sum((s.astype(F32) for s in summands), kept).astype(BF16)
+            for kept, summands in zip(residuals, chunks)
+        ],
+        axis=0,
+    )
 
 
 def solution(mesh):

time: 120 us -> 93.9 us (0.78)
  starting transfers between devices: 53.8 us -> 32.6 us
  waiting for transfers between devices: 19.2 us -> 31.7 us
  Pallas kernels: 36.9 us -> 25.5 us
  local copies, waits for them, and re-layouts: 8.07 us -> 2.51 us
    ppermute x18, starting transfers between devices: 48.4 us -> 27.1 us  [exchange(): lax.ppermute(piece, 'exp', between_places(lax.axis_size('exp') // 2, d))]
    ppermute x18, waiting for transfers between devices: 8.73 us -> 25 us  [exchange(): lax.ppermute(piece, 'exp', between_places(lax.axis_size('exp') // 2, d))]
    pallas_call x5 -> x2, Pallas kernels: 19.6 us -> 12.6 us  [call(): pl.pallas_call(kernel, grid=(1,), out_shape=tuple(outs), in_specs=([] if...]
    unnamed x28 -> x30, local copies, waits for them, and re-layouts: 8.07 us -> 2.5 us
    pallas_call x3 -> x8, Pallas kernels: 17.3 us -> 12.8 us  [the longest x6 8.32 us: resident(): pl.pallas_call(kernel, out_shape=tuple(outs), in_specs=([] if scalars is...]
    ppermute x3, waiting for transfers between devices: 1.92 us -> 0.01 us  [per_device(): sib = tuple((lax.ppermute(w, 'exp', swap) for w in own))]
    ppermute x3, waiting for transfers between devices: 6.82 us -> 5.08 us  [per_device(): lax.ppermute(total, 'seq', [(i, i ^ d) for i in range(seqs)])]
  transfers between devices with their start and end apart: 26 -> 26, of which waited for: 7 -> 13; matrix products, arithmetic and copies ran while one was open for 1% -> 0% of each run, Pallas kernels for 23% -> 24%
where the time goes in v3:
time: 93.9 us; the launch traced here: 93.7 us
  starting transfers between devices  32.6 us (35%)
  waiting for transfers between devices  31.7 us (34%)
  Pallas kernels  25.5 us (27%)
  local copies, waits for them, and re-layouts  2.51 us (3%)
  other arithmetic  1.14 us (1%)
    ppermute x18, starting transfers between devices, exchange(): lax.ppermute(piece, 'exp', between_places(lax.axis_size('exp') // 2, d))  27.1 us
    ppermute x18, waiting for transfers between devices, exchange(): lax.ppermute(piece, 'exp', between_places(lax.axis_size('exp') // 2, d))  25 us
    pallas_call x2, Pallas kernels, call(): pl.pallas_call(kernel, grid=(1,), out_shape=tuple(outs), in_specs=([] if...  12.6 us
    pallas_call x6, Pallas kernels, resident(): pl.pallas_call(kernel, out_shape=tuple(outs), in_specs=([] if scalars is...  8.32 us
    ppermute x3, waiting for transfers between devices, per_device(): lax.ppermute(total, 'seq', [(i, i ^ d) for i in range(seqs)])  5.08 us
    pallas_call x2, Pallas kernels, fetch(): pl.pallas_call(fetch_kernel, out_shape=tuple((shape(a.shape, a.dtype) for...  4.51 us
    ppermute x3, starting transfers between devices, per_device(): lax.ppermute(total, 'seq', [(i, i ^ d) for i in range(seqs)])  4.47 us
    unnamed x30, local copies, waits for them, and re-layouts  2.5 us
  transfers between devices with their start and end apart: 26, of which 13 were waited for; matrix products, arithmetic and copies ran while one was open for 0% of the time, Pallas kernels for 24%

profile of v3, /device:TPU:0, one launch (start us, length us, event | category | flops | bytes accessed | tf_op | source)
XLA Modules:
  0.0 93.7 jit_solution(2640591735853452209)
XLA Ops:
  0.0 0.5 collective-permute-start
  0.5 0.5 collective-permute-start.5
  1.0 0.1 pad_add_fusion.spot_ref
  1.1 10.0 %shard_map.145 = (bf16[4,4,128,256]{3,2,1,0:T(8,128)(2,1)}, bf16[4,4,128,256]{3,2,1,0:T(8,128)(2,1)}, bf16[4,128,256]{2,1,0:T(8,128)(2,1)}) custom-call(bf16[512,256]{1,0:T(8,128)(2,1)} %key_ref.3, bf16[512,512]{1,0:T(8,128)(2,1)} %value_ref.1, f32[4,512]{1,0:T(4,128)} %decay_ref.3, f32[4,512]{1,0:T(4,128)} %rate_ref.1), custom_call_target="tpu_custom_call" | custom-call | flops 10000000000 | bytes 3162112 | tf_op jit(solution)/shard_map/pallas_call | solution.py:79
  11.2 2.9 %collective-permute-start.1 = (bf16[4,128,256]{2,1,0:T(8,128)(2,1)}, bf16[4,128,256]{2,1,0:T(8,128)(2,1)S(1)}, u32[]{:S(2)}, u32[]{:S(2)}) collective-permute-start(bf16[4,128,256]{2,1,0:T(8,128)(2,1)} %get-tuple-element.72), channel_id=1, source_target_pairs={{0,8},{8,0},{16,24},{24,16},{1,9},{9,1},{17,25},{25,17},{2,10},{10... | collective-permute-start | bytes 786440 | tf_op jit(solution)/shard_map/ppermute | solution.py:483
  14.1 1.5 %collective-permute-start.2 = (bf16[4,128,256]{2,1,0:T(8,128)(2,1)}, bf16[4,128,256]{2,1,0:T(8,128)(2,1)S(1)}, u32[]{:S(2)}, u32[]{:S(2)}) collective-permute-start(bf16[4,128,256]{2,1,0:T(8,128)(2,1)} %get-tuple-element.72), channel_id=1, source_target_pairs={{0,16},{8,24},{16,0},{24,8},{1,17},{9,25},{17,1},{25,9},{2,18},{10... | collective-permute-start | bytes 786440 | tf_op jit(solution)/shard_map/ppermute | solution.py:483
  15.7 1.2 %copy-done.13 = bf16[4,4,128,256]{3,2,1,0:T(8,128)(2,1)S(1)} copy-done((bf16[4,4,128,256]{3,2,1,0:T(8,128)(2,1)S(1)}, bf16[4,4,128,256]{3,2,1,0:T(8,128)(2,1)}, u32[]{:S(2)}) %copy-start.13) | copy-done | bytes 1048600
  16.9 1.2 %copy-done.14 = bf16[4,4,128,256]{3,2,1,0:T(8,128)(2,1)S(1)} copy-done((bf16[4,4,128,256]{3,2,1,0:T(8,128)(2,1)S(1)}, bf16[4,4,128,256]{3,2,1,0:T(8,128)(2,1)}, u32[]{:S(2)}) %copy-start.14) | copy-done | bytes 1048600
  18.1 2.6 %shard_map.146 = (bf16[512,512]{1,0:T(8,128)(2,1)S(1)}, f32[512,512]{1,0:T(8,128)S(1)}, bf16[64,128]{1,0:T(8,128)(2,1)S(1)}) custom-call(bf16[512,256]{1,0:T(8,128)(2,1)S(1)} %copy-done.7, bf16[512,256]{1,0:T(8,128)(2,1)S(1)} %copy-done.8, f32[4,512]{1,0:T(4,128)S(1)} %copy-done.9, s32[4,64]{1,0:T(4,128)S(1)} %bitcast.9, bf16[4,64]{1,0:T(4,128)(2,1)S(1)} %bitcast.10, ...), custom_call_target="tpu_custom_call" | custom-call | flops 4000000000 | bytes 4220416 | tf_op jit(solution)/shard_map/pallas_call | solution.py:79
  20.8 2.0 %shard_map.147 = (bf16[512,512]{1,0:T(8,128)(2,1)S(1)}, bf16[512,2048]{1,0:T(8,128)(2,1)S(1)}, bf16[512,2048]{1,0:T(8,128)(2,1)S(1)}) custom-call(bf16[512,512]{1,0:T(8,128)(2,1)S(1)} %copy-done.5, bf16[512,2048]{1,0:T(8,128)(2,1)S(1)} %copy-done.3, bf16[512,2048]{1,0:T(8,128)(2,1)} %collective-permute-done.refs_2_), custom_call_target="tpu_custom_call" | custom-call | bytes 9437184 | tf_op jit(solution)/shard_map/pallas_call | solution.py:46
  22.8 5.1 %collective-permute-done.2.refs_1_ = bf16[4,128,256]{2,1,0:T(8,128)(2,1)S(1)} collective-permute-done((bf16[4,128,256]{2,1,0:T(8,128)(2,1)}, bf16[4,128,256]{2,1,0:T(8,128)(2,1)S(1)}, u32[]{:S(2)}, u32[]{:S(2)}) %collective-permute-start.2) | collective-permute-done | bytes 262176 | tf_op jit(solution)/shard_map/ppermute | solution.py:483
  27.9 1.7 %shard_map.148 = (bf16[4,64,512]{2,1,0:T(8,128)(2,1)S(1)}, bf16[4,64,512]{2,1,0:T(8,128)(2,1)S(1)}) custom-call(s32[3]{0:T(128)S(1)} %pad_add_fusion.spot_ref, f32[1,128]{1,0:T(1,128)S(1)} %bitcast.11, bf16[512,512]{1,0:T(8,128)(2,1)S(1)} %get-tuple-element.77.gate_ref, bf16[512,512]{1,0:T(8,128)(2,1)S(1)} %get-tuple-element.78.lin_ref, ...), custom_call_target="tpu_custom_call" | custom-call | flops 1000000000 | bytes 3408384 | tf_op jit(solution)/shard_map/pallas_call | solution.py:61
  29.7 1.5 %collective-permute-done.7.got_ref = bf16[4,64,512]{2,1,0:T(8,128)(2,1)S(1)} collective-permute-done((bf16[4,64,512]{2,1,0:T(8,128)(2,1)S(1)}, bf16[4,64,512]{2,1,0:T(8,128)(2,1)S(1)}, u32[]{:S(2)}, u32[]{:S(2)}) %collective-permute-start.7) | collective-permute-done | bytes 262176 | tf_op jit(solution)/shard_map/ppermute | solution.py:502
  31.2 1.2 %shard_map.149 = (bf16[32,2048]{1,0:T(8,128)(2,1)S(1)}, bf16[32,2048]{1,0:T(8,128)(2,1)S(1)}, bf16[32,2048]{1,0:T(8,128)(2,1)S(1)}, bf16[32,2048]{1,0:T(8,128)(2...) custom-call(bf16[4,64,512]{2,1,0:T(8,128)(2,1)S(1)} %get-tuple-eleme, ...), custom_call_target="tpu_custom_call" | custom-call | bytes 5767168 | tf_op jit(solution)/shard_map/pallas_call | solution.py:61
  32.5 1.6 %collective-permute-start.9 = (bf16[32,2048]{1,0:T(8,128)(2,1)S(1)}, bf16[32,2048]{1,0:T(8,128)(2,1)S(1)}, u32[]{:S(2)}, u32[]{:S(2)}) collective-permute-start(bf16[32,2048]{1,0:T(8,128)(2,1)S(1)} %get-tuple-element.91), channel_id=1, source_target_pairs={{0,2},{1,3},{2,0},{3,1},{4,6},{5,7},{6,4},{7,5},{8,10},{9,11},{10,... | collective-permute-start | bytes 393224 | tf_op jit(solution)/shard_map/ppermute | solution.py:395
  34.1 0.4 collective-permute-start.8
  34.6 4.3 %collective-permute-done.9 = bf16[32,2048]{1,0:T(8,128)(2,1)S(1)} collective-permute-done((bf16[32,2048]{1,0:T(8,128)(2,1)S(1)}, bf16[32,2048]{1,0:T(8,128)(2,1)S(1)}, u32[]{:S(2)}, u32[]{:S(2)}) %collective-permute-start.9) | collective-permute-done | bytes 131104 | tf_op jit(solution)/shard_map/ppermute | solution.py:395
  38.9 2.6 %collective-permute-start.10 = (bf16[32,2048]{1,0:T(8,128)(2,1)S(1)}, bf16[32,2048]{1,0:T(8,128)(2,1)S(1)}, u32[]{:S(2)}, u32[]{:S(2)}) collective-permute-start(bf16[32,2048]{1,0:T(8,128)(2,1)S(1)} %add_convert_fusion.5), channel_id=1, source_target_pairs={{0,4},{1,5},{2,6},{3,7},{4,0},{5,1},{6,2},{7,3},{8,12},{9,13},{10,... | collective-permute-start | bytes 393224 | tf_op jit(solution)/shard_map/ppermute | solution.py:395
  41.6 1.6 %collective-permute-start.11 = (bf16[32,2048]{1,0:T(8,128)(2,1)S(1)}, bf16[32,2048]{1,0:T(8,128)(2,1)S(1)}, u32[]{:S(2)}, u32[]{:S(2)}) collective-permute-start(bf16[32,2048]{1,0:T(8,128)(2,1)S(1)} %get-tuple-element.105), channel_id=1, source_target_pairs={{0,2},{1,3},{2,0},{3,1},{4,6},{5,7},{6,4},{7,5},{8,10},{9,11},{10,... | collective-permute-start | bytes 393224 | tf_op jit(solution)/shard_map/ppermute | solution.py:395
  43.2 2.0 %collective-permute-start.14 = (bf16[32,2304]{1,0:T(8,128)(2,1)S(1)}, bf16[32,2304]{1,0:T(8,128)(2,1)S(1)}, u32[]{:S(2)}, u32[]{:S(2)}) collective-permute-start(bf16[32,2304]{1,0:T(8,128)(2,1)S(1)} %pad.4), channel_id=1, source_target_pairs={{0,4},{1,5},{2,6},{3,7},{4,0},{5,1},{6,2},{7,3},{8,12},{9,13},{10,... | collective-permute-start | bytes 442376 | tf_op jit(solution)/shard_map/ppermute | solution.py:395
  45.2 2.5 %shard_map.150 = (bf16[1,2048,512]{2,1,0:T(8,128)(2,1)S(1)}, bf16[1,2048,512]{2,1,0:T(8,128)(2,1)S(1)}, bf16[1,512,2048]{2,1,0:T(8,128)(2,1)S(1)}) custom-call(bf16[1,2048,512]{2,1,0:T(8,128)(2,1)S(1)} %collective-permute-done.4.refs_0_, bf16[1,2048,512]{2,1,0:T(8,128)(2,1)} %collective-permute-done.5.refs_1_, ...), custom_call_target="tpu_custom_call" | custom-call | bytes 12582912 | tf_op jit(solution)/shard_map/pallas_call | solution.py:46
  47.7 0.8 collective-permute-done.10.refs_1_
  48.6 0.2 shard_map.151
  48.8 1.9 %collective-permute-start.12 = (bf16[32,2176]{1,0:T(8,128)(2,1)S(1)}, bf16[32,2176]{1,0:T(8,128)(2,1)S(1)}, u32[]{:S(2)}, u32[]{:S(2)}) collective-permute-start(bf16[32,2176]{1,0:T(8,128)(2,1)S(1)} %get-tuple-element.107.refs_0_), channel_id=1, source_target_pairs={{0,2},{1,3},{2,0},{3,1},{4,6},{5,7},{6,4},{7,5},{8,10},{9,11},{10,... | collective-permute-start | bytes 417800 | tf_op jit(solution)/shard_map/ppermute | solution.py:395
  50.6 3.9 %collective-permute-start.13 = (bf16[32,2176]{1,0:T(8,128)(2,1)S(1)}, bf16[32,2176]{1,0:T(8,128)(2,1)S(1)}, u32[]{:S(2)}, u32[]{:S(2)}) collective-permute-start(bf16[32,2176]{1,0:T(8,128)(2,1)S(1)} %get-tuple-element.107.refs_0_), channel_id=1, source_target_pairs={{0,4},{1,5},{2,6},{3,7},{4,0},{5,1},{6,2},{7,3},{8,12},{9,13},{10,... | collective-permute-start | bytes 417800 | tf_op jit(solution)/shard_map/ppermute | solution.py:395
  54.5 0.1 collective-permute-start.15
  54.6 4.6 %collective-permute-done.12.refs_1_ = bf16[32,2176]{1,0:T(8,128)(2,1)S(1)} collective-permute-done((bf16[32,2176]{1,0:T(8,128)(2,1)S(1)}, bf16[32,2176]{1,0:T(8,128)(2,1)S(1)}, u32[]{:S(2)}, u32[]{:S(2)}) %collective-permute-start.12) | collective-permute-done | bytes 139296 | tf_op jit(solution)/shard_map/ppermute | solution.py:395
  59.2 1.4 %collective-permute-done.15.refs_2_ = bf16[32,2048]{1,0:T(8,128)(2,1)S(1)} collective-permute-done((bf16[32,2048]{1,0:T(8,128)(2,1)S(1)}, bf16[32,2048]{1,0:T(8,128)(2,1)S(1)}, u32[]{:S(2)}, u32[]{:S(2)}) %collective-permute-start.15) | collective-permute-done | bytes 131104 | tf_op jit(solution)/shard_map/ppermute | solution.py:395
  60.6 0.2 shard_map.152
  60.8 1.7 %collective-permute-start.18 = (bf16[32,2176]{1,0:T(8,128)(2,1)S(1)}, bf16[32,2176]{1,0:T(8,128)(2,1)S(1)}, u32[]{:S(2)}, u32[]{:S(2)}) collective-permute-start(bf16[32,2176]{1,0:T(8,128)(2,1)S(1)} %get-tuple-element.116.refs_0_), channel_id=1, source_target_pairs={{0,4},{1,5},{2,6},{3,7},{4,0},{5,1},{6,2},{7,3},{8,12},{9,13},{10,... | collective-permute-start | bytes 417800 | tf_op jit(solution)/shard_map/ppermute | solution.py:395
  62.5 2.5 %collective-permute-start.16 = (bf16[32,2176]{1,0:T(8,128)(2,1)S(1)}, bf16[32,2176]{1,0:T(8,128)(2,1)S(1)}, u32[]{:S(2)}, u32[]{:S(2)}) collective-permute-start(bf16[32,2176]{1,0:T(8,128)(2,1)S(1)} %collective-permute-done.13.refs_2_), channel_id=1, source_target_pairs={{0,2},{1,3},{2,0},{3,1},{4,6},{5,7},{6,4},{7,5},{8,10},{9,11},{10,... | collective-permute-start | bytes 417800 | tf_op jit(solution)/shard_map/ppermute | solution.py:395
  64.9 0.1 pad_add_fusion.1.spot_ref
  65.0 2.6 %collective-permute-done.18.refs_2_ = bf16[32,2176]{1,0:T(8,128)(2,1)S(1)} collective-permute-done((bf16[32,2176]{1,0:T(8,128)(2,1)S(1)}, bf16[32,2176]{1,0:T(8,128)(2,1)S(1)}, u32[]{:S(2)}, u32[]{:S(2)}) %collective-permute-start.18) | collective-permute-done | bytes 139296 | tf_op jit(solution)/shard_map/ppermute | solution.py:395
  67.6 1.9 %collective-permute-start.19 = (bf16[32,2176]{1,0:T(8,128)(2,1)S(1)}, bf16[32,2176]{1,0:T(8,128)(2,1)S(1)}, u32[]{:S(2)}, u32[]{:S(2)}) collective-permute-start(bf16[32,2176]{1,0:T(8,128)(2,1)S(1)} %collective-permute-done.18.refs_2_), channel_id=1, source_target_pairs={{0,2},{1,3},{2,0},{3,1},{4,6},{5,7},{6,4},{7,5},{8,10},{9,11},{10,... | collective-permute-start | bytes 417800 | tf_op jit(solution)/shard_map/ppermute | solution.py:395
  69.5 0.6 collective-permute-done.16.refs_3_
  70.1 2.5 %shard_map.153 = (bf16[32,2048]{1,0:T(8,128)(2,1)S(1)}, bf16[32,2048]{1,0:T(8,128)(2,1)S(1)}, bf16[32,2048]{1,0:T(8,128)(2,1)S(1)}, bf16[32,2048]{1,0:T(8,128)(2,1)S(1)}) custom-call(s32[2]{0:T(128)S(1)} %pad_add_fusion.1.spot_ref, bf16[32,2176]{1,0:T(8,128)(2,1)S(1)} %get-tuple-element.107.refs_0_, bf16[32,2176]{1,0:T(8,128)(2,1)S(1)} %collective-permute-done.12.refs_1_, ...), custom_call_target="tpu_custom_call" | custom-call | flops 3000000000 | bytes 13664256 | tf_op jit(solution)/shard_map/pallas_call | solution.py:61
  72.6 1.3 %collective-permute-start.21 = (bf16[32,2048]{1,0:T(8,128)(2,1)S(1)}, bf16[32,2048]{1,0:T(8,128)(2,1)S(1)}, u32[]{:S(2)}, u32[]{:S(2)}) collective-permute-start(bf16[32,2048]{1,0:T(8,128)(2,1)S(1)} %get-tuple-element.121), channel_id=1, source_target_pairs={{0,2},{1,3},{2,0},{3,1},{4,6},{5,7},{6,4},{7,5},{8,10},{9,11},{10,... | collective-permute-start | bytes 393224 | tf_op jit(solution)/shard_map/ppermute | solution.py:395
  73.9 1.6 %collective-permute-done.19.refs_3_ = bf16[32,2176]{1,0:T(8,128)(2,1)S(1)} collective-permute-done((bf16[32,2176]{1,0:T(8,128)(2,1)S(1)}, bf16[32,2176]{1,0:T(8,128)(2,1)S(1)}, u32[]{:S(2)}, u32[]{:S(2)}) %collective-permute-start.19) | collective-permute-done | bytes 139296 | tf_op jit(solution)/shard_map/ppermute | solution.py:395
  75.6 2.5 %shard_map.154 = (bf16[32,2048]{1,0:T(8,128)(2,1)S(1)}, bf16[32,2048]{1,0:T(8,128)(2,1)S(1)}, bf16[32,2048]{1,0:T(8,128)(2,1)S(1)}, bf16[32,2048]{1,0:T(8,128)(2,1)S(1)}) custom-call(s32[2]{0:T(128)S(1)} %pad_add_fusion.1.spot_ref, bf16[32,2176]{1,0:T(8,128)(2,1)S(1)} %get-tuple-element.116.refs_0_, bf16[32,2176]{1,0:T(8,128)(2,1)S(1)} %collective-permute-done.17.refs_1_, ...), custom_call_target="tpu_custom_call" | custom-call | flops 3000000000 | bytes 13664256 | tf_op jit(solution)/shard_map/pallas_call | solution.py:61
  78.0 0.3 collective-permute-start.20
  78.3 2.9 %collective-permute-start.22 = (bf16[32,2048]{1,0:T(8,128)(2,1)S(1)}, bf16[32,2048]{1,0:T(8,128)(2,1)S(1)}, u32[]{:S(2)}, u32[]{:S(2)}) collective-permute-start(bf16[32,2048]{1,0:T(8,128)(2,1)S(1)} %add_convert_fusion.3), channel_id=1, source_target_pairs={{0,4},{1,5},{2,6},{3,7},{4,0},{5,1},{6,2},{7,3},{8,12},{9,13},{10,... | collective-permute-start | bytes 393224 | tf_op jit(solution)/shard_map/ppermute | solution.py:395
  81.3 4.2 %collective-permute-done.20 = bf16[32,2048]{1,0:T(8,128)(2,1)S(1)} collective-permute-done((bf16[32,2048]{1,0:T(8,128)(2,1)S(1)}, bf16[32,2048]{1,0:T(8,128)(2,1)S(1)}, u32[]{:S(2)}, u32[]{:S(2)}) %collective-permute-start.20) | collective-permute-done | bytes 131104 | tf_op jit(solution)/shard_map/ppermute | solution.py:395
  85.5 0.2 collective-permute-start.24
  85.7 2.2 %collective-permute-start.25 = (bf16[32,2048]{1,0:T(8,128)(2,1)S(1)}, bf16[32,2048]{1,0:T(8,128)(2,1)S(1)}, u32[]{:S(2)}, u32[]{:S(2)}) collective-permute-start(bf16[32,2048]{1,0:T(8,128)(2,1)S(1)} %get-tuple-element.130), channel_id=1, source_target_pairs={{0,2},{1,3},{2,0},{3,1},{4,6},{5,7},{6,4},{7,5},{8,10},{9,11},{10,... | collective-permute-start | bytes 393224 | tf_op jit(solution)/shard_map/ppermute | solution.py:395
  87.9 1.0 %collective-permute-done.23 = bf16[32,2048]{1,0:T(8,128)(2,1)S(1)} collective-permute-done((bf16[32,2048]{1,0:T(8,128)(2,1)S(1)}, bf16[32,2048]{1,0:T(8,128)(2,1)S(1)}, u32[]{:S(2)}, u32[]{:S(2)}) %collective-permute-start.23) | collective-permute-done | bytes 131104 | tf_op jit(solution)/shard_map/ppermute | solution.py:395
  89.0 2.4 %collective-permute-done.25 = bf16[32,2048]{1,0:T(8,128)(2,1)S(1)} collective-permute-done((bf16[32,2048]{1,0:T(8,128)(2,1)S(1)}, bf16[32,2048]{1,0:T(8,128)(2,1)S(1)}, u32[]{:S(2)}, u32[]{:S(2)}) %collective-permute-start.25) | collective-permute-done | bytes 131104 | tf_op jit(solution)/shard_map/ppermute | solution.py:395
  91.4 1.5 %collective-permute-done.24 = bf16[32,2048]{1,0:T(8,128)(2,1)S(1)} collective-permute-done((bf16[32,2048]{1,0:T(8,128)(2,1)S(1)}, bf16[32,2048]{1,0:T(8,128)(2,1)S(1)}, u32[]{:S(2)}, u32[]{:S(2)}) %collective-permute-start.24) | collective-permute-done | bytes 131104 | tf_op jit(solution)/shard_map/ppermute | solution.py:395
  92.9 0.7 pad_maximum_fusion
  (54 shorter events, 0.6 us)
Async XLA Ops:
  0.0 11.2 %collective-permute-start = (bf16[512,2048]{1,0:T(8,128)(2,1)}, bf16[512,2048]{1,0:T(8,128)(2,1)}, u32[]{:S(2)}, u32[]{:S(2)}) collective-permute-start(bf16[512,2048]{1,0:T(8,128)(2,1)} %refs_1_.1), channel_id=1, source_target_pairs={{0,1},{1,0},{2,3},{3,2},{4,5},{5,4},{6,7},{7,6},{8,9},{9,8},{10,11... | collective-permute-start | bytes 6291464 | tf_op jit(solution)/shard_map/ppermute | solution.py:448
  0.5 15.2 %collective-permute-start.4 = (bf16[1,2048,512]{2,1,0:T(8,128)(2,1)}, bf16[1,2048,512]{2,1,0:T(8,128)(2,1)S(1)}, u32[]{:S(2)}, u32[]{:S(2)}) collective-permute-start(bf16[1,2048,512]{2,1,0:T(8,128)(2,1)} %refs_4_.3), channel_id=1, source_target_pairs={{0,1},{1,0},{2,3},{3,2},{4,5},{5,4},{6,7},{7,6},{8,9},{9,8},{10,11... | collective-permute-start | bytes 6291464 | tf_op jit(solution)/shard_map/ppermute | solution.py:450
  0.5 22.2 %collective-permute-start.5 = (bf16[1,2048,512]{2,1,0:T(8,128)(2,1)}, bf16[1,2048,512]{2,1,0:T(8,128)(2,1)}, u32[]{:S(2)}, u32[]{:S(2)}) collective-permute-start(bf16[1,2048,512]{2,1,0:T(8,128)(2,1)} %refs_5_.3), channel_id=1, source_target_pairs={{0,1},{1,0},{2,3},{3,2},{4,5},{5,4},{6,7},{7,6},{8,9},{9,8},{10,11... | collective-permute-start | bytes 6291464 | tf_op jit(solution)/shard_map/ppermute | solution.py:450
  1.0 21.8 %collective-permute-start.6 = (bf16[1,512,2048]{2,1,0:T(8,128)(2,1)}, bf16[1,512,2048]{2,1,0:T(8,128)(2,1)}, u32[]{:S(2)}, u32[]{:S(2)}) collective-permute-start(bf16[1,512,2048]{2,1,0:T(8,128)(2,1)} %refs_6_.3), channel_id=1, source_target_pairs={{0,1},{1,0},{2,3},{3,2},{4,5},{5,4},{6,7},{7,6},{8,9},{9,8},{10,11... | collective-permute-start | bytes 6291464 | tf_op jit(solution)/shard_map/ppermute | solution.py:450
  1.1 14.5 %copy-start.7 = (bf16[512,256]{1,0:T(8,128)(2,1)S(1)}, bf16[512,256]{1,0:T(8,128)(2,1)}, u32[]{:S(2)}) copy-start(bf16[512,256]{1,0:T(8,128)(2,1)} %query_ref.1) | copy-start | bytes 786436
  1.1 14.5 %copy-start.8 = (bf16[512,256]{1,0:T(8,128)(2,1)S(1)}, bf16[512,256]{1,0:T(8,128)(2,1)}, u32[]{:S(2)}) copy-start(bf16[512,256]{1,0:T(8,128)(2,1)} %key_ref.3) | copy-start | bytes 786436
  1.1 14.5 %copy-start.9 = (f32[4,512]{1,0:T(4,128)S(1)}, f32[4,512]{1,0:T(4,128)}, u32[]{:S(2)}) copy-start(f32[4,512]{1,0:T(4,128)} %decay_ref.3) | copy-start | bytes 24580
  1.1 14.5 %copy-start.10 = (s32[64,4]{0,1:T(4,128)S(1)}, s32[64,4]{0,1:T(4,128)}, u32[]{:S(2)}) copy-start(s32[64,4]{0,1:T(4,128)} %param.25) | copy-start | bytes 3076
  1.1 14.5 %copy-start.11 = (bf16[64,4]{0,1:T(4,128)(2,1)S(1)}, bf16[64,4]{0,1:T(4,128)(2,1)}, u32[]{:S(2)}) copy-start(bf16[64,4]{0,1:T(4,128)(2,1)} %param.26) | copy-start | bytes 1540
  11.2 11.6 %collective-permute-start.1 = (bf16[4,128,256]{2,1,0:T(8,128)(2,1)}, bf16[4,128,256]{2,1,0:T(8,128)(2,1)S(1)}, u32[]{:S(2)}, u32[]{:S(2)}) collective-permute-start(bf16[4,128,256]{2,1,0:T(8,128)(2,1)} %get-tuple-element.72), channel_id=1, source_target_pairs={{0,8},{8,0},{16,24},{24,16},{1,9},{9,1},{17,25},{25,17},{2,10},{10... | collective-permute-start | bytes 786440 | tf_op jit(solution)/shard_map/ppermute | solution.py:483
  14.1 13.8 %collective-permute-start.2 = (bf16[4,128,256]{2,1,0:T(8,128)(2,1)}, bf16[4,128,256]{2,1,0:T(8,128)(2,1)S(1)}, u32[]{:S(2)}, u32[]{:S(2)}) collective-permute-start(bf16[4,128,256]{2,1,0:T(8,128)(2,1)} %get-tuple-element.72), channel_id=1, source_target_pairs={{0,16},{8,24},{16,0},{24,8},{1,17},{9,25},{17,1},{25,9},{2,18},{10... | collective-permute-start | bytes 786440 | tf_op jit(solution)/shard_map/ppermute | solution.py:483
  15.6 12.2 %collective-permute-start.3 = (bf16[4,128,256]{2,1,0:T(8,128)(2,1)}, bf16[4,128,256]{2,1,0:T(8,128)(2,1)S(1)}, u32[]{:S(2)}, u32[]{:S(2)}) collective-permute-start(bf16[4,128,256]{2,1,0:T(8,128)(2,1)} %get-tuple-element.72), channel_id=1, source_target_pairs={{0,24},{8,16},{16,8},{24,0},{1,25},{9,17},{17,9},{25,1},{2,26},{10... | collective-permute-start | bytes 786440 | tf_op jit(solution)/shard_map/ppermute | solution.py:483
  15.7 1.2 %copy-start.13 = (bf16[4,4,128,256]{3,2,1,0:T(8,128)(2,1)S(1)}, bf16[4,4,128,256]{3,2,1,0:T(8,128)(2,1)}, u32[]{:S(2)}) copy-start(bf16[4,4,128,256]{3,2,1,0:T(8,128)(2,1)} %get-tuple-element.68.wu_ref) | copy-start | bytes 3145732
  16.9 1.2 %copy-start.14 = (bf16[4,4,128,256]{3,2,1,0:T(8,128)(2,1)S(1)}, bf16[4,4,128,256]{3,2,1,0:T(8,128)(2,1)}, u32[]{:S(2)}) copy-start(bf16[4,4,128,256]{3,2,1,0:T(8,128)(2,1)} %get-tuple-element.69.prefix_ref) | copy-start | bytes 3145732
  18.1 2.6 %copy-start.3 = (bf16[512,2048]{1,0:T(8,128)(2,1)S(1)}, bf16[512,2048]{1,0:T(8,128)(2,1)}, u32[]{:S(2)}) copy-start(bf16[512,2048]{1,0:T(8,128)(2,1)} %refs_1_.1) | copy-start | bytes 6291460
  18.1 2.6 %copy-start.5 = (bf16[512,512]{1,0:T(8,128)(2,1)S(1)}, bf16[512,512]{1,0:T(8,128)(2,1)}, u32[]{:S(2)}) copy-start(bf16[512,512]{1,0:T(8,128)(2,1)} %refs_0_.1) | copy-start | bytes 1572868
  20.8 7.1 %copy-start.12 = (f32[128]{0:T(128)S(1)}, f32[128]{0:T(128)}, u32[]{:S(2)}) copy-start(f32[128]{0:T(128)} %param.22) | copy-start | bytes 1540
  29.6 1.6 %collective-permute-start.7 = (bf16[4,64,512]{2,1,0:T(8,128)(2,1)S(1)}, bf16[4,64,512]{2,1,0:T(8,128)(2,1)S(1)}, u32[]{:S(2)}, u32[]{:S(2)}) collective-permute-start(bf16[4,64,512]{2,1,0:T(8,128)(2,1)S(1)} %get-tuple-element.84), channel_id=1, source_target_pairs={{0,1},{1,0},{2,3},{3,2},{4,5},{5,4},{6,7},{7,6},{8,9},{9,8},{10,11... | collective-permute-start | bytes 786440 | tf_op jit(solution)/shard_map/ppermute | solution.py:502
  32.5 6.4 %collective-permute-start.9 = (bf16[32,2048]{1,0:T(8,128)(2,1)S(1)}, bf16[32,2048]{1,0:T(8,128)(2,1)S(1)}, u32[]{:S(2)}, u32[]{:S(2)}) collective-permute-start(bf16[32,2048]{1,0:T(8,128)(2,1)S(1)} %get-tuple-element.91), channel_id=1, source_target_pairs={{0,2},{1,3},{2,0},{3,1},{4,6},{5,7},{6,4},{7,5},{8,10},{9,11},{10,... | collective-permute-start | bytes 393224 | tf_op jit(solution)/shard_map/ppermute | solution.py:395
  34.1 7.5 %collective-permute-start.8 = (bf16[32,2048]{1,0:T(8,128)(2,1)S(1)}, bf16[32,2048]{1,0:T(8,128)(2,1)S(1)}, u32[]{:S(2)}, u32[]{:S(2)}) collective-permute-start(bf16[32,2048]{1,0:T(8,128)(2,1)S(1)} %get-tuple-element.89), channel_id=1, source_target_pairs={{0,2},{1,3},{2,0},{3,1},{4,6},{5,7},{6,4},{7,5},{8,10},{9,11},{10,... | collective-permute-start | bytes 393224 | tf_op jit(solution)/shard_map/ppermute | solution.py:395
  38.9 9.7 %copy-start.4 = (bf16[64,2048]{1,0:T(8,128)(2,1)S(1)}, bf16[64,2048]{1,0:T(8,128)(2,1)}, u32[]{:S(2)}) copy-start(bf16[64,2048]{1,0:T(8,128)(2,1)} %hidden_ref.3) | copy-start | bytes 786436
  38.9 9.6 %collective-permute-start.10 = (bf16[32,2048]{1,0:T(8,128)(2,1)S(1)}, bf16[32,2048]{1,0:T(8,128)(2,1)S(1)}, u32[]{:S(2)}, u32[]{:S(2)}) collective-permute-start(bf16[32,2048]{1,0:T(8,128)(2,1)S(1)} %add_convert_fusion.5), channel_id=1, source_target_pairs={{0,4},{1,5},{2,6},{3,7},{4,0},{5,1},{6,2},{7,3},{8,12},{9,13},{10,... | collective-permute-start | bytes 393224 | tf_op jit(solution)/shard_map/ppermute | solution.py:395
  41.6 7.0 %collective-permute-start.11 = (bf16[32,2048]{1,0:T(8,128)(2,1)S(1)}, bf16[32,2048]{1,0:T(8,128)(2,1)S(1)}, u32[]{:S(2)}, u32[]{:S(2)}) collective-permute-start(bf16[32,2048]{1,0:T(8,128)(2,1)S(1)} %get-tuple-element.105), channel_id=1, source_target_pairs={{0,2},{1,3},{2,0},{3,1},{4,6},{5,7},{6,4},{7,5},{8,10},{9,11},{10,... | collective-permute-start | bytes 393224 | tf_op jit(solution)/shard_map/ppermute | solution.py:395
  43.2 17.4 %collective-permute-start.14 = (bf16[32,2304]{1,0:T(8,128)(2,1)S(1)}, bf16[32,2304]{1,0:T(8,128)(2,1)S(1)}, u32[]{:S(2)}, u32[]{:S(2)}) collective-permute-start(bf16[32,2304]{1,0:T(8,128)(2,1)S(1)} %pad.4), channel_id=1, source_target_pairs={{0,4},{1,5},{2,6},{3,7},{4,0},{5,1},{6,2},{7,3},{8,12},{9,13},{10,... | collective-permute-start | bytes 442376 | tf_op jit(solution)/shard_map/ppermute | solution.py:395
  45.2 3.4 %copy-start.6 = (f32[2048]{0:T(1024)S(1)}, f32[2048]{0:T(1024)}, u32[]{:S(2)}) copy-start(f32[2048]{0:T(1024)} %param.24) | copy-start | bytes 24580
  45.2 24.9 %copy-start = (bf16[1,2048,512]{2,1,0:T(8,128)(2,1)S(1)}, bf16[1,2048,512]{2,1,0:T(8,128)(2,1)}, u32[]{:S(2)}) copy-start(bf16[1,2048,512]{2,1,0:T(8,128)(2,1)} %refs_4_.3) | copy-start | bytes 6291460
  45.2 24.9 %copy-start.1 = (bf16[1,2048,512]{2,1,0:T(8,128)(2,1)S(1)}, bf16[1,2048,512]{2,1,0:T(8,128)(2,1)}, u32[]{:S(2)}) copy-start(bf16[1,2048,512]{2,1,0:T(8,128)(2,1)} %refs_5_.3) | copy-start | bytes 6291460
  45.2 24.9 %copy-start.2 = (bf16[1,512,2048]{2,1,0:T(8,128)(2,1)S(1)}, bf16[1,512,2048]{2,1,0:T(8,128)(2,1)}, u32[]{:S(2)}) copy-start(bf16[1,512,2048]{2,1,0:T(8,128)(2,1)} %refs_6_.3) | copy-start | bytes 6291460
  48.8 10.4 %collective-permute-start.12 = (bf16[32,2176]{1,0:T(8,128)(2,1)S(1)}, bf16[32,2176]{1,0:T(8,128)(2,1)S(1)}, u32[]{:S(2)}, u32[]{:S(2)}) collective-permute-start(bf16[32,2176]{1,0:T(8,128)(2,1)S(1)} %get-tuple-element.107.refs_0_), channel_id=1, source_target_pairs={{0,2},{1,3},{2,0},{3,1},{4,6},{5,7},{6,4},{7,5},{8,10},{9,11},{10,... | collective-permute-start | bytes 417800 | tf_op jit(solution)/shard_map/ppermute | solution.py:395
  50.6 11.8 %collective-permute-start.13 = (bf16[32,2176]{1,0:T(8,128)(2,1)S(1)}, bf16[32,2176]{1,0:T(8,128)(2,1)S(1)}, u32[]{:S(2)}, u32[]{:S(2)}) collective-permute-start(bf16[32,2176]{1,0:T(8,128)(2,1)S(1)} %get-tuple-element.107.refs_0_), channel_id=1, source_target_pairs={{0,4},{1,5},{2,6},{3,7},{4,0},{5,1},{6,2},{7,3},{8,12},{9,13},{10,... | collective-permute-start | bytes 417800 | tf_op jit(solution)/shard_map/ppermute | solution.py:395
  54.5 6.1 %collective-permute-start.15 = (bf16[32,2048]{1,0:T(8,128)(2,1)S(1)}, bf16[32,2048]{1,0:T(8,128)(2,1)S(1)}, u32[]{:S(2)}, u32[]{:S(2)}) collective-permute-start(bf16[32,2048]{1,0:T(8,128)(2,1)S(1)} %get-tuple-element.112), channel_id=1, source_target_pairs={{0,2},{1,3},{2,0},{3,1},{4,6},{5,7},{6,4},{7,5},{8,10},{9,11},{10,... | collective-permute-start | bytes 393224 | tf_op jit(solution)/shard_map/ppermute | solution.py:395
  60.8 6.8 %collective-permute-start.18 = (bf16[32,2176]{1,0:T(8,128)(2,1)S(1)}, bf16[32,2176]{1,0:T(8,128)(2,1)S(1)}, u32[]{:S(2)}, u32[]{:S(2)}) collective-permute-start(bf16[32,2176]{1,0:T(8,128)(2,1)S(1)} %get-tuple-element.116.refs_0_), channel_id=1, source_target_pairs={{0,4},{1,5},{2,6},{3,7},{4,0},{5,1},{6,2},{7,3},{8,12},{9,13},{10,... | collective-permute-start | bytes 417800 | tf_op jit(solution)/shard_map/ppermute | solution.py:395
  62.5 7.6 %collective-permute-start.16 = (bf16[32,2176]{1,0:T(8,128)(2,1)S(1)}, bf16[32,2176]{1,0:T(8,128)(2,1)S(1)}, u32[]{:S(2)}, u32[]{:S(2)}) collective-permute-start(bf16[32,2176]{1,0:T(8,128)(2,1)S(1)} %collective-permute-done.13.refs_2_), channel_id=1, source_target_pairs={{0,2},{1,3},{2,0},{3,1},{4,6},{5,7},{6,4},{7,5},{8,10},{9,11},{10,... | collective-permute-start | bytes 417800 | tf_op jit(solution)/shard_map/ppermute | solution.py:395
  65.0 8.9 %collective-permute-start.17 = (bf16[32,2176]{1,0:T(8,128)(2,1)S(1)}, bf16[32,2176]{1,0:T(8,128)(2,1)S(1)}, u32[]{:S(2)}, u32[]{:S(2)}) collective-permute-start(bf16[32,2176]{1,0:T(8,128)(2,1)S(1)} %get-tuple-element.116.refs_0_), channel_id=1, source_target_pairs={{0,2},{1,3},{2,0},{3,1},{4,6},{5,7},{6,4},{7,5},{8,10},{9,11},{10,... | collective-permute-start | bytes 417800 | tf_op jit(solution)/shard_map/ppermute | solution.py:395
  67.6 7.9 %collective-permute-start.19 = (bf16[32,2176]{1,0:T(8,128)(2,1)S(1)}, bf16[32,2176]{1,0:T(8,128)(2,1)S(1)}, u32[]{:S(2)}, u32[]{:S(2)}) collective-permute-start(bf16[32,2176]{1,0:T(8,128)(2,1)S(1)} %collective-permute-done.18.refs_2_), channel_id=1, source_target_pairs={{0,2},{1,3},{2,0},{3,1},{4,6},{5,7},{6,4},{7,5},{8,10},{9,11},{10,... | collective-permute-start | bytes 417800 | tf_op jit(solution)/shard_map/ppermute | solution.py:395
  72.6 5.7 %collective-permute-start.21 = (bf16[32,2048]{1,0:T(8,128)(2,1)S(1)}, bf16[32,2048]{1,0:T(8,128)(2,1)S(1)}, u32[]{:S(2)}, u32[]{:S(2)}) collective-permute-start(bf16[32,2048]{1,0:T(8,128)(2,1)S(1)} %get-tuple-element.121), channel_id=1, source_target_pairs={{0,2},{1,3},{2,0},{3,1},{4,6},{5,7},{6,4},{7,5},{8,10},{9,11},{10,... | collective-permute-start | bytes 393224 | tf_op jit(solution)/shard_map/ppermute | solution.py:395
  78.0 7.4 %collective-permute-start.20 = (bf16[32,2048]{1,0:T(8,128)(2,1)S(1)}, bf16[32,2048]{1,0:T(8,128)(2,1)S(1)}, u32[]{:S(2)}, u32[]{:S(2)}) collective-permute-start(bf16[32,2048]{1,0:T(8,128)(2,1)S(1)} %get-tuple-element.119), channel_id=1, source_target_pairs={{0,2},{1,3},{2,0},{3,1},{4,6},{5,7},{6,4},{7,5},{8,10},{9,11},{10,... | collective-permute-start | bytes 393224 | tf_op jit(solution)/shard_map/ppermute | solution.py:395
  78.3 10.5 %collective-permute-start.22 = (bf16[32,2048]{1,0:T(8,128)(2,1)S(1)}, bf16[32,2048]{1,0:T(8,128)(2,1)S(1)}, u32[]{:S(2)}, u32[]{:S(2)}) collective-permute-start(bf16[32,2048]{1,0:T(8,128)(2,1)S(1)} %add_convert_fusion.3), channel_id=1, source_target_pairs={{0,4},{1,5},{2,6},{3,7},{4,0},{5,1},{6,2},{7,3},{8,12},{9,13},{10,... | collective-permute-start | bytes 393224 | tf_op jit(solution)/shard_map/ppermute | solution.py:395
  81.3 7.6 %collective-permute-start.23 = (bf16[32,2048]{1,0:T(8,128)(2,1)S(1)}, bf16[32,2048]{1,0:T(8,128)(2,1)S(1)}, u32[]{:S(2)}, u32[]{:S(2)}) collective-permute-start(bf16[32,2048]{1,0:T(8,128)(2,1)S(1)} %get-tuple-element.125), channel_id=1, source_target_pairs={{0,2},{1,3},{2,0},{3,1},{4,6},{5,7},{6,4},{7,5},{8,10},{9,11},{10,... | collective-permute-start | bytes 393224 | tf_op jit(solution)/shard_map/ppermute | solution.py:395
  85.5 7.3 %collective-permute-start.24 = (bf16[32,2048]{1,0:T(8,128)(2,1)S(1)}, bf16[32,2048]{1,0:T(8,128)(2,1)S(1)}, u32[]{:S(2)}, u32[]{:S(2)}) collective-permute-start(bf16[32,2048]{1,0:T(8,128)(2,1)S(1)} %add_convert_fusion.2), channel_id=1, source_target_pairs={{0,4},{1,5},{2,6},{3,7},{4,0},{5,1},{6,2},{7,3},{8,12},{9,13},{10,... | collective-permute-start | bytes 393224 | tf_op jit(solution)/shard_map/ppermute | solution.py:395
  85.7 5.6 %collective-permute-start.25 = (bf16[32,2048]{1,0:T(8,128)(2,1)S(1)}, bf16[32,2048]{1,0:T(8,128)(2,1)S(1)}, u32[]{:S(2)}, u32[]{:S(2)}) collective-permute-start(bf16[32,2048]{1,0:T(8,128)(2,1)S(1)} %get-tuple-element.130), channel_id=1, source_target_pairs={{0,2},{1,3},{2,0},{3,1},{4,6},{5,7},{6,4},{7,5},{8,10},{9,11},{10,... | collective-permute-start | bytes 393224 | tf_op jit(solution)/shard_map/ppermute | solution.py:395

commit v4 on v3

--- a/solution.py
+++ b/solution.py
@@ -18,7 +18,7 @@
 LARGE_VMEM = 60 * 1024 * 1024
 SMALL_VMEM = 24 * 1024 * 1024
 FETCH_VMEM = 24 * 1024 * 1024
-CHUNKS = 2
+SIZES = (32, 32)
 SPARE = 256
 PAIRS_AT_ONCE = 16
 
@@ -112,15 +112,6 @@
     return jnp.dot(
         jnp.concatenate([high, low], axis=1),
         jnp.concatenate([b, b], axis=0),
-        preferred_element_type=F32,
-    )
-
-
-def mm_right2(a, b):
-    high, low = split(b)
-    return jnp.dot(
-        jnp.concatenate([a, a], axis=1),
-        jnp.concatenate([high, low], axis=0),
         preferred_element_type=F32,
     )
 
@@ -208,11 +199,11 @@
             cum_row, cum_col = cum_rows[at : at + 1, :], cum_cols[:, at : at + 1]
             rate_row = rate_rows[at : at + 1, :]
             end = cum_row[:, BLOCK - 1 :]
-            w = mm_left2(solve[c, h] * (rate_row * jnp.exp(cum_row) * unit_rows[c, g]), keys[c, g])
-            u = mm_left2(solve[c, h] * rate_row, value_ref[tokens, h * DV : (h + 1) * DV])
+            w = mm(solve[c, h] * (rate_row * jnp.exp(cum_row) * unit_rows[c, g]), keys[c, g])
+            u = mm(solve[c, h] * rate_row, value_ref[tokens, h * DV : (h + 1) * DV])
             wu = jnp.concatenate([w, u], axis=1)
             wu_ref[h, c] = wu.astype(BF16)
-            tails[c, h] = mm_right2(keys_t[c, g], wu * (jnp.exp(end - cum_col) * unit_cols[c, g]))
+            tails[c, h] = mm(keys_t[c, g], wu * (jnp.exp(end - cum_col) * unit_cols[c, g]))
         for c, h in some:
             at = c * heads + h
             kept = jnp.exp(cum_rows[at : at + 1, BLOCK - 1 :])
@@ -309,35 +300,39 @@
 
 def project_kernel(keep_ref, got_ref, own_ref, sib_ref, *out_refs):
     places, rows, depth = keep_ref.shape
-    part, width = out_refs[0].shape
+    width = out_refs[0].shape[1]
     tile = 512
     for lead in range(0, width, tile):
         lanes = slice(lead, lead + tile)
         product = jnp.dot(
             keep_ref[...].reshape(-1, depth), own_ref[:, lanes], preferred_element_type=F32
         ) + jnp.dot(got_ref[...].reshape(-1, depth), sib_ref[:, lanes], preferred_element_type=F32)
-        for number, out_ref in enumerate(out_refs):
-            start = number % places * rows + number // places * part
-            out_ref[:, lanes] = product[start : start + part].astype(BF16)
-
-
-def project(keep, got, own, sib):
+        start = 0
+        for lead_ref in range(0, len(out_refs), places):
+            part = out_refs[lead_ref].shape[0]
+            for d in range(places):
+                at = d * rows + start
+                out_refs[lead_ref + d][:, lanes] = product[at : at + part].astype(BF16)
+            start += part
+
+
+def project(keep, got, own, sib, sizes):
     places, rows, _ = keep.shape
     outs = resident(
         project_kernel,
-        (shape((rows // CHUNKS, own.shape[1]), BF16),) * (places * CHUNKS),
+        [shape((size, own.shape[1]), BF16) for size in sizes for _ in range(places)],
         keep,
         got,
         own,
         sib,
     )
-    return [outs[c * places : (c + 1) * places] for c in range(CHUNKS)]
-
-
-def norm_kernel(chunk, hidden_ref, gain_ref, routes_ref, *refs):
+    return [outs[c * places : (c + 1) * places] for c in range(len(sizes))]
+
+
+def norm_kernel(start, hidden_ref, gain_ref, routes_ref, *refs):
     *part_refs, residual_ref, out_ref = refs
     rows = residual_ref.shape[0]
-    tokens = slice(chunk * rows, (chunk + 1) * rows)
+    tokens = slice(start, start + rows)
     residual = hidden_ref[tokens, :].astype(F32)
     for part_ref in part_refs:
         residual += part_ref[:, : residual.shape[1]].astype(F32)
@@ -501,17 +496,18 @@
     )
     got = lax.ppermute(send, "exp", swap)
     spot = jnp.stack([place, core])
-    rows = tok // CHUNKS
-    chunks, joined = reduce_places(project(keep, got, out_own, out_sib), SPARE)
+    sizes = SIZES if sum(SIZES) == tok else (tok // 2, tok // 2)
+    starts = [sum(sizes[:i]) for i in range(len(sizes))]
+    chunks, joined = reduce_places(project(keep, got, out_own, out_sib, sizes), SPARE)
     sib = fetch(*(after(w, joined) for w in sib))
     chunks[0][0] = after(chunks[0][0], *sib)
     residuals, slots = [], []
     for chunk, summands in enumerate(chunks):
         if slots:
-            summands[0] = after(summands[0], slots[-1][1])
+            summands[0] = after(summands[0], *slots[-1][1:3])
         kept, sent = resident(
-            functools.partial(norm_kernel, chunk),
-            (shape((rows, width), F32), shape((rows, width + LANES), BF16)),
+            functools.partial(norm_kernel, starts[chunk]),
+            (shape((sizes[chunk], width), F32), shape((sizes[chunk], width + LANES), BF16)),
             hidden_in,
             post_gain.reshape(1, width),
             routes,

time: 93.9 us -> 91.3 us (0.972)
  Pallas kernels: 25.5 us -> 22.9 us
  starting transfers between devices: 32.6 us -> 33.6 us
  waiting for transfers between devices: 31.7 us -> 30.7 us
    pallas_call x2, Pallas kernels: 12.6 us -> 10.1 us  [call(): pl.pallas_call(kernel, grid=(1,), out_shape=tuple(outs), in_specs=([] if...]
  transfers between devices with their start and end apart: 26 -> 26, of which waited for: 13 -> 13; matrix products, arithmetic and copies ran while one was open for 0% -> 0% of each run, Pallas kernels for 24% -> 22%
where the time goes in v4:
time: 91.3 us; the launch traced here: 91.1 us
  starting transfers between devices  33.6 us (37%)
  waiting for transfers between devices  30.7 us (34%)
  Pallas kernels  22.9 us (25%)
  local copies, waits for them, and re-layouts  2.51 us (3%)
  other arithmetic  1.14 us (1%)
    ppermute x18, starting transfers between devices, exchange(): lax.ppermute(piece, 'exp', between_places(lax.axis_size('exp') // 2, d))  27.2 us
    ppermute x18, waiting for transfers between devices, exchange(): lax.ppermute(piece, 'exp', between_places(lax.axis_size('exp') // 2, d))  24.9 us
    pallas_call x2, Pallas kernels, call(): pl.pallas_call(kernel, grid=(1,), out_shape=tuple(outs), in_specs=([] if...  10.1 us
    pallas_call x6, Pallas kernels, resident(): pl.pallas_call(kernel, out_shape=tuple(outs), in_specs=([] if scalars is...  8.34 us
    ppermute x3, starting transfers between devices, per_device(): lax.ppermute(total, 'seq', [(i, i ^ d) for i in range(seqs)])  5.32 us
    pallas_call x2, Pallas kernels, fetch(): pl.pallas_call(fetch_kernel, out_shape=tuple((shape(a.shape, a.dtype) for...  4.51 us
    ppermute x3, waiting for transfers between devices, per_device(): lax.ppermute(total, 'seq', [(i, i ^ d) for i in range(seqs)])  4.24 us
    unnamed x30, local copies, waits for them, and re-layouts  2.5 us
  transfers between devices with their start and end apart: 26, of which 13 were waited for; matrix products, arithmetic and copies ran while one was open for 0% of the time, Pallas kernels for 22%

profile of v4, /device:TPU:0, one launch (start us, length us, event | category | flops | bytes accessed | tf_op | source)
XLA Modules:
  0.0 91.1 jit_solution(16590583784428036275)
XLA Ops:
  0.0 0.5 collective-permute-start
  0.5 0.5 collective-permute-start.5
  1.0 0.1 pad_add_fusion.spot_ref
  1.1 7.5 %shard_map.145 = (bf16[4,4,128,256]{3,2,1,0:T(8,128)(2,1)}, bf16[4,4,128,256]{3,2,1,0:T(8,128)(2,1)}, bf16[4,128,256]{2,1,0:T(8,128)(2,1)}) custom-call(bf16[512,256]{1,0:T(8,128)(2,1)} %key_ref.3, bf16[512,512]{1,0:T(8,128)(2,1)} %value_ref.1, f32[4,512]{1,0:T(4,128)} %decay_ref.3, f32[4,512]{1,0:T(4,128)} %rate_ref.1), custom_call_target="tpu_custom_call" | custom-call | flops 10000000000 | bytes 3162112 | tf_op jit(solution)/shard_map/pallas_call | solution.py:79
  8.6 2.9 %collective-permute-start.1 = (bf16[4,128,256]{2,1,0:T(8,128)(2,1)}, bf16[4,128,256]{2,1,0:T(8,128)(2,1)S(1)}, u32[]{:S(2)}, u32[]{:S(2)}) collective-permute-start(bf16[4,128,256]{2,1,0:T(8,128)(2,1)} %get-tuple-element.72), channel_id=1, source_target_pairs={{0,8},{8,0},{16,24},{24,16},{1,9},{9,1},{17,25},{25,17},{2,10},{10... | collective-permute-start | bytes 786440 | tf_op jit(solution)/shard_map/ppermute | solution.py:478
  11.5 1.5 %collective-permute-start.2 = (bf16[4,128,256]{2,1,0:T(8,128)(2,1)}, bf16[4,128,256]{2,1,0:T(8,128)(2,1)S(1)}, u32[]{:S(2)}, u32[]{:S(2)}) collective-permute-start(bf16[4,128,256]{2,1,0:T(8,128)(2,1)} %get-tuple-element.72), channel_id=1, source_target_pairs={{0,16},{8,24},{16,0},{24,8},{1,17},{9,25},{17,1},{25,9},{2,18},{10... | collective-permute-start | bytes 786440 | tf_op jit(solution)/shard_map/ppermute | solution.py:478
  13.0 0.9 collective-permute-start.3
  13.9 1.2 %copy-done.13 = bf16[4,4,128,256]{3,2,1,0:T(8,128)(2,1)S(1)} copy-done((bf16[4,4,128,256]{3,2,1,0:T(8,128)(2,1)S(1)}, bf16[4,4,128,256]{3,2,1,0:T(8,128)(2,1)}, u32[]{:S(2)}) %copy-start.13) | copy-done | bytes 1048600
  15.2 1.2 %copy-done.14 = bf16[4,4,128,256]{3,2,1,0:T(8,128)(2,1)S(1)} copy-done((bf16[4,4,128,256]{3,2,1,0:T(8,128)(2,1)S(1)}, bf16[4,4,128,256]{3,2,1,0:T(8,128)(2,1)}, u32[]{:S(2)}) %copy-start.14) | copy-done | bytes 1048600
  16.4 2.6 %shard_map.146 = (bf16[512,512]{1,0:T(8,128)(2,1)S(1)}, f32[512,512]{1,0:T(8,128)S(1)}, bf16[64,128]{1,0:T(8,128)(2,1)S(1)}) custom-call(bf16[512,256]{1,0:T(8,128)(2,1)S(1)} %copy-done.7, bf16[512,256]{1,0:T(8,128)(2,1)S(1)} %copy-done.8, f32[4,512]{1,0:T(4,128)S(1)} %copy-done.9, s32[4,64]{1,0:T(4,128)S(1)} %bitcast.9, bf16[4,64]{1,0:T(4,128)(2,1)S(1)} %bitcast.10, ...), custom_call_target="tpu_custom_call" | custom-call | flops 4000000000 | bytes 4220416 | tf_op jit(solution)/shard_map/pallas_call | solution.py:79
  19.0 2.0 %shard_map.147 = (bf16[512,512]{1,0:T(8,128)(2,1)S(1)}, bf16[512,2048]{1,0:T(8,128)(2,1)S(1)}, bf16[512,2048]{1,0:T(8,128)(2,1)S(1)}) custom-call(bf16[512,512]{1,0:T(8,128)(2,1)S(1)} %copy-done.5, bf16[512,2048]{1,0:T(8,128)(2,1)S(1)} %copy-done.3, bf16[512,2048]{1,0:T(8,128)(2,1)} %collective-permute-done.refs_2_), custom_call_target="tpu_custom_call" | custom-call | bytes 9437184 | tf_op jit(solution)/shard_map/pallas_call | solution.py:46
  21.1 4.2 %collective-permute-done.2.refs_1_ = bf16[4,128,256]{2,1,0:T(8,128)(2,1)S(1)} collective-permute-done((bf16[4,128,256]{2,1,0:T(8,128)(2,1)}, bf16[4,128,256]{2,1,0:T(8,128)(2,1)S(1)}, u32[]{:S(2)}, u32[]{:S(2)}) %collective-permute-start.2) | collective-permute-done | bytes 262176 | tf_op jit(solution)/shard_map/ppermute | solution.py:478
  25.3 1.8 %shard_map.148 = (bf16[4,64,512]{2,1,0:T(8,128)(2,1)S(1)}, bf16[4,64,512]{2,1,0:T(8,128)(2,1)S(1)}) custom-call(s32[3]{0:T(128)S(1)} %pad_add_fusion.spot_ref, f32[1,128]{1,0:T(1,128)S(1)} %bitcast.11, bf16[512,512]{1,0:T(8,128)(2,1)S(1)} %get-tuple-element.77.gate_ref, bf16[512,512]{1,0:T(8,128)(2,1)S(1)} %get-tuple-element.78.lin_ref, ...), custom_call_target="tpu_custom_call" | custom-call | flops 1000000000 | bytes 3408384 | tf_op jit(solution)/shard_map/pallas_call | solution.py:61
  27.1 1.5 %collective-permute-done.7.got_ref = bf16[4,64,512]{2,1,0:T(8,128)(2,1)S(1)} collective-permute-done((bf16[4,64,512]{2,1,0:T(8,128)(2,1)S(1)}, bf16[4,64,512]{2,1,0:T(8,128)(2,1)S(1)}, u32[]{:S(2)}, u32[]{:S(2)}) %collective-permute-start.7) | collective-permute-done | bytes 262176 | tf_op jit(solution)/shard_map/ppermute | solution.py:497
  28.7 1.2 %shard_map.149 = (bf16[32,2048]{1,0:T(8,128)(2,1)S(1)}, bf16[32,2048]{1,0:T(8,128)(2,1)S(1)}, bf16[32,2048]{1,0:T(8,128)(2,1)S(1)}, bf16[32,2048]{1,0:T(8,128)(2...) custom-call(bf16[4,64,512]{2,1,0:T(8,128)(2,1)S(1)} %get-tuple-eleme, ...), custom_call_target="tpu_custom_call" | custom-call | bytes 5767168 | tf_op jit(solution)/shard_map/pallas_call | solution.py:61
  29.9 1.6 %collective-permute-start.9 = (bf16[32,2048]{1,0:T(8,128)(2,1)S(1)}, bf16[32,2048]{1,0:T(8,128)(2,1)S(1)}, u32[]{:S(2)}, u32[]{:S(2)}) collective-permute-start(bf16[32,2048]{1,0:T(8,128)(2,1)S(1)} %get-tuple-element.91), channel_id=1, source_target_pairs={{0,2},{1,3},{2,0},{3,1},{4,6},{5,7},{6,4},{7,5},{8,10},{9,11},{10,... | collective-permute-start | bytes 393224 | tf_op jit(solution)/shard_map/ppermute | solution.py:390
  31.5 0.5 collective-permute-start.8
  32.0 4.3 %collective-permute-done.9 = bf16[32,2048]{1,0:T(8,128)(2,1)S(1)} collective-permute-done((bf16[32,2048]{1,0:T(8,128)(2,1)S(1)}, bf16[32,2048]{1,0:T(8,128)(2,1)S(1)}, u32[]{:S(2)}, u32[]{:S(2)}) %collective-permute-start.9) | collective-permute-done | bytes 131104 | tf_op jit(solution)/shard_map/ppermute | solution.py:390
  36.4 2.6 %collective-permute-start.10 = (bf16[32,2048]{1,0:T(8,128)(2,1)S(1)}, bf16[32,2048]{1,0:T(8,128)(2,1)S(1)}, u32[]{:S(2)}, u32[]{:S(2)}) collective-permute-start(bf16[32,2048]{1,0:T(8,128)(2,1)S(1)} %add_convert_fusion.5), channel_id=1, source_target_pairs={{0,4},{1,5},{2,6},{3,7},{4,0},{5,1},{6,2},{7,3},{8,12},{9,13},{10,... | collective-permute-start | bytes 393224 | tf_op jit(solution)/shard_map/ppermute | solution.py:390
  39.0 1.6 %collective-permute-start.11 = (bf16[32,2048]{1,0:T(8,128)(2,1)S(1)}, bf16[32,2048]{1,0:T(8,128)(2,1)S(1)}, u32[]{:S(2)}, u32[]{:S(2)}) collective-permute-start(bf16[32,2048]{1,0:T(8,128)(2,1)S(1)} %get-tuple-element.105), channel_id=1, source_target_pairs={{0,2},{1,3},{2,0},{3,1},{4,6},{5,7},{6,4},{7,5},{8,10},{9,11},{10,... | collective-permute-start | bytes 393224 | tf_op jit(solution)/shard_map/ppermute | solution.py:390
  40.6 2.0 %collective-permute-start.14 = (bf16[32,2304]{1,0:T(8,128)(2,1)S(1)}, bf16[32,2304]{1,0:T(8,128)(2,1)S(1)}, u32[]{:S(2)}, u32[]{:S(2)}) collective-permute-start(bf16[32,2304]{1,0:T(8,128)(2,1)S(1)} %pad.4), channel_id=1, source_target_pairs={{0,4},{1,5},{2,6},{3,7},{4,0},{5,1},{6,2},{7,3},{8,12},{9,13},{10,... | collective-permute-start | bytes 442376 | tf_op jit(solution)/shard_map/ppermute | solution.py:390
  42.6 2.5 %shard_map.150 = (bf16[1,2048,512]{2,1,0:T(8,128)(2,1)S(1)}, bf16[1,2048,512]{2,1,0:T(8,128)(2,1)S(1)}, bf16[1,512,2048]{2,1,0:T(8,128)(2,1)S(1)}) custom-call(bf16[1,2048,512]{2,1,0:T(8,128)(2,1)S(1)} %collective-permute-done.4.refs_0_, bf16[1,2048,512]{2,1,0:T(8,128)(2,1)} %collective-permute-done.5.refs_1_, ...), custom_call_target="tpu_custom_call" | custom-call | bytes 12582912 | tf_op jit(solution)/shard_map/pallas_call | solution.py:46
  45.2 0.8 collective-permute-done.10.refs_1_
  46.0 0.2 shard_map.151
  46.2 1.9 %collective-permute-start.12 = (bf16[32,2176]{1,0:T(8,128)(2,1)S(1)}, bf16[32,2176]{1,0:T(8,128)(2,1)S(1)}, u32[]{:S(2)}, u32[]{:S(2)}) collective-permute-start(bf16[32,2176]{1,0:T(8,128)(2,1)S(1)} %get-tuple-element.107.refs_0_), channel_id=1, source_target_pairs={{0,2},{1,3},{2,0},{3,1},{4,6},{5,7},{6,4},{7,5},{8,10},{9,11},{10,... | collective-permute-start | bytes 417800 | tf_op jit(solution)/shard_map/ppermute | solution.py:390
  48.1 3.9 %collective-permute-start.13 = (bf16[32,2176]{1,0:T(8,128)(2,1)S(1)}, bf16[32,2176]{1,0:T(8,128)(2,1)S(1)}, u32[]{:S(2)}, u32[]{:S(2)}) collective-permute-start(bf16[32,2176]{1,0:T(8,128)(2,1)S(1)} %get-tuple-element.107.refs_0_), channel_id=1, source_target_pairs={{0,4},{1,5},{2,6},{3,7},{4,0},{5,1},{6,2},{7,3},{8,12},{9,13},{10,... | collective-permute-start | bytes 417800 | tf_op jit(solution)/shard_map/ppermute | solution.py:390
  51.9 0.1 collective-permute-start.15
  52.0 4.6 %collective-permute-done.12.refs_1_ = bf16[32,2176]{1,0:T(8,128)(2,1)S(1)} collective-permute-done((bf16[32,2176]{1,0:T(8,128)(2,1)S(1)}, bf16[32,2176]{1,0:T(8,128)(2,1)S(1)}, u32[]{:S(2)}, u32[]{:S(2)}) %collective-permute-start.12) | collective-permute-done | bytes 139296 | tf_op jit(solution)/shard_map/ppermute | solution.py:390
  56.6 1.4 %collective-permute-done.15.refs_2_ = bf16[32,2048]{1,0:T(8,128)(2,1)S(1)} collective-permute-done((bf16[32,2048]{1,0:T(8,128)(2,1)S(1)}, bf16[32,2048]{1,0:T(8,128)(2,1)S(1)}, u32[]{:S(2)}, u32[]{:S(2)}) %collective-permute-start.15) | collective-permute-done | bytes 131104 | tf_op jit(solution)/shard_map/ppermute | solution.py:390
  58.0 0.2 shard_map.152
  58.2 1.7 %collective-permute-start.18 = (bf16[32,2176]{1,0:T(8,128)(2,1)S(1)}, bf16[32,2176]{1,0:T(8,128)(2,1)S(1)}, u32[]{:S(2)}, u32[]{:S(2)}) collective-permute-start(bf16[32,2176]{1,0:T(8,128)(2,1)S(1)} %get-tuple-element.116.refs_0_), channel_id=1, source_target_pairs={{0,4},{1,5},{2,6},{3,7},{4,0},{5,1},{6,2},{7,3},{8,12},{9,13},{10,... | collective-permute-start | bytes 417800 | tf_op jit(solution)/shard_map/ppermute | solution.py:390
  59.9 2.5 %collective-permute-start.16 = (bf16[32,2176]{1,0:T(8,128)(2,1)S(1)}, bf16[32,2176]{1,0:T(8,128)(2,1)S(1)}, u32[]{:S(2)}, u32[]{:S(2)}) collective-permute-start(bf16[32,2176]{1,0:T(8,128)(2,1)S(1)} %collective-permute-done.13.refs_2_), channel_id=1, source_target_pairs={{0,2},{1,3},{2,0},{3,1},{4,6},{5,7},{6,4},{7,5},{8,10},{9,11},{10,... | collective-permute-start | bytes 417800 | tf_op jit(solution)/shard_map/ppermute | solution.py:390
  62.5 2.6 %collective-permute-done.18.refs_2_ = bf16[32,2176]{1,0:T(8,128)(2,1)S(1)} collective-permute-done((bf16[32,2176]{1,0:T(8,128)(2,1)S(1)}, bf16[32,2176]{1,0:T(8,128)(2,1)S(1)}, u32[]{:S(2)}, u32[]{:S(2)}) %collective-permute-start.18) | collective-permute-done | bytes 139296 | tf_op jit(solution)/shard_map/ppermute | solution.py:390
  65.0 1.9 %collective-permute-start.19 = (bf16[32,2176]{1,0:T(8,128)(2,1)S(1)}, bf16[32,2176]{1,0:T(8,128)(2,1)S(1)}, u32[]{:S(2)}, u32[]{:S(2)}) collective-permute-start(bf16[32,2176]{1,0:T(8,128)(2,1)S(1)} %collective-permute-done.18.refs_2_), channel_id=1, source_target_pairs={{0,2},{1,3},{2,0},{3,1},{4,6},{5,7},{6,4},{7,5},{8,10},{9,11},{10,... | collective-permute-start | bytes 417800 | tf_op jit(solution)/shard_map/ppermute | solution.py:390
  67.0 0.6 collective-permute-done.16.refs_3_
  67.5 2.5 %shard_map.153 = (bf16[32,2048]{1,0:T(8,128)(2,1)S(1)}, bf16[32,2048]{1,0:T(8,128)(2,1)S(1)}, bf16[32,2048]{1,0:T(8,128)(2,1)S(1)}, bf16[32,2048]{1,0:T(8,128)(2,1)S(1)}) custom-call(s32[2]{0:T(128)S(1)} %pad_add_fusion.1.spot_ref, bf16[32,2176]{1,0:T(8,128)(2,1)S(1)} %get-tuple-element.107.refs_0_, bf16[32,2176]{1,0:T(8,128)(2,1)S(1)} %collective-permute-done.12.refs_1_, ...), custom_call_target="tpu_custom_call" | custom-call | flops 3000000000 | bytes 13664256 | tf_op jit(solution)/shard_map/pallas_call | solution.py:61
  70.1 1.3 %collective-permute-start.21 = (bf16[32,2048]{1,0:T(8,128)(2,1)S(1)}, bf16[32,2048]{1,0:T(8,128)(2,1)S(1)}, u32[]{:S(2)}, u32[]{:S(2)}) collective-permute-start(bf16[32,2048]{1,0:T(8,128)(2,1)S(1)} %get-tuple-element.121), channel_id=1, source_target_pairs={{0,2},{1,3},{2,0},{3,1},{4,6},{5,7},{6,4},{7,5},{8,10},{9,11},{10,... | collective-permute-start | bytes 393224 | tf_op jit(solution)/shard_map/ppermute | solution.py:390
  71.4 1.6 %collective-permute-done.19.refs_3_ = bf16[32,2176]{1,0:T(8,128)(2,1)S(1)} collective-permute-done((bf16[32,2176]{1,0:T(8,128)(2,1)S(1)}, bf16[32,2176]{1,0:T(8,128)(2,1)S(1)}, u32[]{:S(2)}, u32[]{:S(2)}) %collective-permute-start.19) | collective-permute-done | bytes 139296 | tf_op jit(solution)/shard_map/ppermute | solution.py:390
  73.0 2.5 %shard_map.154 = (bf16[32,2048]{1,0:T(8,128)(2,1)S(1)}, bf16[32,2048]{1,0:T(8,128)(2,1)S(1)}, bf16[32,2048]{1,0:T(8,128)(2,1)S(1)}, bf16[32,2048]{1,0:T(8,128)(2,1)S(1)}) custom-call(s32[2]{0:T(128)S(1)} %pad_add_fusion.1.spot_ref, bf16[32,2176]{1,0:T(8,128)(2,1)S(1)} %get-tuple-element.116.refs_0_, bf16[32,2176]{1,0:T(8,128)(2,1)S(1)} %collective-permute-done.17.refs_1_, ...), custom_call_target="tpu_custom_call" | custom-call | flops 3000000000 | bytes 13664256 | tf_op jit(solution)/shard_map/pallas_call | solution.py:61
  75.5 0.3 collective-permute-start.20
  75.8 2.9 %collective-permute-start.22 = (bf16[32,2048]{1,0:T(8,128)(2,1)S(1)}, bf16[32,2048]{1,0:T(8,128)(2,1)S(1)}, u32[]{:S(2)}, u32[]{:S(2)}) collective-permute-start(bf16[32,2048]{1,0:T(8,128)(2,1)S(1)} %add_convert_fusion.3), channel_id=1, source_target_pairs={{0,4},{1,5},{2,6},{3,7},{4,0},{5,1},{6,2},{7,3},{8,12},{9,13},{10,... | collective-permute-start | bytes 393224 | tf_op jit(solution)/shard_map/ppermute | solution.py:390
  78.8 4.2 %collective-permute-done.20 = bf16[32,2048]{1,0:T(8,128)(2,1)S(1)} collective-permute-done((bf16[32,2048]{1,0:T(8,128)(2,1)S(1)}, bf16[32,2048]{1,0:T(8,128)(2,1)S(1)}, u32[]{:S(2)}, u32[]{:S(2)}) %collective-permute-start.20) | collective-permute-done | bytes 131104 | tf_op jit(solution)/shard_map/ppermute | solution.py:390
  83.0 0.2 collective-permute-start.24
  83.2 2.1 %collective-permute-start.25 = (bf16[32,2048]{1,0:T(8,128)(2,1)S(1)}, bf16[32,2048]{1,0:T(8,128)(2,1)S(1)}, u32[]{:S(2)}, u32[]{:S(2)}) collective-permute-start(bf16[32,2048]{1,0:T(8,128)(2,1)S(1)} %get-tuple-element.130), channel_id=1, source_target_pairs={{0,2},{1,3},{2,0},{3,1},{4,6},{5,7},{6,4},{7,5},{8,10},{9,11},{10,... | collective-permute-start | bytes 393224 | tf_op jit(solution)/shard_map/ppermute | solution.py:390
  85.3 1.0 %collective-permute-done.23 = bf16[32,2048]{1,0:T(8,128)(2,1)S(1)} collective-permute-done((bf16[32,2048]{1,0:T(8,128)(2,1)S(1)}, bf16[32,2048]{1,0:T(8,128)(2,1)S(1)}, u32[]{:S(2)}, u32[]{:S(2)}) %collective-permute-start.23) | collective-permute-done | bytes 131104 | tf_op jit(solution)/shard_map/ppermute | solution.py:390
  86.4 2.4 %collective-permute-done.25 = bf16[32,2048]{1,0:T(8,128)(2,1)S(1)} collective-permute-done((bf16[32,2048]{1,0:T(8,128)(2,1)S(1)}, bf16[32,2048]{1,0:T(8,128)(2,1)S(1)}, u32[]{:S(2)}, u32[]{:S(2)}) %collective-permute-start.25) | collective-permute-done | bytes 131104 | tf_op jit(solution)/shard_map/ppermute | solution.py:390
  88.8 1.5 %collective-permute-done.24 = bf16[32,2048]{1,0:T(8,128)(2,1)S(1)} collective-permute-done((bf16[32,2048]{1,0:T(8,128)(2,1)S(1)}, bf16[32,2048]{1,0:T(8,128)(2,1)S(1)}, u32[]{:S(2)}, u32[]{:S(2)}) %collective-permute-start.24) | collective-permute-done | bytes 131104 | tf_op jit(solution)/shard_map/ppermute | solution.py:390
  90.4 0.7 pad_maximum_fusion
  (54 shorter events, 0.7 us)
Async XLA Ops:
  0.0 8.6 %collective-permute-start = (bf16[512,2048]{1,0:T(8,128)(2,1)}, bf16[512,2048]{1,0:T(8,128)(2,1)}, u32[]{:S(2)}, u32[]{:S(2)}) collective-permute-start(bf16[512,2048]{1,0:T(8,128)(2,1)} %refs_1_.1), channel_id=1, source_target_pairs={{0,1},{1,0},{2,3},{3,2},{4,5},{5,4},{6,7},{7,6},{8,9},{9,8},{10,11... | collective-permute-start | bytes 6291464 | tf_op jit(solution)/shard_map/ppermute | solution.py:443
  0.5 12.6 %collective-permute-start.4 = (bf16[1,2048,512]{2,1,0:T(8,128)(2,1)}, bf16[1,2048,512]{2,1,0:T(8,128)(2,1)S(1)}, u32[]{:S(2)}, u32[]{:S(2)}) collective-permute-start(bf16[1,2048,512]{2,1,0:T(8,128)(2,1)} %refs_4_.3), channel_id=1, source_target_pairs={{0,1},{1,0},{2,3},{3,2},{4,5},{5,4},{6,7},{7,6},{8,9},{9,8},{10,11... | collective-permute-start | bytes 6291464 | tf_op jit(solution)/shard_map/ppermute | solution.py:445
  0.5 20.5 %collective-permute-start.5 = (bf16[1,2048,512]{2,1,0:T(8,128)(2,1)}, bf16[1,2048,512]{2,1,0:T(8,128)(2,1)}, u32[]{:S(2)}, u32[]{:S(2)}) collective-permute-start(bf16[1,2048,512]{2,1,0:T(8,128)(2,1)} %refs_5_.3), channel_id=1, source_target_pairs={{0,1},{1,0},{2,3},{3,2},{4,5},{5,4},{6,7},{7,6},{8,9},{9,8},{10,11... | collective-permute-start | bytes 6291464 | tf_op jit(solution)/shard_map/ppermute | solution.py:445
  1.0 20.1 %collective-permute-start.6 = (bf16[1,512,2048]{2,1,0:T(8,128)(2,1)}, bf16[1,512,2048]{2,1,0:T(8,128)(2,1)}, u32[]{:S(2)}, u32[]{:S(2)}) collective-permute-start(bf16[1,512,2048]{2,1,0:T(8,128)(2,1)} %refs_6_.3), channel_id=1, source_target_pairs={{0,1},{1,0},{2,3},{3,2},{4,5},{5,4},{6,7},{7,6},{8,9},{9,8},{10,11... | collective-permute-start | bytes 6291464 | tf_op jit(solution)/shard_map/ppermute | solution.py:445
  1.1 12.8 %copy-start.7 = (bf16[512,256]{1,0:T(8,128)(2,1)S(1)}, bf16[512,256]{1,0:T(8,128)(2,1)}, u32[]{:S(2)}) copy-start(bf16[512,256]{1,0:T(8,128)(2,1)} %query_ref.1) | copy-start | bytes 786436
  1.1 12.8 %copy-start.8 = (bf16[512,256]{1,0:T(8,128)(2,1)S(1)}, bf16[512,256]{1,0:T(8,128)(2,1)}, u32[]{:S(2)}) copy-start(bf16[512,256]{1,0:T(8,128)(2,1)} %key_ref.3) | copy-start | bytes 786436
  1.1 12.8 %copy-start.9 = (f32[4,512]{1,0:T(4,128)S(1)}, f32[4,512]{1,0:T(4,128)}, u32[]{:S(2)}) copy-start(f32[4,512]{1,0:T(4,128)} %decay_ref.3) | copy-start | bytes 24580
  1.1 12.8 %copy-start.10 = (s32[64,4]{0,1:T(4,128)S(1)}, s32[64,4]{0,1:T(4,128)}, u32[]{:S(2)}) copy-start(s32[64,4]{0,1:T(4,128)} %param.25) | copy-start | bytes 3076
  1.1 12.8 %copy-start.11 = (bf16[64,4]{0,1:T(4,128)(2,1)S(1)}, bf16[64,4]{0,1:T(4,128)(2,1)}, u32[]{:S(2)}) copy-start(bf16[64,4]{0,1:T(4,128)(2,1)} %param.26) | copy-start | bytes 1540
  8.6 12.5 %collective-permute-start.1 = (bf16[4,128,256]{2,1,0:T(8,128)(2,1)}, bf16[4,128,256]{2,1,0:T(8,128)(2,1)S(1)}, u32[]{:S(2)}, u32[]{:S(2)}) collective-permute-start(bf16[4,128,256]{2,1,0:T(8,128)(2,1)} %get-tuple-element.72), channel_id=1, source_target_pairs={{0,8},{8,0},{16,24},{24,16},{1,9},{9,1},{17,25},{25,17},{2,10},{10... | collective-permute-start | bytes 786440 | tf_op jit(solution)/shard_map/ppermute | solution.py:478
  11.5 13.8 %collective-permute-start.2 = (bf16[4,128,256]{2,1,0:T(8,128)(2,1)}, bf16[4,128,256]{2,1,0:T(8,128)(2,1)S(1)}, u32[]{:S(2)}, u32[]{:S(2)}) collective-permute-start(bf16[4,128,256]{2,1,0:T(8,128)(2,1)} %get-tuple-element.72), channel_id=1, source_target_pairs={{0,16},{8,24},{16,0},{24,8},{1,17},{9,25},{17,1},{25,9},{2,18},{10... | collective-permute-start | bytes 786440 | tf_op jit(solution)/shard_map/ppermute | solution.py:478
  13.0 12.2 %collective-permute-start.3 = (bf16[4,128,256]{2,1,0:T(8,128)(2,1)}, bf16[4,128,256]{2,1,0:T(8,128)(2,1)S(1)}, u32[]{:S(2)}, u32[]{:S(2)}) collective-permute-start(bf16[4,128,256]{2,1,0:T(8,128)(2,1)} %get-tuple-element.72), channel_id=1, source_target_pairs={{0,24},{8,16},{16,8},{24,0},{1,25},{9,17},{17,9},{25,1},{2,26},{10... | collective-permute-start | bytes 786440 | tf_op jit(solution)/shard_map/ppermute | solution.py:478
  13.9 1.2 %copy-start.13 = (bf16[4,4,128,256]{3,2,1,0:T(8,128)(2,1)S(1)}, bf16[4,4,128,256]{3,2,1,0:T(8,128)(2,1)}, u32[]{:S(2)}) copy-start(bf16[4,4,128,256]{3,2,1,0:T(8,128)(2,1)} %get-tuple-element.68.wu_ref) | copy-start | bytes 3145732
  15.2 1.2 %copy-start.14 = (bf16[4,4,128,256]{3,2,1,0:T(8,128)(2,1)S(1)}, bf16[4,4,128,256]{3,2,1,0:T(8,128)(2,1)}, u32[]{:S(2)}) copy-start(bf16[4,4,128,256]{3,2,1,0:T(8,128)(2,1)} %get-tuple-element.69.prefix_ref) | copy-start | bytes 3145732
  16.4 2.6 %copy-start.3 = (bf16[512,2048]{1,0:T(8,128)(2,1)S(1)}, bf16[512,2048]{1,0:T(8,128)(2,1)}, u32[]{:S(2)}) copy-start(bf16[512,2048]{1,0:T(8,128)(2,1)} %refs_1_.1) | copy-start | bytes 6291460
  16.4 2.6 %copy-start.5 = (bf16[512,512]{1,0:T(8,128)(2,1)S(1)}, bf16[512,512]{1,0:T(8,128)(2,1)}, u32[]{:S(2)}) copy-start(bf16[512,512]{1,0:T(8,128)(2,1)} %refs_0_.1) | copy-start | bytes 1572868
  19.0 6.3 %copy-start.12 = (f32[128]{0:T(128)S(1)}, f32[128]{0:T(128)}, u32[]{:S(2)}) copy-start(f32[128]{0:T(128)} %param.22) | copy-start | bytes 1540
  27.1 1.6 %collective-permute-start.7 = (bf16[4,64,512]{2,1,0:T(8,128)(2,1)S(1)}, bf16[4,64,512]{2,1,0:T(8,128)(2,1)S(1)}, u32[]{:S(2)}, u32[]{:S(2)}) collective-permute-start(bf16[4,64,512]{2,1,0:T(8,128)(2,1)S(1)} %get-tuple-element.84), channel_id=1, source_target_pairs={{0,1},{1,0},{2,3},{3,2},{4,5},{5,4},{6,7},{7,6},{8,9},{9,8},{10,11... | collective-permute-start | bytes 786440 | tf_op jit(solution)/shard_map/ppermute | solution.py:497
  29.9 6.4 %collective-permute-start.9 = (bf16[32,2048]{1,0:T(8,128)(2,1)S(1)}, bf16[32,2048]{1,0:T(8,128)(2,1)S(1)}, u32[]{:S(2)}, u32[]{:S(2)}) collective-permute-start(bf16[32,2048]{1,0:T(8,128)(2,1)S(1)} %get-tuple-element.91), channel_id=1, source_target_pairs={{0,2},{1,3},{2,0},{3,1},{4,6},{5,7},{6,4},{7,5},{8,10},{9,11},{10,... | collective-permute-start | bytes 393224 | tf_op jit(solution)/shard_map/ppermute | solution.py:390
  31.5 7.5 %collective-permute-start.8 = (bf16[32,2048]{1,0:T(8,128)(2,1)S(1)}, bf16[32,2048]{1,0:T(8,128)(2,1)S(1)}, u32[]{:S(2)}, u32[]{:S(2)}) collective-permute-start(bf16[32,2048]{1,0:T(8,128)(2,1)S(1)} %get-tuple-element.89), channel_id=1, source_target_pairs={{0,2},{1,3},{2,0},{3,1},{4,6},{5,7},{6,4},{7,5},{8,10},{9,11},{10,... | collective-permute-start | bytes 393224 | tf_op jit(solution)/shard_map/ppermute | solution.py:390
  36.3 9.7 %copy-start.4 = (bf16[64,2048]{1,0:T(8,128)(2,1)S(1)}, bf16[64,2048]{1,0:T(8,128)(2,1)}, u32[]{:S(2)}) copy-start(bf16[64,2048]{1,0:T(8,128)(2,1)} %hidden_ref.3) | copy-start | bytes 786436
  36.4 9.6 %collective-permute-start.10 = (bf16[32,2048]{1,0:T(8,128)(2,1)S(1)}, bf16[32,2048]{1,0:T(8,128)(2,1)S(1)}, u32[]{:S(2)}, u32[]{:S(2)}) collective-permute-start(bf16[32,2048]{1,0:T(8,128)(2,1)S(1)} %add_convert_fusion.5), channel_id=1, source_target_pairs={{0,4},{1,5},{2,6},{3,7},{4,0},{5,1},{6,2},{7,3},{8,12},{9,13},{10,... | collective-permute-start | bytes 393224 | tf_op jit(solution)/shard_map/ppermute | solution.py:390
  39.0 7.0 %collective-permute-start.11 = (bf16[32,2048]{1,0:T(8,128)(2,1)S(1)}, bf16[32,2048]{1,0:T(8,128)(2,1)S(1)}, u32[]{:S(2)}, u32[]{:S(2)}) collective-permute-start(bf16[32,2048]{1,0:T(8,128)(2,1)S(1)} %get-tuple-element.105), channel_id=1, source_target_pairs={{0,2},{1,3},{2,0},{3,1},{4,6},{5,7},{6,4},{7,5},{8,10},{9,11},{10,... | collective-permute-start | bytes 393224 | tf_op jit(solution)/shard_map/ppermute | solution.py:390
  40.6 17.4 %collective-permute-start.14 = (bf16[32,2304]{1,0:T(8,128)(2,1)S(1)}, bf16[32,2304]{1,0:T(8,128)(2,1)S(1)}, u32[]{:S(2)}, u32[]{:S(2)}) collective-permute-start(bf16[32,2304]{1,0:T(8,128)(2,1)S(1)} %pad.4), channel_id=1, source_target_pairs={{0,4},{1,5},{2,6},{3,7},{4,0},{5,1},{6,2},{7,3},{8,12},{9,13},{10,... | collective-permute-start | bytes 442376 | tf_op jit(solution)/shard_map/ppermute | solution.py:390
  42.6 3.4 %copy-start.6 = (f32[2048]{0:T(1024)S(1)}, f32[2048]{0:T(1024)}, u32[]{:S(2)}) copy-start(f32[2048]{0:T(1024)} %param.24) | copy-start | bytes 24580
  42.6 24.9 %copy-start = (bf16[1,2048,512]{2,1,0:T(8,128)(2,1)S(1)}, bf16[1,2048,512]{2,1,0:T(8,128)(2,1)}, u32[]{:S(2)}) copy-start(bf16[1,2048,512]{2,1,0:T(8,128)(2,1)} %refs_4_.3) | copy-start | bytes 6291460
  42.6 24.9 %copy-start.1 = (bf16[1,2048,512]{2,1,0:T(8,128)(2,1)S(1)}, bf16[1,2048,512]{2,1,0:T(8,128)(2,1)}, u32[]{:S(2)}) copy-start(bf16[1,2048,512]{2,1,0:T(8,128)(2,1)} %refs_5_.3) | copy-start | bytes 6291460
  42.6 24.9 %copy-start.2 = (bf16[1,512,2048]{2,1,0:T(8,128)(2,1)S(1)}, bf16[1,512,2048]{2,1,0:T(8,128)(2,1)}, u32[]{:S(2)}) copy-start(bf16[1,512,2048]{2,1,0:T(8,128)(2,1)} %refs_6_.3) | copy-start | bytes 6291460
  46.2 10.5 %collective-permute-start.12 = (bf16[32,2176]{1,0:T(8,128)(2,1)S(1)}, bf16[32,2176]{1,0:T(8,128)(2,1)S(1)}, u32[]{:S(2)}, u32[]{:S(2)}) collective-permute-start(bf16[32,2176]{1,0:T(8,128)(2,1)S(1)} %get-tuple-element.107.refs_0_), channel_id=1, source_target_pairs={{0,2},{1,3},{2,0},{3,1},{4,6},{5,7},{6,4},{7,5},{8,10},{9,11},{10,... | collective-permute-start | bytes 417800 | tf_op jit(solution)/shard_map/ppermute | solution.py:390
  48.1 8.6 %collective-permute-start.13 = (bf16[32,2176]{1,0:T(8,128)(2,1)S(1)}, bf16[32,2176]{1,0:T(8,128)(2,1)S(1)}, u32[]{:S(2)}, u32[]{:S(2)}) collective-permute-start(bf16[32,2176]{1,0:T(8,128)(2,1)S(1)} %get-tuple-element.107.refs_0_), channel_id=1, source_target_pairs={{0,4},{1,5},{2,6},{3,7},{4,0},{5,1},{6,2},{7,3},{8,12},{9,13},{10,... | collective-permute-start | bytes 417800 | tf_op jit(solution)/shard_map/ppermute | solution.py:390
  51.9 6.1 %collective-permute-start.15 = (bf16[32,2048]{1,0:T(8,128)(2,1)S(1)}, bf16[32,2048]{1,0:T(8,128)(2,1)S(1)}, u32[]{:S(2)}, u32[]{:S(2)}) collective-permute-start(bf16[32,2048]{1,0:T(8,128)(2,1)S(1)} %get-tuple-element.112), channel_id=1, source_target_pairs={{0,2},{1,3},{2,0},{3,1},{4,6},{5,7},{6,4},{7,5},{8,10},{9,11},{10,... | collective-permute-start | bytes 393224 | tf_op jit(solution)/shard_map/ppermute | solution.py:390
  58.2 6.8 %collective-permute-start.18 = (bf16[32,2176]{1,0:T(8,128)(2,1)S(1)}, bf16[32,2176]{1,0:T(8,128)(2,1)S(1)}, u32[]{:S(2)}, u32[]{:S(2)}) collective-permute-start(bf16[32,2176]{1,0:T(8,128)(2,1)S(1)} %get-tuple-element.116.refs_0_), channel_id=1, source_target_pairs={{0,4},{1,5},{2,6},{3,7},{4,0},{5,1},{6,2},{7,3},{8,12},{9,13},{10,... | collective-permute-start | bytes 417800 | tf_op jit(solution)/shard_map/ppermute | solution.py:390
  59.9 7.6 %collective-permute-start.16 = (bf16[32,2176]{1,0:T(8,128)(2,1)S(1)}, bf16[32,2176]{1,0:T(8,128)(2,1)S(1)}, u32[]{:S(2)}, u32[]{:S(2)}) collective-permute-start(bf16[32,2176]{1,0:T(8,128)(2,1)S(1)} %collective-permute-done.13.refs_2_), channel_id=1, source_target_pairs={{0,2},{1,3},{2,0},{3,1},{4,6},{5,7},{6,4},{7,5},{8,10},{9,11},{10,... | collective-permute-start | bytes 417800 | tf_op jit(solution)/shard_map/ppermute | solution.py:390
  62.5 8.9 %collective-permute-start.17 = (bf16[32,2176]{1,0:T(8,128)(2,1)S(1)}, bf16[32,2176]{1,0:T(8,128)(2,1)S(1)}, u32[]{:S(2)}, u32[]{:S(2)}) collective-permute-start(bf16[32,2176]{1,0:T(8,128)(2,1)S(1)} %get-tuple-element.116.refs_0_), channel_id=1, source_target_pairs={{0,2},{1,3},{2,0},{3,1},{4,6},{5,7},{6,4},{7,5},{8,10},{9,11},{10,... | collective-permute-start | bytes 417800 | tf_op jit(solution)/shard_map/ppermute | solution.py:390
  65.0 7.9 %collective-permute-start.19 = (bf16[32,2176]{1,0:T(8,128)(2,1)S(1)}, bf16[32,2176]{1,0:T(8,128)(2,1)S(1)}, u32[]{:S(2)}, u32[]{:S(2)}) collective-permute-start(bf16[32,2176]{1,0:T(8,128)(2,1)S(1)} %collective-permute-done.18.refs_2_), channel_id=1, source_target_pairs={{0,2},{1,3},{2,0},{3,1},{4,6},{5,7},{6,4},{7,5},{8,10},{9,11},{10,... | collective-permute-start | bytes 417800 | tf_op jit(solution)/shard_map/ppermute | solution.py:390
  70.1 5.7 %collective-permute-start.21 = (bf16[32,2048]{1,0:T(8,128)(2,1)S(1)}, bf16[32,2048]{1,0:T(8,128)(2,1)S(1)}, u32[]{:S(2)}, u32[]{:S(2)}) collective-permute-start(bf16[32,2048]{1,0:T(8,128)(2,1)S(1)} %get-tuple-element.121), channel_id=1, source_target_pairs={{0,2},{1,3},{2,0},{3,1},{4,6},{5,7},{6,4},{7,5},{8,10},{9,11},{10,... | collective-permute-start | bytes 393224 | tf_op jit(solution)/shard_map/ppermute | solution.py:390
  75.5 7.4 %collective-permute-start.20 = (bf16[32,2048]{1,0:T(8,128)(2,1)S(1)}, bf16[32,2048]{1,0:T(8,128)(2,1)S(1)}, u32[]{:S(2)}, u32[]{:S(2)}) collective-permute-start(bf16[32,2048]{1,0:T(8,128)(2,1)S(1)} %get-tuple-element.119), channel_id=1, source_target_pairs={{0,2},{1,3},{2,0},{3,1},{4,6},{5,7},{6,4},{7,5},{8,10},{9,11},{10,... | collective-permute-start | bytes 393224 | tf_op jit(solution)/shard_map/ppermute | solution.py:390
  75.8 10.5 %collective-permute-start.22 = (bf16[32,2048]{1,0:T(8,128)(2,1)S(1)}, bf16[32,2048]{1,0:T(8,128)(2,1)S(1)}, u32[]{:S(2)}, u32[]{:S(2)}) collective-permute-start(bf16[32,2048]{1,0:T(8,128)(2,1)S(1)} %add_convert_fusion.3), channel_id=1, source_target_pairs={{0,4},{1,5},{2,6},{3,7},{4,0},{5,1},{6,2},{7,3},{8,12},{9,13},{10,... | collective-permute-start | bytes 393224 | tf_op jit(solution)/shard_map/ppermute | solution.py:390
  78.7 7.6 %collective-permute-start.23 = (bf16[32,2048]{1,0:T(8,128)(2,1)S(1)}, bf16[32,2048]{1,0:T(8,128)(2,1)S(1)}, u32[]{:S(2)}, u32[]{:S(2)}) collective-permute-start(bf16[32,2048]{1,0:T(8,128)(2,1)S(1)} %get-tuple-element.125), channel_id=1, source_target_pairs={{0,2},{1,3},{2,0},{3,1},{4,6},{5,7},{6,4},{7,5},{8,10},{9,11},{10,... | collective-permute-start | bytes 393224 | tf_op jit(solution)/shard_map/ppermute | solution.py:390
  83.0 7.3 %collective-permute-start.24 = (bf16[32,2048]{1,0:T(8,128)(2,1)S(1)}, bf16[32,2048]{1,0:T(8,128)(2,1)S(1)}, u32[]{:S(2)}, u32[]{:S(2)}) collective-permute-start(bf16[32,2048]{1,0:T(8,128)(2,1)S(1)} %add_convert_fusion.2), channel_id=1, source_target_pairs={{0,4},{1,5},{2,6},{3,7},{4,0},{5,1},{6,2},{7,3},{8,12},{9,13},{10,... | collective-permute-start | bytes 393224 | tf_op jit(solution)/shard_map/ppermute | solution.py:390
  83.2 5.7 %collective-permute-start.25 = (bf16[32,2048]{1,0:T(8,128)(2,1)S(1)}, bf16[32,2048]{1,0:T(8,128)(2,1)S(1)}, u32[]{:S(2)}, u32[]{:S(2)}) collective-permute-start(bf16[32,2048]{1,0:T(8,128)(2,1)S(1)} %get-tuple-element.130), channel_id=1, source_target_pairs={{0,2},{1,3},{2,0},{3,1},{4,6},{5,7},{6,4},{7,5},{8,10},{9,11},{10,... | collective-permute-start | bytes 393224 | tf_op jit(solution)/shard_map/ppermute | solution.py:390

commit v5 on v4

--- a/solution.py
+++ b/solution.py
@@ -269,22 +269,35 @@
                     own_ref[tokens, lanes] = mixed_wu[:, DK:] + spread[:, DK:]
 
 
-def mix_kernel(spot_ref, gain_ref, gate_ref, lin_ref, own_ref, *refs):
-    *total_refs, keep_ref, send_ref, totals_ref = refs
-    core, place, here = spot_ref[0], spot_ref[1], spot_ref[2]
-    heads = total_refs[0].shape[0]
-    places = keep_ref.shape[0]
-    rows = keep_ref.shape[1]
-    for d, total_ref in enumerate(total_refs):
-        totals_ref[d] = total_ref[...]
-    states = [jnp.zeros((DK, DV), F32) for _ in range(heads)]
-    for source in range(len(total_refs)):
-        at = jnp.maximum(jnp.bitwise_xor(here, source) - 1, 0)
-        for h in range(heads):
-            step = totals_ref[at, h]
-            moved = mm(step[:, :DK], states[h]) + step[:, DK:].astype(F32)
-            states[h] = jnp.where(source < here, moved, states[h])
-    states = [state.astype(BF16) for state in states]
+def with_map(bias):
+    return jnp.concatenate([jnp.zeros((DK, DK), F32), bias.astype(F32)], axis=1)
+
+
+def scan_kernel(last, later_ref, own_ref, got_ref, before_ref, total_ref, prefix_ref):
+    later = later_ref[0] == 1
+    for h in range(own_ref.shape[0]):
+        own, got, before = own_ref[h], got_ref[h], before_ref[h]
+        first = jnp.where(later, got, own)
+        second = jnp.where(later, own, got)
+        if last:
+            total = mm(second[:, :DK], first[:, DK:]) + second[:, DK:].astype(F32)
+        else:
+            total = mm(second[:, :DK], first) + with_map(second[:, DK:])
+        total_ref[h] = total.astype(BF16)
+        joined = mm(before[:, :DK], got) + with_map(before[:, DK:])
+        prefix_ref[h] = jnp.where(later, joined.astype(BF16), before)
+
+
+def mix_kernel(spot_ref, gain_ref, gate_ref, lin_ref, own_ref, prefix_ref, got_ref, keep_ref, send_ref):
+    core, place, later = spot_ref[0], spot_ref[1], spot_ref[2] == 1
+    heads = prefix_ref.shape[0]
+    places, rows, _ = keep_ref.shape
+    states = []
+    for h in range(heads):
+        prefix = prefix_ref[h]
+        bias = prefix[:, DK:].astype(F32)
+        joined = mm(prefix[:, :DK], got_ref[h]) + bias
+        states.append(jnp.where(later, joined, bias).astype(BF16))
     for d in range(places):
         at = jnp.bitwise_xor(place, d)
         for out_ref, side in ((send_ref, 1 - core), (keep_ref, core)):
@@ -474,11 +487,26 @@
         stay=True,
     )
 
-    totals = [
-        lax.ppermute(total, "seq", [(i, i ^ d) for i in range(seqs)]) for d in range(1, seqs)
-    ]
+    start = jnp.concatenate([jnp.eye(DK, dtype=BF16), jnp.zeros((DK, DV), BF16)], axis=1)
+    before = jnp.broadcast_to(start, total.shape)
+    summed, step = total, 1
+    while True:
+        later = lax.rem(lax.div(here, step), 2)
+        got = lax.ppermute(summed, "seq", [(i, i ^ step) for i in range(seqs)])
+        if 2 * step >= seqs:
+            break
+        last = 4 * step >= seqs
+        summed, before = resident(
+            functools.partial(scan_kernel, last),
+            (shape((heads, DK, DV if last else DK + DV), BF16), shape(total.shape, BF16)),
+            summed,
+            after(got, lin) if step == 1 else got,
+            before,
+            scalars=later.reshape(1),
+        )
+        step *= 2
     fetched = fetch(gate_proj, out_weight, out_sib)
-    totals, fetched, sib = lax.optimization_barrier((totals, fetched, sib))
+    got, before, fetched, sib = lax.optimization_barrier((got, before, fetched, sib))
     gate_here, out_own, out_sib = fetched
 
     half = shape((places, tok, heads * DV), BF16)
@@ -489,10 +517,10 @@
         gate_here,
         lin,
         own_read,
-        *totals,
-        scalars=jnp.stack([core, place, here]),
+        before,
+        got,
+        scalars=jnp.stack([core, place, later]),
         flops=10**9,
-        scratch=[pltpu.VMEM((seqs - 1, *total.shape), BF16)],
     )
     got = lax.ppermute(send, "exp", swap)
     spot = jnp.stack([place, core])

time: 91.3 us -> 89.7 us (0.982)
  waiting for transfers between devices: 30.7 us -> 27.2 us
  local copies, waits for them, and re-layouts: 2.51 us -> 5 us
    ppermute x3 -> x2, waiting for transfers between devices: 4.24 us -> 0.74 us  [per_device(): got = lax.ppermute(summed, 'seq', [(i, i ^ step) for i in range(seqs)])]
    unnamed x30 -> x40, local copies, waits for them, and re-layouts: 2.5 us -> 4.97 us
    ppermute x3 -> x2, starting transfers between devices: 5.32 us -> 4.78 us  [per_device(): got = lax.ppermute(summed, 'seq', [(i, i ^ step) for i in range(seqs)])]
    pallas_call x6 -> x7, Pallas kernels: 8.34 us -> 8.28 us  [resident(): pl.pallas_call(kernel, out_shape=tuple(outs), in_specs=([] if scalars is...]
  transfers between devices with their start and end apart: 26 -> 25, of which waited for: 13 -> 13; matrix products, arithmetic and copies ran while one was open for 0% -> 0% of each run, Pallas kernels for 22% -> 22%
where the time goes in v5:
time: 89.7 us; the launch traced here: 89.5 us
  starting transfers between devices  33 us (37%)
  waiting for transfers between devices  27.2 us (30%)
  Pallas kernels  22.8 us (25%)
  local copies, waits for them, and re-layouts  5 us (6%)
  other arithmetic  1.17 us (1%)
    ppermute x18, starting transfers between devices, exchange(): lax.ppermute(piece, 'exp', between_places(lax.axis_size('exp') // 2, d))  27.1 us
    ppermute x18, waiting for transfers between devices, exchange(): lax.ppermute(piece, 'exp', between_places(lax.axis_size('exp') // 2, d))  25 us
    pallas_call x2, Pallas kernels, call(): pl.pallas_call(kernel, grid=(1,), out_shape=tuple(outs), in_specs=([] if...  10.1 us
    pallas_call x7, Pallas kernels, resident(): pl.pallas_call(kernel, out_shape=tuple(outs), in_specs=([] if scalars is...  8.28 us
    unnamed x40, local copies, waits for them, and re-layouts  4.97 us
    ppermute x2, starting transfers between devices, per_device(): got = lax.ppermute(summed, 'seq', [(i, i ^ step) for i in range(seqs)])  4.78 us
    pallas_call x2, Pallas kernels, fetch(): pl.pallas_call(fetch_kernel, out_shape=tuple((shape(a.shape, a.dtype) for...  4.43 us
  transfers between devices with their start and end apart: 25, of which 13 were waited for; matrix products, arithmetic and copies ran while one was open for 0% of the time, Pallas kernels for 22%

profile of v5, /device:TPU:0, one launch (start us, length us, event | category | flops | bytes accessed | tf_op | source)
XLA Modules:
  0.0 89.5 jit_solution(5939678945913892401)
XLA Ops:
  0.0 0.5 collective-permute-start
  0.5 0.5 collective-permute-start.4
  1.1 7.4 %shard_map.145 = (bf16[4,4,128,256]{3,2,1,0:T(8,128)(2,1)}, bf16[4,4,128,256]{3,2,1,0:T(8,128)(2,1)}, bf16[4,128,256]{2,1,0:T(8,128)(2,1)}) custom-call(bf16[512,256]{1,0:T(8,128)(2,1)} %key_ref.3, bf16[512,512]{1,0:T(8,128)(2,1)} %value_ref.1, f32[4,512]{1,0:T(4,128)} %decay_ref.3, f32[4,512]{1,0:T(4,128)} %rate_ref.1), custom_call_target="tpu_custom_call" | custom-call | flops 10000000000 | bytes 3162112 | tf_op jit(solution)/shard_map/pallas_call | solution.py:79
  8.6 2.9 %collective-permute-start.1 = (bf16[4,128,256]{2,1,0:T(8,128)(2,1)}, bf16[4,128,256]{2,1,0:T(8,128)(2,1)S(1)}, u32[]{:S(2)}, u32[]{:S(2)}) collective-permute-start(bf16[4,128,256]{2,1,0:T(8,128)(2,1)} %get-tuple-element.74.own_ref), channel_id=1, source_target_pairs={{0,8},{8,0},{16,24},{24,16},{1,9},{9,1},{17,25},{25,17},{2,10},{10... | collective-permute-start | bytes 786440 | tf_op jit(solution)/shard_map/ppermute | solution.py:495
  11.5 1.2 %copy-done.18 = bf16[4,4,128,256]{3,2,1,0:T(8,128)(2,1)S(1)} copy-done((bf16[4,4,128,256]{3,2,1,0:T(8,128)(2,1)S(1)}, bf16[4,4,128,256]{3,2,1,0:T(8,128)(2,1)}, u32[]{:S(2)}) %copy-start.18) | copy-done | bytes 1048600
  12.8 1.2 %copy-done.19 = bf16[4,4,128,256]{3,2,1,0:T(8,128)(2,1)S(1)} copy-done((bf16[4,4,128,256]{3,2,1,0:T(8,128)(2,1)S(1)}, bf16[4,4,128,256]{3,2,1,0:T(8,128)(2,1)}, u32[]{:S(2)}) %copy-start.19) | copy-done | bytes 1048600
  14.0 2.6 %shard_map.146 = (bf16[512,512]{1,0:T(8,128)(2,1)S(1)}, f32[512,512]{1,0:T(8,128)S(1)}, bf16[64,128]{1,0:T(8,128)(2,1)S(1)}) custom-call(bf16[512,256]{1,0:T(8,128)(2,1)S(1)} %copy-done.8, bf16[512,256]{1,0:T(8,128)(2,1)S(1)} %copy-done.9, f32[4,512]{1,0:T(4,128)S(1)} %copy-done.10, s32[4,64]{1,0:T(4,128)S(1)} %bitcast.10, bf16[4,64]{1,0:T(4,128)(2,1)S(1)} %bitcast.11, ...), custom_call_target="tpu_custom_call" | custom-call | flops 4000000000 | bytes 4220416 | tf_op jit(solution)/shard_map/pallas_call | solution.py:79
  16.6 0.8 copy-done.16
  17.5 0.7 collective-permute-done.1.got_ref
  18.2 0.3 shard_map.147
  18.5 1.8 %collective-permute-start.2 = (bf16[4,128,128]{2,1,0:T(8,128)(2,1)S(1)}, bf16[4,128,128]{2,1,0:T(8,128)(2,1)S(1)}, u32[]{:S(2)}, u32[]{:S(2)}) collective-permute-start(bf16[4,128,128]{2,1,0:T(8,128)(2,1)S(1)} %get-tuple-element.77), channel_id=1, source_target_pairs={{0,16},{8,24},{16,0},{24,8},{1,17},{9,25},{17,1},{25,9},{2,18},{10... | collective-permute-start | bytes 393224 | tf_op jit(solution)/shard_map/ppermute | solution.py:495
  20.4 1.6 %copy-done.3 = bf16[512,2048]{1,0:T(8,128)(2,1)S(1)} copy-done((bf16[512,2048]{1,0:T(8,128)(2,1)S(1)}, bf16[512,2048]{1,0:T(8,128)(2,1)}, u32[]{:S(2)}) %copy-start.3) | copy-done | bytes 2097176
  22.0 1.9 %shard_map.148 = (bf16[512,512]{1,0:T(8,128)(2,1)S(1)}, bf16[512,2048]{1,0:T(8,128)(2,1)S(1)}, bf16[512,2048]{1,0:T(8,128)(2,1)S(1)}) custom-call(bf16[512,512]{1,0:T(8,128)(2,1)S(1)} %copy-done.5, bf16[512,2048]{1,0:T(8,128)(2,1)S(1)} %copy-done.3, bf16[512,2048]{1,0:T(8,128)(2,1)} %collective-permute-done.refs_2_), custom_call_target="tpu_custom_call" | custom-call | bytes 9437184 | tf_op jit(solution)/shard_map/pallas_call | solution.py:46
  24.0 1.4 %shard_map.149 = (bf16[4,64,512]{2,1,0:T(8,128)(2,1)S(1)}, bf16[4,64,512]{2,1,0:T(8,128)(2,1)S(1)}) custom-call(s32[3]{0:T(128)S(1)} %pad_add_fusion.spot_ref, f32[1,128]{1,0:T(1,128)S(1)} %bitcast.12, bf16[512,512]{1,0:T(8,128)(2,1)S(1)} %get-tuple-element.83.gate_ref, bf16[512,512]{1,0:T(8,128)(2,1)S(1)} %copy-done.17, f32[512,512]{1,0:T(8,128)S(1)} %copy-done.15, ...), custom_call_target="tpu_custom_call" | custom-call | flops 1000000000 | bytes 3015168 | tf_op jit(solution)/shard_map/pallas_call | solution.py:61
  25.5 1.5 %collective-permute-done.6.got_ref = bf16[4,64,512]{2,1,0:T(8,128)(2,1)S(1)} collective-permute-done((bf16[4,64,512]{2,1,0:T(8,128)(2,1)S(1)}, bf16[4,64,512]{2,1,0:T(8,128)(2,1)S(1)}, u32[]{:S(2)}, u32[]{:S(2)}) %collective-permute-start.6) | collective-permute-done | bytes 262176 | tf_op jit(solution)/shard_map/ppermute | solution.py:525
  27.1 1.2 %shard_map.150 = (bf16[32,2048]{1,0:T(8,128)(2,1)S(1)}, bf16[32,2048]{1,0:T(8,128)(2,1)S(1)}, bf16[32,2048]{1,0:T(8,128)(2,1)S(1)}, bf16[32,2048]{1,0:T(8,128)(2...) custom-call(bf16[4,64,512]{2,1,0:T(8,128)(2,1)S(1)} %get-tuple-eleme, ...), custom_call_target="tpu_custom_call" | custom-call | bytes 5767168 | tf_op jit(solution)/shard_map/pallas_call | solution.py:61
  28.3 1.6 %collective-permute-start.8 = (bf16[32,2048]{1,0:T(8,128)(2,1)S(1)}, bf16[32,2048]{1,0:T(8,128)(2,1)S(1)}, u32[]{:S(2)}, u32[]{:S(2)}) collective-permute-start(bf16[32,2048]{1,0:T(8,128)(2,1)S(1)} %get-tuple-element.95), channel_id=1, source_target_pairs={{0,2},{1,3},{2,0},{3,1},{4,6},{5,7},{6,4},{7,5},{8,10},{9,11},{10,... | collective-permute-start | bytes 393224 | tf_op jit(solution)/shard_map/ppermute | solution.py:403
  30.0 0.4 collective-permute-start.7
  30.4 4.3 %collective-permute-done.8 = bf16[32,2048]{1,0:T(8,128)(2,1)S(1)} collective-permute-done((bf16[32,2048]{1,0:T(8,128)(2,1)S(1)}, bf16[32,2048]{1,0:T(8,128)(2,1)S(1)}, u32[]{:S(2)}, u32[]{:S(2)}) %collective-permute-start.8) | collective-permute-done | bytes 131104 | tf_op jit(solution)/shard_map/ppermute | solution.py:403
  34.8 2.6 %collective-permute-start.9 = (bf16[32,2048]{1,0:T(8,128)(2,1)S(1)}, bf16[32,2048]{1,0:T(8,128)(2,1)S(1)}, u32[]{:S(2)}, u32[]{:S(2)}) collective-permute-start(bf16[32,2048]{1,0:T(8,128)(2,1)S(1)} %add_convert_fusion.5), channel_id=1, source_target_pairs={{0,4},{1,5},{2,6},{3,7},{4,0},{5,1},{6,2},{7,3},{8,12},{9,13},{10,... | collective-permute-start | bytes 393224 | tf_op jit(solution)/shard_map/ppermute | solution.py:403
  37.4 1.6 %collective-permute-start.10 = (bf16[32,2048]{1,0:T(8,128)(2,1)S(1)}, bf16[32,2048]{1,0:T(8,128)(2,1)S(1)}, u32[]{:S(2)}, u32[]{:S(2)}) collective-permute-start(bf16[32,2048]{1,0:T(8,128)(2,1)S(1)} %get-tuple-element.109), channel_id=1, source_target_pairs={{0,2},{1,3},{2,0},{3,1},{4,6},{5,7},{6,4},{7,5},{8,10},{9,11},{10,... | collective-permute-start | bytes 393224 | tf_op jit(solution)/shard_map/ppermute | solution.py:403
  39.0 2.0 %collective-permute-start.13 = (bf16[32,2304]{1,0:T(8,128)(2,1)S(1)}, bf16[32,2304]{1,0:T(8,128)(2,1)S(1)}, u32[]{:S(2)}, u32[]{:S(2)}) collective-permute-start(bf16[32,2304]{1,0:T(8,128)(2,1)S(1)} %pad.6), channel_id=1, source_target_pairs={{0,4},{1,5},{2,6},{3,7},{4,0},{5,1},{6,2},{7,3},{8,12},{9,13},{10,... | collective-permute-start | bytes 442376 | tf_op jit(solution)/shard_map/ppermute | solution.py:403
  41.0 2.5 %shard_map.151 = (bf16[1,2048,512]{2,1,0:T(8,128)(2,1)S(1)}, bf16[1,2048,512]{2,1,0:T(8,128)(2,1)S(1)}, bf16[1,512,2048]{2,1,0:T(8,128)(2,1)S(1)}) custom-call(bf16[1,2048,512]{2,1,0:T(8,128)(2,1)S(1)} %collective-permute-done.3.refs_0_, bf16[1,2048,512]{2,1,0:T(8,128)(2,1)} %collective-permute-done.4.refs_1_, ...), custom_call_target="tpu_custom_call" | custom-call | bytes 12582912 | tf_op jit(solution)/shard_map/pallas_call | solution.py:46
  43.6 0.7 collective-permute-done.9.refs_1_
  44.3 0.2 shard_map.152
  44.5 1.9 %collective-permute-start.11 = (bf16[32,2176]{1,0:T(8,128)(2,1)S(1)}, bf16[32,2176]{1,0:T(8,128)(2,1)S(1)}, u32[]{:S(2)}, u32[]{:S(2)}) collective-permute-start(bf16[32,2176]{1,0:T(8,128)(2,1)S(1)} %get-tuple-element.111.refs_0_), channel_id=1, source_target_pairs={{0,2},{1,3},{2,0},{3,1},{4,6},{5,7},{6,4},{7,5},{8,10},{9,11},{10,... | collective-permute-start | bytes 417800 | tf_op jit(solution)/shard_map/ppermute | solution.py:403
  46.5 3.9 %collective-permute-start.12 = (bf16[32,2176]{1,0:T(8,128)(2,1)S(1)}, bf16[32,2176]{1,0:T(8,128)(2,1)S(1)}, u32[]{:S(2)}, u32[]{:S(2)}) collective-permute-start(bf16[32,2176]{1,0:T(8,128)(2,1)S(1)} %get-tuple-element.111.refs_0_), channel_id=1, source_target_pairs={{0,4},{1,5},{2,6},{3,7},{4,0},{5,1},{6,2},{7,3},{8,12},{9,13},{10,... | collective-permute-start | bytes 417800 | tf_op jit(solution)/shard_map/ppermute | solution.py:403
  50.4 4.6 %collective-permute-done.11.refs_1_ = bf16[32,2176]{1,0:T(8,128)(2,1)S(1)} collective-permute-done((bf16[32,2176]{1,0:T(8,128)(2,1)S(1)}, bf16[32,2176]{1,0:T(8,128)(2,1)S(1)}, u32[]{:S(2)}, u32[]{:S(2)}) %collective-permute-start.11) | collective-permute-done | bytes 139296 | tf_op jit(solution)/shard_map/ppermute | solution.py:403
  55.0 1.4 %collective-permute-done.14.refs_2_ = bf16[32,2048]{1,0:T(8,128)(2,1)S(1)} collective-permute-done((bf16[32,2048]{1,0:T(8,128)(2,1)S(1)}, bf16[32,2048]{1,0:T(8,128)(2,1)S(1)}, u32[]{:S(2)}, u32[]{:S(2)}) %collective-permute-start.14) | collective-permute-done | bytes 131104 | tf_op jit(solution)/shard_map/ppermute | solution.py:403
  56.4 0.2 shard_map.153
  56.6 1.7 %collective-permute-start.17 = (bf16[32,2176]{1,0:T(8,128)(2,1)S(1)}, bf16[32,2176]{1,0:T(8,128)(2,1)S(1)}, u32[]{:S(2)}, u32[]{:S(2)}) collective-permute-start(bf16[32,2176]{1,0:T(8,128)(2,1)S(1)} %get-tuple-element.120.refs_0_), channel_id=1, source_target_pairs={{0,4},{1,5},{2,6},{3,7},{4,0},{5,1},{6,2},{7,3},{8,12},{9,13},{10,... | collective-permute-start | bytes 417800 | tf_op jit(solution)/shard_map/ppermute | solution.py:403
  58.3 2.5 %collective-permute-start.15 = (bf16[32,2176]{1,0:T(8,128)(2,1)S(1)}, bf16[32,2176]{1,0:T(8,128)(2,1)S(1)}, u32[]{:S(2)}, u32[]{:S(2)}) collective-permute-start(bf16[32,2176]{1,0:T(8,128)(2,1)S(1)} %collective-permute-done.12.refs_2_), channel_id=1, source_target_pairs={{0,2},{1,3},{2,0},{3,1},{4,6},{5,7},{6,4},{7,5},{8,10},{9,11},{10,... | collective-permute-start | bytes 417800 | tf_op jit(solution)/shard_map/ppermute | solution.py:403
  60.9 2.6 %collective-permute-done.17.refs_2_ = bf16[32,2176]{1,0:T(8,128)(2,1)S(1)} collective-permute-done((bf16[32,2176]{1,0:T(8,128)(2,1)S(1)}, bf16[32,2176]{1,0:T(8,128)(2,1)S(1)}, u32[]{:S(2)}, u32[]{:S(2)}) %collective-permute-start.17) | collective-permute-done | bytes 139296 | tf_op jit(solution)/shard_map/ppermute | solution.py:403
  63.4 1.9 %collective-permute-start.18 = (bf16[32,2176]{1,0:T(8,128)(2,1)S(1)}, bf16[32,2176]{1,0:T(8,128)(2,1)S(1)}, u32[]{:S(2)}, u32[]{:S(2)}) collective-permute-start(bf16[32,2176]{1,0:T(8,128)(2,1)S(1)} %collective-permute-done.17.refs_2_), channel_id=1, source_target_pairs={{0,2},{1,3},{2,0},{3,1},{4,6},{5,7},{6,4},{7,5},{8,10},{9,11},{10,... | collective-permute-start | bytes 417800 | tf_op jit(solution)/shard_map/ppermute | solution.py:403
  65.4 0.6 collective-permute-done.15.refs_3_
  65.9 2.5 %shard_map.154 = (bf16[32,2048]{1,0:T(8,128)(2,1)S(1)}, bf16[32,2048]{1,0:T(8,128)(2,1)S(1)}, bf16[32,2048]{1,0:T(8,128)(2,1)S(1)}, bf16[32,2048]{1,0:T(8,128)(2,1)S(1)}) custom-call(s32[2]{0:T(128)S(1)} %pad_add_fusion.1.spot_ref, bf16[32,2176]{1,0:T(8,128)(2,1)S(1)} %get-tuple-element.111.refs_0_, bf16[32,2176]{1,0:T(8,128)(2,1)S(1)} %collective-permute-done.11.refs_1_, ...), custom_call_target="tpu_custom_call" | custom-call | flops 3000000000 | bytes 13664256 | tf_op jit(solution)/shard_map/pallas_call | solution.py:61
  68.5 1.3 %collective-permute-start.20 = (bf16[32,2048]{1,0:T(8,128)(2,1)S(1)}, bf16[32,2048]{1,0:T(8,128)(2,1)S(1)}, u32[]{:S(2)}, u32[]{:S(2)}) collective-permute-start(bf16[32,2048]{1,0:T(8,128)(2,1)S(1)} %get-tuple-element.125), channel_id=1, source_target_pairs={{0,2},{1,3},{2,0},{3,1},{4,6},{5,7},{6,4},{7,5},{8,10},{9,11},{10,... | collective-permute-start | bytes 393224 | tf_op jit(solution)/shard_map/ppermute | solution.py:403
  69.8 1.6 %collective-permute-done.18.refs_3_ = bf16[32,2176]{1,0:T(8,128)(2,1)S(1)} collective-permute-done((bf16[32,2176]{1,0:T(8,128)(2,1)S(1)}, bf16[32,2176]{1,0:T(8,128)(2,1)S(1)}, u32[]{:S(2)}, u32[]{:S(2)}) %collective-permute-start.18) | collective-permute-done | bytes 139296 | tf_op jit(solution)/shard_map/ppermute | solution.py:403
  71.4 2.5 %shard_map.155 = (bf16[32,2048]{1,0:T(8,128)(2,1)S(1)}, bf16[32,2048]{1,0:T(8,128)(2,1)S(1)}, bf16[32,2048]{1,0:T(8,128)(2,1)S(1)}, bf16[32,2048]{1,0:T(8,128)(2,1)S(1)}) custom-call(s32[2]{0:T(128)S(1)} %pad_add_fusion.1.spot_ref, bf16[32,2176]{1,0:T(8,128)(2,1)S(1)} %get-tuple-element.120.refs_0_, bf16[32,2176]{1,0:T(8,128)(2,1)S(1)} %collective-permute-done.16.refs_1_, ...), custom_call_target="tpu_custom_call" | custom-call | flops 3000000000 | bytes 13664256 | tf_op jit(solution)/shard_map/pallas_call | solution.py:61
  73.9 0.3 collective-permute-start.19
  74.2 2.9 %collective-permute-start.21 = (bf16[32,2048]{1,0:T(8,128)(2,1)S(1)}, bf16[32,2048]{1,0:T(8,128)(2,1)S(1)}, u32[]{:S(2)}, u32[]{:S(2)}) collective-permute-start(bf16[32,2048]{1,0:T(8,128)(2,1)S(1)} %add_convert_fusion.3), channel_id=1, source_target_pairs={{0,4},{1,5},{2,6},{3,7},{4,0},{5,1},{6,2},{7,3},{8,12},{9,13},{10,... | collective-permute-start | bytes 393224 | tf_op jit(solution)/shard_map/ppermute | solution.py:403
  77.2 4.2 %collective-permute-done.19 = bf16[32,2048]{1,0:T(8,128)(2,1)S(1)} collective-permute-done((bf16[32,2048]{1,0:T(8,128)(2,1)S(1)}, bf16[32,2048]{1,0:T(8,128)(2,1)S(1)}, u32[]{:S(2)}, u32[]{:S(2)}) %collective-permute-start.19) | collective-permute-done | bytes 131104 | tf_op jit(solution)/shard_map/ppermute | solution.py:403
  81.4 0.2 collective-permute-start.23
  81.6 2.1 %collective-permute-start.24 = (bf16[32,2048]{1,0:T(8,128)(2,1)S(1)}, bf16[32,2048]{1,0:T(8,128)(2,1)S(1)}, u32[]{:S(2)}, u32[]{:S(2)}) collective-permute-start(bf16[32,2048]{1,0:T(8,128)(2,1)S(1)} %get-tuple-element.134), channel_id=1, source_target_pairs={{0,2},{1,3},{2,0},{3,1},{4,6},{5,7},{6,4},{7,5},{8,10},{9,11},{10,... | collective-permute-start | bytes 393224 | tf_op jit(solution)/shard_map/ppermute | solution.py:403
  83.7 1.0 %collective-permute-done.22 = bf16[32,2048]{1,0:T(8,128)(2,1)S(1)} collective-permute-done((bf16[32,2048]{1,0:T(8,128)(2,1)S(1)}, bf16[32,2048]{1,0:T(8,128)(2,1)S(1)}, u32[]{:S(2)}, u32[]{:S(2)}) %collective-permute-start.22) | collective-permute-done | bytes 131104 | tf_op jit(solution)/shard_map/ppermute | solution.py:403
  84.8 2.4 %collective-permute-done.24 = bf16[32,2048]{1,0:T(8,128)(2,1)S(1)} collective-permute-done((bf16[32,2048]{1,0:T(8,128)(2,1)S(1)}, bf16[32,2048]{1,0:T(8,128)(2,1)S(1)}, u32[]{:S(2)}, u32[]{:S(2)}) %collective-permute-start.24) | collective-permute-done | bytes 131104 | tf_op jit(solution)/shard_map/ppermute | solution.py:403
  87.2 1.5 %collective-permute-done.23 = bf16[32,2048]{1,0:T(8,128)(2,1)S(1)} collective-permute-done((bf16[32,2048]{1,0:T(8,128)(2,1)S(1)}, bf16[32,2048]{1,0:T(8,128)(2,1)S(1)}, u32[]{:S(2)}, u32[]{:S(2)}) %collective-permute-start.23) | collective-permute-done | bytes 131104 | tf_op jit(solution)/shard_map/ppermute | solution.py:403
  88.8 0.7 pad_maximum_fusion
  (66 shorter events, 1.0 us)
Async XLA Ops:
  0.0 8.6 %collective-permute-start = (bf16[512,2048]{1,0:T(8,128)(2,1)}, bf16[512,2048]{1,0:T(8,128)(2,1)}, u32[]{:S(2)}, u32[]{:S(2)}) collective-permute-start(bf16[512,2048]{1,0:T(8,128)(2,1)} %refs_1_.1), channel_id=1, source_target_pairs={{0,1},{1,0},{2,3},{3,2},{4,5},{5,4},{6,7},{7,6},{8,9},{9,8},{10,11... | collective-permute-start | bytes 6291464 | tf_op jit(solution)/shard_map/ppermute | solution.py:456
  0.5 23.5 %collective-permute-start.3 = (bf16[1,2048,512]{2,1,0:T(8,128)(2,1)}, bf16[1,2048,512]{2,1,0:T(8,128)(2,1)S(1)}, u32[]{:S(2)}, u32[]{:S(2)}) collective-permute-start(bf16[1,2048,512]{2,1,0:T(8,128)(2,1)} %refs_4_.3), channel_id=1, source_target_pairs={{0,1},{1,0},{2,3},{3,2},{4,5},{5,4},{6,7},{7,6},{8,9},{9,8},{10,11... | collective-permute-start | bytes 6291464 | tf_op jit(solution)/shard_map/ppermute | solution.py:458
  0.5 23.4 %collective-permute-start.4 = (bf16[1,2048,512]{2,1,0:T(8,128)(2,1)}, bf16[1,2048,512]{2,1,0:T(8,128)(2,1)}, u32[]{:S(2)}, u32[]{:S(2)}) collective-permute-start(bf16[1,2048,512]{2,1,0:T(8,128)(2,1)} %refs_5_.3), channel_id=1, source_target_pairs={{0,1},{1,0},{2,3},{3,2},{4,5},{5,4},{6,7},{7,6},{8,9},{9,8},{10,11... | collective-permute-start | bytes 6291464 | tf_op jit(solution)/shard_map/ppermute | solution.py:458
  1.0 23.0 %collective-permute-start.5 = (bf16[1,512,2048]{2,1,0:T(8,128)(2,1)}, bf16[1,512,2048]{2,1,0:T(8,128)(2,1)}, u32[]{:S(2)}, u32[]{:S(2)}) collective-permute-start(bf16[1,512,2048]{2,1,0:T(8,128)(2,1)} %refs_6_.3), channel_id=1, source_target_pairs={{0,1},{1,0},{2,3},{3,2},{4,5},{5,4},{6,7},{7,6},{8,9},{9,8},{10,11... | collective-permute-start | bytes 6291464 | tf_op jit(solution)/shard_map/ppermute | solution.py:458
  1.1 10.5 %copy-start.8 = (bf16[512,256]{1,0:T(8,128)(2,1)S(1)}, bf16[512,256]{1,0:T(8,128)(2,1)}, u32[]{:S(2)}) copy-start(bf16[512,256]{1,0:T(8,128)(2,1)} %query_ref.1) | copy-start | bytes 786436
  1.1 10.4 %copy-start.9 = (bf16[512,256]{1,0:T(8,128)(2,1)S(1)}, bf16[512,256]{1,0:T(8,128)(2,1)}, u32[]{:S(2)}) copy-start(bf16[512,256]{1,0:T(8,128)(2,1)} %key_ref.3) | copy-start | bytes 786436
  1.1 10.4 %copy-start.10 = (f32[4,512]{1,0:T(4,128)S(1)}, f32[4,512]{1,0:T(4,128)}, u32[]{:S(2)}) copy-start(f32[4,512]{1,0:T(4,128)} %decay_ref.3) | copy-start | bytes 24580
  1.1 10.4 %copy-start.11 = (s32[64,4]{0,1:T(4,128)S(1)}, s32[64,4]{0,1:T(4,128)}, u32[]{:S(2)}) copy-start(s32[64,4]{0,1:T(4,128)} %param.25) | copy-start | bytes 3076
  1.1 10.4 %copy-start.12 = (bf16[64,4]{0,1:T(4,128)(2,1)S(1)}, bf16[64,4]{0,1:T(4,128)(2,1)}, u32[]{:S(2)}) copy-start(bf16[64,4]{0,1:T(4,128)(2,1)} %param.26) | copy-start | bytes 1540
  8.6 9.6 %collective-permute-start.1 = (bf16[4,128,256]{2,1,0:T(8,128)(2,1)}, bf16[4,128,256]{2,1,0:T(8,128)(2,1)S(1)}, u32[]{:S(2)}, u32[]{:S(2)}) collective-permute-start(bf16[4,128,256]{2,1,0:T(8,128)(2,1)} %get-tuple-element.74.own_ref), channel_id=1, source_target_pairs={{0,8},{8,0},{16,24},{24,16},{1,9},{9,1},{17,25},{25,17},{2,10},{10... | collective-permute-start | bytes 786440 | tf_op jit(solution)/shard_map/ppermute | solution.py:495
  11.5 1.2 %copy-start.18 = (bf16[4,4,128,256]{3,2,1,0:T(8,128)(2,1)S(1)}, bf16[4,4,128,256]{3,2,1,0:T(8,128)(2,1)}, u32[]{:S(2)}) copy-start(bf16[4,4,128,256]{3,2,1,0:T(8,128)(2,1)} %get-tuple-element.70.wu_ref) | copy-start | bytes 3145732
  12.8 1.2 %copy-start.19 = (bf16[4,4,128,256]{3,2,1,0:T(8,128)(2,1)S(1)}, bf16[4,4,128,256]{3,2,1,0:T(8,128)(2,1)}, u32[]{:S(2)}) copy-start(bf16[4,4,128,256]{3,2,1,0:T(8,128)(2,1)} %get-tuple-element.71.prefix_ref) | copy-start | bytes 3145732
  14.0 4.2 %copy-start.6 = (bf16[4,128,256]{2,1,0:T(8,128)(2,1)S(1)}, bf16[4,128,256]{2,1,0:T(8,128)(2,1)}, u32[]{:S(2)}) copy-start(bf16[4,128,256]{2,1,0:T(8,128)(2,1)} %get-tuple-element.74.own_ref) | copy-start | bytes 786436
  14.0 6.4 %copy-start.5 = (bf16[512,512]{1,0:T(8,128)(2,1)S(1)}, bf16[512,512]{1,0:T(8,128)(2,1)}, u32[]{:S(2)}) copy-start(bf16[512,512]{1,0:T(8,128)(2,1)} %refs_0_.1) | copy-start | bytes 1572868
  16.6 0.8 copy-start.16
  17.5 1.1 %copy-start.14 = (f32[512,512]{1,0:T(8,128)}, f32[512,512]{1,0:T(8,128)S(1)}, u32[]{:S(2)}) copy-start(f32[512,512]{1,0:T(8,128)S(1)} %get-tuple-element.84.own_ref) | copy-start | bytes 3145732
  18.5 5.5 %collective-permute-start.2 = (bf16[4,128,128]{2,1,0:T(8,128)(2,1)S(1)}, bf16[4,128,128]{2,1,0:T(8,128)(2,1)S(1)}, u32[]{:S(2)}, u32[]{:S(2)}) collective-permute-start(bf16[4,128,128]{2,1,0:T(8,128)(2,1)S(1)} %get-tuple-element.77), channel_id=1, source_target_pairs={{0,16},{8,24},{16,0},{24,8},{1,17},{9,25},{17,1},{25,9},{2,18},{10... | collective-permute-start | bytes 393224 | tf_op jit(solution)/shard_map/ppermute | solution.py:495
  20.4 1.6 %copy-start.3 = (bf16[512,2048]{1,0:T(8,128)(2,1)S(1)}, bf16[512,2048]{1,0:T(8,128)(2,1)}, u32[]{:S(2)}) copy-start(bf16[512,2048]{1,0:T(8,128)(2,1)} %refs_1_.1) | copy-start | bytes 6291460
  22.0 2.0 %copy-start.13 = (f32[128]{0:T(128)S(1)}, f32[128]{0:T(128)}, u32[]{:S(2)}) copy-start(f32[128]{0:T(128)} %param.22) | copy-start | bytes 1540
  22.0 2.0 %copy-start.15 = (f32[512,512]{1,0:T(8,128)S(1)}, f32[512,512]{1,0:T(8,128)}, u32[]{:S(2)}) copy-start(f32[512,512]{1,0:T(8,128)} %copy-done.14) | copy-start | bytes 3145732
  22.0 2.0 %copy-start.17 = (bf16[512,512]{1,0:T(8,128)(2,1)S(1)}, bf16[512,512]{1,0:T(8,128)(2,1)}, u32[]{:S(2)}) copy-start(bf16[512,512]{1,0:T(8,128)(2,1)} %copy-done.16) | copy-start | bytes 1572868
  25.5 1.6 %collective-permute-start.6 = (bf16[4,64,512]{2,1,0:T(8,128)(2,1)S(1)}, bf16[4,64,512]{2,1,0:T(8,128)(2,1)S(1)}, u32[]{:S(2)}, u32[]{:S(2)}) collective-permute-start(bf16[4,64,512]{2,1,0:T(8,128)(2,1)S(1)} %get-tuple-element.88), channel_id=1, source_target_pairs={{0,1},{1,0},{2,3},{3,2},{4,5},{5,4},{6,7},{7,6},{8,9},{9,8},{10,11... | collective-permute-start | bytes 786440 | tf_op jit(solution)/shard_map/ppermute | solution.py:525
  28.3 6.4 %collective-permute-start.8 = (bf16[32,2048]{1,0:T(8,128)(2,1)S(1)}, bf16[32,2048]{1,0:T(8,128)(2,1)S(1)}, u32[]{:S(2)}, u32[]{:S(2)}) collective-permute-start(bf16[32,2048]{1,0:T(8,128)(2,1)S(1)} %get-tuple-element.95), channel_id=1, source_target_pairs={{0,2},{1,3},{2,0},{3,1},{4,6},{5,7},{6,4},{7,5},{8,10},{9,11},{10,... | collective-permute-start | bytes 393224 | tf_op jit(solution)/shard_map/ppermute | solution.py:403
  30.0 7.5 %collective-permute-start.7 = (bf16[32,2048]{1,0:T(8,128)(2,1)S(1)}, bf16[32,2048]{1,0:T(8,128)(2,1)S(1)}, u32[]{:S(2)}, u32[]{:S(2)}) collective-permute-start(bf16[32,2048]{1,0:T(8,128)(2,1)S(1)} %get-tuple-element.93), channel_id=1, source_target_pairs={{0,2},{1,3},{2,0},{3,1},{4,6},{5,7},{6,4},{7,5},{8,10},{9,11},{10,... | collective-permute-start | bytes 393224 | tf_op jit(solution)/shard_map/ppermute | solution.py:403
  34.7 9.6 %copy-start.4 = (bf16[64,2048]{1,0:T(8,128)(2,1)S(1)}, bf16[64,2048]{1,0:T(8,128)(2,1)}, u32[]{:S(2)}) copy-start(bf16[64,2048]{1,0:T(8,128)(2,1)} %hidden_ref.3) | copy-start | bytes 786436
  34.8 9.6 %collective-permute-start.9 = (bf16[32,2048]{1,0:T(8,128)(2,1)S(1)}, bf16[32,2048]{1,0:T(8,128)(2,1)S(1)}, u32[]{:S(2)}, u32[]{:S(2)}) collective-permute-start(bf16[32,2048]{1,0:T(8,128)(2,1)S(1)} %add_convert_fusion.5), channel_id=1, source_target_pairs={{0,4},{1,5},{2,6},{3,7},{4,0},{5,1},{6,2},{7,3},{8,12},{9,13},{10,... | collective-permute-start | bytes 393224 | tf_op jit(solution)/shard_map/ppermute | solution.py:403
  37.4 6.9 %collective-permute-start.10 = (bf16[32,2048]{1,0:T(8,128)(2,1)S(1)}, bf16[32,2048]{1,0:T(8,128)(2,1)S(1)}, u32[]{:S(2)}, u32[]{:S(2)}) collective-permute-start(bf16[32,2048]{1,0:T(8,128)(2,1)S(1)} %get-tuple-element.109), channel_id=1, source_target_pairs={{0,2},{1,3},{2,0},{3,1},{4,6},{5,7},{6,4},{7,5},{8,10},{9,11},{10,... | collective-permute-start | bytes 393224 | tf_op jit(solution)/shard_map/ppermute | solution.py:403
  39.0 17.4 %collective-permute-start.13 = (bf16[32,2304]{1,0:T(8,128)(2,1)S(1)}, bf16[32,2304]{1,0:T(8,128)(2,1)S(1)}, u32[]{:S(2)}, u32[]{:S(2)}) collective-permute-start(bf16[32,2304]{1,0:T(8,128)(2,1)S(1)} %pad.6), channel_id=1, source_target_pairs={{0,4},{1,5},{2,6},{3,7},{4,0},{5,1},{6,2},{7,3},{8,12},{9,13},{10,... | collective-permute-start | bytes 442376 | tf_op jit(solution)/shard_map/ppermute | solution.py:403
  41.0 3.3 %copy-start.7 = (f32[2048]{0:T(1024)S(1)}, f32[2048]{0:T(1024)}, u32[]{:S(2)}) copy-start(f32[2048]{0:T(1024)} %param.24) | copy-start | bytes 24580
  41.0 24.9 %copy-start = (bf16[1,2048,512]{2,1,0:T(8,128)(2,1)S(1)}, bf16[1,2048,512]{2,1,0:T(8,128)(2,1)}, u32[]{:S(2)}) copy-start(bf16[1,2048,512]{2,1,0:T(8,128)(2,1)} %refs_4_.3) | copy-start | bytes 6291460
  41.0 24.9 %copy-start.1 = (bf16[1,2048,512]{2,1,0:T(8,128)(2,1)S(1)}, bf16[1,2048,512]{2,1,0:T(8,128)(2,1)}, u32[]{:S(2)}) copy-start(bf16[1,2048,512]{2,1,0:T(8,128)(2,1)} %refs_5_.3) | copy-start | bytes 6291460
  41.0 24.9 %copy-start.2 = (bf16[1,512,2048]{2,1,0:T(8,128)(2,1)S(1)}, bf16[1,512,2048]{2,1,0:T(8,128)(2,1)}, u32[]{:S(2)}) copy-start(bf16[1,512,2048]{2,1,0:T(8,128)(2,1)} %refs_6_.3) | copy-start | bytes 6291460
  44.5 10.5 %collective-permute-start.11 = (bf16[32,2176]{1,0:T(8,128)(2,1)S(1)}, bf16[32,2176]{1,0:T(8,128)(2,1)S(1)}, u32[]{:S(2)}, u32[]{:S(2)}) collective-permute-start(bf16[32,2176]{1,0:T(8,128)(2,1)S(1)} %get-tuple-element.111.refs_0_), channel_id=1, source_target_pairs={{0,2},{1,3},{2,0},{3,1},{4,6},{5,7},{6,4},{7,5},{8,10},{9,11},{10,... | collective-permute-start | bytes 417800 | tf_op jit(solution)/shard_map/ppermute | solution.py:403
  46.5 8.6 %collective-permute-start.12 = (bf16[32,2176]{1,0:T(8,128)(2,1)S(1)}, bf16[32,2176]{1,0:T(8,128)(2,1)S(1)}, u32[]{:S(2)}, u32[]{:S(2)}) collective-permute-start(bf16[32,2176]{1,0:T(8,128)(2,1)S(1)} %get-tuple-element.111.refs_0_), channel_id=1, source_target_pairs={{0,4},{1,5},{2,6},{3,7},{4,0},{5,1},{6,2},{7,3},{8,12},{9,13},{10,... | collective-permute-start | bytes 417800 | tf_op jit(solution)/shard_map/ppermute | solution.py:403
  50.3 6.1 %collective-permute-start.14 = (bf16[32,2048]{1,0:T(8,128)(2,1)S(1)}, bf16[32,2048]{1,0:T(8,128)(2,1)S(1)}, u32[]{:S(2)}, u32[]{:S(2)}) collective-permute-start(bf16[32,2048]{1,0:T(8,128)(2,1)S(1)} %get-tuple-element.116), channel_id=1, source_target_pairs={{0,2},{1,3},{2,0},{3,1},{4,6},{5,7},{6,4},{7,5},{8,10},{9,11},{10,... | collective-permute-start | bytes 393224 | tf_op jit(solution)/shard_map/ppermute | solution.py:403
  56.6 6.8 %collective-permute-start.17 = (bf16[32,2176]{1,0:T(8,128)(2,1)S(1)}, bf16[32,2176]{1,0:T(8,128)(2,1)S(1)}, u32[]{:S(2)}, u32[]{:S(2)}) collective-permute-start(bf16[32,2176]{1,0:T(8,128)(2,1)S(1)} %get-tuple-element.120.refs_0_), channel_id=1, source_target_pairs={{0,4},{1,5},{2,6},{3,7},{4,0},{5,1},{6,2},{7,3},{8,12},{9,13},{10,... | collective-permute-start | bytes 417800 | tf_op jit(solution)/shard_map/ppermute | solution.py:403
  58.3 7.6 %collective-permute-start.15 = (bf16[32,2176]{1,0:T(8,128)(2,1)S(1)}, bf16[32,2176]{1,0:T(8,128)(2,1)S(1)}, u32[]{:S(2)}, u32[]{:S(2)}) collective-permute-start(bf16[32,2176]{1,0:T(8,128)(2,1)S(1)} %collective-permute-done.12.refs_2_), channel_id=1, source_target_pairs={{0,2},{1,3},{2,0},{3,1},{4,6},{5,7},{6,4},{7,5},{8,10},{9,11},{10,... | collective-permute-start | bytes 417800 | tf_op jit(solution)/shard_map/ppermute | solution.py:403
  60.8 9.0 %collective-permute-start.16 = (bf16[32,2176]{1,0:T(8,128)(2,1)S(1)}, bf16[32,2176]{1,0:T(8,128)(2,1)S(1)}, u32[]{:S(2)}, u32[]{:S(2)}) collective-permute-start(bf16[32,2176]{1,0:T(8,128)(2,1)S(1)} %get-tuple-element.120.refs_0_), channel_id=1, source_target_pairs={{0,2},{1,3},{2,0},{3,1},{4,6},{5,7},{6,4},{7,5},{8,10},{9,11},{10,... | collective-permute-start | bytes 417800 | tf_op jit(solution)/shard_map/ppermute | solution.py:403
  63.4 7.9 %collective-permute-start.18 = (bf16[32,2176]{1,0:T(8,128)(2,1)S(1)}, bf16[32,2176]{1,0:T(8,128)(2,1)S(1)}, u32[]{:S(2)}, u32[]{:S(2)}) collective-permute-start(bf16[32,2176]{1,0:T(8,128)(2,1)S(1)} %collective-permute-done.17.refs_2_), channel_id=1, source_target_pairs={{0,2},{1,3},{2,0},{3,1},{4,6},{5,7},{6,4},{7,5},{8,10},{9,11},{10,... | collective-permute-start | bytes 417800 | tf_op jit(solution)/shard_map/ppermute | solution.py:403
  68.5 5.7 %collective-permute-start.20 = (bf16[32,2048]{1,0:T(8,128)(2,1)S(1)}, bf16[32,2048]{1,0:T(8,128)(2,1)S(1)}, u32[]{:S(2)}, u32[]{:S(2)}) collective-permute-start(bf16[32,2048]{1,0:T(8,128)(2,1)S(1)} %get-tuple-element.125), channel_id=1, source_target_pairs={{0,2},{1,3},{2,0},{3,1},{4,6},{5,7},{6,4},{7,5},{8,10},{9,11},{10,... | collective-permute-start | bytes 393224 | tf_op jit(solution)/shard_map/ppermute | solution.py:403
  73.9 7.4 %collective-permute-start.19 = (bf16[32,2048]{1,0:T(8,128)(2,1)S(1)}, bf16[32,2048]{1,0:T(8,128)(2,1)S(1)}, u32[]{:S(2)}, u32[]{:S(2)}) collective-permute-start(bf16[32,2048]{1,0:T(8,128)(2,1)S(1)} %get-tuple-element.123), channel_id=1, source_target_pairs={{0,2},{1,3},{2,0},{3,1},{4,6},{5,7},{6,4},{7,5},{8,10},{9,11},{10,... | collective-permute-start | bytes 393224 | tf_op jit(solution)/shard_map/ppermute | solution.py:403
  74.2 10.5 %collective-permute-start.21 = (bf16[32,2048]{1,0:T(8,128)(2,1)S(1)}, bf16[32,2048]{1,0:T(8,128)(2,1)S(1)}, u32[]{:S(2)}, u32[]{:S(2)}) collective-permute-start(bf16[32,2048]{1,0:T(8,128)(2,1)S(1)} %add_convert_fusion.3), channel_id=1, source_target_pairs={{0,4},{1,5},{2,6},{3,7},{4,0},{5,1},{6,2},{7,3},{8,12},{9,13},{10,... | collective-permute-start | bytes 393224 | tf_op jit(solution)/shard_map/ppermute | solution.py:403
  77.1 7.6 %collective-permute-start.22 = (bf16[32,2048]{1,0:T(8,128)(2,1)S(1)}, bf16[32,2048]{1,0:T(8,128)(2,1)S(1)}, u32[]{:S(2)}, u32[]{:S(2)}) collective-permute-start(bf16[32,2048]{1,0:T(8,128)(2,1)S(1)} %get-tuple-element.129), channel_id=1, source_target_pairs={{0,2},{1,3},{2,0},{3,1},{4,6},{5,7},{6,4},{7,5},{8,10},{9,11},{10,... | collective-permute-start | bytes 393224 | tf_op jit(solution)/shard_map/ppermute | solution.py:403
  81.4 7.3 %collective-permute-start.23 = (bf16[32,2048]{1,0:T(8,128)(2,1)S(1)}, bf16[32,2048]{1,0:T(8,128)(2,1)S(1)}, u32[]{:S(2)}, u32[]{:S(2)}) collective-permute-start(bf16[32,2048]{1,0:T(8,128)(2,1)S(1)} %add_convert_fusion.2), channel_id=1, source_target_pairs={{0,4},{1,5},{2,6},{3,7},{4,0},{5,1},{6,2},{7,3},{8,12},{9,13},{10,... | collective-permute-start | bytes 393224 | tf_op jit(solution)/shard_map/ppermute | solution.py:403
  81.6 5.6 %collective-permute-start.24 = (bf16[32,2048]{1,0:T(8,128)(2,1)S(1)}, bf16[32,2048]{1,0:T(8,128)(2,1)S(1)}, u32[]{:S(2)}, u32[]{:S(2)}) collective-permute-start(bf16[32,2048]{1,0:T(8,128)(2,1)S(1)} %get-tuple-element.134), channel_id=1, source_target_pairs={{0,2},{1,3},{2,0},{3,1},{4,6},{5,7},{6,4},{7,5},{8,10},{9,11},{10,... | collective-permute-start | bytes 393224 | tf_op jit(solution)/shard_map/ppermute | solution.py:403

commit v6 on v5

--- a/solution.py
+++ b/solution.py
@@ -14,7 +14,6 @@
 LANES = 128
 F32 = jnp.float32
 BF16 = jnp.bfloat16
-EXACT = lax.Precision.HIGHEST
 LARGE_VMEM = 60 * 1024 * 1024
 SMALL_VMEM = 24 * 1024 * 1024
 FETCH_VMEM = 24 * 1024 * 1024
@@ -96,9 +95,9 @@
     return jnp.dot(a.astype(BF16), b.astype(BF16), preferred_element_type=F32)
 
 
-def mm_nt(a, b, precision=None):
+def mm_nt(a, b):
     return lax.dot_general(
-        a, b, (((1,), (1,)), ((), ())), preferred_element_type=F32, precision=precision
+        a, b, (((1,), (1,)), ((), ())), preferred_element_type=F32
     )
 
 
@@ -136,12 +135,27 @@
     return jnp.concatenate([ref[:, c * BLOCK : (c + 1) * BLOCK] for c in range(blocks)], axis=0)
 
 
+def thirds(matrix):
+    parts = []
+    for _ in range(3):
+        parts.append(matrix.astype(BF16))
+        matrix = matrix - parts[-1].astype(F32)
+    return jnp.concatenate(parts, axis=0)
+
+
+def turned(mask, matrix):
+    rows = matrix.shape[0]
+    product = mm_nt(mask, thirds(matrix))
+    return product[:, :rows] + product[:, rows : 2 * rows] + product[:, 2 * rows :]
+
+
 def decays(decay_ref, blocks, row, col):
     by_row = stacked(decay_ref, blocks)
-    upto = jnp.where(row >= col, 1.0, 0.0).astype(F32)
-    cum_rows = mm_nt(by_row, upto, EXACT)
-    cum_cols = mm_nt(upto, by_row, EXACT)
-    return cum_rows, cum_cols
+    upto = jnp.where(row >= col, 1.0, 0.0).astype(BF16)
+    rows = by_row.shape[0]
+    product = mm_nt(thirds(by_row), upto)
+    cum_rows = product[:rows] + product[rows : 2 * rows] + product[2 * rows :]
+    return cum_rows, turned(upto, by_row)
 
 
 def state_kernel(key_ref, value_ref, decay_ref, rate_ref, wu_ref, prefix_ref, total_ref):
@@ -156,7 +170,7 @@
     eye = jnp.where(diagonal, 1.0, 0.0).astype(F32)
     cum_rows, cum_cols = decays(decay_ref, blocks, row, col)
     rate_rows = stacked(rate_ref, blocks)
-    rate_cols = mm_nt(eye, rate_rows, EXACT)
+    rate_cols = turned(eye.astype(BF16), rate_rows)
     carried = [None] * heads
     pairs = [(c, h) for c in range(blocks) for h in range(heads)]
     unit_rows, unit_cols, keys, keys_t, grams = {}, {}, {}, {}, {}
@@ -288,58 +302,80 @@
         prefix_ref[h] = jnp.where(later, joined.astype(BF16), before)
 
 
-def mix_kernel(spot_ref, gain_ref, gate_ref, lin_ref, own_ref, prefix_ref, got_ref, keep_ref, send_ref):
+def mixed_rows(tokens, states, gain_ref, gate_ref, lin_ref, own_ref):
+    parts = []
+    for h, state in enumerate(states):
+        lanes = slice(h * DV, (h + 1) * DV)
+        readout = own_ref[tokens, lanes] + mm(lin_ref[tokens, lanes], state)
+        scale = lax.rsqrt(jnp.mean(readout * readout, axis=1, keepdims=True) + EPS)
+        gate = gate_ref[tokens, lanes].astype(F32)
+        gated = gain_ref[...] * gate / (1.0 + jnp.exp(-gate))
+        parts.append((readout * scale * gated).astype(BF16))
+    return jnp.concatenate(parts, axis=1)
+
+
+def rows_of(place, side, d, rows):
+    at = 2 * jnp.bitwise_xor(place, d) + side
+    return pl.ds(pl.multiple_of(at * rows, rows), rows)
+
+
+def send_kernel(spot_ref, gain_ref, gate_ref, lin_ref, own_ref, prefix_ref, got_ref, state_ref, send_ref):
     core, place, later = spot_ref[0], spot_ref[1], spot_ref[2] == 1
-    heads = prefix_ref.shape[0]
-    places, rows, _ = keep_ref.shape
+    places, rows, _ = send_ref.shape
     states = []
-    for h in range(heads):
+    for h in range(prefix_ref.shape[0]):
         prefix = prefix_ref[h]
         bias = prefix[:, DK:].astype(F32)
         joined = mm(prefix[:, :DK], got_ref[h]) + bias
         states.append(jnp.where(later, joined, bias).astype(BF16))
+        state_ref[h] = states[h]
     for d in range(places):
-        at = jnp.bitwise_xor(place, d)
-        for out_ref, side in ((send_ref, 1 - core), (keep_ref, core)):
-            tokens = pl.ds(pl.multiple_of((2 * at + side) * rows, rows), rows)
-            for h in range(heads):
-                lanes = slice(h * DV, (h + 1) * DV)
-                readout = own_ref[tokens, lanes] + mm(lin_ref[tokens, lanes], states[h])
-                scale = lax.rsqrt(jnp.mean(readout * readout, axis=1, keepdims=True) + EPS)
-                gate = gate_ref[tokens, lanes].astype(F32)
-                gated = gain_ref[...] * gate / (1.0 + jnp.exp(-gate))
-                out_ref[d, :, lanes] = (readout * scale * gated).astype(BF16)
-
-
-def project_kernel(keep_ref, got_ref, own_ref, sib_ref, *out_refs):
+        tokens = rows_of(place, 1 - core, d, rows)
+        send_ref[d] = mixed_rows(tokens, states, gain_ref, gate_ref, lin_ref, own_ref)
+
+
+def keep_kernel(spot_ref, gain_ref, gate_ref, lin_ref, own_ref, state_ref, keep_ref):
+    core, place = spot_ref[0], spot_ref[1]
+    states = [state_ref[h] for h in range(state_ref.shape[0])]
+    places, rows, _ = keep_ref.shape
+    for d in range(places):
+        tokens = rows_of(place, core, d, rows)
+        keep_ref[d] = mixed_rows(tokens, states, gain_ref, gate_ref, lin_ref, own_ref)
+
+
+def project_kernel(start, keep_ref, got_ref, own_ref, sib_ref, *out_refs):
     places, rows, depth = keep_ref.shape
-    width = out_refs[0].shape[1]
+    part, width = out_refs[0].shape
+    keep, got = (
+        jnp.concatenate([ref[d, start : start + part] for d in range(places)], axis=0)
+        for ref in (keep_ref, got_ref)
+    )
     tile = 512
     for lead in range(0, width, tile):
         lanes = slice(lead, lead + tile)
-        product = jnp.dot(
-            keep_ref[...].reshape(-1, depth), own_ref[:, lanes], preferred_element_type=F32
-        ) + jnp.dot(got_ref[...].reshape(-1, depth), sib_ref[:, lanes], preferred_element_type=F32)
-        start = 0
-        for lead_ref in range(0, len(out_refs), places):
-            part = out_refs[lead_ref].shape[0]
-            for d in range(places):
-                at = d * rows + start
-                out_refs[lead_ref + d][:, lanes] = product[at : at + part].astype(BF16)
-            start += part
+        product = jnp.dot(keep, own_ref[:, lanes], preferred_element_type=F32) + jnp.dot(
+            got, sib_ref[:, lanes], preferred_element_type=F32
+        )
+        for d, out_ref in enumerate(out_refs):
+            out_ref[:, lanes] = product[d * part : (d + 1) * part].astype(BF16)
 
 
 def project(keep, got, own, sib, sizes):
-    places, rows, _ = keep.shape
-    outs = resident(
-        project_kernel,
-        [shape((size, own.shape[1]), BF16) for size in sizes for _ in range(places)],
-        keep,
-        got,
-        own,
-        sib,
-    )
-    return [outs[c * places : (c + 1) * places] for c in range(len(sizes))]
+    places = keep.shape[0]
+    chunks = []
+    for number, size in enumerate(sizes):
+        chunks.append(
+            resident(
+                functools.partial(project_kernel, sum(sizes[:number])),
+                (shape((size, own.shape[1]), BF16),) * places,
+                keep,
+                after(got, chunks[-1][0]) if chunks else got,
+                own,
+                sib,
+                flops=5 * 10**8,
+            )
+        )
+    return chunks
 
 
 def norm_kernel(start, hidden_ref, gain_ref, routes_ref, *refs):
@@ -510,19 +546,26 @@
     gate_here, out_own, out_sib = fetched
 
     half = shape((places, tok, heads * DV), BF16)
-    keep, send = resident(
-        mix_kernel,
-        (half, half),
-        head_gain.reshape(1, DV),
-        gate_here,
-        lin,
-        own_read,
+    where = jnp.stack([core, place, later])
+    readout_parts = (head_gain.reshape(1, DV), gate_here, lin, own_read)
+    state, send = resident(
+        send_kernel,
+        (shape((heads, DK, DV), BF16), half),
+        *readout_parts,
         before,
         got,
-        scalars=jnp.stack([core, place, later]),
+        scalars=where,
         flops=10**9,
     )
     got = lax.ppermute(send, "exp", swap)
+    (keep,) = resident(
+        keep_kernel,
+        (half,),
+        *readout_parts,
+        state,
+        scalars=where,
+        flops=10**9,
+    )
     spot = jnp.stack([place, core])
     sizes = SIZES if sum(SIZES) == tok else (tok // 2, tok // 2)
     starts = [sum(sizes[:i]) for i in range(len(sizes))]

time: 89.7 us -> 88.4 us (0.986)
  waiting for transfers between devices: 27.2 us -> 24.5 us
    ppermute x18, waiting for transfers between devices: 25 us -> 23.1 us  [exchange(): lax.ppermute(piece, 'exp', between_places(lax.axis_size('exp') // 2, d))]
    ppermute x1, waiting for transfers between devices: 1.52 us -> 0.54 us  [per_device(): got = lax.ppermute(send, 'exp', swap)]
    pallas_call x7 -> x9, Pallas kernels: 8.28 us -> 9.14 us  [resident(): pl.pallas_call(kernel, out_shape=tuple(outs), in_specs=([] if scalars is...]
  transfers between devices with their start and end apart: 25 -> 25, of which waited for: 13 -> 14; matrix products, arithmetic and copies ran while one was open for 0% -> 0% of each run, Pallas kernels for 22% -> 24%
where the time goes in v6:
time: 88.4 us; the launch traced here: 88.1 us
  starting transfers between devices  33.7 us (38%)
  waiting for transfers between devices  24.5 us (28%)
  Pallas kernels  23.5 us (27%)
  local copies, waits for them, and re-layouts  5.01 us (6%)
  other arithmetic  1.17 us (1%)
    ppermute x18, starting transfers between devices, exchange(): lax.ppermute(piece, 'exp', between_places(lax.axis_size('exp') // 2, d))  27.8 us
    ppermute x18, waiting for transfers between devices, exchange(): lax.ppermute(piece, 'exp', between_places(lax.axis_size('exp') // 2, d))  23.1 us
    pallas_call x2, Pallas kernels, call(): pl.pallas_call(kernel, grid=(1,), out_shape=tuple(outs), in_specs=([] if...  9.95 us
    pallas_call x9, Pallas kernels, resident(): pl.pallas_call(kernel, out_shape=tuple(outs), in_specs=([] if scalars is...  9.14 us
    unnamed x40, local copies, waits for them, and re-layouts  4.98 us
    ppermute x2, starting transfers between devices, per_device(): got = lax.ppermute(summed, 'seq', [(i, i ^ step) for i in range(seqs)])  4.76 us
    pallas_call x2, Pallas kernels, fetch(): pl.pallas_call(fetch_kernel, out_shape=tuple((shape(a.shape, a.dtype) for...  4.43 us
  transfers between devices with their start and end apart: 25, of which 14 were waited for; matrix products, arithmetic and copies ran while one was open for 0% of the time, Pallas kernels for 24%

profile of v6, /device:TPU:0, one launch (start us, length us, event | category | flops | bytes accessed | tf_op | source)
XLA Modules:
  0.0 88.1 jit_solution(1557832127417308594)
XLA Ops:
  0.0 0.5 collective-permute-start
  0.5 0.5 collective-permute-start.4
  1.1 7.4 %shard_map.145 = (bf16[4,4,128,256]{3,2,1,0:T(8,128)(2,1)}, bf16[4,4,128,256]{3,2,1,0:T(8,128)(2,1)}, bf16[4,128,256]{2,1,0:T(8,128)(2,1)}) custom-call(bf16[512,256]{1,0:T(8,128)(2,1)} %key_ref.3, bf16[512,512]{1,0:T(8,128)(2,1)} %value_ref.1, f32[4,512]{1,0:T(4,128)} %decay_ref.3, f32[4,512]{1,0:T(4,128)} %rate_ref.1), custom_call_target="tpu_custom_call" | custom-call | flops 10000000000 | bytes 3162112 | tf_op jit(solution)/shard_map/pallas_call | solution.py:78
  8.5 2.9 %collective-permute-start.1 = (bf16[4,128,256]{2,1,0:T(8,128)(2,1)}, bf16[4,128,256]{2,1,0:T(8,128)(2,1)S(1)}, u32[]{:S(2)}, u32[]{:S(2)}) collective-permute-start(bf16[4,128,256]{2,1,0:T(8,128)(2,1)} %get-tuple-element.75.own_ref), channel_id=1, source_target_pairs={{0,8},{8,0},{16,24},{24,16},{1,9},{9,1},{17,25},{25,17},{2,10},{10... | collective-permute-start | bytes 786440 | tf_op jit(solution)/shard_map/ppermute | solution.py:531
  11.5 1.2 %copy-done.18 = bf16[4,4,128,256]{3,2,1,0:T(8,128)(2,1)S(1)} copy-done((bf16[4,4,128,256]{3,2,1,0:T(8,128)(2,1)S(1)}, bf16[4,4,128,256]{3,2,1,0:T(8,128)(2,1)}, u32[]{:S(2)}) %copy-start.18) | copy-done | bytes 1048600
  12.7 1.2 %copy-done.19 = bf16[4,4,128,256]{3,2,1,0:T(8,128)(2,1)S(1)} copy-done((bf16[4,4,128,256]{3,2,1,0:T(8,128)(2,1)S(1)}, bf16[4,4,128,256]{3,2,1,0:T(8,128)(2,1)}, u32[]{:S(2)}) %copy-start.19) | copy-done | bytes 1048600
  13.9 2.6 %shard_map.146 = (bf16[512,512]{1,0:T(8,128)(2,1)S(1)}, f32[512,512]{1,0:T(8,128)S(1)}, bf16[64,128]{1,0:T(8,128)(2,1)S(1)}) custom-call(bf16[512,256]{1,0:T(8,128)(2,1)S(1)} %copy-done.8, bf16[512,256]{1,0:T(8,128)(2,1)S(1)} %copy-done.9, f32[4,512]{1,0:T(4,128)S(1)} %copy-done.10, s32[4,64]{1,0:T(4,128)S(1)} %bitcast.10, bf16[4,64]{1,0:T(4,128)(2,1)S(1)} %bitcast.11, ...), custom_call_target="tpu_custom_call" | custom-call | flops 4000000000 | bytes 4220416 | tf_op jit(solution)/shard_map/pallas_call | solution.py:78
  16.5 0.8 copy-done.16
  17.3 0.8 collective-permute-done.1.got_ref
  18.4 1.8 %collective-permute-start.2 = (bf16[4,128,128]{2,1,0:T(8,128)(2,1)S(1)}, bf16[4,128,128]{2,1,0:T(8,128)(2,1)S(1)}, u32[]{:S(2)}, u32[]{:S(2)}) collective-permute-start(bf16[4,128,128]{2,1,0:T(8,128)(2,1)S(1)} %get-tuple-element.78), channel_id=1, source_target_pairs={{0,16},{8,24},{16,0},{24,8},{1,17},{9,25},{17,1},{25,9},{2,18},{10... | collective-permute-start | bytes 393224 | tf_op jit(solution)/shard_map/ppermute | solution.py:531
  20.3 1.6 %copy-done.3 = bf16[512,2048]{1,0:T(8,128)(2,1)S(1)} copy-done((bf16[512,2048]{1,0:T(8,128)(2,1)S(1)}, bf16[512,2048]{1,0:T(8,128)(2,1)}, u32[]{:S(2)}) %copy-start.3) | copy-done | bytes 2097176
  21.9 1.9 %shard_map.148 = (bf16[512,512]{1,0:T(8,128)(2,1)S(1)}, bf16[512,2048]{1,0:T(8,128)(2,1)S(1)}, bf16[512,2048]{1,0:T(8,128)(2,1)S(1)}) custom-call(bf16[512,512]{1,0:T(8,128)(2,1)S(1)} %copy-done.5, bf16[512,2048]{1,0:T(8,128)(2,1)S(1)} %copy-done.3, bf16[512,2048]{1,0:T(8,128)(2,1)} %collective-permute-done.refs_2_), custom_call_target="tpu_custom_call" | custom-call | bytes 9437184 | tf_op jit(solution)/shard_map/pallas_call | solution.py:45
  23.9 1.1 %shard_map.149 = (bf16[4,128,128]{2,1,0:T(8,128)(2,1)S(1)}, bf16[4,64,512]{2,1,0:T(8,128)(2,1)S(1)}) custom-call(s32[3]{0:T(128)S(1)} %pad_add_fusion.spot_ref, f32[1,128]{1,0:T(1,128)S(1)} %bitcast.12, bf16[512,512]{1,0:T(8,128)(2,1)S(1)} %get-tuple-element.84.gate_ref, bf16[512,512]{1,0:T(8,128)(2,1)S(1)} %copy-done.17, f32[512,512]{1,0:T(8,128)S(1)} %copy-done.15, ...), custom_call_target="tpu_custom_call" | custom-call | flops 1000000000 | bytes 2884096 | tf_op jit(solution)/shard_map/pallas_call | solution.py:60
  25.1 1.0 %shard_map.150.keep_ref = bf16[4,64,512]{2,1,0:T(8,128)(2,1)S(1)} custom-call(s32[3]{0:T(128)S(1)} %pad_add_fusion.spot_ref, f32[1,128]{1,0:T(1,128)S(1)} %bitcast.13, bf16[512,512]{1,0:T(8,128)(2,1)S(1)} %get-tuple-element.84.gate_ref, bf16[512,512]{1,0:T(8,128)(2,1)S(1)} %copy-done.17, f32[512,512]{1,0:T(8,128)S(1)} %copy-done.15, ...), custom_call_target="tpu_custom_call" | custom-call | flops 1000000000 | bytes 2490880 | tf_op jit(solution)/shard_map/pallas_call | solution.py:60
  26.1 0.5 collective-permute-done.6.got_ref
  26.7 0.7 shard_map.151
  27.4 1.7 %collective-permute-start.8 = (bf16[32,2048]{1,0:T(8,128)(2,1)S(1)}, bf16[32,2048]{1,0:T(8,128)(2,1)S(1)}, u32[]{:S(2)}, u32[]{:S(2)}) collective-permute-start(bf16[32,2048]{1,0:T(8,128)(2,1)S(1)} %get-tuple-element.97), channel_id=1, source_target_pairs={{0,2},{1,3},{2,0},{3,1},{4,6},{5,7},{6,4},{7,5},{8,10},{9,11},{10,... | collective-permute-start | bytes 393224 | tf_op jit(solution)/shard_map/ppermute | solution.py:439
  29.0 0.7 shard_map.152
  29.8 0.5 collective-permute-start.7
  30.3 3.4 %collective-permute-done.8 = bf16[32,2048]{1,0:T(8,128)(2,1)S(1)} collective-permute-done((bf16[32,2048]{1,0:T(8,128)(2,1)S(1)}, bf16[32,2048]{1,0:T(8,128)(2,1)S(1)}, u32[]{:S(2)}, u32[]{:S(2)}) %collective-permute-start.8) | collective-permute-done | bytes 131104 | tf_op jit(solution)/shard_map/ppermute | solution.py:439
  33.7 2.7 %collective-permute-start.9 = (bf16[32,2048]{1,0:T(8,128)(2,1)S(1)}, bf16[32,2048]{1,0:T(8,128)(2,1)S(1)}, u32[]{:S(2)}, u32[]{:S(2)}) collective-permute-start(bf16[32,2048]{1,0:T(8,128)(2,1)S(1)} %add_convert_fusion.5), channel_id=1, source_target_pairs={{0,4},{1,5},{2,6},{3,7},{4,0},{5,1},{6,2},{7,3},{8,12},{9,13},{10,... | collective-permute-start | bytes 393224 | tf_op jit(solution)/shard_map/ppermute | solution.py:439
  36.4 1.7 %collective-permute-start.10 = (bf16[32,2048]{1,0:T(8,128)(2,1)S(1)}, bf16[32,2048]{1,0:T(8,128)(2,1)S(1)}, u32[]{:S(2)}, u32[]{:S(2)}) collective-permute-start(bf16[32,2048]{1,0:T(8,128)(2,1)S(1)} %get-tuple-element.111), channel_id=1, source_target_pairs={{0,2},{1,3},{2,0},{3,1},{4,6},{5,7},{6,4},{7,5},{8,10},{9,11},{10,... | collective-permute-start | bytes 393224 | tf_op jit(solution)/shard_map/ppermute | solution.py:439
  38.2 2.0 %collective-permute-start.13 = (bf16[32,2304]{1,0:T(8,128)(2,1)S(1)}, bf16[32,2304]{1,0:T(8,128)(2,1)S(1)}, u32[]{:S(2)}, u32[]{:S(2)}) collective-permute-start(bf16[32,2304]{1,0:T(8,128)(2,1)S(1)} %pad.6), channel_id=1, source_target_pairs={{0,4},{1,5},{2,6},{3,7},{4,0},{5,1},{6,2},{7,3},{8,12},{9,13},{10,... | collective-permute-start | bytes 442376 | tf_op jit(solution)/shard_map/ppermute | solution.py:439
  40.1 2.5 %shard_map.153 = (bf16[1,2048,512]{2,1,0:T(8,128)(2,1)S(1)}, bf16[1,2048,512]{2,1,0:T(8,128)(2,1)S(1)}, bf16[1,512,2048]{2,1,0:T(8,128)(2,1)S(1)}) custom-call(bf16[1,2048,512]{2,1,0:T(8,128)(2,1)S(1)} %collective-permute-done.3.refs_0_, bf16[1,2048,512]{2,1,0:T(8,128)(2,1)} %collective-permute-done.4.refs_1_, ...), custom_call_target="tpu_custom_call" | custom-call | bytes 12582912 | tf_op jit(solution)/shard_map/pallas_call | solution.py:45
  42.7 0.7 collective-permute-done.9.refs_1_
  43.6 1.9 %collective-permute-start.11 = (bf16[32,2176]{1,0:T(8,128)(2,1)S(1)}, bf16[32,2176]{1,0:T(8,128)(2,1)S(1)}, u32[]{:S(2)}, u32[]{:S(2)}) collective-permute-start(bf16[32,2176]{1,0:T(8,128)(2,1)S(1)} %get-tuple-element.113.refs_0_), channel_id=1, source_target_pairs={{0,2},{1,3},{2,0},{3,1},{4,6},{5,7},{6,4},{7,5},{8,10},{9,11},{10,... | collective-permute-start | bytes 417800 | tf_op jit(solution)/shard_map/ppermute | solution.py:439
  45.4 3.8 %collective-permute-start.12 = (bf16[32,2176]{1,0:T(8,128)(2,1)S(1)}, bf16[32,2176]{1,0:T(8,128)(2,1)S(1)}, u32[]{:S(2)}, u32[]{:S(2)}) collective-permute-start(bf16[32,2176]{1,0:T(8,128)(2,1)S(1)} %get-tuple-element.113.refs_0_), channel_id=1, source_target_pairs={{0,4},{1,5},{2,6},{3,7},{4,0},{5,1},{6,2},{7,3},{8,12},{9,13},{10,... | collective-permute-start | bytes 417800 | tf_op jit(solution)/shard_map/ppermute | solution.py:439
  49.3 4.8 %collective-permute-done.11.refs_1_ = bf16[32,2176]{1,0:T(8,128)(2,1)S(1)} collective-permute-done((bf16[32,2176]{1,0:T(8,128)(2,1)S(1)}, bf16[32,2176]{1,0:T(8,128)(2,1)S(1)}, u32[]{:S(2)}, u32[]{:S(2)}) %collective-permute-start.11) | collective-permute-done | bytes 139296 | tf_op jit(solution)/shard_map/ppermute | solution.py:439
  54.3 1.2 %collective-permute-done.14.refs_2_ = bf16[32,2048]{1,0:T(8,128)(2,1)S(1)} collective-permute-done((bf16[32,2048]{1,0:T(8,128)(2,1)S(1)}, bf16[32,2048]{1,0:T(8,128)(2,1)S(1)}, u32[]{:S(2)}, u32[]{:S(2)}) %collective-permute-start.14) | collective-permute-done | bytes 131104 | tf_op jit(solution)/shard_map/ppermute | solution.py:439
  55.7 1.7 %collective-permute-start.17 = (bf16[32,2176]{1,0:T(8,128)(2,1)S(1)}, bf16[32,2176]{1,0:T(8,128)(2,1)S(1)}, u32[]{:S(2)}, u32[]{:S(2)}) collective-permute-start(bf16[32,2176]{1,0:T(8,128)(2,1)S(1)} %get-tuple-element.122.refs_0_), channel_id=1, source_target_pairs={{0,4},{1,5},{2,6},{3,7},{4,0},{5,1},{6,2},{7,3},{8,12},{9,13},{10,... | collective-permute-start | bytes 417800 | tf_op jit(solution)/shard_map/ppermute | solution.py:439
  57.3 2.5 %collective-permute-start.15 = (bf16[32,2176]{1,0:T(8,128)(2,1)S(1)}, bf16[32,2176]{1,0:T(8,128)(2,1)S(1)}, u32[]{:S(2)}, u32[]{:S(2)}) collective-permute-start(bf16[32,2176]{1,0:T(8,128)(2,1)S(1)} %collective-permute-done.12.refs_2_), channel_id=1, source_target_pairs={{0,2},{1,3},{2,0},{3,1},{4,6},{5,7},{6,4},{7,5},{8,10},{9,11},{10,... | collective-permute-start | bytes 417800 | tf_op jit(solution)/shard_map/ppermute | solution.py:439
  59.9 2.6 %collective-permute-done.17.refs_2_ = bf16[32,2176]{1,0:T(8,128)(2,1)S(1)} collective-permute-done((bf16[32,2176]{1,0:T(8,128)(2,1)S(1)}, bf16[32,2176]{1,0:T(8,128)(2,1)S(1)}, u32[]{:S(2)}, u32[]{:S(2)}) %collective-permute-start.17) | collective-permute-done | bytes 139296 | tf_op jit(solution)/shard_map/ppermute | solution.py:439
  62.5 1.9 %collective-permute-start.18 = (bf16[32,2176]{1,0:T(8,128)(2,1)S(1)}, bf16[32,2176]{1,0:T(8,128)(2,1)S(1)}, u32[]{:S(2)}, u32[]{:S(2)}) collective-permute-start(bf16[32,2176]{1,0:T(8,128)(2,1)S(1)} %collective-permute-done.17.refs_2_), channel_id=1, source_target_pairs={{0,2},{1,3},{2,0},{3,1},{4,6},{5,7},{6,4},{7,5},{8,10},{9,11},{10,... | collective-permute-start | bytes 417800 | tf_op jit(solution)/shard_map/ppermute | solution.py:439
  64.4 0.6 collective-permute-done.15.refs_3_
  65.0 2.5 %shard_map.156 = (bf16[32,2048]{1,0:T(8,128)(2,1)S(1)}, bf16[32,2048]{1,0:T(8,128)(2,1)S(1)}, bf16[32,2048]{1,0:T(8,128)(2,1)S(1)}, bf16[32,2048]{1,0:T(8,128)(2,1)S(1)}) custom-call(s32[2]{0:T(128)S(1)} %pad_add_fusion.1.spot_ref, bf16[32,2176]{1,0:T(8,128)(2,1)S(1)} %get-tuple-element.113.refs_0_, bf16[32,2176]{1,0:T(8,128)(2,1)S(1)} %collective-permute-done.11.refs_1_, ...), custom_call_target="tpu_custom_call" | custom-call | flops 3000000000 | bytes 13664256 | tf_op jit(solution)/shard_map/pallas_call | solution.py:60
  67.5 1.4 %collective-permute-start.20 = (bf16[32,2048]{1,0:T(8,128)(2,1)S(1)}, bf16[32,2048]{1,0:T(8,128)(2,1)S(1)}, u32[]{:S(2)}, u32[]{:S(2)}) collective-permute-start(bf16[32,2048]{1,0:T(8,128)(2,1)S(1)} %get-tuple-element.127), channel_id=1, source_target_pairs={{0,2},{1,3},{2,0},{3,1},{4,6},{5,7},{6,4},{7,5},{8,10},{9,11},{10,... | collective-permute-start | bytes 393224 | tf_op jit(solution)/shard_map/ppermute | solution.py:439
  68.9 1.5 %collective-permute-done.18.refs_3_ = bf16[32,2176]{1,0:T(8,128)(2,1)S(1)} collective-permute-done((bf16[32,2176]{1,0:T(8,128)(2,1)S(1)}, bf16[32,2176]{1,0:T(8,128)(2,1)S(1)}, u32[]{:S(2)}, u32[]{:S(2)}) %collective-permute-start.18) | collective-permute-done | bytes 139296 | tf_op jit(solution)/shard_map/ppermute | solution.py:439
  70.5 2.5 %shard_map.157 = (bf16[32,2048]{1,0:T(8,128)(2,1)S(1)}, bf16[32,2048]{1,0:T(8,128)(2,1)S(1)}, bf16[32,2048]{1,0:T(8,128)(2,1)S(1)}, bf16[32,2048]{1,0:T(8,128)(2,1)S(1)}) custom-call(s32[2]{0:T(128)S(1)} %pad_add_fusion.1.spot_ref, bf16[32,2176]{1,0:T(8,128)(2,1)S(1)} %get-tuple-element.122.refs_0_, bf16[32,2176]{1,0:T(8,128)(2,1)S(1)} %collective-permute-done.16.refs_1_, ...), custom_call_target="tpu_custom_call" | custom-call | flops 3000000000 | bytes 13664256 | tf_op jit(solution)/shard_map/pallas_call | solution.py:60
  73.0 0.3 collective-permute-start.19
  73.3 2.9 %collective-permute-start.21 = (bf16[32,2048]{1,0:T(8,128)(2,1)S(1)}, bf16[32,2048]{1,0:T(8,128)(2,1)S(1)}, u32[]{:S(2)}, u32[]{:S(2)}) collective-permute-start(bf16[32,2048]{1,0:T(8,128)(2,1)S(1)} %add_convert_fusion.3), channel_id=1, source_target_pairs={{0,4},{1,5},{2,6},{3,7},{4,0},{5,1},{6,2},{7,3},{8,12},{9,13},{10,... | collective-permute-start | bytes 393224 | tf_op jit(solution)/shard_map/ppermute | solution.py:439
  76.2 1.5 %collective-permute-start.22 = (bf16[32,2048]{1,0:T(8,128)(2,1)S(1)}, bf16[32,2048]{1,0:T(8,128)(2,1)S(1)}, u32[]{:S(2)}, u32[]{:S(2)}) collective-permute-start(bf16[32,2048]{1,0:T(8,128)(2,1)S(1)} %get-tuple-element.131), channel_id=1, source_target_pairs={{0,2},{1,3},{2,0},{3,1},{4,6},{5,7},{6,4},{7,5},{8,10},{9,11},{10,... | collective-permute-start | bytes 393224 | tf_op jit(solution)/shard_map/ppermute | solution.py:439
  77.8 2.2 %collective-permute-done.19 = bf16[32,2048]{1,0:T(8,128)(2,1)S(1)} collective-permute-done((bf16[32,2048]{1,0:T(8,128)(2,1)S(1)}, bf16[32,2048]{1,0:T(8,128)(2,1)S(1)}, u32[]{:S(2)}, u32[]{:S(2)}) %collective-permute-start.19) | collective-permute-done | bytes 131104 | tf_op jit(solution)/shard_map/ppermute | solution.py:439
  80.0 0.6 collective-permute-start.23
  80.7 0.8 collective-permute-start.24
  81.4 2.4 %collective-permute-done.22 = bf16[32,2048]{1,0:T(8,128)(2,1)S(1)} collective-permute-done((bf16[32,2048]{1,0:T(8,128)(2,1)S(1)}, bf16[32,2048]{1,0:T(8,128)(2,1)S(1)}, u32[]{:S(2)}, u32[]{:S(2)}) %collective-permute-start.22) | collective-permute-done | bytes 131104 | tf_op jit(solution)/shard_map/ppermute | solution.py:439
  83.9 2.6 %collective-permute-done.24 = bf16[32,2048]{1,0:T(8,128)(2,1)S(1)} collective-permute-done((bf16[32,2048]{1,0:T(8,128)(2,1)S(1)}, bf16[32,2048]{1,0:T(8,128)(2,1)S(1)}, u32[]{:S(2)}, u32[]{:S(2)}) %collective-permute-start.24) | collective-permute-done | bytes 131104 | tf_op jit(solution)/shard_map/ppermute | solution.py:439
  86.4 0.9 %collective-permute-done.23 = bf16[32,2048]{1,0:T(8,128)(2,1)S(1)} collective-permute-done((bf16[32,2048]{1,0:T(8,128)(2,1)S(1)}, bf16[32,2048]{1,0:T(8,128)(2,1)S(1)}, u32[]{:S(2)}, u32[]{:S(2)}) %collective-permute-start.23) | collective-permute-done | bytes 131104 | tf_op jit(solution)/shard_map/ppermute | solution.py:439
  87.4 0.7 pad_maximum_fusion
  (68 shorter events, 1.7 us)
Async XLA Ops:
  0.0 8.5 %collective-permute-start = (bf16[512,2048]{1,0:T(8,128)(2,1)}, bf16[512,2048]{1,0:T(8,128)(2,1)}, u32[]{:S(2)}, u32[]{:S(2)}) collective-permute-start(bf16[512,2048]{1,0:T(8,128)(2,1)} %refs_1_.1), channel_id=1, source_target_pairs={{0,1},{1,0},{2,3},{3,2},{4,5},{5,4},{6,7},{7,6},{8,9},{9,8},{10,11... | collective-permute-start | bytes 6291464 | tf_op jit(solution)/shard_map/ppermute | solution.py:492
  0.5 23.4 %collective-permute-start.3 = (bf16[1,2048,512]{2,1,0:T(8,128)(2,1)}, bf16[1,2048,512]{2,1,0:T(8,128)(2,1)S(1)}, u32[]{:S(2)}, u32[]{:S(2)}) collective-permute-start(bf16[1,2048,512]{2,1,0:T(8,128)(2,1)} %refs_4_.3), channel_id=1, source_target_pairs={{0,1},{1,0},{2,3},{3,2},{4,5},{5,4},{6,7},{7,6},{8,9},{9,8},{10,11... | collective-permute-start | bytes 6291464 | tf_op jit(solution)/shard_map/ppermute | solution.py:494
  0.5 23.3 %collective-permute-start.4 = (bf16[1,2048,512]{2,1,0:T(8,128)(2,1)}, bf16[1,2048,512]{2,1,0:T(8,128)(2,1)}, u32[]{:S(2)}, u32[]{:S(2)}) collective-permute-start(bf16[1,2048,512]{2,1,0:T(8,128)(2,1)} %refs_5_.3), channel_id=1, source_target_pairs={{0,1},{1,0},{2,3},{3,2},{4,5},{5,4},{6,7},{7,6},{8,9},{9,8},{10,11... | collective-permute-start | bytes 6291464 | tf_op jit(solution)/shard_map/ppermute | solution.py:494
  1.0 22.9 %collective-permute-start.5 = (bf16[1,512,2048]{2,1,0:T(8,128)(2,1)}, bf16[1,512,2048]{2,1,0:T(8,128)(2,1)}, u32[]{:S(2)}, u32[]{:S(2)}) collective-permute-start(bf16[1,512,2048]{2,1,0:T(8,128)(2,1)} %refs_6_.3), channel_id=1, source_target_pairs={{0,1},{1,0},{2,3},{3,2},{4,5},{5,4},{6,7},{7,6},{8,9},{9,8},{10,11... | collective-permute-start | bytes 6291464 | tf_op jit(solution)/shard_map/ppermute | solution.py:494
  1.1 10.4 %copy-start.8 = (bf16[512,256]{1,0:T(8,128)(2,1)S(1)}, bf16[512,256]{1,0:T(8,128)(2,1)}, u32[]{:S(2)}) copy-start(bf16[512,256]{1,0:T(8,128)(2,1)} %query_ref.1) | copy-start | bytes 786436
  1.1 10.4 %copy-start.9 = (bf16[512,256]{1,0:T(8,128)(2,1)S(1)}, bf16[512,256]{1,0:T(8,128)(2,1)}, u32[]{:S(2)}) copy-start(bf16[512,256]{1,0:T(8,128)(2,1)} %key_ref.3) | copy-start | bytes 786436
  1.1 10.3 %copy-start.10 = (f32[4,512]{1,0:T(4,128)S(1)}, f32[4,512]{1,0:T(4,128)}, u32[]{:S(2)}) copy-start(f32[4,512]{1,0:T(4,128)} %decay_ref.3) | copy-start | bytes 24580
  1.1 10.3 %copy-start.11 = (s32[64,4]{0,1:T(4,128)S(1)}, s32[64,4]{0,1:T(4,128)}, u32[]{:S(2)}) copy-start(s32[64,4]{0,1:T(4,128)} %param.25) | copy-start | bytes 3076
  1.1 10.3 %copy-start.12 = (bf16[64,4]{0,1:T(4,128)(2,1)S(1)}, bf16[64,4]{0,1:T(4,128)(2,1)}, u32[]{:S(2)}) copy-start(bf16[64,4]{0,1:T(4,128)(2,1)} %param.26) | copy-start | bytes 1540
  8.5 9.6 %collective-permute-start.1 = (bf16[4,128,256]{2,1,0:T(8,128)(2,1)}, bf16[4,128,256]{2,1,0:T(8,128)(2,1)S(1)}, u32[]{:S(2)}, u32[]{:S(2)}) collective-permute-start(bf16[4,128,256]{2,1,0:T(8,128)(2,1)} %get-tuple-element.75.own_ref), channel_id=1, source_target_pairs={{0,8},{8,0},{16,24},{24,16},{1,9},{9,1},{17,25},{25,17},{2,10},{10... | collective-permute-start | bytes 786440 | tf_op jit(solution)/shard_map/ppermute | solution.py:531
  11.4 1.2 %copy-start.18 = (bf16[4,4,128,256]{3,2,1,0:T(8,128)(2,1)S(1)}, bf16[4,4,128,256]{3,2,1,0:T(8,128)(2,1)}, u32[]{:S(2)}) copy-start(bf16[4,4,128,256]{3,2,1,0:T(8,128)(2,1)} %get-tuple-element.71.wu_ref) | copy-start | bytes 3145732
  12.7 1.2 %copy-start.19 = (bf16[4,4,128,256]{3,2,1,0:T(8,128)(2,1)S(1)}, bf16[4,4,128,256]{3,2,1,0:T(8,128)(2,1)}, u32[]{:S(2)}) copy-start(bf16[4,4,128,256]{3,2,1,0:T(8,128)(2,1)} %get-tuple-element.72.prefix_ref) | copy-start | bytes 3145732
  13.9 4.2 %copy-start.6 = (bf16[4,128,256]{2,1,0:T(8,128)(2,1)S(1)}, bf16[4,128,256]{2,1,0:T(8,128)(2,1)}, u32[]{:S(2)}) copy-start(bf16[4,128,256]{2,1,0:T(8,128)(2,1)} %get-tuple-element.75.own_ref) | copy-start | bytes 786436
  13.9 6.4 %copy-start.5 = (bf16[512,512]{1,0:T(8,128)(2,1)S(1)}, bf16[512,512]{1,0:T(8,128)(2,1)}, u32[]{:S(2)}) copy-start(bf16[512,512]{1,0:T(8,128)(2,1)} %refs_0_.1) | copy-start | bytes 1572868
  16.5 0.8 copy-start.16
  17.3 1.1 %copy-start.14 = (f32[512,512]{1,0:T(8,128)}, f32[512,512]{1,0:T(8,128)S(1)}, u32[]{:S(2)}) copy-start(f32[512,512]{1,0:T(8,128)S(1)} %get-tuple-element.85.own_ref) | copy-start | bytes 3145732
  18.4 5.4 %collective-permute-start.2 = (bf16[4,128,128]{2,1,0:T(8,128)(2,1)S(1)}, bf16[4,128,128]{2,1,0:T(8,128)(2,1)S(1)}, u32[]{:S(2)}, u32[]{:S(2)}) collective-permute-start(bf16[4,128,128]{2,1,0:T(8,128)(2,1)S(1)} %get-tuple-element.78), channel_id=1, source_target_pairs={{0,16},{8,24},{16,0},{24,8},{1,17},{9,25},{17,1},{25,9},{2,18},{10... | collective-permute-start | bytes 393224 | tf_op jit(solution)/shard_map/ppermute | solution.py:531
  20.3 1.6 %copy-start.3 = (bf16[512,2048]{1,0:T(8,128)(2,1)S(1)}, bf16[512,2048]{1,0:T(8,128)(2,1)}, u32[]{:S(2)}) copy-start(bf16[512,2048]{1,0:T(8,128)(2,1)} %refs_1_.1) | copy-start | bytes 6291460
  21.9 2.0 %copy-start.13 = (f32[128]{0:T(128)S(1)}, f32[128]{0:T(128)}, u32[]{:S(2)}) copy-start(f32[128]{0:T(128)} %param.22) | copy-start | bytes 1540
  21.9 2.0 %copy-start.15 = (f32[512,512]{1,0:T(8,128)S(1)}, f32[512,512]{1,0:T(8,128)}, u32[]{:S(2)}) copy-start(f32[512,512]{1,0:T(8,128)} %copy-done.14) | copy-start | bytes 3145732
  21.9 2.0 %copy-start.17 = (bf16[512,512]{1,0:T(8,128)(2,1)S(1)}, bf16[512,512]{1,0:T(8,128)(2,1)}, u32[]{:S(2)}) copy-start(bf16[512,512]{1,0:T(8,128)(2,1)} %copy-done.16) | copy-start | bytes 1572868
  25.1 1.6 %collective-permute-start.6 = (bf16[4,64,512]{2,1,0:T(8,128)(2,1)S(1)}, bf16[4,64,512]{2,1,0:T(8,128)(2,1)S(1)}, u32[]{:S(2)}, u32[]{:S(2)}) collective-permute-start(bf16[4,64,512]{2,1,0:T(8,128)(2,1)S(1)} %get-tuple-element.89), channel_id=1, source_target_pairs={{0,1},{1,0},{2,3},{3,2},{4,5},{5,4},{6,7},{7,6},{8,9},{9,8},{10,11... | collective-permute-start | bytes 786440 | tf_op jit(solution)/shard_map/ppermute | solution.py:560
  27.4 6.3 %collective-permute-start.8 = (bf16[32,2048]{1,0:T(8,128)(2,1)S(1)}, bf16[32,2048]{1,0:T(8,128)(2,1)S(1)}, u32[]{:S(2)}, u32[]{:S(2)}) collective-permute-start(bf16[32,2048]{1,0:T(8,128)(2,1)S(1)} %get-tuple-element.97), channel_id=1, source_target_pairs={{0,2},{1,3},{2,0},{3,1},{4,6},{5,7},{6,4},{7,5},{8,10},{9,11},{10,... | collective-permute-start | bytes 393224 | tf_op jit(solution)/shard_map/ppermute | solution.py:439
  29.8 6.6 %collective-permute-start.7 = (bf16[32,2048]{1,0:T(8,128)(2,1)S(1)}, bf16[32,2048]{1,0:T(8,128)(2,1)S(1)}, u32[]{:S(2)}, u32[]{:S(2)}) collective-permute-start(bf16[32,2048]{1,0:T(8,128)(2,1)S(1)} %get-tuple-element.95), channel_id=1, source_target_pairs={{0,2},{1,3},{2,0},{3,1},{4,6},{5,7},{6,4},{7,5},{8,10},{9,11},{10,... | collective-permute-start | bytes 393224 | tf_op jit(solution)/shard_map/ppermute | solution.py:439
  33.7 9.7 %collective-permute-start.9 = (bf16[32,2048]{1,0:T(8,128)(2,1)S(1)}, bf16[32,2048]{1,0:T(8,128)(2,1)S(1)}, u32[]{:S(2)}, u32[]{:S(2)}) collective-permute-start(bf16[32,2048]{1,0:T(8,128)(2,1)S(1)} %add_convert_fusion.5), channel_id=1, source_target_pairs={{0,4},{1,5},{2,6},{3,7},{4,0},{5,1},{6,2},{7,3},{8,12},{9,13},{10,... | collective-permute-start | bytes 393224 | tf_op jit(solution)/shard_map/ppermute | solution.py:439
  36.4 7.0 %collective-permute-start.10 = (bf16[32,2048]{1,0:T(8,128)(2,1)S(1)}, bf16[32,2048]{1,0:T(8,128)(2,1)S(1)}, u32[]{:S(2)}, u32[]{:S(2)}) collective-permute-start(bf16[32,2048]{1,0:T(8,128)(2,1)S(1)} %get-tuple-element.111), channel_id=1, source_target_pairs={{0,2},{1,3},{2,0},{3,1},{4,6},{5,7},{6,4},{7,5},{8,10},{9,11},{10,... | collective-permute-start | bytes 393224 | tf_op jit(solution)/shard_map/ppermute | solution.py:439
  38.1 5.3 %copy-start.4 = (bf16[64,2048]{1,0:T(8,128)(2,1)S(1)}, bf16[64,2048]{1,0:T(8,128)(2,1)}, u32[]{:S(2)}) copy-start(bf16[64,2048]{1,0:T(8,128)(2,1)} %hidden_ref.3) | copy-start | bytes 786436
  38.2 5.3 %copy-start.7 = (f32[2048]{0:T(1024)S(1)}, f32[2048]{0:T(1024)}, u32[]{:S(2)}) copy-start(f32[2048]{0:T(1024)} %param.24) | copy-start | bytes 24580
  38.2 17.3 %collective-permute-start.13 = (bf16[32,2304]{1,0:T(8,128)(2,1)S(1)}, bf16[32,2304]{1,0:T(8,128)(2,1)S(1)}, u32[]{:S(2)}, u32[]{:S(2)}) collective-permute-start(bf16[32,2304]{1,0:T(8,128)(2,1)S(1)} %pad.6), channel_id=1, source_target_pairs={{0,4},{1,5},{2,6},{3,7},{4,0},{5,1},{6,2},{7,3},{8,12},{9,13},{10,... | collective-permute-start | bytes 442376 | tf_op jit(solution)/shard_map/ppermute | solution.py:439
  40.1 24.9 %copy-start = (bf16[1,2048,512]{2,1,0:T(8,128)(2,1)S(1)}, bf16[1,2048,512]{2,1,0:T(8,128)(2,1)}, u32[]{:S(2)}) copy-start(bf16[1,2048,512]{2,1,0:T(8,128)(2,1)} %refs_4_.3) | copy-start | bytes 6291460
  40.1 24.9 %copy-start.1 = (bf16[1,2048,512]{2,1,0:T(8,128)(2,1)S(1)}, bf16[1,2048,512]{2,1,0:T(8,128)(2,1)}, u32[]{:S(2)}) copy-start(bf16[1,2048,512]{2,1,0:T(8,128)(2,1)} %refs_5_.3) | copy-start | bytes 6291460
  40.1 24.9 %copy-start.2 = (bf16[1,512,2048]{2,1,0:T(8,128)(2,1)S(1)}, bf16[1,512,2048]{2,1,0:T(8,128)(2,1)}, u32[]{:S(2)}) copy-start(bf16[1,512,2048]{2,1,0:T(8,128)(2,1)} %refs_6_.3) | copy-start | bytes 6291460
  43.6 10.5 %collective-permute-start.11 = (bf16[32,2176]{1,0:T(8,128)(2,1)S(1)}, bf16[32,2176]{1,0:T(8,128)(2,1)S(1)}, u32[]{:S(2)}, u32[]{:S(2)}) collective-permute-start(bf16[32,2176]{1,0:T(8,128)(2,1)S(1)} %get-tuple-element.113.refs_0_), channel_id=1, source_target_pairs={{0,2},{1,3},{2,0},{3,1},{4,6},{5,7},{6,4},{7,5},{8,10},{9,11},{10,... | collective-permute-start | bytes 417800 | tf_op jit(solution)/shard_map/ppermute | solution.py:439
  45.4 8.8 %collective-permute-start.12 = (bf16[32,2176]{1,0:T(8,128)(2,1)S(1)}, bf16[32,2176]{1,0:T(8,128)(2,1)S(1)}, u32[]{:S(2)}, u32[]{:S(2)}) collective-permute-start(bf16[32,2176]{1,0:T(8,128)(2,1)S(1)} %get-tuple-element.113.refs_0_), channel_id=1, source_target_pairs={{0,4},{1,5},{2,6},{3,7},{4,0},{5,1},{6,2},{7,3},{8,12},{9,13},{10,... | collective-permute-start | bytes 417800 | tf_op jit(solution)/shard_map/ppermute | solution.py:439
  49.2 6.3 %collective-permute-start.14 = (bf16[32,2048]{1,0:T(8,128)(2,1)S(1)}, bf16[32,2048]{1,0:T(8,128)(2,1)S(1)}, u32[]{:S(2)}, u32[]{:S(2)}) collective-permute-start(bf16[32,2048]{1,0:T(8,128)(2,1)S(1)} %get-tuple-element.118), channel_id=1, source_target_pairs={{0,2},{1,3},{2,0},{3,1},{4,6},{5,7},{6,4},{7,5},{8,10},{9,11},{10,... | collective-permute-start | bytes 393224 | tf_op jit(solution)/shard_map/ppermute | solution.py:439
  55.7 6.9 %collective-permute-start.17 = (bf16[32,2176]{1,0:T(8,128)(2,1)S(1)}, bf16[32,2176]{1,0:T(8,128)(2,1)S(1)}, u32[]{:S(2)}, u32[]{:S(2)}) collective-permute-start(bf16[32,2176]{1,0:T(8,128)(2,1)S(1)} %get-tuple-element.122.refs_0_), channel_id=1, source_target_pairs={{0,4},{1,5},{2,6},{3,7},{4,0},{5,1},{6,2},{7,3},{8,12},{9,13},{10,... | collective-permute-start | bytes 417800 | tf_op jit(solution)/shard_map/ppermute | solution.py:439
  57.3 7.7 %collective-permute-start.15 = (bf16[32,2176]{1,0:T(8,128)(2,1)S(1)}, bf16[32,2176]{1,0:T(8,128)(2,1)S(1)}, u32[]{:S(2)}, u32[]{:S(2)}) collective-permute-start(bf16[32,2176]{1,0:T(8,128)(2,1)S(1)} %collective-permute-done.12.refs_2_), channel_id=1, source_target_pairs={{0,2},{1,3},{2,0},{3,1},{4,6},{5,7},{6,4},{7,5},{8,10},{9,11},{10,... | collective-permute-start | bytes 417800 | tf_op jit(solution)/shard_map/ppermute | solution.py:439
  59.9 9.1 %collective-permute-start.16 = (bf16[32,2176]{1,0:T(8,128)(2,1)S(1)}, bf16[32,2176]{1,0:T(8,128)(2,1)S(1)}, u32[]{:S(2)}, u32[]{:S(2)}) collective-permute-start(bf16[32,2176]{1,0:T(8,128)(2,1)S(1)} %get-tuple-element.122.refs_0_), channel_id=1, source_target_pairs={{0,2},{1,3},{2,0},{3,1},{4,6},{5,7},{6,4},{7,5},{8,10},{9,11},{10,... | collective-permute-start | bytes 417800 | tf_op jit(solution)/shard_map/ppermute | solution.py:439
  62.5 7.9 %collective-permute-start.18 = (bf16[32,2176]{1,0:T(8,128)(2,1)S(1)}, bf16[32,2176]{1,0:T(8,128)(2,1)S(1)}, u32[]{:S(2)}, u32[]{:S(2)}) collective-permute-start(bf16[32,2176]{1,0:T(8,128)(2,1)S(1)} %collective-permute-done.17.refs_2_), channel_id=1, source_target_pairs={{0,2},{1,3},{2,0},{3,1},{4,6},{5,7},{6,4},{7,5},{8,10},{9,11},{10,... | collective-permute-start | bytes 417800 | tf_op jit(solution)/shard_map/ppermute | solution.py:439
  67.5 5.8 %collective-permute-start.20 = (bf16[32,2048]{1,0:T(8,128)(2,1)S(1)}, bf16[32,2048]{1,0:T(8,128)(2,1)S(1)}, u32[]{:S(2)}, u32[]{:S(2)}) collective-permute-start(bf16[32,2048]{1,0:T(8,128)(2,1)S(1)} %get-tuple-element.127), channel_id=1, source_target_pairs={{0,2},{1,3},{2,0},{3,1},{4,6},{5,7},{6,4},{7,5},{8,10},{9,11},{10,... | collective-permute-start | bytes 393224 | tf_op jit(solution)/shard_map/ppermute | solution.py:439
  73.0 7.0 %collective-permute-start.19 = (bf16[32,2048]{1,0:T(8,128)(2,1)S(1)}, bf16[32,2048]{1,0:T(8,128)(2,1)S(1)}, u32[]{:S(2)}, u32[]{:S(2)}) collective-permute-start(bf16[32,2048]{1,0:T(8,128)(2,1)S(1)} %get-tuple-element.125), channel_id=1, source_target_pairs={{0,2},{1,3},{2,0},{3,1},{4,6},{5,7},{6,4},{7,5},{8,10},{9,11},{10,... | collective-permute-start | bytes 393224 | tf_op jit(solution)/shard_map/ppermute | solution.py:439
  73.3 10.5 %collective-permute-start.21 = (bf16[32,2048]{1,0:T(8,128)(2,1)S(1)}, bf16[32,2048]{1,0:T(8,128)(2,1)S(1)}, u32[]{:S(2)}, u32[]{:S(2)}) collective-permute-start(bf16[32,2048]{1,0:T(8,128)(2,1)S(1)} %add_convert_fusion.3), channel_id=1, source_target_pairs={{0,4},{1,5},{2,6},{3,7},{4,0},{5,1},{6,2},{7,3},{8,12},{9,13},{10,... | collective-permute-start | bytes 393224 | tf_op jit(solution)/shard_map/ppermute | solution.py:439
  76.2 7.5 %collective-permute-start.22 = (bf16[32,2048]{1,0:T(8,128)(2,1)S(1)}, bf16[32,2048]{1,0:T(8,128)(2,1)S(1)}, u32[]{:S(2)}, u32[]{:S(2)}) collective-permute-start(bf16[32,2048]{1,0:T(8,128)(2,1)S(1)} %get-tuple-element.131), channel_id=1, source_target_pairs={{0,2},{1,3},{2,0},{3,1},{4,6},{5,7},{6,4},{7,5},{8,10},{9,11},{10,... | collective-permute-start | bytes 393224 | tf_op jit(solution)/shard_map/ppermute | solution.py:439
  80.0 7.3 %collective-permute-start.23 = (bf16[32,2048]{1,0:T(8,128)(2,1)S(1)}, bf16[32,2048]{1,0:T(8,128)(2,1)S(1)}, u32[]{:S(2)}, u32[]{:S(2)}) collective-permute-start(bf16[32,2048]{1,0:T(8,128)(2,1)S(1)} %add_convert_fusion.2), channel_id=1, source_target_pairs={{0,4},{1,5},{2,6},{3,7},{4,0},{5,1},{6,2},{7,3},{8,12},{9,13},{10,... | collective-permute-start | bytes 393224 | tf_op jit(solution)/shard_map/ppermute | solution.py:439
  80.7 5.8 %collective-permute-start.24 = (bf16[32,2048]{1,0:T(8,128)(2,1)S(1)}, bf16[32,2048]{1,0:T(8,128)(2,1)S(1)}, u32[]{:S(2)}, u32[]{:S(2)}) collective-permute-start(bf16[32,2048]{1,0:T(8,128)(2,1)S(1)} %get-tuple-element.136), channel_id=1, source_target_pairs={{0,2},{1,3},{2,0},{3,1},{4,6},{5,7},{6,4},{7,5},{8,10},{9,11},{10,... | collective-permute-start | bytes 393224 | tf_op jit(solution)/shard_map/ppermute | solution.py:439

commit v7 on v6

--- a/solution.py
+++ b/solution.py
@@ -392,6 +392,19 @@
     out_ref[:, width:] = routes_ref[tokens, :]
 
 
+def finish_kernel(*refs):
+    *in_refs, out_ref = refs
+    chunks = sum(ref.dtype == F32 for ref in in_refs)
+    each = len(in_refs) // chunks - 1
+    start = 0
+    for number, kept_ref in enumerate(in_refs[:chunks]):
+        total = kept_ref[...]
+        for ref in in_refs[chunks + number * each : chunks + (number + 1) * each]:
+            total += ref[...].astype(F32)
+        out_ref[start : start + total.shape[0], :] = total.astype(BF16)
+        start += total.shape[0]
+
+
 def expert_kernel(places, spot_ref, *refs):
     slots = refs[:places]
     weights = refs[places : places + 6]
@@ -456,7 +469,7 @@
     return [
         [after(pieces[0], done)]
         + [exchange(sent, 2 * i + 2) for i, sent in enumerate(mine)]
-        + [exchange(after(pieces[1], mine[-1]), 1)]
+        + [exchange(after(pieces[1], joined[0][-1] if spare else mine[-1]), 1)]
         for pieces, mine in zip(chunks, joined)
     ], done
 
@@ -599,13 +612,13 @@
             slot[0] = after(slot[0], made[-1][0])
         made.append(experts(spot, slot, (*own, *sib)))
     chunks, _ = reduce_places(made)
-    return jnp.concatenate(
-        [
-            sum((s.astype(F32) for s in summands), kept).astype(BF16)
-            for kept, summands in zip(residuals, chunks)
-        ],
-        axis=0,
-    )
+    return call(
+        finish_kernel,
+        (shape((tok, width), BF16),),
+        *residuals,
+        *(summand for summands in chunks for summand in summands),
+        vmem=SMALL_VMEM,
+    )[0]
 
 
 def solution(mesh):

time: 88.4 us -> 88.5 us (level)
  waiting for transfers between devices: 24.5 us -> 25.8 us
  starting transfers between devices: 33.7 us -> 32.5 us
  Pallas kernels: 23.5 us -> 24.4 us
    ppermute x18, waiting for transfers between devices: 23.1 us -> 24.4 us  [exchange(): lax.ppermute(piece, 'exp', between_places(lax.axis_size('exp') // 2, d))]
    ppermute x18, starting transfers between devices: 27.8 us -> 26.7 us  [exchange(): lax.ppermute(piece, 'exp', between_places(lax.axis_size('exp') // 2, d))]
    pallas_call x2 -> x3, Pallas kernels: 9.95 us -> 10.8 us  [call(): pl.pallas_call(kernel, grid=(1,), out_shape=tuple(outs), in_specs=([] if...]
where the time goes in v7:
time: 88.5 us; the launch traced here: 88.3 us
  starting transfers between devices  32.5 us (37%)
  waiting for transfers between devices  25.8 us (29%)
  Pallas kernels  24.4 us (28%)
  local copies, waits for them, and re-layouts  5.01 us (6%)
    ppermute x18, starting transfers between devices, exchange(): lax.ppermute(piece, 'exp', between_places(lax.axis_size('exp') // 2, d))  26.7 us
    ppermute x18, waiting for transfers between devices, exchange(): lax.ppermute(piece, 'exp', between_places(lax.axis_size('exp') // 2, d))  24.4 us
    pallas_call x3, Pallas kernels, call(): pl.pallas_call(kernel, grid=(1,), out_shape=tuple(outs), in_specs=([] if...  10.8 us
    pallas_call x9, Pallas kernels, resident(): pl.pallas_call(kernel, out_shape=tuple(outs), in_specs=([] if scalars is...  9.14 us
    unnamed x40, local copies, waits for them, and re-layouts  4.98 us
    ppermute x2, starting transfers between devices, per_device(): got = lax.ppermute(summed, 'seq', [(i, i ^ step) for i in range(seqs)])  4.76 us
    pallas_call x2, Pallas kernels, fetch(): pl.pallas_call(fetch_kernel, out_shape=tuple((shape(a.shape, a.dtype) for...  4.43 us
  transfers between devices with their start and end apart: 25, of which 14 were waited for; matrix products, arithmetic and copies ran while one was open for 0% of the time, Pallas kernels for 24%

profile of v7, /device:TPU:0, one launch (start us, length us, event | category | flops | bytes accessed | tf_op | source)
XLA Modules:
  0.0 88.3 jit_solution(6309010694742177968)
XLA Ops:
  0.0 0.5 collective-permute-start
  0.5 0.5 collective-permute-start.4
  1.1 7.4 %shard_map.145 = (bf16[4,4,128,256]{3,2,1,0:T(8,128)(2,1)}, bf16[4,4,128,256]{3,2,1,0:T(8,128)(2,1)}, bf16[4,128,256]{2,1,0:T(8,128)(2,1)}) custom-call(bf16[512,256]{1,0:T(8,128)(2,1)} %key_ref.3, bf16[512,512]{1,0:T(8,128)(2,1)} %value_ref.1, f32[4,512]{1,0:T(4,128)} %decay_ref.3, f32[4,512]{1,0:T(4,128)} %rate_ref.1), custom_call_target="tpu_custom_call" | custom-call | flops 10000000000 | bytes 3162112 | tf_op jit(solution)/shard_map/pallas_call | solution.py:78
  8.5 2.9 %collective-permute-start.1 = (bf16[4,128,256]{2,1,0:T(8,128)(2,1)}, bf16[4,128,256]{2,1,0:T(8,128)(2,1)S(1)}, u32[]{:S(2)}, u32[]{:S(2)}) collective-permute-start(bf16[4,128,256]{2,1,0:T(8,128)(2,1)} %get-tuple-element.75.own_ref), channel_id=1, source_target_pairs={{0,8},{8,0},{16,24},{24,16},{1,9},{9,1},{17,25},{25,17},{2,10},{10... | collective-permute-start | bytes 786440 | tf_op jit(solution)/shard_map/ppermute | solution.py:544
  11.5 1.2 %copy-done.18 = bf16[4,4,128,256]{3,2,1,0:T(8,128)(2,1)S(1)} copy-done((bf16[4,4,128,256]{3,2,1,0:T(8,128)(2,1)S(1)}, bf16[4,4,128,256]{3,2,1,0:T(8,128)(2,1)}, u32[]{:S(2)}) %copy-start.18) | copy-done | bytes 1048600
  12.7 1.2 %copy-done.19 = bf16[4,4,128,256]{3,2,1,0:T(8,128)(2,1)S(1)} copy-done((bf16[4,4,128,256]{3,2,1,0:T(8,128)(2,1)S(1)}, bf16[4,4,128,256]{3,2,1,0:T(8,128)(2,1)}, u32[]{:S(2)}) %copy-start.19) | copy-done | bytes 1048600
  13.9 2.6 %shard_map.146 = (bf16[512,512]{1,0:T(8,128)(2,1)S(1)}, f32[512,512]{1,0:T(8,128)S(1)}, bf16[64,128]{1,0:T(8,128)(2,1)S(1)}) custom-call(bf16[512,256]{1,0:T(8,128)(2,1)S(1)} %copy-done.8, bf16[512,256]{1,0:T(8,128)(2,1)S(1)} %copy-done.9, f32[4,512]{1,0:T(4,128)S(1)} %copy-done.10, s32[4,64]{1,0:T(4,128)S(1)} %bitcast.10, bf16[4,64]{1,0:T(4,128)(2,1)S(1)} %bitcast.11, ...), custom_call_target="tpu_custom_call" | custom-call | flops 4000000000 | bytes 4220416 | tf_op jit(solution)/shard_map/pallas_call | solution.py:78
  16.5 0.8 copy-done.16
  17.3 0.8 collective-permute-done.1.got_ref
  18.4 1.8 %collective-permute-start.2 = (bf16[4,128,128]{2,1,0:T(8,128)(2,1)S(1)}, bf16[4,128,128]{2,1,0:T(8,128)(2,1)S(1)}, u32[]{:S(2)}, u32[]{:S(2)}) collective-permute-start(bf16[4,128,128]{2,1,0:T(8,128)(2,1)S(1)} %get-tuple-element.78), channel_id=1, source_target_pairs={{0,16},{8,24},{16,0},{24,8},{1,17},{9,25},{17,1},{25,9},{2,18},{10... | collective-permute-start | bytes 393224 | tf_op jit(solution)/shard_map/ppermute | solution.py:544
  20.3 1.6 %copy-done.3 = bf16[512,2048]{1,0:T(8,128)(2,1)S(1)} copy-done((bf16[512,2048]{1,0:T(8,128)(2,1)S(1)}, bf16[512,2048]{1,0:T(8,128)(2,1)}, u32[]{:S(2)}) %copy-start.3) | copy-done | bytes 2097176
  21.9 1.9 %shard_map.148 = (bf16[512,512]{1,0:T(8,128)(2,1)S(1)}, bf16[512,2048]{1,0:T(8,128)(2,1)S(1)}, bf16[512,2048]{1,0:T(8,128)(2,1)S(1)}) custom-call(bf16[512,512]{1,0:T(8,128)(2,1)S(1)} %copy-done.5, bf16[512,2048]{1,0:T(8,128)(2,1)S(1)} %copy-done.3, bf16[512,2048]{1,0:T(8,128)(2,1)} %collective-permute-done.refs_2_), custom_call_target="tpu_custom_call" | custom-call | bytes 9437184 | tf_op jit(solution)/shard_map/pallas_call | solution.py:45
  23.9 1.1 %shard_map.149 = (bf16[4,128,128]{2,1,0:T(8,128)(2,1)S(1)}, bf16[4,64,512]{2,1,0:T(8,128)(2,1)S(1)}) custom-call(s32[3]{0:T(128)S(1)} %pad_add_fusion.spot_ref, f32[1,128]{1,0:T(1,128)S(1)} %bitcast.12, bf16[512,512]{1,0:T(8,128)(2,1)S(1)} %get-tuple-element.84.gate_ref, bf16[512,512]{1,0:T(8,128)(2,1)S(1)} %copy-done.17, f32[512,512]{1,0:T(8,128)S(1)} %copy-done.15, ...), custom_call_target="tpu_custom_call" | custom-call | flops 1000000000 | bytes 2884096 | tf_op jit(solution)/shard_map/pallas_call | solution.py:60
  25.1 1.0 %shard_map.150.keep_ref = bf16[4,64,512]{2,1,0:T(8,128)(2,1)S(1)} custom-call(s32[3]{0:T(128)S(1)} %pad_add_fusion.spot_ref, f32[1,128]{1,0:T(1,128)S(1)} %bitcast.13, bf16[512,512]{1,0:T(8,128)(2,1)S(1)} %get-tuple-element.84.gate_ref, bf16[512,512]{1,0:T(8,128)(2,1)S(1)} %copy-done.17, f32[512,512]{1,0:T(8,128)S(1)} %copy-done.15, ...), custom_call_target="tpu_custom_call" | custom-call | flops 1000000000 | bytes 2490880 | tf_op jit(solution)/shard_map/pallas_call | solution.py:60
  26.1 0.5 collective-permute-done.6.got_ref
  26.7 0.7 shard_map.151
  27.4 1.7 %collective-permute-start.8 = (bf16[32,2048]{1,0:T(8,128)(2,1)S(1)}, bf16[32,2048]{1,0:T(8,128)(2,1)S(1)}, u32[]{:S(2)}, u32[]{:S(2)}) collective-permute-start(bf16[32,2048]{1,0:T(8,128)(2,1)S(1)} %get-tuple-element.97), channel_id=1, source_target_pairs={{0,2},{1,3},{2,0},{3,1},{4,6},{5,7},{6,4},{7,5},{8,10},{9,11},{10,... | collective-permute-start | bytes 393224 | tf_op jit(solution)/shard_map/ppermute | solution.py:452
  29.0 0.7 shard_map.152
  29.8 0.5 collective-permute-start.7
  30.3 3.4 %collective-permute-done.8 = bf16[32,2048]{1,0:T(8,128)(2,1)S(1)} collective-permute-done((bf16[32,2048]{1,0:T(8,128)(2,1)S(1)}, bf16[32,2048]{1,0:T(8,128)(2,1)S(1)}, u32[]{:S(2)}, u32[]{:S(2)}) %collective-permute-start.8) | collective-permute-done | bytes 131104 | tf_op jit(solution)/shard_map/ppermute | solution.py:452
  33.7 2.7 %collective-permute-start.9 = (bf16[32,2048]{1,0:T(8,128)(2,1)S(1)}, bf16[32,2048]{1,0:T(8,128)(2,1)S(1)}, u32[]{:S(2)}, u32[]{:S(2)}) collective-permute-start(bf16[32,2048]{1,0:T(8,128)(2,1)S(1)} %add_convert_fusion.3), channel_id=1, source_target_pairs={{0,4},{1,5},{2,6},{3,7},{4,0},{5,1},{6,2},{7,3},{8,12},{9,13},{10,... | collective-permute-start | bytes 393224 | tf_op jit(solution)/shard_map/ppermute | solution.py:452
  36.4 1.7 %collective-permute-start.10 = (bf16[32,2048]{1,0:T(8,128)(2,1)S(1)}, bf16[32,2048]{1,0:T(8,128)(2,1)S(1)}, u32[]{:S(2)}, u32[]{:S(2)}) collective-permute-start(bf16[32,2048]{1,0:T(8,128)(2,1)S(1)} %get-tuple-element.111), channel_id=1, source_target_pairs={{0,2},{1,3},{2,0},{3,1},{4,6},{5,7},{6,4},{7,5},{8,10},{9,11},{10,... | collective-permute-start | bytes 393224 | tf_op jit(solution)/shard_map/ppermute | solution.py:452
  38.2 1.1 %collective-permute-start.13 = (bf16[32,2304]{1,0:T(8,128)(2,1)S(1)}, bf16[32,2304]{1,0:T(8,128)(2,1)S(1)}, u32[]{:S(2)}, u32[]{:S(2)}) collective-permute-start(bf16[32,2304]{1,0:T(8,128)(2,1)S(1)} %pad.6), channel_id=1, source_target_pairs={{0,4},{1,5},{2,6},{3,7},{4,0},{5,1},{6,2},{7,3},{8,12},{9,13},{10,... | collective-permute-start | bytes 442376 | tf_op jit(solution)/shard_map/ppermute | solution.py:452
  39.2 2.5 %shard_map.153 = (bf16[1,2048,512]{2,1,0:T(8,128)(2,1)S(1)}, bf16[1,2048,512]{2,1,0:T(8,128)(2,1)S(1)}, bf16[1,512,2048]{2,1,0:T(8,128)(2,1)S(1)}) custom-call(bf16[1,2048,512]{2,1,0:T(8,128)(2,1)S(1)} %collective-permute-done.3.refs_0_, bf16[1,2048,512]{2,1,0:T(8,128)(2,1)} %collective-permute-done.4.refs_1_, ...), custom_call_target="tpu_custom_call" | custom-call | bytes 12582912 | tf_op jit(solution)/shard_map/pallas_call | solution.py:45
  41.8 0.8 collective-permute-done.10.refs_2_
  42.5 1.2 %collective-permute-done.9.refs_1_ = bf16[32,2048]{1,0:T(8,128)(2,1)S(1)} collective-permute-done((bf16[32,2048]{1,0:T(8,128)(2,1)S(1)}, bf16[32,2048]{1,0:T(8,128)(2,1)S(1)}, u32[]{:S(2)}, u32[]{:S(2)}) %collective-permute-start.9) | collective-permute-done | bytes 131104 | tf_op jit(solution)/shard_map/ppermute | solution.py:452
  44.0 1.7 %collective-permute-start.11 = (bf16[32,2176]{1,0:T(8,128)(2,1)S(1)}, bf16[32,2176]{1,0:T(8,128)(2,1)S(1)}, u32[]{:S(2)}, u32[]{:S(2)}) collective-permute-start(bf16[32,2176]{1,0:T(8,128)(2,1)S(1)} %get-tuple-element.115.refs_0_), channel_id=1, source_target_pairs={{0,2},{1,3},{2,0},{3,1},{4,6},{5,7},{6,4},{7,5},{8,10},{9,11},{10,... | collective-permute-start | bytes 417800 | tf_op jit(solution)/shard_map/ppermute | solution.py:452
  45.6 3.9 %collective-permute-start.12 = (bf16[32,2176]{1,0:T(8,128)(2,1)S(1)}, bf16[32,2176]{1,0:T(8,128)(2,1)S(1)}, u32[]{:S(2)}, u32[]{:S(2)}) collective-permute-start(bf16[32,2176]{1,0:T(8,128)(2,1)S(1)} %get-tuple-element.115.refs_0_), channel_id=1, source_target_pairs={{0,4},{1,5},{2,6},{3,7},{4,0},{5,1},{6,2},{7,3},{8,12},{9,13},{10,... | collective-permute-start | bytes 417800 | tf_op jit(solution)/shard_map/ppermute | solution.py:452
  49.6 4.4 %collective-permute-done.11.refs_1_ = bf16[32,2176]{1,0:T(8,128)(2,1)S(1)} collective-permute-done((bf16[32,2176]{1,0:T(8,128)(2,1)S(1)}, bf16[32,2176]{1,0:T(8,128)(2,1)S(1)}, u32[]{:S(2)}, u32[]{:S(2)}) %collective-permute-start.11) | collective-permute-done | bytes 139296 | tf_op jit(solution)/shard_map/ppermute | solution.py:452
  54.0 0.3 collective-permute-done.12.refs_2_
  54.3 1.2 %collective-permute-done.14.refs_2_ = bf16[32,2048]{1,0:T(8,128)(2,1)S(1)} collective-permute-done((bf16[32,2048]{1,0:T(8,128)(2,1)S(1)}, bf16[32,2048]{1,0:T(8,128)(2,1)S(1)}, u32[]{:S(2)}, u32[]{:S(2)}) %collective-permute-start.14) | collective-permute-done | bytes 131104 | tf_op jit(solution)/shard_map/ppermute | solution.py:452
  55.7 1.8 %collective-permute-start.17 = (bf16[32,2176]{1,0:T(8,128)(2,1)S(1)}, bf16[32,2176]{1,0:T(8,128)(2,1)S(1)}, u32[]{:S(2)}, u32[]{:S(2)}) collective-permute-start(bf16[32,2176]{1,0:T(8,128)(2,1)S(1)} %get-tuple-element.123.refs_0_), channel_id=1, source_target_pairs={{0,4},{1,5},{2,6},{3,7},{4,0},{5,1},{6,2},{7,3},{8,12},{9,13},{10,... | collective-permute-start | bytes 417800 | tf_op jit(solution)/shard_map/ppermute | solution.py:452
  57.5 2.5 %collective-permute-start.15 = (bf16[32,2176]{1,0:T(8,128)(2,1)S(1)}, bf16[32,2176]{1,0:T(8,128)(2,1)S(1)}, u32[]{:S(2)}, u32[]{:S(2)}) collective-permute-start(bf16[32,2176]{1,0:T(8,128)(2,1)S(1)} %collective-permute-done.12.refs_2_), channel_id=1, source_target_pairs={{0,2},{1,3},{2,0},{3,1},{4,6},{5,7},{6,4},{7,5},{8,10},{9,11},{10,... | collective-permute-start | bytes 417800 | tf_op jit(solution)/shard_map/ppermute | solution.py:452
  60.0 2.4 %collective-permute-done.17.refs_2_ = bf16[32,2176]{1,0:T(8,128)(2,1)S(1)} collective-permute-done((bf16[32,2176]{1,0:T(8,128)(2,1)S(1)}, bf16[32,2176]{1,0:T(8,128)(2,1)S(1)}, u32[]{:S(2)}, u32[]{:S(2)}) %collective-permute-start.17) | collective-permute-done | bytes 139296 | tf_op jit(solution)/shard_map/ppermute | solution.py:452
  62.5 2.1 %collective-permute-start.18 = (bf16[32,2176]{1,0:T(8,128)(2,1)S(1)}, bf16[32,2176]{1,0:T(8,128)(2,1)S(1)}, u32[]{:S(2)}, u32[]{:S(2)}) collective-permute-start(bf16[32,2176]{1,0:T(8,128)(2,1)S(1)} %collective-permute-done.17.refs_2_), channel_id=1, source_target_pairs={{0,2},{1,3},{2,0},{3,1},{4,6},{5,7},{6,4},{7,5},{8,10},{9,11},{10,... | collective-permute-start | bytes 417800 | tf_op jit(solution)/shard_map/ppermute | solution.py:452
  64.5 0.5 collective-permute-done.15.refs_3_
  65.0 2.5 %shard_map.156 = (bf16[32,2048]{1,0:T(8,128)(2,1)S(1)}, bf16[32,2048]{1,0:T(8,128)(2,1)S(1)}, bf16[32,2048]{1,0:T(8,128)(2,1)S(1)}, bf16[32,2048]{1,0:T(8,128)(2,1)S(1)}) custom-call(s32[2]{0:T(128)S(1)} %pad_add_fusion.1.spot_ref, bf16[32,2176]{1,0:T(8,128)(2,1)S(1)} %get-tuple-element.115.refs_0_, bf16[32,2176]{1,0:T(8,128)(2,1)S(1)} %collective-permute-done.11.refs_1_, ...), custom_call_target="tpu_custom_call" | custom-call | flops 3000000000 | bytes 13664256 | tf_op jit(solution)/shard_map/pallas_call | solution.py:60
  67.5 1.5 %collective-permute-start.20 = (bf16[32,2048]{1,0:T(8,128)(2,1)S(1)}, bf16[32,2048]{1,0:T(8,128)(2,1)S(1)}, u32[]{:S(2)}, u32[]{:S(2)}) collective-permute-start(bf16[32,2048]{1,0:T(8,128)(2,1)S(1)} %get-tuple-element.128), channel_id=1, source_target_pairs={{0,2},{1,3},{2,0},{3,1},{4,6},{5,7},{6,4},{7,5},{8,10},{9,11},{10,... | collective-permute-start | bytes 393224 | tf_op jit(solution)/shard_map/ppermute | solution.py:452
  69.0 1.6 %collective-permute-done.18.refs_3_ = bf16[32,2176]{1,0:T(8,128)(2,1)S(1)} collective-permute-done((bf16[32,2176]{1,0:T(8,128)(2,1)S(1)}, bf16[32,2176]{1,0:T(8,128)(2,1)S(1)}, u32[]{:S(2)}, u32[]{:S(2)}) %collective-permute-start.18) | collective-permute-done | bytes 139296 | tf_op jit(solution)/shard_map/ppermute | solution.py:452
  70.5 2.5 %shard_map.157 = (bf16[32,2048]{1,0:T(8,128)(2,1)S(1)}, bf16[32,2048]{1,0:T(8,128)(2,1)S(1)}, bf16[32,2048]{1,0:T(8,128)(2,1)S(1)}, bf16[32,2048]{1,0:T(8,128)(2,1)S(1)}) custom-call(s32[2]{0:T(128)S(1)} %pad_add_fusion.1.spot_ref, bf16[32,2176]{1,0:T(8,128)(2,1)S(1)} %get-tuple-element.123.refs_0_, bf16[32,2176]{1,0:T(8,128)(2,1)S(1)} %collective-permute-done.16.refs_1_, ...), custom_call_target="tpu_custom_call" | custom-call | flops 3000000000 | bytes 13664256 | tf_op jit(solution)/shard_map/pallas_call | solution.py:60
  73.0 0.3 collective-permute-start.19
  73.4 2.7 %collective-permute-start.21 = (bf16[32,2048]{1,0:T(8,128)(2,1)S(1)}, bf16[32,2048]{1,0:T(8,128)(2,1)S(1)}, u32[]{:S(2)}, u32[]{:S(2)}) collective-permute-start(bf16[32,2048]{1,0:T(8,128)(2,1)S(1)} %add_convert_fusion.1), channel_id=1, source_target_pairs={{0,4},{1,5},{2,6},{3,7},{4,0},{5,1},{6,2},{7,3},{8,12},{9,13},{10,... | collective-permute-start | bytes 393224 | tf_op jit(solution)/shard_map/ppermute | solution.py:452
  76.1 2.1 %collective-permute-start.22 = (bf16[32,2048]{1,0:T(8,128)(2,1)S(1)}, bf16[32,2048]{1,0:T(8,128)(2,1)S(1)}, u32[]{:S(2)}, u32[]{:S(2)}) collective-permute-start(bf16[32,2048]{1,0:T(8,128)(2,1)S(1)} %get-tuple-element.132), channel_id=1, source_target_pairs={{0,2},{1,3},{2,0},{3,1},{4,6},{5,7},{6,4},{7,5},{8,10},{9,11},{10,... | collective-permute-start | bytes 393224 | tf_op jit(solution)/shard_map/ppermute | solution.py:452
  78.2 2.8 %collective-permute-done.19 = bf16[32,2048]{1,0:T(8,128)(2,1)S(1)} collective-permute-done((bf16[32,2048]{1,0:T(8,128)(2,1)S(1)}, bf16[32,2048]{1,0:T(8,128)(2,1)S(1)}, u32[]{:S(2)}, u32[]{:S(2)}) %collective-permute-start.19) | collective-permute-done | bytes 131104 | tf_op jit(solution)/shard_map/ppermute | solution.py:452
  81.1 0.5 collective-permute-start.23
  81.6 2.2 %collective-permute-done.22.refs_4_ = bf16[32,2048]{1,0:T(8,128)(2,1)S(1)} collective-permute-done((bf16[32,2048]{1,0:T(8,128)(2,1)S(1)}, bf16[32,2048]{1,0:T(8,128)(2,1)S(1)}, u32[]{:S(2)}, u32[]{:S(2)}) %collective-permute-start.22) | collective-permute-done | bytes 131104 | tf_op jit(solution)/shard_map/ppermute | solution.py:452
  83.8 3.6 %collective-permute-done.24.refs_7_ = bf16[32,2048]{1,0:T(8,128)(2,1)S(1)} collective-permute-done((bf16[32,2048]{1,0:T(8,128)(2,1)S(1)}, bf16[32,2048]{1,0:T(8,128)(2,1)S(1)}, u32[]{:S(2)}, u32[]{:S(2)}) %collective-permute-start.24) | collective-permute-done | bytes 131104 | tf_op jit(solution)/shard_map/ppermute | solution.py:452
  87.5 0.8 shard_map.158
  (66 shorter events, 1.4 us)
Async XLA Ops:
  0.0 8.5 %collective-permute-start = (bf16[512,2048]{1,0:T(8,128)(2,1)}, bf16[512,2048]{1,0:T(8,128)(2,1)}, u32[]{:S(2)}, u32[]{:S(2)}) collective-permute-start(bf16[512,2048]{1,0:T(8,128)(2,1)} %refs_1_.1), channel_id=1, source_target_pairs={{0,1},{1,0},{2,3},{3,2},{4,5},{5,4},{6,7},{7,6},{8,9},{9,8},{10,11... | collective-permute-start | bytes 6291464 | tf_op jit(solution)/shard_map/ppermute | solution.py:505
  0.5 23.4 %collective-permute-start.3 = (bf16[1,2048,512]{2,1,0:T(8,128)(2,1)}, bf16[1,2048,512]{2,1,0:T(8,128)(2,1)S(1)}, u32[]{:S(2)}, u32[]{:S(2)}) collective-permute-start(bf16[1,2048,512]{2,1,0:T(8,128)(2,1)} %refs_4_.3), channel_id=1, source_target_pairs={{0,1},{1,0},{2,3},{3,2},{4,5},{5,4},{6,7},{7,6},{8,9},{9,8},{10,11... | collective-permute-start | bytes 6291464 | tf_op jit(solution)/shard_map/ppermute | solution.py:507
  0.5 23.3 %collective-permute-start.4 = (bf16[1,2048,512]{2,1,0:T(8,128)(2,1)}, bf16[1,2048,512]{2,1,0:T(8,128)(2,1)}, u32[]{:S(2)}, u32[]{:S(2)}) collective-permute-start(bf16[1,2048,512]{2,1,0:T(8,128)(2,1)} %refs_5_.3), channel_id=1, source_target_pairs={{0,1},{1,0},{2,3},{3,2},{4,5},{5,4},{6,7},{7,6},{8,9},{9,8},{10,11... | collective-permute-start | bytes 6291464 | tf_op jit(solution)/shard_map/ppermute | solution.py:507
  1.0 22.9 %collective-permute-start.5 = (bf16[1,512,2048]{2,1,0:T(8,128)(2,1)}, bf16[1,512,2048]{2,1,0:T(8,128)(2,1)}, u32[]{:S(2)}, u32[]{:S(2)}) collective-permute-start(bf16[1,512,2048]{2,1,0:T(8,128)(2,1)} %refs_6_.3), channel_id=1, source_target_pairs={{0,1},{1,0},{2,3},{3,2},{4,5},{5,4},{6,7},{7,6},{8,9},{9,8},{10,11... | collective-permute-start | bytes 6291464 | tf_op jit(solution)/shard_map/ppermute | solution.py:507
  1.1 10.4 %copy-start.8 = (bf16[512,256]{1,0:T(8,128)(2,1)S(1)}, bf16[512,256]{1,0:T(8,128)(2,1)}, u32[]{:S(2)}) copy-start(bf16[512,256]{1,0:T(8,128)(2,1)} %query_ref.1) | copy-start | bytes 786436
  1.1 10.4 %copy-start.9 = (bf16[512,256]{1,0:T(8,128)(2,1)S(1)}, bf16[512,256]{1,0:T(8,128)(2,1)}, u32[]{:S(2)}) copy-start(bf16[512,256]{1,0:T(8,128)(2,1)} %key_ref.3) | copy-start | bytes 786436
  1.1 10.3 %copy-start.10 = (f32[4,512]{1,0:T(4,128)S(1)}, f32[4,512]{1,0:T(4,128)}, u32[]{:S(2)}) copy-start(f32[4,512]{1,0:T(4,128)} %decay_ref.3) | copy-start | bytes 24580
  1.1 10.3 %copy-start.11 = (s32[64,4]{0,1:T(4,128)S(1)}, s32[64,4]{0,1:T(4,128)}, u32[]{:S(2)}) copy-start(s32[64,4]{0,1:T(4,128)} %param.25) | copy-start | bytes 3076
  1.1 10.3 %copy-start.12 = (bf16[64,4]{0,1:T(4,128)(2,1)S(1)}, bf16[64,4]{0,1:T(4,128)(2,1)}, u32[]{:S(2)}) copy-start(bf16[64,4]{0,1:T(4,128)(2,1)} %param.26) | copy-start | bytes 1540
  8.5 9.6 %collective-permute-start.1 = (bf16[4,128,256]{2,1,0:T(8,128)(2,1)}, bf16[4,128,256]{2,1,0:T(8,128)(2,1)S(1)}, u32[]{:S(2)}, u32[]{:S(2)}) collective-permute-start(bf16[4,128,256]{2,1,0:T(8,128)(2,1)} %get-tuple-element.75.own_ref), channel_id=1, source_target_pairs={{0,8},{8,0},{16,24},{24,16},{1,9},{9,1},{17,25},{25,17},{2,10},{10... | collective-permute-start | bytes 786440 | tf_op jit(solution)/shard_map/ppermute | solution.py:544
  11.4 1.2 %copy-start.18 = (bf16[4,4,128,256]{3,2,1,0:T(8,128)(2,1)S(1)}, bf16[4,4,128,256]{3,2,1,0:T(8,128)(2,1)}, u32[]{:S(2)}) copy-start(bf16[4,4,128,256]{3,2,1,0:T(8,128)(2,1)} %get-tuple-element.71.wu_ref) | copy-start | bytes 3145732
  12.7 1.2 %copy-start.19 = (bf16[4,4,128,256]{3,2,1,0:T(8,128)(2,1)S(1)}, bf16[4,4,128,256]{3,2,1,0:T(8,128)(2,1)}, u32[]{:S(2)}) copy-start(bf16[4,4,128,256]{3,2,1,0:T(8,128)(2,1)} %get-tuple-element.72.prefix_ref) | copy-start | bytes 3145732
  13.9 4.2 %copy-start.6 = (bf16[4,128,256]{2,1,0:T(8,128)(2,1)S(1)}, bf16[4,128,256]{2,1,0:T(8,128)(2,1)}, u32[]{:S(2)}) copy-start(bf16[4,128,256]{2,1,0:T(8,128)(2,1)} %get-tuple-element.75.own_ref) | copy-start | bytes 786436
  13.9 6.4 %copy-start.5 = (bf16[512,512]{1,0:T(8,128)(2,1)S(1)}, bf16[512,512]{1,0:T(8,128)(2,1)}, u32[]{:S(2)}) copy-start(bf16[512,512]{1,0:T(8,128)(2,1)} %refs_0_.1) | copy-start | bytes 1572868
  16.5 0.8 copy-start.16
  17.3 1.1 %copy-start.14 = (f32[512,512]{1,0:T(8,128)}, f32[512,512]{1,0:T(8,128)S(1)}, u32[]{:S(2)}) copy-start(f32[512,512]{1,0:T(8,128)S(1)} %get-tuple-element.85.own_ref) | copy-start | bytes 3145732
  18.4 5.4 %collective-permute-start.2 = (bf16[4,128,128]{2,1,0:T(8,128)(2,1)S(1)}, bf16[4,128,128]{2,1,0:T(8,128)(2,1)S(1)}, u32[]{:S(2)}, u32[]{:S(2)}) collective-permute-start(bf16[4,128,128]{2,1,0:T(8,128)(2,1)S(1)} %get-tuple-element.78), channel_id=1, source_target_pairs={{0,16},{8,24},{16,0},{24,8},{1,17},{9,25},{17,1},{25,9},{2,18},{10... | collective-permute-start | bytes 393224 | tf_op jit(solution)/shard_map/ppermute | solution.py:544
  20.3 1.6 %copy-start.3 = (bf16[512,2048]{1,0:T(8,128)(2,1)S(1)}, bf16[512,2048]{1,0:T(8,128)(2,1)}, u32[]{:S(2)}) copy-start(bf16[512,2048]{1,0:T(8,128)(2,1)} %refs_1_.1) | copy-start | bytes 6291460
  21.9 2.0 %copy-start.13 = (f32[128]{0:T(128)S(1)}, f32[128]{0:T(128)}, u32[]{:S(2)}) copy-start(f32[128]{0:T(128)} %param.22) | copy-start | bytes 1540
  21.9 2.0 %copy-start.15 = (f32[512,512]{1,0:T(8,128)S(1)}, f32[512,512]{1,0:T(8,128)}, u32[]{:S(2)}) copy-start(f32[512,512]{1,0:T(8,128)} %copy-done.14) | copy-start | bytes 3145732
  21.9 2.0 %copy-start.17 = (bf16[512,512]{1,0:T(8,128)(2,1)S(1)}, bf16[512,512]{1,0:T(8,128)(2,1)}, u32[]{:S(2)}) copy-start(bf16[512,512]{1,0:T(8,128)(2,1)} %copy-done.16) | copy-start | bytes 1572868
  25.1 1.6 %collective-permute-start.6 = (bf16[4,64,512]{2,1,0:T(8,128)(2,1)S(1)}, bf16[4,64,512]{2,1,0:T(8,128)(2,1)S(1)}, u32[]{:S(2)}, u32[]{:S(2)}) collective-permute-start(bf16[4,64,512]{2,1,0:T(8,128)(2,1)S(1)} %get-tuple-element.89), channel_id=1, source_target_pairs={{0,1},{1,0},{2,3},{3,2},{4,5},{5,4},{6,7},{7,6},{8,9},{9,8},{10,11... | collective-permute-start | bytes 786440 | tf_op jit(solution)/shard_map/ppermute | solution.py:573
  27.4 6.3 %collective-permute-start.8 = (bf16[32,2048]{1,0:T(8,128)(2,1)S(1)}, bf16[32,2048]{1,0:T(8,128)(2,1)S(1)}, u32[]{:S(2)}, u32[]{:S(2)}) collective-permute-start(bf16[32,2048]{1,0:T(8,128)(2,1)S(1)} %get-tuple-element.97), channel_id=1, source_target_pairs={{0,2},{1,3},{2,0},{3,1},{4,6},{5,7},{6,4},{7,5},{8,10},{9,11},{10,... | collective-permute-start | bytes 393224 | tf_op jit(solution)/shard_map/ppermute | solution.py:452
  29.8 8.3 %collective-permute-start.7 = (bf16[32,2048]{1,0:T(8,128)(2,1)S(1)}, bf16[32,2048]{1,0:T(8,128)(2,1)S(1)}, u32[]{:S(2)}, u32[]{:S(2)}) collective-permute-start(bf16[32,2048]{1,0:T(8,128)(2,1)S(1)} %get-tuple-element.95), channel_id=1, source_target_pairs={{0,2},{1,3},{2,0},{3,1},{4,6},{5,7},{6,4},{7,5},{8,10},{9,11},{10,... | collective-permute-start | bytes 393224 | tf_op jit(solution)/shard_map/ppermute | solution.py:452
  33.7 10.0 %collective-permute-start.9 = (bf16[32,2048]{1,0:T(8,128)(2,1)S(1)}, bf16[32,2048]{1,0:T(8,128)(2,1)S(1)}, u32[]{:S(2)}, u32[]{:S(2)}) collective-permute-start(bf16[32,2048]{1,0:T(8,128)(2,1)S(1)} %add_convert_fusion.3), channel_id=1, source_target_pairs={{0,4},{1,5},{2,6},{3,7},{4,0},{5,1},{6,2},{7,3},{8,12},{9,13},{10,... | collective-permute-start | bytes 393224 | tf_op jit(solution)/shard_map/ppermute | solution.py:452
  36.4 6.2 %collective-permute-start.10 = (bf16[32,2048]{1,0:T(8,128)(2,1)S(1)}, bf16[32,2048]{1,0:T(8,128)(2,1)S(1)}, u32[]{:S(2)}, u32[]{:S(2)}) collective-permute-start(bf16[32,2048]{1,0:T(8,128)(2,1)S(1)} %get-tuple-element.111), channel_id=1, source_target_pairs={{0,2},{1,3},{2,0},{3,1},{4,6},{5,7},{6,4},{7,5},{8,10},{9,11},{10,... | collective-permute-start | bytes 393224 | tf_op jit(solution)/shard_map/ppermute | solution.py:452
  38.1 5.6 %copy-start.4 = (bf16[64,2048]{1,0:T(8,128)(2,1)S(1)}, bf16[64,2048]{1,0:T(8,128)(2,1)}, u32[]{:S(2)}) copy-start(bf16[64,2048]{1,0:T(8,128)(2,1)} %hidden_ref.3) | copy-start | bytes 786436
  38.2 5.6 %copy-start.7 = (f32[2048]{0:T(1024)S(1)}, f32[2048]{0:T(1024)}, u32[]{:S(2)}) copy-start(f32[2048]{0:T(1024)} %param.24) | copy-start | bytes 24580
  38.2 17.4 %collective-permute-start.13 = (bf16[32,2304]{1,0:T(8,128)(2,1)S(1)}, bf16[32,2304]{1,0:T(8,128)(2,1)S(1)}, u32[]{:S(2)}, u32[]{:S(2)}) collective-permute-start(bf16[32,2304]{1,0:T(8,128)(2,1)S(1)} %pad.6), channel_id=1, source_target_pairs={{0,4},{1,5},{2,6},{3,7},{4,0},{5,1},{6,2},{7,3},{8,12},{9,13},{10,... | collective-permute-start | bytes 442376 | tf_op jit(solution)/shard_map/ppermute | solution.py:452
  39.2 25.8 %copy-start = (bf16[1,2048,512]{2,1,0:T(8,128)(2,1)S(1)}, bf16[1,2048,512]{2,1,0:T(8,128)(2,1)}, u32[]{:S(2)}) copy-start(bf16[1,2048,512]{2,1,0:T(8,128)(2,1)} %refs_4_.3) | copy-start | bytes 6291460
  39.2 25.8 %copy-start.1 = (bf16[1,2048,512]{2,1,0:T(8,128)(2,1)S(1)}, bf16[1,2048,512]{2,1,0:T(8,128)(2,1)}, u32[]{:S(2)}) copy-start(bf16[1,2048,512]{2,1,0:T(8,128)(2,1)} %refs_5_.3) | copy-start | bytes 6291460
  39.2 25.8 %copy-start.2 = (bf16[1,512,2048]{2,1,0:T(8,128)(2,1)S(1)}, bf16[1,512,2048]{2,1,0:T(8,128)(2,1)}, u32[]{:S(2)}) copy-start(bf16[1,512,2048]{2,1,0:T(8,128)(2,1)} %refs_6_.3) | copy-start | bytes 6291460
  44.0 10.0 %collective-permute-start.11 = (bf16[32,2176]{1,0:T(8,128)(2,1)S(1)}, bf16[32,2176]{1,0:T(8,128)(2,1)S(1)}, u32[]{:S(2)}, u32[]{:S(2)}) collective-permute-start(bf16[32,2176]{1,0:T(8,128)(2,1)S(1)} %get-tuple-element.115.refs_0_), channel_id=1, source_target_pairs={{0,2},{1,3},{2,0},{3,1},{4,6},{5,7},{6,4},{7,5},{8,10},{9,11},{10,... | collective-permute-start | bytes 417800 | tf_op jit(solution)/shard_map/ppermute | solution.py:452
  45.6 8.7 %collective-permute-start.12 = (bf16[32,2176]{1,0:T(8,128)(2,1)S(1)}, bf16[32,2176]{1,0:T(8,128)(2,1)S(1)}, u32[]{:S(2)}, u32[]{:S(2)}) collective-permute-start(bf16[32,2176]{1,0:T(8,128)(2,1)S(1)} %get-tuple-element.115.refs_0_), channel_id=1, source_target_pairs={{0,4},{1,5},{2,6},{3,7},{4,0},{5,1},{6,2},{7,3},{8,12},{9,13},{10,... | collective-permute-start | bytes 417800 | tf_op jit(solution)/shard_map/ppermute | solution.py:452
  49.5 6.0 %collective-permute-start.14 = (bf16[32,2048]{1,0:T(8,128)(2,1)S(1)}, bf16[32,2048]{1,0:T(8,128)(2,1)S(1)}, u32[]{:S(2)}, u32[]{:S(2)}) collective-permute-start(bf16[32,2048]{1,0:T(8,128)(2,1)S(1)} %get-tuple-element.118), channel_id=1, source_target_pairs={{0,2},{1,3},{2,0},{3,1},{4,6},{5,7},{6,4},{7,5},{8,10},{9,11},{10,... | collective-permute-start | bytes 393224 | tf_op jit(solution)/shard_map/ppermute | solution.py:452
  55.7 6.8 %collective-permute-start.17 = (bf16[32,2176]{1,0:T(8,128)(2,1)S(1)}, bf16[32,2176]{1,0:T(8,128)(2,1)S(1)}, u32[]{:S(2)}, u32[]{:S(2)}) collective-permute-start(bf16[32,2176]{1,0:T(8,128)(2,1)S(1)} %get-tuple-element.123.refs_0_), channel_id=1, source_target_pairs={{0,4},{1,5},{2,6},{3,7},{4,0},{5,1},{6,2},{7,3},{8,12},{9,13},{10,... | collective-permute-start | bytes 417800 | tf_op jit(solution)/shard_map/ppermute | solution.py:452
  57.5 7.6 %collective-permute-start.15 = (bf16[32,2176]{1,0:T(8,128)(2,1)S(1)}, bf16[32,2176]{1,0:T(8,128)(2,1)S(1)}, u32[]{:S(2)}, u32[]{:S(2)}) collective-permute-start(bf16[32,2176]{1,0:T(8,128)(2,1)S(1)} %collective-permute-done.12.refs_2_), channel_id=1, source_target_pairs={{0,2},{1,3},{2,0},{3,1},{4,6},{5,7},{6,4},{7,5},{8,10},{9,11},{10,... | collective-permute-start | bytes 417800 | tf_op jit(solution)/shard_map/ppermute | solution.py:452
  60.0 9.0 %collective-permute-start.16 = (bf16[32,2176]{1,0:T(8,128)(2,1)S(1)}, bf16[32,2176]{1,0:T(8,128)(2,1)S(1)}, u32[]{:S(2)}, u32[]{:S(2)}) collective-permute-start(bf16[32,2176]{1,0:T(8,128)(2,1)S(1)} %get-tuple-element.123.refs_0_), channel_id=1, source_target_pairs={{0,2},{1,3},{2,0},{3,1},{4,6},{5,7},{6,4},{7,5},{8,10},{9,11},{10,... | collective-permute-start | bytes 417800 | tf_op jit(solution)/shard_map/ppermute | solution.py:452
  62.5 8.1 %collective-permute-start.18 = (bf16[32,2176]{1,0:T(8,128)(2,1)S(1)}, bf16[32,2176]{1,0:T(8,128)(2,1)S(1)}, u32[]{:S(2)}, u32[]{:S(2)}) collective-permute-start(bf16[32,2176]{1,0:T(8,128)(2,1)S(1)} %collective-permute-done.17.refs_2_), channel_id=1, source_target_pairs={{0,2},{1,3},{2,0},{3,1},{4,6},{5,7},{6,4},{7,5},{8,10},{9,11},{10,... | collective-permute-start | bytes 417800 | tf_op jit(solution)/shard_map/ppermute | solution.py:452
  67.5 5.8 %collective-permute-start.20 = (bf16[32,2048]{1,0:T(8,128)(2,1)S(1)}, bf16[32,2048]{1,0:T(8,128)(2,1)S(1)}, u32[]{:S(2)}, u32[]{:S(2)}) collective-permute-start(bf16[32,2048]{1,0:T(8,128)(2,1)S(1)} %get-tuple-element.128), channel_id=1, source_target_pairs={{0,2},{1,3},{2,0},{3,1},{4,6},{5,7},{6,4},{7,5},{8,10},{9,11},{10,... | collective-permute-start | bytes 393224 | tf_op jit(solution)/shard_map/ppermute | solution.py:452
  73.0 7.9 %collective-permute-start.19 = (bf16[32,2048]{1,0:T(8,128)(2,1)S(1)}, bf16[32,2048]{1,0:T(8,128)(2,1)S(1)}, u32[]{:S(2)}, u32[]{:S(2)}) collective-permute-start(bf16[32,2048]{1,0:T(8,128)(2,1)S(1)} %get-tuple-element.126), channel_id=1, source_target_pairs={{0,2},{1,3},{2,0},{3,1},{4,6},{5,7},{6,4},{7,5},{8,10},{9,11},{10,... | collective-permute-start | bytes 393224 | tf_op jit(solution)/shard_map/ppermute | solution.py:452
  73.4 10.4 %collective-permute-start.21 = (bf16[32,2048]{1,0:T(8,128)(2,1)S(1)}, bf16[32,2048]{1,0:T(8,128)(2,1)S(1)}, u32[]{:S(2)}, u32[]{:S(2)}) collective-permute-start(bf16[32,2048]{1,0:T(8,128)(2,1)S(1)} %add_convert_fusion.1), channel_id=1, source_target_pairs={{0,4},{1,5},{2,6},{3,7},{4,0},{5,1},{6,2},{7,3},{8,12},{9,13},{10,... | collective-permute-start | bytes 393224 | tf_op jit(solution)/shard_map/ppermute | solution.py:452
  76.1 7.7 %collective-permute-start.22 = (bf16[32,2048]{1,0:T(8,128)(2,1)S(1)}, bf16[32,2048]{1,0:T(8,128)(2,1)S(1)}, u32[]{:S(2)}, u32[]{:S(2)}) collective-permute-start(bf16[32,2048]{1,0:T(8,128)(2,1)S(1)} %get-tuple-element.132), channel_id=1, source_target_pairs={{0,2},{1,3},{2,0},{3,1},{4,6},{5,7},{6,4},{7,5},{8,10},{9,11},{10,... | collective-permute-start | bytes 393224 | tf_op jit(solution)/shard_map/ppermute | solution.py:452
  81.0 6.4 %collective-permute-start.24 = (bf16[32,2048]{1,0:T(8,128)(2,1)S(1)}, bf16[32,2048]{1,0:T(8,128)(2,1)S(1)}, u32[]{:S(2)}, u32[]{:S(2)}) collective-permute-start(bf16[32,2048]{1,0:T(8,128)(2,1)S(1)} %get-tuple-element.136), channel_id=1, source_target_pairs={{0,2},{1,3},{2,0},{3,1},{4,6},{5,7},{6,4},{7,5},{8,10},{9,11},{10,... | collective-permute-start | bytes 393224 | tf_op jit(solution)/shard_map/ppermute | solution.py:452
  81.1 6.4 %collective-permute-start.23 = (bf16[32,2048]{1,0:T(8,128)(2,1)S(1)}, bf16[32,2048]{1,0:T(8,128)(2,1)S(1)}, u32[]{:S(2)}, u32[]{:S(2)}) collective-permute-start(bf16[32,2048]{1,0:T(8,128)(2,1)S(1)} %add_convert_fusion), channel_id=1, source_target_pairs={{0,4},{1,5},{2,6},{3,7},{4,0},{5,1},{6,2},{7,3},{8,12},{9,13},{10,... | collective-permute-start | bytes 393224 | tf_op jit(solution)/shard_map/ppermute | solution.py:452
